TPU v7x, 32 devices: a whole 2x2x4 slice. The times are simulated.
32 devices in a mesh: dp: 16 (over z, x, core), tensor: 2 (over y).
Axes of the slice: x: 2, y: 2, z: 4, core: 2. Of those that a mesh axis runs over, the one named last changes fastest.
Arguments:
- layer_input: bfloat16 [8192, 1024], P(('dp', 'tensor')), may hold values from -6 to 6
- input_gain: bfloat16 [1024], replicated, may hold values from 0.5 to 1.5
- middle_gain: bfloat16 [1024], replicated, may hold values from 0.5 to 1.5
- mamba_gate: bfloat16 [1024, 1536], P(None, 'tensor'), may hold values from -0.1875 to 0.1875
- mamba_input: bfloat16 [1024, 1536], P(None, 'tensor'), may hold values from -0.1875 to 0.1875
- step_weight: bfloat16 [1024, 24], P(None, 'tensor'), may hold values from -0.1875 to 0.1875
- state_weight: bfloat16 [1024, 256], replicated, may hold values from -0.046875 to 0.046875
- input_kernel: bfloat16 [4, 1536], P(None, 'tensor'), may hold values from -3 to 3
- input_shift: bfloat16 [1536], P('tensor'), may hold values from -3 to 3
- state_kernel: bfloat16 [4, 256], replicated, may hold values from -3 to 3
- state_shift: bfloat16 [256], replicated, may hold values from -2 to 2
- step_bias: bfloat16 [24], P('tensor'), may hold values from -5 to 0
- decay_log: bfloat16 [24], P('tensor'), may hold values from -1 to 2
- skip_gain: bfloat16 [24], P('tensor'), may hold values from 0.5 to 1.5
- mamba_output: bfloat16 [1536, 1024], P('tensor'), may hold values from -0.15625 to 0.15625
- query_weight: bfloat16 [1024, 512], P(None, 'tensor'), may hold values from -0.1875 to 0.1875
- keyvalue_weight: bfloat16 [1024, 256], replicated, may hold values from -0.1875 to 0.1875
- context_weight: bfloat16 [512, 1024], P('tensor'), may hold values from -0.75 to 0.75
- gate_weight: bfloat16 [1024, 2048], P(None, 'tensor'), may hold values from -0.1875 to 0.1875
- up_weight: bfloat16 [1024, 2048], P(None, 'tensor'), may hold values from -0.1875 to 0.1875
- down_weight: bfloat16 [2048, 1024], P('tensor'), may hold values from -0.125 to 0.125
- cotangent: bfloat16 [8192, 1024], P(('dp', 'tensor')), may hold values from -6 to 6
Outputs:
- layer_output: bfloat16 [8192, 1024], P(('dp', 'tensor'))
- input_grad: float32 [8192, 1024], P(('dp', 'tensor'))
- grad_input_gain: float32 [1024], replicated
- grad_middle_gain: float32 [1024], replicated
- grad_mamba_gate: float32 [1024, 1536], P(None, 'tensor')
- grad_mamba_input: float32 [1024, 1536], P(None, 'tensor')
- grad_step_weight: float32 [1024, 24], P(None, 'tensor')
- grad_state_weight: float32 [1024, 256], replicated
- grad_input_kernel: float32 [4, 1536], P(None, 'tensor')
- grad_input_shift: float32 [1536], P('tensor')
- grad_state_kernel: float32 [4, 256], replicated
- grad_state_shift: float32 [256], replicated
- grad_step_bias: float32 [24], P('tensor')
- grad_decay_log: float32 [24], P('tensor')
- grad_skip_gain: float32 [24], P('tensor')
- grad_mamba_output: float32 [1536, 1024], P('tensor')
- grad_query_weight: float32 [1024, 512], P(None, 'tensor')
- grad_keyvalue_weight: float32 [1024, 256], replicated
- grad_context_weight: float32 [512, 1024], P('tensor')
- grad_gate_weight: float32 [1024, 2048], P(None, 'tensor')
- grad_up_weight: float32 [1024, 2048], P(None, 'tensor')
- grad_down_weight: float32 [2048, 1024], P('tensor')
All inputs are finite; a program needn't handle non-finite values.
Results may differ from a plain program's by a relative error of at most 0.03.
Values may be sent and summed in bfloat16 or wider, within the bound.
No kernel may reach another device: no remote copies, remote signals or barrier semaphores. Data moves between devices by JAX's collectives and lax.ppermute only.
A program may use at most 192 MiB of HBM per device.

v0:
```python
from functools import partial

import jax
import jax.numpy as jnp
from jax import lax
from jax.sharding import PartitionSpec as P

HD = 64
HQ = 8
KVH = 2
SPAN = 128
SEQ_LEN = 1024


EPSILON = 1e-05
ROPE_BASE = 10000.0
PRECISE = lax.Precision.HIGHEST


def ssd_block(rates, carry, block):
    inputs, steps, entry, readout = block
    logdec = steps * rates[None, :]
    cumul = jnp.cumsum(logdec, axis=0)
    count = cumul.shape[0]
    lower = jnp.arange(count)[:, None] >= jnp.arange(count)[None, :]
    spread = cumul[:, None, :] - cumul[None, :, :]
    decay = jnp.exp(jnp.where(lower[:, :, None], spread, -jnp.inf))
    intersection = jnp.dot(readout, entry.T, precision=PRECISE)
    scaled = inputs * steps[:, :, None]
    within = jnp.einsum("ijh,jhp->ihp", decay * intersection[:, :, None], scaled, precision=PRECISE)
    carried = (
        jnp.einsum("in,hpn->ihp", readout, carry, precision=PRECISE) * jnp.exp(cumul)[:, :, None]
    )
    tail = jnp.exp(cumul[-1][None, :] - cumul)
    update = jnp.einsum("jhp,jn->hpn", scaled * tail[:, :, None], entry, precision=PRECISE)
    carry = carry * jnp.exp(cumul[-1])[:, None, None] + update
    return (carry, within + carried)


def ssd_sequence(inputs, steps, entry, readout, rates):
    length = inputs.shape[0]
    blocks = length // SPAN
    heads = inputs.shape[1]
    size = inputs.shape[2]
    states = entry.shape[1]
    stacked = (
        inputs.reshape(blocks, SPAN, heads, size),
        steps.reshape(blocks, SPAN, heads),
        entry.reshape(blocks, SPAN, states),
        readout.reshape(blocks, SPAN, states),
    )
    start = jnp.zeros((heads, size, states), jnp.float32)
    final, outputs = lax.scan(jax.checkpoint(partial(ssd_block, rates)), start, stacked)
    return outputs.reshape(length, heads, size)


def ssm_branch(
    ssm_gate,
    ssm_input,
    step_raw,
    state_raw,
    input_kernel,
    input_shift,
    state_kernel,
    state_shift,
    step_bias,
    decay_log,
    skip_gain,
    length,
):
    total_rows = ssm_input.shape[0]
    seqs = total_rows // length
    heads = step_raw.shape[1]
    channels = ssm_input.shape[1]
    head_size = channels // heads
    states = state_raw.shape[1] // 2
    joined = jnp.concatenate([ssm_input, state_raw], axis=1)
    kernel = jnp.concatenate([input_kernel, state_kernel], axis=1)
    shifts = jnp.concatenate([input_shift, state_shift], axis=0)
    taps = kernel.shape[0]
    seqwise = joined.reshape(seqs, length, joined.shape[1])
    padded = jnp.pad(seqwise, ((0, 0), (taps - 1, 0), (0, 0)))
    filtered = jnp.broadcast_to(shifts, seqwise.shape)
    for index in range(taps):
        filtered = filtered + kernel[index] * padded[:, index : index + length]
    active = jax.nn.silu(filtered)
    inputs = active[:, :, :channels].reshape(seqs, length, heads, head_size)
    entry = active[:, :, channels : channels + states]
    readout = active[:, :, channels + states :]
    steps = jax.nn.softplus(step_raw.reshape(seqs, length, heads) + step_bias)
    rates = -jnp.exp(decay_log)
    outputs = lax.map(
        lambda group: ssd_sequence(group[0], group[1], group[2], group[3], rates),
        (inputs, steps, entry, readout),
    )
    outputs = outputs + skip_gain[:, None] * inputs
    return outputs.reshape(total_rows, channels) * jax.nn.silu(ssm_gate)


def rope_tables(length, head_size):
    half = head_size // 2
    freqs = ROPE_BASE ** (-jnp.arange(half, dtype=jnp.float32) * 2.0 / head_size)
    angles = jnp.arange(length, dtype=jnp.float32)[:, None] * freqs[None, :]
    return (jnp.cos(angles), jnp.sin(angles))


def rotate(vecs, cosine, sine):
    half = vecs.shape[-1] // 2
    first = vecs[..., :half]
    second = vecs[..., half:]
    cosine = cosine[:, None, :]
    sine = sine[:, None, :]
    return jnp.concatenate(
        [first * cosine - second * sine, second * cosine + first * sine], axis=-1
    )


def unrotate(vecs, cosine, sine):
    half = vecs.shape[-1] // 2
    first = vecs[..., :half]
    second = vecs[..., half:]
    cosine = cosine[:, None, :]
    sine = sine[:, None, :]
    return jnp.concatenate(
        [first * cosine + second * sine, second * cosine - first * sine], axis=-1
    )


def forward_dot(left, right):
    return jnp.dot(left, right, preferred_element_type=jnp.float32)


def inner_rows(left, right):
    return lax.dot_general(
        left, right, (((0,), (0,)), ((), ())), preferred_element_type=jnp.float32
    )


def against(left, right):
    return lax.dot_general(
        left, right, (((1,), (1,)), ((), ())), preferred_element_type=jnp.float32
    )


def norm_back(upstream, gain, normal, factor):
    scaled = upstream * gain
    return factor * (scaled - normal * jnp.mean(scaled * normal, axis=-1, keepdims=True))


def body(
    layer_input,
    input_gain,
    middle_gain,
    mamba_gate,
    mamba_input,
    step_weight,
    state_weight,
    input_kernel,
    input_shift,
    state_kernel,
    state_shift,
    step_bias,
    decay_log,
    skip_gain,
    mamba_output,
    query_weight,
    keyvalue_weight,
    context_weight,
    gate_weight,
    up_weight,
    down_weight,
    cotangent,
):
    rows = layer_input.astype(jnp.float32)
    gain_first = input_gain.astype(jnp.float32)
    gain_second = middle_gain.astype(jnp.float32)
    factor_first = lax.rsqrt(jnp.mean(rows * rows, axis=-1, keepdims=True) + EPSILON)
    normal_first = rows * factor_first
    normed = (normal_first * gain_first).astype(jnp.bfloat16)
    whole = lax.all_gather(normed, "tensor", axis=0, tiled=True)
    group = whole.shape[0]
    length = min(SEQ_LEN, group)
    seqs = group // length
    heads_here = query_weight.shape[1] // HD
    kv_head = lax.axis_index("tensor") * heads_here // (HQ // KVH)
    key_cols = lax.dynamic_slice_in_dim(keyvalue_weight, kv_head * HD, HD, 1)
    value_cols = lax.dynamic_slice_in_dim(keyvalue_weight, (KVH + kv_head) * HD, HD, 1)
    pair_weight = jnp.concatenate([key_cols, value_cols], axis=1)
    gate_raw = forward_dot(whole, mamba_gate)
    input_raw = forward_dot(whole, mamba_input)
    step_raw = forward_dot(whole, step_weight)
    state_raw = forward_dot(whole, state_weight)
    query_raw = forward_dot(whole, query_weight)
    pair_raw = forward_dot(whole, pair_weight)
    small = (
        input_kernel.astype(jnp.float32),
        input_shift.astype(jnp.float32),
        state_kernel.astype(jnp.float32),
        state_shift.astype(jnp.float32),
        step_bias.astype(jnp.float32),
        decay_log.astype(jnp.float32),
        skip_gain.astype(jnp.float32),
    )
    gated, mamba_pull = jax.vjp(
        partial(ssm_branch, length=length),
        gate_raw,
        input_raw,
        step_raw,
        state_raw,
        small[0],
        small[1],
        small[2],
        small[3],
        small[4],
        small[5],
        small[6],
    )
    gated_low = gated.astype(jnp.bfloat16)
    cosine, sine = rope_tables(length, HD)
    scale = HD ** (-0.5)
    causal = jnp.arange(length)[:, None] >= jnp.arange(length)[None, :]

    def attend_forward(seq):
        query_seq, pair_seq = seq
        query = rotate(query_seq.reshape(length, heads_here, HD), cosine, sine).astype(jnp.bfloat16)
        key = rotate(pair_seq[:, None, :HD], cosine, sine)[:, 0].astype(jnp.bfloat16)
        value = pair_seq[:, HD:].astype(jnp.bfloat16)
        scores = jnp.einsum("ihd,jd->hij", query, key, preferred_element_type=jnp.float32) * scale
        scores = jnp.where(causal[None], scores, -jnp.inf)
        peak = jnp.max(scores, axis=-1, keepdims=True)
        total = jnp.log(jnp.sum(jnp.exp(scores - peak), axis=-1, keepdims=True)) + peak
        probs = jnp.exp(scores - total).astype(jnp.bfloat16)
        context = jnp.einsum("hij,jd->ihd", probs, value, preferred_element_type=jnp.float32)
        return (
            context.reshape(length, heads_here * HD).astype(jnp.bfloat16),
            total,
            query,
            key,
            value,
        )

    context_seq, totals, queries, keys, values = lax.map(
        attend_forward,
        (query_raw.reshape(seqs, length, heads_here * HD), pair_raw.reshape(seqs, length, 2 * HD)),
    )
    context_rows = context_seq.reshape(group, heads_here * HD)
    left = gated_low
    right = context_rows
    mixed = lax.psum_scatter(
        (forward_dot(left, mamba_output) + forward_dot(right, context_weight)).astype(jnp.bfloat16),
        "tensor",
        scatter_dimension=0,
        tiled=True,
    ).astype(jnp.float32)
    resid = rows + mixed
    factor_second = lax.rsqrt(jnp.mean(resid * resid, axis=-1, keepdims=True) + EPSILON)
    normal_second = resid * factor_second
    normed_mid = (normal_second * gain_second).astype(jnp.bfloat16)
    whole_mid = lax.all_gather(normed_mid, "tensor", axis=0, tiled=True)
    gate = forward_dot(whole_mid, gate_weight)
    upper = forward_dot(whole_mid, up_weight)
    sigmoid_gate = jax.nn.sigmoid(gate)
    silu_gate = gate * sigmoid_gate
    hidden = (silu_gate * upper).astype(jnp.bfloat16)
    feed = lax.psum_scatter(
        forward_dot(hidden, down_weight).astype(jnp.bfloat16),
        "tensor",
        scatter_dimension=0,
        tiled=True,
    ).astype(jnp.float32)
    layer_output = (resid + feed).astype(jnp.bfloat16)
    cotan = cotangent.astype(jnp.float32)
    grad_all = lax.all_gather(cotangent, "tensor", axis=0, tiled=True)
    grad_down = inner_rows(hidden, grad_all)
    grad_hidden = against(grad_all, down_weight)
    slope = sigmoid_gate * (1.0 + gate * (1.0 - sigmoid_gate))
    grad_gate_low = (grad_hidden * upper * slope).astype(jnp.bfloat16)
    grad_upper_low = (grad_hidden * silu_gate).astype(jnp.bfloat16)
    grad_gate = inner_rows(whole_mid, grad_gate_low)
    grad_up = inner_rows(whole_mid, grad_upper_low)
    left = grad_gate_low
    right = grad_upper_low
    back_mid = lax.psum_scatter(
        (against(left, gate_weight) + against(right, up_weight)).astype(jnp.bfloat16),
        "tensor",
        scatter_dimension=0,
        tiled=True,
    ).astype(jnp.float32)
    grad_middle = jnp.sum(back_mid * normal_second, axis=0)
    grad_resid = cotan + norm_back(back_mid, gain_second, normal_second, factor_second)
    resid_low = grad_resid.astype(jnp.bfloat16)
    mixer_all = lax.all_gather(resid_low, "tensor", axis=0, tiled=True)
    grad_mamba_out = inner_rows(gated_low, mixer_all)
    grad_gated = against(mixer_all, mamba_output)
    pulled = mamba_pull(grad_gated)
    grad_gate_raw = pulled[0].astype(jnp.bfloat16)
    grad_input_raw = pulled[1].astype(jnp.bfloat16)
    grad_step_raw = pulled[2].astype(jnp.bfloat16)
    grad_state_raw = pulled[3].astype(jnp.bfloat16)
    grad_context_w = inner_rows(context_rows, mixer_all)
    grad_context = against(mixer_all, context_weight).astype(jnp.bfloat16)

    def attend_backward(seq):
        grad_seq, query, key, value, total = seq
        grad_seq = grad_seq.reshape(length, heads_here, HD)
        scores = jnp.einsum("ihd,jd->hij", query, key, preferred_element_type=jnp.float32) * scale
        scores = jnp.where(causal[None], scores, -jnp.inf)
        probs = jnp.exp(scores - total)
        grad_value = jnp.einsum(
            "hij,ihd->jd", probs.astype(jnp.bfloat16), grad_seq, preferred_element_type=jnp.float32
        )
        grad_probs = jnp.einsum("ihd,jd->hij", grad_seq, value, preferred_element_type=jnp.float32)
        grad_scores = (
            probs * (grad_probs - jnp.sum(probs * grad_probs, axis=-1, keepdims=True))
        ).astype(jnp.bfloat16)
        grad_query = (
            jnp.einsum("hij,jd->ihd", grad_scores, key, preferred_element_type=jnp.float32) * scale
        )
        grad_key = (
            jnp.einsum("hij,ihd->jd", grad_scores, query, preferred_element_type=jnp.float32)
            * scale
        )
        grad_query = (
            unrotate(grad_query, cosine, sine).reshape(length, heads_here * HD).astype(jnp.bfloat16)
        )
        grad_key = unrotate(grad_key[:, None, :], cosine, sine)[:, 0]
        return (grad_query, jnp.concatenate([grad_key, grad_value], axis=1).astype(jnp.bfloat16))

    grad_query_seq, grad_pair_seq = lax.map(
        attend_backward,
        (grad_context.reshape(seqs, length, heads_here * HD), queries, keys, values, totals),
    )
    grad_query_raw = grad_query_seq.reshape(group, heads_here * HD)
    grad_pair_raw = grad_pair_seq.reshape(group, 2 * HD)
    grad_mamba_gate = inner_rows(whole, grad_gate_raw)
    grad_mamba_input = inner_rows(whole, grad_input_raw)
    grad_step = inner_rows(whole, grad_step_raw)
    grad_state = inner_rows(whole, grad_state_raw)
    grad_query = inner_rows(whole, grad_query_raw)
    grad_pair = inner_rows(whole, grad_pair_raw)
    grad_keyvalue = jnp.zeros(keyvalue_weight.shape, jnp.float32)
    grad_keyvalue = lax.dynamic_update_slice_in_dim(
        grad_keyvalue, grad_pair[:, :HD], kv_head * HD, 1
    )
    grad_keyvalue = lax.dynamic_update_slice_in_dim(
        grad_keyvalue, grad_pair[:, HD:], (KVH + kv_head) * HD, 1
    )
    total = against(grad_gate_raw, mamba_gate)
    total = total + against(grad_input_raw, mamba_input)
    total = total + against(grad_step_raw, step_weight)
    total = total + against(grad_state_raw, state_weight)
    total = total + against(grad_query_raw, query_weight)
    total = total + against(grad_pair_raw, pair_weight)
    back_in = lax.psum_scatter(
        total.astype(jnp.bfloat16), "tensor", scatter_dimension=0, tiled=True
    ).astype(jnp.float32)
    grad_first = jnp.sum(back_in * normal_first, axis=0)
    input_grad = grad_resid + norm_back(back_in, gain_first, normal_first, factor_first)
    (
        grad_mamba_gate,
        grad_mamba_input,
        grad_step,
        grad_in_kernel,
        grad_in_shift,
        grad_bias,
        grad_decay,
        grad_skip,
        grad_mamba_out,
        grad_query,
        grad_context_w,
        grad_gate,
        grad_up,
        grad_down,
    ) = (
        lax.psum(grad_mamba_gate.astype(jnp.bfloat16), "dp").astype(jnp.float32),
        lax.psum(grad_mamba_input.astype(jnp.bfloat16), "dp").astype(jnp.float32),
        lax.psum(grad_step.astype(jnp.bfloat16), "dp").astype(jnp.float32),
        lax.psum(pulled[4].astype(jnp.bfloat16), "dp").astype(jnp.float32),
        lax.psum(pulled[5].astype(jnp.bfloat16), "dp").astype(jnp.float32),
        lax.psum(pulled[8].astype(jnp.bfloat16), "dp").astype(jnp.float32),
        lax.psum(pulled[9].astype(jnp.bfloat16), "dp").astype(jnp.float32),
        lax.psum(pulled[10].astype(jnp.bfloat16), "dp").astype(jnp.float32),
        lax.psum(grad_mamba_out.astype(jnp.bfloat16), "dp").astype(jnp.float32),
        lax.psum(grad_query.astype(jnp.bfloat16), "dp").astype(jnp.float32),
        lax.psum(grad_context_w.astype(jnp.bfloat16), "dp").astype(jnp.float32),
        lax.psum(grad_gate.astype(jnp.bfloat16), "dp").astype(jnp.float32),
        lax.psum(grad_up.astype(jnp.bfloat16), "dp").astype(jnp.float32),
        lax.psum(grad_down.astype(jnp.bfloat16), "dp").astype(jnp.float32),
    )
    grad_first, grad_middle, grad_state, grad_st_kernel, grad_st_shift, grad_keyvalue = lax.psum(
        (grad_first, grad_middle, grad_state, pulled[6], pulled[7], grad_keyvalue), ("dp", "tensor")
    )
    return (
        layer_output,
        input_grad,
        grad_first,
        grad_middle,
        grad_mamba_gate,
        grad_mamba_input,
        grad_step,
        grad_state,
        grad_in_kernel,
        grad_in_shift,
        grad_st_kernel,
        grad_st_shift,
        grad_bias,
        grad_decay,
        grad_skip,
        grad_mamba_out,
        grad_query,
        grad_keyvalue,
        grad_context_w,
        grad_gate,
        grad_up,
        grad_down,
    )


def solution(mesh):
    in_specs = (
        P(("dp", "tensor"), None),
        P(),
        P(),
        P(None, "tensor"),
        P(None, "tensor"),
        P(None, "tensor"),
        P(),
        P(None, "tensor"),
        P("tensor"),
        P(),
        P(),
        P("tensor"),
        P("tensor"),
        P("tensor"),
        P("tensor", None),
        P(None, "tensor"),
        P(),
        P("tensor", None),
        P(None, "tensor"),
        P(None, "tensor"),
        P("tensor", None),
        P(("dp", "tensor"), None),
    )
    out_specs = (
        P(("dp", "tensor"), None),
        P(("dp", "tensor"), None),
        P(),
        P(),
        P(None, "tensor"),
        P(None, "tensor"),
        P(None, "tensor"),
        P(),
        P(None, "tensor"),
        P("tensor"),
        P(),
        P(),
        P("tensor"),
        P("tensor"),
        P("tensor"),
        P("tensor", None),
        P(None, "tensor"),
        P(),
        P("tensor", None),
        P(None, "tensor"),
        P(None, "tensor"),
        P("tensor", None),
    )
    return jax.shard_map(body, mesh=mesh, in_specs=in_specs, out_specs=out_specs, check_vma=False)
```

profile of v0, /device:TPU:0, one launch (start us, length us, event | category | flops | bytes accessed | tf_op | source)
XLA Modules:
  0.0 1033.4 jit_solution(5247655265679134732)
XLA Ops:
  18.0 18.2 %all-gather.5.cloned.1.call-done = bf16[512,1024]{1,0:T(8,128)(2,1)} async-done(((bf16[256,1024]{1,0:T(8,128)(2,1)}), bf16[512,1024]{1,0:T(8,128)(2,1)}) %all-gather.5.cloned.1.call-update) | async-done | bytes 1048592 | tf_op jit(solution)/shard_map/all_gather | solution.py:180
  38.1 2.6 fusion.162
  41.9 2.6 fusion.84
  49.3 3.0 copy.156
  52.3 2.9 reshape.610
  55.2 2.8 copy.158
  59.5 121.1 %while.52 = (s32[]{:T(128)}, f32[12,64,128]{2,1,0:T(8,128)S(1)}, f32[4,128,12,64]{1,0,3,2:T(4,128)}, f32[4,12,64,128]{3,2,1,0:T(8,128)}, f32[4,128,12]{2,1,0:T(8...) while((s32[]{:T(128)}, f32[12,64,128]{2,1,0:T(8,128)S(1)}, ...), condition=%wide.region_3.4_spmd.clone, body=%wide.region_1.3_spmd.clone.sunk | while | flops 479921664 | bytes 5272568 | solution.py:53
  75.4 3.6 fusion.289
  79.0 10.7 %dynamic_update_slice.121 = f32[4,128,12,64]{1,0,3,2:T(4,128)} dynamic-update-slice(f32[4,128,12,64]{1,0,3,2:T(4,128)} %get-tuple-element.1086, f32[1,128,12,64]{1,0,3,2:T(1,128)} %bitcast.380, s32[]{:T(128)S(6)} %copy.256, s32[]{:T(128)} %constant.255.clone.1..sunk, s32[]{:T(128)} %constant.255.clone.1..sunk, s32[]{:T(128)} %constant.255.clone.1..sunk) | dynamic-update-slice | bytes 786436 | tf_op jit(solution)/shard_map/jvp()/while/body/eval_jaxpr/while/body/jit(dynamic_update_index_in_dim)/dynamic_update_slice | solution.py:53
  105.7 3.6 fusion.289
  109.3 10.7 %dynamic_update_slice.121 = f32[4,128,12,64]{1,0,3,2:T(4,128)} dynamic-update-slice(f32[4,128,12,64]{1,0,3,2:T(4,128)} %get-tuple-element.1086, f32[1,128,12,64]{1,0,3,2:T(1,128)} %bitcast.380, s32[]{:T(128)S(6)} %copy.256, s32[]{:T(128)} %constant.255.clone.1..sunk, s32[]{:T(128)} %constant.255.clone.1..sunk, s32[]{:T(128)} %constant.255.clone.1..sunk) | dynamic-update-slice | bytes 786436 | tf_op jit(solution)/shard_map/jvp()/while/body/eval_jaxpr/while/body/jit(dynamic_update_index_in_dim)/dynamic_update_slice | solution.py:53
  136.0 3.6 fusion.289
  139.6 10.7 %dynamic_update_slice.121 = f32[4,128,12,64]{1,0,3,2:T(4,128)} dynamic-update-slice(f32[4,128,12,64]{1,0,3,2:T(4,128)} %get-tuple-element.1086, f32[1,128,12,64]{1,0,3,2:T(1,128)} %bitcast.380, s32[]{:T(128)S(6)} %copy.256, s32[]{:T(128)} %constant.255.clone.1..sunk, s32[]{:T(128)} %constant.255.clone.1..sunk, s32[]{:T(128)} %constant.255.clone.1..sunk) | dynamic-update-slice | bytes 786436 | tf_op jit(solution)/shard_map/jvp()/while/body/eval_jaxpr/while/body/jit(dynamic_update_index_in_dim)/dynamic_update_slice | solution.py:53
  166.3 3.6 fusion.289
  169.9 10.7 %dynamic_update_slice.121 = f32[4,128,12,64]{1,0,3,2:T(4,128)} dynamic-update-slice(f32[4,128,12,64]{1,0,3,2:T(4,128)} %get-tuple-element.1086, f32[1,128,12,64]{1,0,3,2:T(1,128)} %bitcast.380, s32[]{:T(128)S(6)} %copy.256, s32[]{:T(128)} %constant.255.clone.1..sunk, s32[]{:T(128)} %constant.255.clone.1..sunk, s32[]{:T(128)} %constant.255.clone.1..sunk) | dynamic-update-slice | bytes 786436 | tf_op jit(solution)/shard_map/jvp()/while/body/eval_jaxpr/while/body/jit(dynamic_update_index_in_dim)/dynamic_update_slice | solution.py:53
  180.6 2.7 copy.219
  183.3 3.1 copy.160
  199.7 20.4 %reduce-scatter.5.cloned.1.call-done = bf16[256,1024]{1,0:T(8,128)(2,1)} async-done(((bf16[512,1024]{1,0:T(8,128)(2,1)}), bf16[256,1024]{1,0:T(8,128)(2,1)}) %reduce-scatter.5.cloned.1.call-update) | async-done | bytes 524304 | tf_op jit(solution)/shard_map/reduce_scatter | solution.py:249
  224.5 20.4 %all-gather.7.cloned.1.call-done = bf16[512,1024]{1,0:T(8,128)(2,1)} async-done(((bf16[256,1024]{1,0:T(8,128)(2,1)}), bf16[512,1024]{1,0:T(8,128)(2,1)}) %all-gather.7.cloned.1.call-update) | async-done | bytes 1048592 | tf_op jit(solution)/shard_map/all_gather | solution.py:259
  244.9 4.6 fusion.166
  249.6 2.6 fusion.167
  252.1 15.6 %all-gather.9.cloned.1.call-done = bf16[512,1024]{1,0:T(8,128)(2,1)} async-done(((bf16[256,1024]{1,0:T(8,128)(2,1)}), bf16[512,1024]{1,0:T(8,128)(2,1)}) %all-gather.9.cloned.1.call-update) | async-done | bytes 1048592 | tf_op jit(solution)/shard_map/all_gather | solution.py:273
  267.7 5.6 multiply_convert_fusion
  278.1 20.4 %reduce-scatter.9.cloned.1.call-done = bf16[256,1024]{1,0:T(8,128)(2,1)} async-done(((bf16[512,1024]{1,0:T(8,128)(2,1)}), bf16[256,1024]{1,0:T(8,128)(2,1)}) %reduce-scatter.9.cloned.1.call-update) | async-done | bytes 524304 | tf_op jit(solution)/shard_map/reduce_scatter | solution.py:283
  303.3 21.4 %all-gather.11.cloned.1.call-done = bf16[512,1024]{1,0:T(8,128)(2,1)} async-done(((bf16[256,1024]{1,0:T(8,128)(2,1)}), bf16[512,1024]{1,0:T(8,128)(2,1)}) %all-gather.11.cloned.1.call-update) | async-done | bytes 1048592 | tf_op jit(solution)/shard_map/all_gather | solution.py:292
  326.5 4.1 fusion.101
  330.7 4.1 fusion.74
  335.5 3.8 fusion.89
  339.3 3.0 copy.162
  342.3 2.9 reshape.615
  348.8 219.0 %while.53 = (s32[]{:T(128)}, f32[12]{0:T(128)}, f32[12,64,128]{2,1,0:T(8,128)}, f32[4,128,12,64]{1,0,3,2:T(4,128)}, f32[4,128,12]{2,1,0:T(8,128)}, /*index=5*/f3...) while((s32[]{:T(128)}, f32[12]{0:T(128)}, ...), condition=%wide.region_23.24_spmd.clone, body=%wide.region_11.23_spmd.clone.sunk | while | flops 1137231872 | bytes 13701068 | solution.py:53
  359.2 3.5 fusion.307
  370.7 3.6 multiply_reduce_fusion.16
  378.2 2.6 reduce_window_sum.54
  384.3 10.7 %dynamic_update_slice.125 = f32[4,128,12,64]{1,0,3,2:T(4,128)} dynamic-update-slice(f32[4,128,12,64]{1,0,3,2:T(4,128)} %get-tuple-element.1131, f32[1,128,12,64]{1,0,3,2:T(1,128)} %bitcast.379, s32[]{:T(128)S(6)} %sub.372, s32[]{:T(128)} %constant.255.clone.1..sunk.1, s32[]{:T(128)} %constant.255.clone.1..sunk.1, s32[]{:T(128)} %constant.255.clone.1..sunk.1) | dynamic-update-slice | bytes 786436 | tf_op jit(solution)/shard_map/transpose(jvp())/while/body/eval_jaxpr/while/body/jit(dynamic_update_index_in_dim)/dynamic_update_slice | solution.py:53
  413.7 3.5 fusion.307
  425.2 3.6 multiply_reduce_fusion.16
  432.7 2.6 reduce_window_sum.54
  439.5 10.7 %dynamic_update_slice.125 = f32[4,128,12,64]{1,0,3,2:T(4,128)} dynamic-update-slice(f32[4,128,12,64]{1,0,3,2:T(4,128)} %get-tuple-element.1131, f32[1,128,12,64]{1,0,3,2:T(1,128)} %bitcast.379, s32[]{:T(128)S(6)} %sub.372, s32[]{:T(128)} %constant.255.clone.1..sunk.1, s32[]{:T(128)} %constant.255.clone.1..sunk.1, s32[]{:T(128)} %constant.255.clone.1..sunk.1) | dynamic-update-slice | bytes 786436 | tf_op jit(solution)/shard_map/transpose(jvp())/while/body/eval_jaxpr/while/body/jit(dynamic_update_index_in_dim)/dynamic_update_slice | solution.py:53
  468.8 3.5 fusion.307
  480.3 3.6 multiply_reduce_fusion.16
  487.8 2.6 reduce_window_sum.54
  494.6 10.7 %dynamic_update_slice.125 = f32[4,128,12,64]{1,0,3,2:T(4,128)} dynamic-update-slice(f32[4,128,12,64]{1,0,3,2:T(4,128)} %get-tuple-element.1131, f32[1,128,12,64]{1,0,3,2:T(1,128)} %bitcast.379, s32[]{:T(128)S(6)} %sub.372, s32[]{:T(128)} %constant.255.clone.1..sunk.1, s32[]{:T(128)} %constant.255.clone.1..sunk.1, s32[]{:T(128)} %constant.255.clone.1..sunk.1) | dynamic-update-slice | bytes 786436 | tf_op jit(solution)/shard_map/transpose(jvp())/while/body/eval_jaxpr/while/body/jit(dynamic_update_index_in_dim)/dynamic_update_slice | solution.py:53
  524.0 3.5 fusion.307
  535.5 3.6 multiply_reduce_fusion.16
  543.0 2.6 reduce_window_sum.54
  549.8 10.7 %dynamic_update_slice.125 = f32[4,128,12,64]{1,0,3,2:T(4,128)} dynamic-update-slice(f32[4,128,12,64]{1,0,3,2:T(4,128)} %get-tuple-element.1131, f32[1,128,12,64]{1,0,3,2:T(1,128)} %bitcast.379, s32[]{:T(128)S(6)} %sub.372, s32[]{:T(128)} %constant.255.clone.1..sunk.1, s32[]{:T(128)} %constant.255.clone.1..sunk.1, s32[]{:T(128)} %constant.255.clone.1..sunk.1) | dynamic-update-slice | bytes 786436 | tf_op jit(solution)/shard_map/transpose(jvp())/while/body/eval_jaxpr/while/body/jit(dynamic_update_index_in_dim)/dynamic_update_slice | solution.py:53
  567.8 2.7 copy.218
  570.5 3.0 copy.167
  576.8 3.9 multiply_reduce_fusion.8
  599.2 3.5 convolution_convert_fusion.6
  603.1 3.9 convolution_convert_fusion.2
  607.0 2.6 convolution_convert_fusion.1
  609.6 2.6 convolution_convert_fusion
  629.1 3.7 dynamic_update_slice.102
  632.8 3.1 dynamic_update_slice.103
  639.0 63.7 %all-reduce.16 = (bf16[1024,12]{0,1:T(8,128)(2,1)S(1)}, bf16[4,768]{1,0:T(4,128)(2,1)S(1)}, bf16[768]{0:T(1024)(128)(2,1)S(1)}, bf16[12]{0:T(256)(128)(2,1)S(1)}...) all-reduce(bf16[1024,12]{0,1:T(8,128)(2,1)S(1)} %convolution_conver, ...), channel_id=1, replica_groups=mesh['dp'=16,'tensor'=2] {'dp'}, use_global_device_ids=true, to_apply=%region_33.34 | all-reduce | flops 16164 | bytes 64656 | tf_op jit(solution)/shard_map/psum | solution.py:377
  707.9 38.7 %all-reduce.14 = (f32[1024]{0:T(1024)}, f32[1024]{0:T(1024)}, f32[4,256]{1,0:T(4,128)}, f32[256]{0:T(256)}) all-reduce(f32[1024]{0:T(1024)S(1)} %get-tuple-element.747, f32[1024]{0:T(1024)S(1)} %copy-done.101, f32[4,256]{1,0:T(4,128)S(1)} %pad_add_fusion.4, f32[256]{0:T(256)S(1)} %copy-done.116), channel_id=1, replica_groups=mesh['dp'=16,'tensor'=2] {'dp','tensor'}, use_global_device_ids=true, to_apply=%region_28.29 | all-reduce | flops 3328 | bytes 26624 | tf_op jit(solution)/shard_map/psum | solution.py:390
  746.6 3.8 fusion.103
  750.4 133.4 %all-reduce.23.cloned.1.call-done = (bf16[1024,768]{1,0:T(8,128)(2,1)}, bf16[1024,768]{1,0:T(8,128)(2,1)}, bf16[768,1024]{1,0:T(8,128)(2,1)}, bf16[1024,256]{1,0...) async-done(((bf16[1024,768]{1,0:T(8,128)(2,1)}, bf16[1024,768]{1,0:T(8,128)(2,1)}, ...) | async-done | bytes 12058640 | tf_op jit(solution)/shard_map/psum | solution.py:375
  883.8 3.4 convert_element_type.236
  893.3 2.5 convert_element_type.256
  898.5 2.5 convert_element_type.260
  901.0 121.8 %all-reduce.21.cloned.1.call-done = (f32[1024,256]{1,0:T(8,128)}, f32[1024,256]{1,0:T(8,128)}) async-done(((f32[1024,256]{1,0:T(8,128)}, f32[1024,256]{1,0:T(8,128)}), (f32[1024,256]{1,0:T(8,128)}, f32[1024,256]{1,0:T(8,128)})) %all-reduce.21.cloned.1.call-update) | async-done | bytes 2097168 | tf_op jit(solution)/shard_map/psum | solution.py:390
  (643 shorter events, 313.0 us)
Async XLA Ops:
  7.2 260.5 %copy-start = (bf16[1024,1024]{1,0:T(8,128)(2,1)S(1)}, bf16[1024,1024]{1,0:T(8,128)(2,1)}, u32[]{:S(2)}) copy-start(bf16[1024,1024]{1,0:T(8,128)(2,1)} %param.46) | copy-start | bytes 6291460
  7.2 5.5 copy-start.123
  7.2 5.5 copy-start.120
  7.2 6.1 copy-start.135
  7.2 6.7 copy-start.122
  7.2 7.4 copy-start.118
  7.3 7.4 copy-start.111
  7.3 8.2 copy-start.62
  7.3 9.2 copy-start.136
  7.3 28.9 %all-gather.5.cloned.1.call-start = ((), (), s32[]{:S(2)}) async-start(), calls=%async_computation.4 | async-start | bytes 1572864 | tf_op jit(solution)/shard_map/all_gather | solution.py:180
  12.0 208.0 %reduce-scatter.5.cloned.1.call-start = ((), (), s32[]{:S(2)}) async-start(), calls=%async_computation.5 | async-start | bytes 1572864 | tf_op jit(solution)/shard_map/reduce_scatter | solution.py:249
  13.3 4.7 copy-start.112
  17.0 24.0 %copy-start.79 = (f32[1,1024]{1,0:T(1,128)}, f32[1,1024]{1,0:T(1,128)S(1)}, u32[]{:S(2)}) copy-start(f32[1,1024]{1,0:T(1,128)S(1)} %get-tuple-element.859) | copy-start | bytes 12292
  17.0 24.0 %copy-start.81 = (f32[1,1024]{1,0:T(1,128)}, f32[1,1024]{1,0:T(1,128)S(1)}, u32[]{:S(2)}) copy-start(f32[1,1024]{1,0:T(1,128)S(1)} %get-tuple-element.860) | copy-start | bytes 12292
  17.0 24.0 %copy-start.83 = (f32[1,1024]{1,0:T(1,128)}, f32[1,1024]{1,0:T(1,128)S(1)}, u32[]{:S(2)}) copy-start(f32[1,1024]{1,0:T(1,128)S(1)} %get-tuple-element.861) | copy-start | bytes 12292
  17.0 24.0 %copy-start.85 = (f32[1,1024]{1,0:T(1,128)}, f32[1,1024]{1,0:T(1,128)S(1)}, u32[]{:S(2)}) copy-start(f32[1,1024]{1,0:T(1,128)S(1)} %get-tuple-element.862) | copy-start | bytes 12292
  183.2 4.7 copy-start.113
  191.9 138.8 %copy-start.75 = (f32[4,512]{1,0:T(4,128)}, f32[4,512]{1,0:T(4,128)S(1)}, u32[]{:S(2)}) copy-start(f32[4,512]{1,0:T(4,128)S(1)} %log_add_fusion) | copy-start | bytes 24580
  198.1 22.0 %copy-start.6 = (bf16[256,1024]{1,0:T(8,128)(2,1)S(1)}, bf16[256,1024]{1,0:T(8,128)(2,1)}, u32[]{:S(2)}) copy-start(bf16[256,1024]{1,0:T(8,128)(2,1)} %param.26) | copy-start | bytes 1572868
  199.6 45.3 %all-gather.7.cloned.1.call-start = ((), (), s32[]{:S(2)}) async-start(), calls=%async_computation.6 | async-start | bytes 1572864 | tf_op jit(solution)/shard_map/all_gather | solution.py:259
  199.7 101.0 %copy-start.73 = (f32[1024]{0:T(1024)}, f32[1024]{0:T(1024)S(1)}, u32[]{:S(2)}) copy-start(f32[1024]{0:T(1024)S(1)} %convert_element_type.216) | copy-start | bytes 12292
  221.4 79.3 %copy-start.97 = (f32[256]{0:T(256)}, f32[256]{0:T(256)S(1)}, u32[]{:S(2)}) copy-start(f32[256]{0:T(256)S(1)} %add_rsqrt_fusion) | copy-start | bytes 3076
  223.5 44.3 %all-gather.9.cloned.1.call-start = ((), (), s32[]{:S(2)}) async-start(), calls=%async_computation.8 | async-start | bytes 1572864 | tf_op jit(solution)/shard_map/all_gather | solution.py:273
  224.0 74.5 %reduce-scatter.9.cloned.1.call-start = ((), (), s32[]{:S(2)}) async-start(), calls=%async_computation.9 | async-start | bytes 1572864 | tf_op jit(solution)/shard_map/reduce_scatter | solution.py:283
  244.9 4.6 copy-start.132
  267.7 5.7 copy-start.124
  275.8 22.8 %copy-start.13 = (bf16[256,1024]{1,0:T(8,128)(2,1)S(1)}, bf16[256,1024]{1,0:T(8,128)(2,1)}, u32[]{:S(2)}) copy-start(bf16[256,1024]{1,0:T(8,128)(2,1)} %reduce-scatter.5.cloned.1.call-done) | copy-start | bytes 1572868
  278.1 46.6 %all-gather.11.cloned.1.call-start = ((), (), s32[]{:S(2)}) async-start(), calls=%async_computation.10 | async-start | bytes 1572864 | tf_op jit(solution)/shard_map/all_gather | solution.py:292
  300.7 25.8 %copy-start.108 = (f32[256]{0:T(256)}, f32[256]{0:T(256)S(1)}, u32[]{:S(2)}) copy-start(f32[256]{0:T(256)S(1)} %broadcast_multiply_fusion.8) | copy-start | bytes 3076
  300.7 25.8 %copy-start.22 = (pred[512,512]{0,1:T(8,128)(4,1)S(1)}, pred[512,512]{0,1:T(8,128)(4,1)}, u32[]{:S(2)}) copy-start(pred[512,512]{0,1:T(8,128)(4,1)} %iota_compare_fusion.1) | copy-start | bytes 786436
  303.2 402.9 %reduce-scatter.11.cloned.1.call-start = ((), (), s32[]{:S(2)}) async-start(), calls=%async_computation.11 | async-start | bytes 1572864 | tf_op jit(solution)/shard_map/reduce_scatter | solution.py:354
  330.7 4.8 copy-start.145
  357.6 6.5 copy-start.64
  370.7 11.5 %copy-start.50 = (f32[128,12]{0,1:T(8,128)}, f32[128,12]{0,1:T(8,128)S(1)}, u32[]{:S(2)}) copy-start(f32[128,12]{0,1:T(8,128)S(1)} %copy.242) | copy-start | bytes 18436 | tf_op jit(solution)/shard_map/transpose(jvp())/while/body/eval_jaxpr/while
  381.6 14.2 %copy-start.10 = (f32[128,12]{1,0:T(8,128)S(1)}, f32[128,12]{1,0:T(8,128)}, u32[]{:S(2)}) copy-start(f32[128,12]{1,0:T(8,128)} %reduce_window_sum.54) | copy-start | bytes 18436 | tf_op jit(solution)/shard_map/transpose(jvp())/while/body/eval_jaxpr/while
  395.8 5.7 copy-start.20
  412.1 6.5 copy-start.64
  425.2 12.1 %copy-start.50 = (f32[128,12]{0,1:T(8,128)}, f32[128,12]{0,1:T(8,128)S(1)}, u32[]{:S(2)}) copy-start(f32[128,12]{0,1:T(8,128)S(1)} %copy.242) | copy-start | bytes 18436 | tf_op jit(solution)/shard_map/transpose(jvp())/while/body/eval_jaxpr/while
  436.1 14.8 %copy-start.10 = (f32[128,12]{1,0:T(8,128)S(1)}, f32[128,12]{1,0:T(8,128)}, u32[]{:S(2)}) copy-start(f32[128,12]{1,0:T(8,128)} %reduce_window_sum.54) | copy-start | bytes 18436 | tf_op jit(solution)/shard_map/transpose(jvp())/while/body/eval_jaxpr/while
  451.0 5.7 copy-start.20
  467.3 6.5 copy-start.64
  480.3 12.1 %copy-start.50 = (f32[128,12]{0,1:T(8,128)}, f32[128,12]{0,1:T(8,128)S(1)}, u32[]{:S(2)}) copy-start(f32[128,12]{0,1:T(8,128)S(1)} %copy.242) | copy-start | bytes 18436 | tf_op jit(solution)/shard_map/transpose(jvp())/while/body/eval_jaxpr/while
  491.3 14.8 %copy-start.10 = (f32[128,12]{1,0:T(8,128)S(1)}, f32[128,12]{1,0:T(8,128)}, u32[]{:S(2)}) copy-start(f32[128,12]{1,0:T(8,128)} %reduce_window_sum.54) | copy-start | bytes 18436 | tf_op jit(solution)/shard_map/transpose(jvp())/while/body/eval_jaxpr/while
  506.1 5.7 copy-start.20
  522.4 6.5 copy-start.64
  535.5 12.1 %copy-start.50 = (f32[128,12]{0,1:T(8,128)}, f32[128,12]{0,1:T(8,128)S(1)}, u32[]{:S(2)}) copy-start(f32[128,12]{0,1:T(8,128)S(1)} %copy.242) | copy-start | bytes 18436 | tf_op jit(solution)/shard_map/transpose(jvp())/while/body/eval_jaxpr/while
  546.4 14.8 %copy-start.10 = (f32[128,12]{1,0:T(8,128)S(1)}, f32[128,12]{1,0:T(8,128)}, u32[]{:S(2)}) copy-start(f32[128,12]{1,0:T(8,128)} %reduce_window_sum.54) | copy-start | bytes 18436 | tf_op jit(solution)/shard_map/transpose(jvp())/while/body/eval_jaxpr/while
  561.3 5.7 copy-start.20
  581.9 6.3 copy-start.9
  583.1 5.2 copy-start.24
  599.1 147.5 %reduce-scatter.7.cloned.1.call-start = ((), (), s32[]{:S(2)}) async-start(), calls=%async_computation.7 | async-start | bytes 1572864 | tf_op jit(solution)/shard_map/reduce_scatter | solution.py:265
  602.7 281.0 %all-reduce.23.cloned.1.call-start = ((), (), s32[]{:S(2)}) async-start(), calls=%async_computation.13 | async-start | bytes 24117248 | tf_op jit(solution)/shard_map/psum | solution.py:375
  621.4 401.4 %all-reduce.21.cloned.1.call-start = ((), (), s32[]{:S(2)}) async-start(), calls=%async_computation.12 | async-start | bytes 4194304 | tf_op jit(solution)/shard_map/psum | solution.py:390
  638.3 67.8 %copy-start.88 = (f32[1024]{0:T(1024)S(1)}, f32[1024]{0:T(1024)}, u32[]{:S(2)}) copy-start(f32[1024]{0:T(1024)} %get-tuple-element.740) | copy-start | bytes 12292
  638.3 67.8 %copy-start.90 = (f32[1024]{0:T(1024)S(1)}, f32[1024]{0:T(1024)}, u32[]{:S(2)}) copy-start(f32[1024]{0:T(1024)} %get-tuple-element.741) | copy-start | bytes 12292
  638.3 67.8 %copy-start.92 = (f32[1024]{0:T(1024)S(1)}, f32[1024]{0:T(1024)}, u32[]{:S(2)}) copy-start(f32[1024]{0:T(1024)} %get-tuple-element.742) | copy-start | bytes 12292
  638.3 67.8 %copy-start.94 = (f32[1024]{0:T(1024)S(1)}, f32[1024]{0:T(1024)}, u32[]{:S(2)}) copy-start(f32[1024]{0:T(1024)} %get-tuple-element.744) | copy-start | bytes 12292
  638.3 67.8 %copy-start.78 = (f32[1024]{0:T(1024)S(1)}, f32[1024]{0:T(1024)}, u32[]{:S(2)}) copy-start(f32[1024]{0:T(1024)} %copy-done.77) | copy-start | bytes 12292
  638.3 67.8 %copy-start.106 = (f32[256]{0:T(256)S(1)}, f32[256]{0:T(256)}, u32[]{:S(2)}) copy-start(f32[256]{0:T(256)} %copy-done.105) | copy-start | bytes 3076
  638.3 69.5 %copy-start.101 = (f32[1024]{0:T(1024)S(1)}, f32[1024]{0:T(1024)}, u32[]{:S(2)}) copy-start(f32[1024]{0:T(1024)} %get-tuple-element.745) | copy-start | bytes 12292
  638.3 69.5 %copy-start.116 = (f32[256]{0:T(256)S(1)}, f32[256]{0:T(256)}, u32[]{:S(2)}) copy-start(f32[256]{0:T(256)} %split.27) | copy-start | bytes 3076
  638.3 108.2 %copy-start.74 = (f32[1024]{0:T(1024)S(1)}, f32[1024]{0:T(1024)}, u32[]{:S(2)}) copy-start(f32[1024]{0:T(1024)} %copy-done.73) | copy-start | bytes 12292
  638.4 108.2 %copy-start.98 = (f32[256]{0:T(256)S(1)}, f32[256]{0:T(256)}, u32[]{:S(2)}) copy-start(f32[256]{0:T(256)} %copy-done.97) | copy-start | bytes 3076
  638.4 108.2 %copy-start.109 = (f32[256]{0:T(256)S(1)}, f32[256]{0:T(256)}, u32[]{:S(2)}) copy-start(f32[256]{0:T(256)} %copy-done.108) | copy-start | bytes 3076
  (108 other events, 238.8 us)
Sparse Core Ops, SparseCore 0:
  12.2 23.9 all-gather.4
  199.7 20.3 reduce-scatter.4
  223.6 21.2 all-gather.6
  246.4 21.2 all-gather.8
  278.2 20.3 reduce-scatter.8
  303.3 21.2 all-gather.10
  599.2 20.3 reduce-scatter.10
  622.5 20.3 reduce-scatter.6
  650.1 233.6 all-reduce.22
  889.1 133.5 all-reduce.20
where the time goes:
time: 1050 us; the launch traced here: 1030 us
  waiting for transfers between devices  372 us (35%)
  local copies, waits for them, and re-layouts  228 us (22%)
  matrix products  181 us (17%)
  other arithmetic  133 us (13%)
  blocking collectives  102 us (10%)
  between operations  16 us (2%)
    psum x1, waiting for transfers between devices, body(): lax.psum(grad_mamba_gate.astype(jnp.bfloat16), 'dp').astype(jnp.float32)  133 us
    psum x1, waiting for transfers between devices, body(): lax.psum((grad_first, grad_middle, grad_state, pulled[6], pulled[7], grad...  122 us
    dynamic_update_slice x8, local copies, waits for them, and re-layouts, ssd_sequence(): lax.scan(jax.checkpoint(partial(ssd_block, rates)), start, stacked)  85.5 us
    psum x1, blocking collectives, body(): lax.psum(grad_step.astype(jnp.bfloat16), 'dp').astype(jnp.float32)  63.7 us
    dot_general x12, matrix products, ssd_block(): jnp.einsum('ijh,jhp->ihp', decay * intersection[:, :, None], scaled, prec...  42.6 us
    psum x1, blocking collectives, body(): lax.psum((grad_first, grad_middle, grad_state, pulled[6], pulled[7], grad...  38.7 us
    unnamed x288, local copies, waits for them, and re-layouts  24.2 us
    dot_general x11, matrix products, against(): lax.dot_general(left, right, (((1,), (1,)), ((), ())), preferred_element_...  24 us
  transfers between devices with their start and end apart: 10, of which 8 were waited for; matrix products, arithmetic and copies ran while one was open for 7% of the time, Pallas kernels for 0%

commit v1 on v0

--- a/solution.py
+++ b/solution.py
@@ -147,7 +147,104 @@
     return factor * (scaled - normal * jnp.mean(scaled * normal, axis=-1, keepdims=True))
 
 
+def bit_pairs(size, bit):
+    return [(index, index ^ (1 << bit)) for index in range(size)]
+
+
+def split_half(part, bit, size):
+    side = (lax.axis_index("dp") >> bit) & 1
+    halves = part.reshape(2, part.shape[0] // 2, part.shape[1])
+    keep = lax.dynamic_index_in_dim(halves, side, 0, False)
+    give = lax.dynamic_index_in_dim(halves, 1 - side, 0, False)
+    got = lax.ppermute(give, "dp", bit_pairs(size, bit))
+    return (keep.astype(jnp.float32) + got.astype(jnp.float32)).astype(jnp.bfloat16)
+
+
+def join_half(part, bit, size):
+    side = (lax.axis_index("dp") >> bit) & 1
+    got = lax.ppermute(part, "dp", bit_pairs(size, bit))
+    return jnp.where(
+        side == 0, jnp.concatenate([part, got], axis=0), jnp.concatenate([got, part], axis=0)
+    )
+
+
+def bit_order(size, swapped):
+    order = list(range(size.bit_length() - 1))
+    if swapped and len(order) > 2:
+        order[1], order[2] = order[2], order[1]
+    return order
+
+
+def sum_dp(part, size, swapped, middle=None):
+    if size & (size - 1) or part.shape[0] % size:
+        part = lax.psum(part, "dp")
+        return part if middle is None else middle(part)
+    order = bit_order(size, swapped)
+    for bit in order:
+        part = split_half(part, bit, size)
+    if middle is not None:
+        part = middle(part)
+    for bit in reversed(order):
+        part = join_half(part, bit, size)
+    return part
+
+
+def other(part):
+    return lax.ppermute(part, "tensor", [(0, 1), (1, 0)])
+
+
+def all_rows(part, shards):
+    if shards != 2:
+        return lax.all_gather(part, "tensor", axis=0, tiled=True)
+    got = other(part)
+    return jnp.where(
+        lax.axis_index("tensor") == 0,
+        jnp.concatenate([part, got], axis=0),
+        jnp.concatenate([got, part], axis=0),
+    )
+
+
+def sum_all(part, shards):
+    if shards != 2:
+        return lax.psum(part, "tensor").astype(jnp.float32)
+    return part.astype(jnp.float32) + other(part).astype(jnp.float32)
+
+
+def sum_own(part, shards):
+    if shards != 2:
+        return lax.psum_scatter(part, "tensor", scatter_dimension=0, tiled=True).astype(jnp.float32)
+    me = lax.axis_index("tensor")
+    halves = part.reshape(2, part.shape[0] // 2, part.shape[1])
+    keep = lax.dynamic_index_in_dim(halves, me, 0, False)
+    got = other(lax.dynamic_index_in_dim(halves, 1 - me, 0, False))
+    return keep.astype(jnp.float32) + got.astype(jnp.float32)
+
+
+def own_rows(part, rows):
+    return lax.dynamic_slice_in_dim(part, lax.axis_index("tensor") * rows, rows, 0)
+
+
+def column_pack(vectors, rows):
+    flat = jnp.concatenate([item.reshape(-1) for item in vectors])
+    width = -(-flat.shape[0] // rows)
+    return jnp.pad(flat, (0, width * rows - flat.shape[0])).reshape(width, rows).T
+
+
+def column_unpack(packed, shapes):
+    flat = packed.T.reshape(-1)
+    out, start = [], 0
+    for shape in shapes:
+        count = 1
+        for size in shape:
+            count *= size
+        out.append(flat[start : start + count].reshape(shape))
+        start += count
+    return out
+
+
 def body(
+    dp_size,
+    shards,
     layer_input,
     input_gain,
     middle_gain,
@@ -171,13 +268,15 @@
     down_weight,
     cotangent,
 ):
-    rows = layer_input.astype(jnp.float32)
+    own = layer_input.shape[0]
+    rows_low = all_rows(layer_input, shards)
+    cotan_low = all_rows(cotangent, shards)
+    rows = rows_low.astype(jnp.float32)
     gain_first = input_gain.astype(jnp.float32)
     gain_second = middle_gain.astype(jnp.float32)
     factor_first = lax.rsqrt(jnp.mean(rows * rows, axis=-1, keepdims=True) + EPSILON)
     normal_first = rows * factor_first
-    normed = (normal_first * gain_first).astype(jnp.bfloat16)
-    whole = lax.all_gather(normed, "tensor", axis=0, tiled=True)
+    whole = (normal_first * gain_first).astype(jnp.bfloat16)
     group = whole.shape[0]
     length = min(SEQ_LEN, group)
     seqs = group // length
@@ -244,60 +343,50 @@
         (query_raw.reshape(seqs, length, heads_here * HD), pair_raw.reshape(seqs, length, 2 * HD)),
     )
     context_rows = context_seq.reshape(group, heads_here * HD)
-    left = gated_low
-    right = context_rows
-    mixed = lax.psum_scatter(
-        (forward_dot(left, mamba_output) + forward_dot(right, context_weight)).astype(jnp.bfloat16),
-        "tensor",
-        scatter_dimension=0,
-        tiled=True,
-    ).astype(jnp.float32)
-    resid = rows + mixed
+    mixed_part = forward_dot(gated_low, mamba_output) + forward_dot(context_rows, context_weight)
+    resid = rows + sum_all(mixed_part.astype(jnp.bfloat16), shards)
     factor_second = lax.rsqrt(jnp.mean(resid * resid, axis=-1, keepdims=True) + EPSILON)
     normal_second = resid * factor_second
-    normed_mid = (normal_second * gain_second).astype(jnp.bfloat16)
-    whole_mid = lax.all_gather(normed_mid, "tensor", axis=0, tiled=True)
+    whole_mid = (normal_second * gain_second).astype(jnp.bfloat16)
     gate = forward_dot(whole_mid, gate_weight)
     upper = forward_dot(whole_mid, up_weight)
     sigmoid_gate = jax.nn.sigmoid(gate)
     silu_gate = gate * sigmoid_gate
     hidden = (silu_gate * upper).astype(jnp.bfloat16)
-    feed = lax.psum_scatter(
-        forward_dot(hidden, down_weight).astype(jnp.bfloat16),
-        "tensor",
-        scatter_dimension=0,
-        tiled=True,
-    ).astype(jnp.float32)
-    layer_output = (resid + feed).astype(jnp.bfloat16)
-    cotan = cotangent.astype(jnp.float32)
-    grad_all = lax.all_gather(cotangent, "tensor", axis=0, tiled=True)
-    grad_down = inner_rows(hidden, grad_all)
-    grad_hidden = against(grad_all, down_weight)
+    grad_hidden = against(cotan_low, down_weight)
     slope = sigmoid_gate * (1.0 + gate * (1.0 - sigmoid_gate))
     grad_gate_low = (grad_hidden * upper * slope).astype(jnp.bfloat16)
     grad_upper_low = (grad_hidden * silu_gate).astype(jnp.bfloat16)
-    grad_gate = inner_rows(whole_mid, grad_gate_low)
-    grad_up = inner_rows(whole_mid, grad_upper_low)
-    left = grad_gate_low
-    right = grad_upper_low
-    back_mid = lax.psum_scatter(
-        (against(left, gate_weight) + against(right, up_weight)).astype(jnp.bfloat16),
-        "tensor",
-        scatter_dimension=0,
-        tiled=True,
-    ).astype(jnp.float32)
-    grad_middle = jnp.sum(back_mid * normal_second, axis=0)
-    grad_resid = cotan + norm_back(back_mid, gain_second, normal_second, factor_second)
-    resid_low = grad_resid.astype(jnp.bfloat16)
-    mixer_all = lax.all_gather(resid_low, "tensor", axis=0, tiled=True)
-    grad_mamba_out = inner_rows(gated_low, mixer_all)
+    back_part = (against(grad_gate_low, gate_weight) + against(grad_upper_low, up_weight)).astype(
+        jnp.bfloat16
+    )
+    back_mid = sum_all(back_part, shards)
+    feed = sum_own(forward_dot(hidden, down_weight).astype(jnp.bfloat16), shards)
+    layer_output = (own_rows(resid, own) + feed).astype(jnp.bfloat16)
+    grad_down = inner_rows(hidden, cotan_low).astype(jnp.bfloat16)
+    grad_gate = inner_rows(whole_mid, grad_gate_low).astype(jnp.bfloat16)
+    grad_up = inner_rows(whole_mid, grad_upper_low).astype(jnp.bfloat16)
+    grad_gate = sum_dp(grad_gate, dp_size, False)
+    grad_up = sum_dp(grad_up, dp_size, True)
+    grad_down = sum_dp(grad_down, dp_size, False)
+    grad_middle = jnp.sum(back_part.astype(jnp.float32) * normal_second, axis=0)
+    grad_resid = cotan_low.astype(jnp.float32) + norm_back(
+        back_mid, gain_second, normal_second, factor_second
+    )
+    mixer_all = grad_resid.astype(jnp.bfloat16)
+    grad_mixer_out = inner_rows(
+        jnp.concatenate([gated_low, context_rows], axis=1), mixer_all
+    ).astype(jnp.bfloat16)
+    grad_mixer_out = sum_dp(grad_mixer_out, dp_size, True)
+    ssm_rows = gated_low.shape[1]
+    grad_mamba_out = grad_mixer_out[:ssm_rows]
+    grad_context_w = grad_mixer_out[ssm_rows:]
     grad_gated = against(mixer_all, mamba_output)
     pulled = mamba_pull(grad_gated)
     grad_gate_raw = pulled[0].astype(jnp.bfloat16)
     grad_input_raw = pulled[1].astype(jnp.bfloat16)
     grad_step_raw = pulled[2].astype(jnp.bfloat16)
     grad_state_raw = pulled[3].astype(jnp.bfloat16)
-    grad_context_w = inner_rows(context_rows, mixer_all)
     grad_context = against(mixer_all, context_weight).astype(jnp.bfloat16)
 
     def attend_backward(seq):
@@ -332,73 +421,95 @@
     )
     grad_query_raw = grad_query_seq.reshape(group, heads_here * HD)
     grad_pair_raw = grad_pair_seq.reshape(group, 2 * HD)
-    grad_mamba_gate = inner_rows(whole, grad_gate_raw)
-    grad_mamba_input = inner_rows(whole, grad_input_raw)
-    grad_step = inner_rows(whole, grad_step_raw)
-    grad_state = inner_rows(whole, grad_state_raw)
-    grad_query = inner_rows(whole, grad_query_raw)
-    grad_pair = inner_rows(whole, grad_pair_raw)
-    grad_keyvalue = jnp.zeros(keyvalue_weight.shape, jnp.float32)
-    grad_keyvalue = lax.dynamic_update_slice_in_dim(
-        grad_keyvalue, grad_pair[:, :HD], kv_head * HD, 1
-    )
-    grad_keyvalue = lax.dynamic_update_slice_in_dim(
-        grad_keyvalue, grad_pair[:, HD:], (KVH + kv_head) * HD, 1
-    )
     total = against(grad_gate_raw, mamba_gate)
     total = total + against(grad_input_raw, mamba_input)
     total = total + against(grad_step_raw, step_weight)
     total = total + against(grad_state_raw, state_weight)
     total = total + against(grad_query_raw, query_weight)
     total = total + against(grad_pair_raw, pair_weight)
-    back_in = lax.psum_scatter(
-        total.astype(jnp.bfloat16), "tensor", scatter_dimension=0, tiled=True
-    ).astype(jnp.float32)
-    grad_first = jnp.sum(back_in * normal_first, axis=0)
-    input_grad = grad_resid + norm_back(back_in, gain_first, normal_first, factor_first)
-    (
-        grad_mamba_gate,
+    total_low = total.astype(jnp.bfloat16)
+    grad_first = jnp.sum(total_low.astype(jnp.float32) * normal_first, axis=0)
+    width = whole.shape[1]
+    gate_cols = grad_gate_raw.shape[1]
+    query_cols = grad_query_raw.shape[1]
+    input_cols = grad_input_raw.shape[1]
+    state_cols = grad_state_raw.shape[1]
+    step_cols = grad_step_raw.shape[1]
+    pair_cols = grad_pair_raw.shape[1]
+
+    own_vectors = (pulled[4], pulled[5], pulled[8], pulled[9], pulled[10])
+    shared_vectors = (grad_first, grad_middle, pulled[6], pulled[7])
+    own_pack = column_pack(own_vectors, width).astype(jnp.bfloat16)
+    shared_pack = column_pack(shared_vectors, width).astype(jnp.bfloat16)
+    own_width = own_pack.shape[1]
+    shared_width = shared_pack.shape[1]
+
+    early = inner_rows(whole, jnp.concatenate([grad_gate_raw, grad_query_raw], axis=1))
+    early = sum_dp(early.astype(jnp.bfloat16), dp_size, False)
+
+    split_pairs = shards == KVH
+    late = inner_rows(
+        whole,
+        jnp.concatenate([grad_input_raw, grad_state_raw, grad_pair_raw, grad_step_raw], axis=1),
+    ).astype(jnp.bfloat16)
+    marks = (input_cols, input_cols + state_cols, input_cols + state_cols + pair_cols)
+    late_pair = late[:, marks[1] : marks[2]]
+    if not split_pairs:
+        spread = jnp.zeros((width, 2 * KVH * HD), jnp.bfloat16)
+        spread = lax.dynamic_update_slice_in_dim(spread, late_pair[:, :HD], kv_head * HD, 1)
+        late_pair = lax.dynamic_update_slice_in_dim(
+            spread, late_pair[:, HD:], (KVH + kv_head) * HD, 1
+        )
+    tail = jnp.concatenate(
+        [late[:, input_cols : marks[1]], late_pair, shared_pack, late[:, marks[2] :], own_pack],
+        axis=1,
+    )
+    sent = state_cols + late_pair.shape[1] + shared_width
+
+    def over_tensor(part):
+        shared, rest = part[:, :sent], part[:, sent:]
+        if not split_pairs:
+            return jnp.concatenate([lax.psum(shared, "tensor"), rest], axis=1)
+        got = other(shared)
+        first = lax.axis_index("tensor") == 0
+        low = jnp.where(first, shared, got)[:, state_cols : state_cols + pair_cols]
+        high = jnp.where(first, got, shared)[:, state_cols : state_cols + pair_cols]
+        both = (shared.astype(jnp.float32) + got.astype(jnp.float32)).astype(jnp.bfloat16)
+        return jnp.concatenate(
+            [
+                both[:, :state_cols],
+                low[:, :HD],
+                high[:, :HD],
+                low[:, HD:],
+                high[:, HD:],
+                both[:, state_cols + pair_cols :],
+                rest,
+            ],
+            axis=1,
+        )
+
+    tail = sum_dp(tail, dp_size, True, over_tensor)
+    grad_mamba_input = sum_dp(late[:, :input_cols], dp_size, False)
+    back_in = sum_own(total_low, shards)
+    normal_own = own_rows(normal_first, own)
+    factor_own = own_rows(factor_first, own)
+    input_grad = own_rows(grad_resid, own) + norm_back(back_in, gain_first, normal_own, factor_own)
+    after = state_cols + keyvalue_weight.shape[1]
+    grad_first, grad_middle, grad_st_kernel, grad_st_shift = column_unpack(
+        tail[:, after : after + shared_width], [item.shape for item in shared_vectors]
+    )
+    after = after + shared_width
+    grad_step = tail[:, after : after + step_cols]
+    grad_in_kernel, grad_in_shift, grad_bias, grad_decay, grad_skip = column_unpack(
+        tail[:, after + step_cols :], [item.shape for item in own_vectors]
+    )
+    results = (
+        grad_first,
+        grad_middle,
+        early[:, :gate_cols],
         grad_mamba_input,
         grad_step,
-        grad_in_kernel,
-        grad_in_shift,
-        grad_bias,
-        grad_decay,
-        grad_skip,
-        grad_mamba_out,
-        grad_query,
-        grad_context_w,
-        grad_gate,
-        grad_up,
-        grad_down,
-    ) = (
-        lax.psum(grad_mamba_gate.astype(jnp.bfloat16), "dp").astype(jnp.float32),
-        lax.psum(grad_mamba_input.astype(jnp.bfloat16), "dp").astype(jnp.float32),
-        lax.psum(grad_step.astype(jnp.bfloat16), "dp").astype(jnp.float32),
-        lax.psum(pulled[4].astype(jnp.bfloat16), "dp").astype(jnp.float32),
-        lax.psum(pulled[5].astype(jnp.bfloat16), "dp").astype(jnp.float32),
-        lax.psum(pulled[8].astype(jnp.bfloat16), "dp").astype(jnp.float32),
-        lax.psum(pulled[9].astype(jnp.bfloat16), "dp").astype(jnp.float32),
-        lax.psum(pulled[10].astype(jnp.bfloat16), "dp").astype(jnp.float32),
-        lax.psum(grad_mamba_out.astype(jnp.bfloat16), "dp").astype(jnp.float32),
-        lax.psum(grad_query.astype(jnp.bfloat16), "dp").astype(jnp.float32),
-        lax.psum(grad_context_w.astype(jnp.bfloat16), "dp").astype(jnp.float32),
-        lax.psum(grad_gate.astype(jnp.bfloat16), "dp").astype(jnp.float32),
-        lax.psum(grad_up.astype(jnp.bfloat16), "dp").astype(jnp.float32),
-        lax.psum(grad_down.astype(jnp.bfloat16), "dp").astype(jnp.float32),
-    )
-    grad_first, grad_middle, grad_state, grad_st_kernel, grad_st_shift, grad_keyvalue = lax.psum(
-        (grad_first, grad_middle, grad_state, pulled[6], pulled[7], grad_keyvalue), ("dp", "tensor")
-    )
-    return (
-        layer_output,
-        input_grad,
-        grad_first,
-        grad_middle,
-        grad_mamba_gate,
-        grad_mamba_input,
-        grad_step,
-        grad_state,
+        tail[:, :state_cols],
         grad_in_kernel,
         grad_in_shift,
         grad_st_kernel,
@@ -407,13 +518,14 @@
         grad_decay,
         grad_skip,
         grad_mamba_out,
-        grad_query,
-        grad_keyvalue,
+        early[:, gate_cols:],
+        tail[:, state_cols : state_cols + keyvalue_weight.shape[1]],
         grad_context_w,
         grad_gate,
         grad_up,
         grad_down,
     )
+    return (layer_output, input_grad) + tuple(item.astype(jnp.float32) for item in results)
 
 
 def solution(mesh):
@@ -465,4 +577,5 @@
         P(None, "tensor"),
         P("tensor", None),
     )
-    return jax.shard_map(body, mesh=mesh, in_specs=in_specs, out_specs=out_specs, check_vma=False)
+    run = partial(body, mesh.shape["dp"], mesh.shape["tensor"])
+    return jax.shard_map(run, mesh=mesh, in_specs=in_specs, out_specs=out_specs, check_vma=False)

time: 1050 us -> 765 us (0.73)
  waiting for transfers between devices: 372 us -> 167 us
  blocking collectives: 102 us -> 0 us
  starting transfers between devices: 1.07 us -> 62.2 us
  matrix products: 181 us -> 144 us
  between operations: 16 us -> 2.95 us
  other arithmetic: 133 us -> 145 us
    psum x2 -> x0, waiting for transfers between devices: 255 us -> none  [the longest x1 133 us: body(): lax.psum(grad_mamba_gate.astype(jnp.bfloat16), 'dp').astype(jnp.float32)]
    ppermute x0 -> x63, waiting for transfers between devices: none -> 167 us  [the longest x28 67 us: join_half(): got = lax.ppermute(part, 'dp', bit_pairs(size, bit))]
    psum x2 -> x0, blocking collectives: 102 us -> none  [the longest x1 63.7 us: body(): lax.psum(grad_step.astype(jnp.bfloat16), 'dp').astype(jnp.float32)]
    all_gather x4 -> x0, waiting for transfers between devices: 75.6 us -> none  [the longest x1 21.4 us: body(): mixer_all = lax.all_gather(resid_low, 'tensor', axis=0, tiled=True)]
    ppermute x0 -> x63, starting transfers between devices: none -> 62.2 us  [the longest x28 34 us: split_half(): got = lax.ppermute(give, 'dp', bit_pairs(size, bit))]
    reduce_scatter x4 -> x0, waiting for transfers between devices: 40.8 us -> none  [the longest x1 20.4 us: body(): lax.psum_scatter((against(left, gate_weight) + against(right, up_weight))...]
    convert_element_type x18 -> x48, other arithmetic: 26.8 us -> 45.6 us  [the longest x16 25.4 us: body(): item.astype(jnp.float32)]
    squeeze x0 -> x27, local copies, waits for them, and re-layouts: none -> 15.4 us  [the longest x24 13.8 us: split_half(): give = lax.dynamic_index_in_dim(halves, 1 - side, 0, False)]
  transfers between devices with their start and end apart: 10 -> 63, of which waited for: 8 -> 27; matrix products, arithmetic and copies ran while one was open for 7% -> 44% of each run, Pallas kernels for 0% -> 0%
where the time goes in v1:
time: 765 us; the launch traced here: 751 us
  local copies, waits for them, and re-layouts  229 us (30%)
  waiting for transfers between devices  167 us (22%)
  other arithmetic  145 us (19%)
  matrix products  144 us (19%)
  starting transfers between devices  62.2 us (8%)
    dynamic_update_slice x8, local copies, waits for them, and re-layouts, ssd_sequence(): lax.scan(jax.checkpoint(partial(ssd_block, rates)), start, stacked)  85.4 us
    ppermute x28, waiting for transfers between devices, join_half(): got = lax.ppermute(part, 'dp', bit_pairs(size, bit))  67 us
    ppermute x7, waiting for transfers between devices, other(): return lax.ppermute(part, 'tensor', [(0, 1), (1, 0)])  51.5 us
    ppermute x28, waiting for transfers between devices, split_half(): got = lax.ppermute(give, 'dp', bit_pairs(size, bit))  48.8 us
    dot_general x12, matrix products, ssd_block(): jnp.einsum('ijh,jhp->ihp', decay * intersection[:, :, None], scaled, prec...  34.5 us
    ppermute x28, starting transfers between devices, split_half(): got = lax.ppermute(give, 'dp', bit_pairs(size, bit))  34 us
    dot_general x11, matrix products, against(): lax.dot_general(left, right, (((1,), (1,)), ((), ())), preferred_element_...  28 us
    unnamed x252, local copies, waits for them, and re-layouts  27.2 us
  transfers between devices with their start and end apart: 63, of which 27 were waited for; matrix products, arithmetic and copies ran while one was open for 44% of the time, Pallas kernels for 0%

profile of v1, /device:TPU:0, one launch (start us, length us, event | category | flops | bytes accessed | tf_op | source)
XLA Modules:
  0.0 750.6 jit_solution(13496546781261394258)
XLA Ops:
  0.7 3.0 collective-permute-start
  22.1 2.6 fusion.95
  29.6 3.0 copy.363
  32.6 2.7 reshape.809
  35.3 2.8 copy.365
  39.5 121.2 %while.52 = (s32[]{:T(128)}, f32[12,64,128]{2,1,0:T(8,128)S(1)}, f32[4,128,12,64]{1,0,3,2:T(4,128)}, f32[4,12,64,128]{3,2,1,0:T(8,128)}, f32[4,128,12]{2,1,0:T(8...) while((s32[]{:T(128)}, f32[12,64,128]{2,1,0:T(8,128)S(1)}, ...), condition=%wide.region_3.4_spmd.clone, body=%wide.region_1.3_spmd.clone.sunk | while | flops 479921664 | bytes 5272568 | solution.py:53
  55.5 3.6 fusion.314
  59.1 10.7 %dynamic_update_slice.113 = f32[4,128,12,64]{1,0,3,2:T(4,128)} dynamic-update-slice(f32[4,128,12,64]{1,0,3,2:T(4,128)} %get-tuple-element.1318, f32[1,128,12,64]{1,0,3,2:T(1,128)} %bitcast.579, s32[]{:T(128)S(6)} %copy.509, s32[]{:T(128)} %constant.412.clone.1..sunk, s32[]{:T(128)} %constant.412.clone.1..sunk, s32[]{:T(128)} %constant.412.clone.1..sunk) | dynamic-update-slice | bytes 786436 | tf_op jit(solution)/shard_map/jvp()/while/body/eval_jaxpr/while/body/jit(dynamic_update_index_in_dim)/dynamic_update_slice | solution.py:53
  85.8 3.6 fusion.314
  89.4 10.7 %dynamic_update_slice.113 = f32[4,128,12,64]{1,0,3,2:T(4,128)} dynamic-update-slice(f32[4,128,12,64]{1,0,3,2:T(4,128)} %get-tuple-element.1318, f32[1,128,12,64]{1,0,3,2:T(1,128)} %bitcast.579, s32[]{:T(128)S(6)} %copy.509, s32[]{:T(128)} %constant.412.clone.1..sunk, s32[]{:T(128)} %constant.412.clone.1..sunk, s32[]{:T(128)} %constant.412.clone.1..sunk) | dynamic-update-slice | bytes 786436 | tf_op jit(solution)/shard_map/jvp()/while/body/eval_jaxpr/while/body/jit(dynamic_update_index_in_dim)/dynamic_update_slice | solution.py:53
  116.1 3.6 fusion.314
  119.7 10.7 %dynamic_update_slice.113 = f32[4,128,12,64]{1,0,3,2:T(4,128)} dynamic-update-slice(f32[4,128,12,64]{1,0,3,2:T(4,128)} %get-tuple-element.1318, f32[1,128,12,64]{1,0,3,2:T(1,128)} %bitcast.579, s32[]{:T(128)S(6)} %copy.509, s32[]{:T(128)} %constant.412.clone.1..sunk, s32[]{:T(128)} %constant.412.clone.1..sunk, s32[]{:T(128)} %constant.412.clone.1..sunk) | dynamic-update-slice | bytes 786436 | tf_op jit(solution)/shard_map/jvp()/while/body/eval_jaxpr/while/body/jit(dynamic_update_index_in_dim)/dynamic_update_slice | solution.py:53
  146.3 3.6 fusion.314
  149.9 10.7 %dynamic_update_slice.113 = f32[4,128,12,64]{1,0,3,2:T(4,128)} dynamic-update-slice(f32[4,128,12,64]{1,0,3,2:T(4,128)} %get-tuple-element.1318, f32[1,128,12,64]{1,0,3,2:T(1,128)} %bitcast.579, s32[]{:T(128)S(6)} %copy.509, s32[]{:T(128)} %constant.412.clone.1..sunk, s32[]{:T(128)} %constant.412.clone.1..sunk, s32[]{:T(128)} %constant.412.clone.1..sunk) | dynamic-update-slice | bytes 786436 | tf_op jit(solution)/shard_map/jvp()/while/body/eval_jaxpr/while/body/jit(dynamic_update_index_in_dim)/dynamic_update_slice | solution.py:53
  160.8 2.7 copy.467
  163.5 3.2 copy.367
  185.0 21.3 %collective-permute-done.1 = bf16[512,1024]{1,0:T(8,128)(2,1)} collective-permute-done((bf16[512,1024]{1,0:T(8,128)(2,1)}, bf16[512,1024]{1,0:T(8,128)(2,1)}, u32[]{:S(2)}, u32[]{:S(2)}) %collective-permute-start.1) | collective-permute-done | bytes 1048608 | tf_op jit(solution)/shard_map/ppermute | solution.py:193
  206.3 2.8 multiply_reduce_fusion.12
  215.7 3.6 multiply_convert_fusion
  231.0 2.9 convolution_convert_fusion.1
  235.2 25.8 %collective-permute-done.2 = bf16[256,1024]{1,0:T(8,128)(2,1)S(1)} collective-permute-done((bf16[256,1024]{1,0:T(8,128)(2,1)S(1)}, bf16[256,1024]{1,0:T(8,128)(2,1)S(1)}, u32[]{:S(2)}, u32[]{:S(2)}) %collective-permute-start.2) | collective-permute-done | bytes 524320 | tf_op jit(solution)/shard_map/ppermute | solution.py:193
  274.8 3.8 fusion.102
  285.9 150.0 %while.53 = (s32[]{:T(128)}, f32[12]{0:T(128)}, f32[12,64,128]{2,1,0:T(8,128)S(1)}, f32[4,128,12,64]{1,0,3,2:T(4,128)}, f32[4,128,12]{2,1,0:T(8,128)}, /*index=5...) while((s32[]{:T(128)}, f32[12]{0:T(128)}, ...), condition=%wide.region_20.21_spmd.clone, body=%wide.region_8.20_spmd.clone.sunk | while | flops 1137231872 | bytes 15576856 | solution.py:53
  297.8 2.7 multiply_reduce_fusion.19
  308.1 10.7 %dynamic_update_slice.117 = f32[4,128,12,64]{1,0,3,2:T(4,128)} dynamic-update-slice(f32[4,128,12,64]{1,0,3,2:T(4,128)} %get-tuple-element.1363, f32[1,128,12,64]{1,0,3,2:T(1,128)S(1)} %bitcast.578, s32[]{:T(128)S(6)} %sub.405, s32[]{:T(128)} %constant.412.clone.1..sunk.1, s32[]{:T(128)} %constant.412.clone.1..sunk.1, s32[]{:T(128)} %constant.412.clone.1..sunk.1) | dynamic-update-slice | bytes 786436 | tf_op jit(solution)/shard_map/transpose(jvp())/while/body/eval_jaxpr/while/body/jit(dynamic_update_index_in_dim)/dynamic_update_slice | solution.py:53
  334.8 2.7 multiply_reduce_fusion.19
  345.8 10.7 %dynamic_update_slice.117 = f32[4,128,12,64]{1,0,3,2:T(4,128)} dynamic-update-slice(f32[4,128,12,64]{1,0,3,2:T(4,128)} %get-tuple-element.1363, f32[1,128,12,64]{1,0,3,2:T(1,128)S(1)} %bitcast.578, s32[]{:T(128)S(6)} %sub.405, s32[]{:T(128)} %constant.412.clone.1..sunk.1, s32[]{:T(128)} %constant.412.clone.1..sunk.1, s32[]{:T(128)} %constant.412.clone.1..sunk.1) | dynamic-update-slice | bytes 786436 | tf_op jit(solution)/shard_map/transpose(jvp())/while/body/eval_jaxpr/while/body/jit(dynamic_update_index_in_dim)/dynamic_update_slice | solution.py:53
  372.5 2.7 multiply_reduce_fusion.19
  383.4 10.7 %dynamic_update_slice.117 = f32[4,128,12,64]{1,0,3,2:T(4,128)} dynamic-update-slice(f32[4,128,12,64]{1,0,3,2:T(4,128)} %get-tuple-element.1363, f32[1,128,12,64]{1,0,3,2:T(1,128)S(1)} %bitcast.578, s32[]{:T(128)S(6)} %sub.405, s32[]{:T(128)} %constant.412.clone.1..sunk.1, s32[]{:T(128)} %constant.412.clone.1..sunk.1, s32[]{:T(128)} %constant.412.clone.1..sunk.1) | dynamic-update-slice | bytes 786436 | tf_op jit(solution)/shard_map/transpose(jvp())/while/body/eval_jaxpr/while/body/jit(dynamic_update_index_in_dim)/dynamic_update_slice | solution.py:53
  410.1 2.7 multiply_reduce_fusion.19
  421.0 10.7 %dynamic_update_slice.117 = f32[4,128,12,64]{1,0,3,2:T(4,128)} dynamic-update-slice(f32[4,128,12,64]{1,0,3,2:T(4,128)} %get-tuple-element.1363, f32[1,128,12,64]{1,0,3,2:T(1,128)S(1)} %bitcast.578, s32[]{:T(128)S(6)} %sub.405, s32[]{:T(128)} %constant.412.clone.1..sunk.1, s32[]{:T(128)} %constant.412.clone.1..sunk.1, s32[]{:T(128)} %constant.412.clone.1..sunk.1) | dynamic-update-slice | bytes 786436 | tf_op jit(solution)/shard_map/transpose(jvp())/while/body/eval_jaxpr/while/body/jit(dynamic_update_index_in_dim)/dynamic_update_slice | solution.py:53
  442.2 3.9 multiply_reduce_fusion.8
  453.5 2.8 fusion.146
  463.1 3.1 concatenate.279
  466.2 2.8 convolution_convert_fusion
  475.0 6.7 multiply_reduce_fusion.10
  486.7 2.6 constant_dynamic-slice_fusion.8
  490.1 2.6 convolution_convert_fusion.5
  524.2 3.7 collective-permute-done.40
  530.7 4.5 collective-permute-done.48
  548.6 2.7 collective-permute-start.9
  552.1 3.1 collective-permute-done.9
  560.8 3.2 collective-permute-done.49
  565.8 3.1 collective-permute-start.42
  569.6 10.9 %collective-permute-done.11 = bf16[64,532]{0,1:T(8,128)(2,1)S(1)} collective-permute-done((bf16[64,532]{0,1:T(8,128)(2,1)S(1)}, bf16[64,532]{0,1:T(8,128)(2,1)S(1)}, u32[]{:S(2)}, u32[]{:S(2)}) %collective-permute-start.11) | collective-permute-done | bytes 68128 | tf_op jit(solution)/shard_map/ppermute | solution.py:165
  580.7 3.0 collective-permute-start.58
  583.7 10.6 %collective-permute-done.50 = bf16[64,1024]{1,0:T(8,128)(2,1)S(1)} collective-permute-done((bf16[64,1024]{1,0:T(8,128)(2,1)S(1)}, bf16[64,1024]{1,0:T(8,128)(2,1)S(1)}, u32[]{:S(2)}, u32[]{:S(2)}) %collective-permute-start.50) | collective-permute-done | bytes 131104 | tf_op jit(solution)/shard_map/ppermute | solution.py:159
  597.1 3.7 collective-permute-done.12
  600.9 3.0 collective-permute-start.59
  612.4 3.6 collective-permute-done.13
  616.4 11.8 %collective-permute-done.44 = bf16[128,1024]{1,0:T(8,128)(2,1)S(1)} collective-permute-done((bf16[128,1024]{1,0:T(8,128)(2,1)S(1)}, bf16[128,1024]{1,0:T(8,128)(2,1)S(1)}, u32[]{:S(2)}, u32[]{:S(2)}) %collective-permute-start.44) | collective-permute-done | bytes 262176 | tf_op jit(solution)/shard_map/ppermute | solution.py:165
  628.8 5.0 collective-permute-done.25
  636.7 6.6 collective-permute-done.26
  646.1 8.7 %collective-permute-done.27 = bf16[64,768]{1,0:T(8,128)(2,1)S(1)} collective-permute-done((bf16[64,768]{1,0:T(8,128)(2,1)S(1)}, bf16[64,768]{1,0:T(8,128)(2,1)S(1)}, u32[]{:S(2)}, u32[]{:S(2)}) %collective-permute-start.27) | collective-permute-done | bytes 98336 | tf_op jit(solution)/shard_map/ppermute | solution.py:165
  654.9 3.0 collective-permute-start.17
  658.2 6.1 collective-permute-done.28
  666.5 7.0 collective-permute-done.33
  689.6 8.7 %collective-permute-done.19 = bf16[64,1024]{1,0:T(8,128)(2,1)S(1)} collective-permute-done((bf16[64,1024]{1,0:T(8,128)(2,1)S(1)}, bf16[64,1024]{1,0:T(8,128)(2,1)S(1)}, u32[]{:S(2)}, u32[]{:S(2)}) %collective-permute-start.19) | collective-permute-done | bytes 131104 | tf_op jit(solution)/shard_map/ppermute | solution.py:165
  701.8 4.8 collective-permute-done.20
  711.1 2.6 copy.395
  717.5 3.3 collective-permute-done.21
  727.5 4.4 fusion.86
  731.8 5.2 fusion.87
  737.0 3.1 fusion.88
  (831 shorter events, 396.3 us)
Async XLA Ops:
  0.7 215.1 %copy-start = (bf16[1024,1024]{1,0:T(8,128)(2,1)S(1)}, bf16[1024,1024]{1,0:T(8,128)(2,1)}, u32[]{:S(2)}) copy-start(bf16[1024,1024]{1,0:T(8,128)(2,1)} %param.46) | copy-start | bytes 6291460
  0.7 15.2 %collective-permute-start = (bf16[256,1024]{1,0:T(8,128)(2,1)}, bf16[256,1024]{1,0:T(8,128)(2,1)S(1)}, u32[]{:S(2)}, u32[]{:S(2)}) collective-permute-start(bf16[256,1024]{1,0:T(8,128)(2,1)} %param.26), channel_id=1, source_target_pairs={{0,1},{1,0},{2,3},{3,2},{4,5},{5,4},{6,7},{7,6},{8,9},{9,8},{10,11... | collective-permute-start | bytes 1572872 | tf_op jit(solution)/shard_map/ppermute | solution.py:193
  179.8 26.4 %collective-permute-start.1 = (bf16[512,1024]{1,0:T(8,128)(2,1)}, bf16[512,1024]{1,0:T(8,128)(2,1)}, u32[]{:S(2)}, u32[]{:S(2)}) collective-permute-start(bf16[512,1024]{1,0:T(8,128)(2,1)} %add_convert_fusion.2), channel_id=1, source_target_pairs={{0,1},{1,0},{2,3},{3,2},{4,5},{5,4},{6,7},{7,6},{8,9},{9,8},{10,11... | collective-permute-start | bytes 3145736 | tf_op jit(solution)/shard_map/ppermute | solution.py:193
  181.6 34.2 %collective-permute-start.3 = (bf16[256,1024]{1,0:T(8,128)(2,1)}, bf16[256,1024]{1,0:T(8,128)(2,1)}, u32[]{:S(2)}, u32[]{:S(2)}) collective-permute-start(bf16[256,1024]{1,0:T(8,128)(2,1)} %param.47), channel_id=1, source_target_pairs={{0,1},{1,0},{2,3},{3,2},{4,5},{5,4},{6,7},{7,6},{8,9},{9,8},{10,11... | collective-permute-start | bytes 1572872 | tf_op jit(solution)/shard_map/ppermute | solution.py:193
  226.2 35.8 %collective-permute-start.4 = (bf16[512,1024]{1,0:T(8,128)(2,1)S(1)}, bf16[512,1024]{1,0:T(8,128)(2,1)S(1)}, u32[]{:S(2)}, u32[]{:S(2)}) collective-permute-start(bf16[512,1024]{1,0:T(8,128)(2,1)S(1)} %add_convert_fusion.1), channel_id=1, source_target_pairs={{0,1},{1,0},{2,3},{3,2},{4,5},{5,4},{6,7},{7,6},{8,9},{9,8},{10,11... | collective-permute-start | bytes 3145736 | tf_op jit(solution)/shard_map/ppermute | solution.py:193
  227.8 33.2 %collective-permute-start.2 = (bf16[256,1024]{1,0:T(8,128)(2,1)S(1)}, bf16[256,1024]{1,0:T(8,128)(2,1)S(1)}, u32[]{:S(2)}, u32[]{:S(2)}) collective-permute-start(bf16[256,1024]{1,0:T(8,128)(2,1)S(1)} %dynamic-slice_bitcast_fusion.18), channel_id=1, source_target_pairs={{0,1},{1,0},{2,3},{3,2},{4,5},{5,4},{6,7},{7,6},{8,9},{9,8},{10,11... | collective-permute-start | bytes 1572872 | tf_op jit(solution)/shard_map/ppermute | solution.py:193
  229.5 273.5 %collective-permute-start.39 = (bf16[512,1024]{1,0:T(8,128)(2,1)}, bf16[512,1024]{1,0:T(8,128)(2,1)}, u32[]{:S(2)}, u32[]{:S(2)}) collective-permute-start(bf16[512,1024]{1,0:T(8,128)(2,1)} %dynamic-slice_bitcast_fusion.8), channel_id=1, source_target_pairs={{0,2},{2,0},{4,6},{6,4},{8,10},{10,8},{12,14},{14,12},{16,18},{18,... | collective-permute-start | bytes 3145736 | tf_op jit(solution)/shard_map/ppermute | solution.py:159
  230.5 275.8 %collective-permute-start.47 = (bf16[512,1024]{1,0:T(8,128)(2,1)}, bf16[512,1024]{1,0:T(8,128)(2,1)}, u32[]{:S(2)}, u32[]{:S(2)}) collective-permute-start(bf16[512,1024]{1,0:T(8,128)(2,1)} %dynamic-slice_bitcast_fusion.7), channel_id=1, source_target_pairs={{0,2},{2,0},{4,6},{6,4},{8,10},{10,8},{12,14},{14,12},{16,18},{18,... | collective-permute-start | bytes 3145736 | tf_op jit(solution)/shard_map/ppermute | solution.py:159
  235.2 273.8 %collective-permute-start.55 = (bf16[512,1024]{1,0:T(8,128)(2,1)}, bf16[512,1024]{1,0:T(8,128)(2,1)}, u32[]{:S(2)}, u32[]{:S(2)}) collective-permute-start(bf16[512,1024]{1,0:T(8,128)(2,1)} %dynamic-slice_bitcast_fusion.6), channel_id=1, source_target_pairs={{0,2},{2,0},{4,6},{6,4},{8,10},{10,8},{12,14},{14,12},{16,18},{18,... | collective-permute-start | bytes 3145736 | tf_op jit(solution)/shard_map/ppermute | solution.py:159
  483.5 37.6 %collective-permute-start.5 = (bf16[256,1024]{1,0:T(8,128)(2,1)}, bf16[256,1024]{1,0:T(8,128)(2,1)}, u32[]{:S(2)}, u32[]{:S(2)}) collective-permute-start(bf16[256,1024]{1,0:T(8,128)(2,1)} %dynamic-slice_bitcast_fusion.17), channel_id=1, source_target_pairs={{0,1},{1,0},{2,3},{3,2},{4,5},{5,4},{6,7},{7,6},{8,9},{9,8},{10,11... | collective-permute-start | bytes 1572872 | tf_op jit(solution)/shard_map/ppermute | solution.py:193
  490.1 23.4 %collective-permute-start.6 = (bf16[512,404]{0,1:T(8,128)(2,1)}, bf16[512,404]{0,1:T(8,128)(2,1)}, u32[]{:S(2)}, u32[]{:S(2)}) collective-permute-start(bf16[512,404]{0,1:T(8,128)(2,1)} %bitcast.482), channel_id=1, source_target_pairs={{0,2},{2,0},{4,6},{6,4},{8,10},{10,8},{12,14},{14,12},{16,18},{18,... | collective-permute-start | bytes 1241096 | tf_op jit(solution)/shard_map/ppermute | solution.py:159
  503.0 98.0 %collective-permute-start.15 = (bf16[512,1024]{1,0:T(8,128)(2,1)}, bf16[512,1024]{1,0:T(8,128)(2,1)}, u32[]{:S(2)}, u32[]{:S(2)}) collective-permute-start(bf16[512,1024]{1,0:T(8,128)(2,1)} %dynamic-slice_bitcast_fusion.10), channel_id=1, source_target_pairs={{0,2},{2,0},{4,6},{6,4},{8,10},{10,8},{12,14},{14,12},{16,18},{18,... | collective-permute-start | bytes 3145736 | tf_op jit(solution)/shard_map/ppermute | solution.py:159
  506.3 50.6 %collective-permute-start.23 = (bf16[512,768]{1,0:T(8,128)(2,1)}, bf16[512,768]{1,0:T(8,128)(2,1)}, u32[]{:S(2)}, u32[]{:S(2)}) collective-permute-start(bf16[512,768]{1,0:T(8,128)(2,1)} %dynamic-slice_bitcast_fusion.11), channel_id=1, source_target_pairs={{0,2},{2,0},{4,6},{6,4},{8,10},{10,8},{12,14},{14,12},{16,18},{18,... | collective-permute-start | bytes 2359304 | tf_op jit(solution)/shard_map/ppermute | solution.py:159
  508.9 96.9 %collective-permute-start.31 = (bf16[512,1024]{1,0:T(8,128)(2,1)}, bf16[512,1024]{1,0:T(8,128)(2,1)}, u32[]{:S(2)}, u32[]{:S(2)}) collective-permute-start(bf16[512,1024]{1,0:T(8,128)(2,1)} %dynamic-slice_bitcast_fusion.9), channel_id=1, source_target_pairs={{0,2},{2,0},{4,6},{6,4},{8,10},{10,8},{12,14},{14,12},{16,18},{18,... | collective-permute-start | bytes 3145736 | tf_op jit(solution)/shard_map/ppermute | solution.py:159
  513.5 14.4 %collective-permute-start.40 = (bf16[256,1024]{1,0:T(8,128)(2,1)}, bf16[256,1024]{1,0:T(8,128)(2,1)}, u32[]{:S(2)}, u32[]{:S(2)}) collective-permute-start(bf16[256,1024]{1,0:T(8,128)(2,1)} %dynamic-slice_bitcast_fusion.14), channel_id=1, source_target_pairs={{0,4},{2,6},{4,0},{6,2},{8,12},{10,14},{12,8},{14,10},{16,20},{18,... | collective-permute-start | bytes 1572872 | tf_op jit(solution)/shard_map/ppermute | solution.py:159
  521.1 14.0 %collective-permute-start.48 = (bf16[256,1024]{1,0:T(8,128)(2,1)}, bf16[256,1024]{1,0:T(8,128)(2,1)S(1)}, u32[]{:S(2)}, u32[]{:S(2)}) collective-permute-start(bf16[256,1024]{1,0:T(8,128)(2,1)} %dynamic-slice_bitcast_fusion.13), channel_id=1, source_target_pairs={{0,8},{2,10},{4,12},{6,14},{8,0},{10,2},{12,4},{14,6},{16,24},{18,... | collective-permute-start | bytes 1572872 | tf_op jit(solution)/shard_map/ppermute | solution.py:159
  527.9 13.2 %collective-permute-start.56 = (bf16[256,1024]{1,0:T(8,128)(2,1)S(1)}, bf16[256,1024]{1,0:T(8,128)(2,1)S(1)}, u32[]{:S(2)}, u32[]{:S(2)}) collective-permute-start(bf16[256,1024]{1,0:T(8,128)(2,1)S(1)} %copy-done.72), channel_id=1, source_target_pairs={{0,4},{2,6},{4,0},{6,2},{8,12},{10,14},{12,8},{14,10},{16,20},{18,... | collective-permute-start | bytes 1572872 | tf_op jit(solution)/shard_map/ppermute | solution.py:159
  535.1 7.8 %collective-permute-start.7 = (bf16[256,404]{0,1:T(8,128)(2,1)S(1)}, bf16[256,404]{0,1:T(8,128)(2,1)S(1)}, u32[]{:S(2)}, u32[]{:S(2)}) collective-permute-start(bf16[256,404]{0,1:T(8,128)(2,1)S(1)} %bitcast.649), channel_id=1, source_target_pairs={{0,8},{2,10},{4,12},{6,14},{8,0},{10,2},{12,4},{14,6},{16,24},{18,... | collective-permute-start | bytes 620552 | tf_op jit(solution)/shard_map/ppermute | solution.py:159
  541.1 17.3 %collective-permute-start.41 = (bf16[128,1024]{1,0:T(8,128)(2,1)S(1)}, bf16[128,1024]{1,0:T(8,128)(2,1)}, u32[]{:S(2)}, u32[]{:S(2)}) collective-permute-start(bf16[128,1024]{1,0:T(8,128)(2,1)S(1)} %dynamic-slice_bitcast_fusion.22), channel_id=1, source_target_pairs={{0,8},{2,10},{4,12},{6,14},{8,0},{10,2},{12,4},{14,6},{16,24},{18,... | collective-permute-start | bytes 786440 | tf_op jit(solution)/shard_map/ppermute | solution.py:159
  543.5 4.7 collective-permute-start.8
  548.6 6.7 collective-permute-start.9
  555.2 8.8 %collective-permute-start.49 = (bf16[128,1024]{1,0:T(8,128)(2,1)}, bf16[128,1024]{1,0:T(8,128)(2,1)S(1)}, u32[]{:S(2)}, u32[]{:S(2)}) collective-permute-start(bf16[128,1024]{1,0:T(8,128)(2,1)} %dynamic-slice_bitcast_fusion.21), channel_id=1, source_target_pairs={{0,4},{2,6},{4,0},{6,2},{8,12},{10,14},{12,8},{14,10},{16,20},{18,... | collective-permute-start | bytes 786440 | tf_op jit(solution)/shard_map/ppermute | solution.py:159
  556.9 8.9 %collective-permute-start.57 = (bf16[128,1024]{1,0:T(8,128)(2,1)}, bf16[128,1024]{1,0:T(8,128)(2,1)S(1)}, u32[]{:S(2)}, u32[]{:S(2)}) collective-permute-start(bf16[128,1024]{1,0:T(8,128)(2,1)} %dynamic-slice_bitcast_fusion.20), channel_id=1, source_target_pairs={{0,8},{2,10},{4,12},{6,14},{8,0},{10,2},{12,4},{14,6},{16,24},{18,... | collective-permute-start | bytes 786440 | tf_op jit(solution)/shard_map/ppermute | solution.py:159
  558.4 10.6 %collective-permute-start.10 = (bf16[64,388]{0,1:T(8,128)(2,1)S(1)}, bf16[64,388]{0,1:T(8,128)(2,1)S(1)}, u32[]{:S(2)}, u32[]{:S(2)}) collective-permute-start(bf16[64,388]{0,1:T(8,128)(2,1)S(1)} %slice.261), channel_id=1, source_target_pairs={{0,1},{1,0},{2,3},{3,2},{4,5},{5,4},{6,7},{7,6},{8,9},{9,8},{10,11... | collective-permute-start | bytes 149000 | tf_op jit(solution)/shard_map/ppermute | solution.py:193
  564.0 47.2 %collective-permute-start.24 = (bf16[256,768]{1,0:T(8,128)(2,1)}, bf16[256,768]{1,0:T(8,128)(2,1)S(1)}, u32[]{:S(2)}, u32[]{:S(2)}) collective-permute-start(bf16[256,768]{1,0:T(8,128)(2,1)} %dynamic-slice_bitcast_fusion.19), channel_id=1, source_target_pairs={{0,4},{2,6},{4,0},{6,2},{8,12},{10,14},{12,8},{14,10},{16,20},{18,... | collective-permute-start | bytes 1179656 | tf_op jit(solution)/shard_map/ppermute | solution.py:159
  565.8 14.9 %collective-permute-start.42 = (bf16[64,1024]{1,0:T(8,128)(2,1)S(1)}, bf16[64,1024]{1,0:T(8,128)(2,1)S(1)}, u32[]{:S(2)}, u32[]{:S(2)}) collective-permute-start(bf16[64,1024]{1,0:T(8,128)(2,1)S(1)} %dynamic-slice_bitcast_fusion.28), channel_id=1, source_target_pairs={{0,16},{2,18},{4,20},{6,22},{8,24},{10,26},{12,28},{14,30},{16,0},... | collective-permute-start | bytes 393224 | tf_op jit(solution)/shard_map/ppermute | solution.py:159
  569.5 11.0 %collective-permute-start.11 = (bf16[64,532]{0,1:T(8,128)(2,1)S(1)}, bf16[64,532]{0,1:T(8,128)(2,1)S(1)}, u32[]{:S(2)}, u32[]{:S(2)}) collective-permute-start(bf16[64,532]{0,1:T(8,128)(2,1)S(1)} %concatenate.283), channel_id=1, source_target_pairs={{0,16},{2,18},{4,20},{6,22},{8,24},{10,26},{12,28},{14,30},{16,0},... | collective-permute-start | bytes 204296 | tf_op jit(solution)/shard_map/ppermute | solution.py:165
  580.5 13.7 %collective-permute-start.50 = (bf16[64,1024]{1,0:T(8,128)(2,1)S(1)}, bf16[64,1024]{1,0:T(8,128)(2,1)S(1)}, u32[]{:S(2)}, u32[]{:S(2)}) collective-permute-start(bf16[64,1024]{1,0:T(8,128)(2,1)S(1)} %dynamic-slice_bitcast_fusion.27), channel_id=1, source_target_pairs={{0,16},{2,18},{4,20},{6,22},{8,24},{10,26},{12,28},{14,30},{16,0},... | collective-permute-start | bytes 393224 | tf_op jit(solution)/shard_map/ppermute | solution.py:159
  580.7 16.4 %collective-permute-start.58 = (bf16[64,1024]{1,0:T(8,128)(2,1)S(1)}, bf16[64,1024]{1,0:T(8,128)(2,1)S(1)}, u32[]{:S(2)}, u32[]{:S(2)}) collective-permute-start(bf16[64,1024]{1,0:T(8,128)(2,1)S(1)} %dynamic-slice_bitcast_fusion.26), channel_id=1, source_target_pairs={{0,16},{2,18},{4,20},{6,22},{8,24},{10,26},{12,28},{14,30},{16,0},... | collective-permute-start | bytes 393224 | tf_op jit(solution)/shard_map/ppermute | solution.py:159
  594.3 6.6 collective-permute-start.12
  597.1 10.6 %collective-permute-start.43 = (bf16[64,1024]{1,0:T(8,128)(2,1)S(1)}, bf16[64,1024]{1,0:T(8,128)(2,1)S(1)}, u32[]{:S(2)}, u32[]{:S(2)}) collective-permute-start(bf16[64,1024]{1,0:T(8,128)(2,1)S(1)} %fusion.139), channel_id=1, source_target_pairs={{0,16},{2,18},{4,20},{6,22},{8,24},{10,26},{12,28},{14,30},{16,0},... | collective-permute-start | bytes 393224 | tf_op jit(solution)/shard_map/ppermute | solution.py:165
  600.8 8.1 %collective-permute-start.51 = (bf16[64,1024]{1,0:T(8,128)(2,1)S(1)}, bf16[64,1024]{1,0:T(8,128)(2,1)S(1)}, u32[]{:S(2)}, u32[]{:S(2)}) collective-permute-start(bf16[64,1024]{1,0:T(8,128)(2,1)S(1)} %fusion.138), channel_id=1, source_target_pairs={{0,16},{2,18},{4,20},{6,22},{8,24},{10,26},{12,28},{14,30},{16,0},... | collective-permute-start | bytes 393224 | tf_op jit(solution)/shard_map/ppermute | solution.py:165
  600.9 10.1 %collective-permute-start.59 = (bf16[64,1024]{1,0:T(8,128)(2,1)S(1)}, bf16[64,1024]{1,0:T(8,128)(2,1)S(1)}, u32[]{:S(2)}, u32[]{:S(2)}) collective-permute-start(bf16[64,1024]{1,0:T(8,128)(2,1)S(1)} %fusion.137), channel_id=1, source_target_pairs={{0,16},{2,18},{4,20},{6,22},{8,24},{10,26},{12,28},{14,30},{16,0},... | collective-permute-start | bytes 393224 | tf_op jit(solution)/shard_map/ppermute | solution.py:165
  605.9 10.0 %collective-permute-start.13 = (bf16[256,532]{0,1:T(8,128)(2,1)S(1)}, bf16[256,532]{0,1:T(8,128)(2,1)S(1)}, u32[]{:S(2)}, u32[]{:S(2)}) collective-permute-start(bf16[256,532]{0,1:T(8,128)(2,1)S(1)} %maximum_select_fusion.22), channel_id=1, source_target_pairs={{0,8},{2,10},{4,12},{6,14},{8,0},{10,2},{12,4},{14,6},{16,24},{18,... | collective-permute-start | bytes 817160 | tf_op jit(solution)/shard_map/ppermute | solution.py:165
  607.7 35.6 %collective-permute-start.16 = (bf16[256,1024]{1,0:T(8,128)(2,1)S(1)}, bf16[256,1024]{1,0:T(8,128)(2,1)S(1)}, u32[]{:S(2)}, u32[]{:S(2)}) collective-permute-start(bf16[256,1024]{1,0:T(8,128)(2,1)S(1)} %dynamic-slice_bitcast_fusion.16), channel_id=1, source_target_pairs={{0,4},{2,6},{4,0},{6,2},{8,12},{10,14},{12,8},{14,10},{16,20},{18,... | collective-permute-start | bytes 1572872 | tf_op jit(solution)/shard_map/ppermute | solution.py:159
  608.9 48.9 %collective-permute-start.32 = (bf16[256,1024]{1,0:T(8,128)(2,1)S(1)}, bf16[256,1024]{1,0:T(8,128)(2,1)S(1)}, u32[]{:S(2)}, u32[]{:S(2)}) collective-permute-start(bf16[256,1024]{1,0:T(8,128)(2,1)S(1)} %dynamic-slice_bitcast_fusion.15), channel_id=1, source_target_pairs={{0,8},{2,10},{4,12},{6,14},{8,0},{10,2},{12,4},{14,6},{16,24},{18,... | collective-permute-start | bytes 1572872 | tf_op jit(solution)/shard_map/ppermute | solution.py:159
  611.1 17.1 %collective-permute-start.44 = (bf16[128,1024]{1,0:T(8,128)(2,1)S(1)}, bf16[128,1024]{1,0:T(8,128)(2,1)S(1)}, u32[]{:S(2)}, u32[]{:S(2)}) collective-permute-start(bf16[128,1024]{1,0:T(8,128)(2,1)S(1)} %maximum_select_fusion.25), channel_id=1, source_target_pairs={{0,8},{2,10},{4,12},{6,14},{8,0},{10,2},{12,4},{14,6},{16,24},{18,... | collective-permute-start | bytes 786440 | tf_op jit(solution)/shard_map/ppermute | solution.py:165
  611.2 17.4 %collective-permute-start.52 = (bf16[128,1024]{1,0:T(8,128)(2,1)S(1)}, bf16[128,1024]{1,0:T(8,128)(2,1)S(1)}, u32[]{:S(2)}, u32[]{:S(2)}) collective-permute-start(bf16[128,1024]{1,0:T(8,128)(2,1)S(1)} %maximum_select_fusion.26), channel_id=1, source_target_pairs={{0,4},{2,6},{4,0},{6,2},{8,12},{10,14},{12,8},{14,10},{16,20},{18,... | collective-permute-start | bytes 786440 | tf_op jit(solution)/shard_map/ppermute | solution.py:165
  615.9 20.5 %collective-permute-start.60 = (bf16[128,1024]{1,0:T(8,128)(2,1)S(1)}, bf16[128,1024]{1,0:T(8,128)(2,1)S(1)}, u32[]{:S(2)}, u32[]{:S(2)}) collective-permute-start(bf16[128,1024]{1,0:T(8,128)(2,1)S(1)} %maximum_select_fusion.27), channel_id=1, source_target_pairs={{0,8},{2,10},{4,12},{6,14},{8,0},{10,2},{12,4},{14,6},{16,24},{18,... | collective-permute-start | bytes 786440 | tf_op jit(solution)/shard_map/ppermute | solution.py:165
  628.2 5.7 collective-permute-start.25
  628.6 54.8 %collective-permute-start.14 = (bf16[512,532]{0,1:T(8,128)(2,1)S(1)}, bf16[512,532]{0,1:T(8,128)(2,1)S(1)}, u32[]{:S(2)}, u32[]{:S(2)}) collective-permute-start(bf16[512,532]{0,1:T(8,128)(2,1)S(1)} %maximum_select_fusion.15), channel_id=1, source_target_pairs={{0,2},{2,0},{4,6},{6,4},{8,10},{10,8},{12,14},{14,12},{16,18},{18,... | collective-permute-start | bytes 1634312 | tf_op jit(solution)/shard_map/ppermute | solution.py:165
  633.8 41.1 %collective-permute-start.45 = (bf16[256,1024]{1,0:T(8,128)(2,1)S(1)}, bf16[256,1024]{1,0:T(8,128)(2,1)S(1)}, u32[]{:S(2)}, u32[]{:S(2)}) collective-permute-start(bf16[256,1024]{1,0:T(8,128)(2,1)S(1)} %maximum_select_fusion.18), channel_id=1, source_target_pairs={{0,4},{2,6},{4,0},{6,2},{8,12},{10,14},{12,8},{14,10},{16,20},{18,... | collective-permute-start | bytes 1572872 | tf_op jit(solution)/shard_map/ppermute | solution.py:165
  636.4 6.9 collective-permute-start.26
  643.3 33.3 %collective-permute-start.53 = (bf16[256,1024]{1,0:T(8,128)(2,1)S(1)}, bf16[256,1024]{1,0:T(8,128)(2,1)S(1)}, u32[]{:S(2)}, u32[]{:S(2)}) collective-permute-start(bf16[256,1024]{1,0:T(8,128)(2,1)S(1)} %maximum_select_fusion.19), channel_id=1, source_target_pairs={{0,8},{2,10},{4,12},{6,14},{8,0},{10,2},{12,4},{14,6},{16,24},{18,... | collective-permute-start | bytes 1572872 | tf_op jit(solution)/shard_map/ppermute | solution.py:165
  643.3 11.5 %collective-permute-start.27 = (bf16[64,768]{1,0:T(8,128)(2,1)S(1)}, bf16[64,768]{1,0:T(8,128)(2,1)S(1)}, u32[]{:S(2)}, u32[]{:S(2)}) collective-permute-start(bf16[64,768]{1,0:T(8,128)(2,1)S(1)} %fusion.144), channel_id=1, source_target_pairs={{0,16},{2,18},{4,20},{6,22},{8,24},{10,26},{12,28},{14,30},{16,0},... | collective-permute-start | bytes 294920 | tf_op jit(solution)/shard_map/ppermute | solution.py:165
  654.9 10.8 %collective-permute-start.17 = (bf16[128,1024]{1,0:T(8,128)(2,1)S(1)}, bf16[128,1024]{1,0:T(8,128)(2,1)S(1)}, u32[]{:S(2)}, u32[]{:S(2)}) collective-permute-start(bf16[128,1024]{1,0:T(8,128)(2,1)S(1)} %dynamic-slice_bitcast_fusion.24), channel_id=1, source_target_pairs={{0,8},{2,10},{4,12},{6,14},{8,0},{10,2},{12,4},{14,6},{16,24},{18,... | collective-permute-start | bytes 786440 | tf_op jit(solution)/shard_map/ppermute | solution.py:159
  657.9 6.4 collective-permute-start.28
  664.3 9.2 %collective-permute-start.33 = (bf16[128,1024]{1,0:T(8,128)(2,1)S(1)}, bf16[128,1024]{1,0:T(8,128)(2,1)S(1)}, u32[]{:S(2)}, u32[]{:S(2)}) collective-permute-start(bf16[128,1024]{1,0:T(8,128)(2,1)S(1)} %dynamic-slice_bitcast_fusion.23), channel_id=1, source_target_pairs={{0,4},{2,6},{4,0},{6,2},{8,12},{10,14},{12,8},{14,10},{16,20},{18,... | collective-permute-start | bytes 786440 | tf_op jit(solution)/shard_map/ppermute | solution.py:159
  665.6 16.3 %collective-permute-start.61 = (bf16[256,1024]{1,0:T(8,128)(2,1)S(1)}, bf16[256,1024]{1,0:T(8,128)(2,1)S(1)}, u32[]{:S(2)}, u32[]{:S(2)}) collective-permute-start(bf16[256,1024]{1,0:T(8,128)(2,1)S(1)} %maximum_select_fusion.20), channel_id=1, source_target_pairs={{0,4},{2,6},{4,0},{6,2},{8,12},{10,14},{12,8},{14,10},{16,20},{18,... | collective-permute-start | bytes 1572872 | tf_op jit(solution)/shard_map/ppermute | solution.py:165
  673.5 49.4 %collective-permute-start.29 = (bf16[256,768]{1,0:T(8,128)(2,1)S(1)}, bf16[256,768]{1,0:T(8,128)(2,1)}, u32[]{:S(2)}, u32[]{:S(2)}) collective-permute-start(bf16[256,768]{1,0:T(8,128)(2,1)S(1)} %maximum_select_fusion.21), channel_id=1, source_target_pairs={{0,4},{2,6},{4,0},{6,2},{8,12},{10,14},{12,8},{14,10},{16,20},{18,... | collective-permute-start | bytes 1179656 | tf_op jit(solution)/shard_map/ppermute | solution.py:165
  674.9 11.5 %collective-permute-start.18 = (bf16[64,1024]{1,0:T(8,128)(2,1)S(1)}, bf16[64,1024]{1,0:T(8,128)(2,1)S(1)}, u32[]{:S(2)}, u32[]{:S(2)}) collective-permute-start(bf16[64,1024]{1,0:T(8,128)(2,1)S(1)} %dynamic-slice_bitcast_fusion.30), channel_id=1, source_target_pairs={{0,16},{2,18},{4,20},{6,22},{8,24},{10,26},{12,28},{14,30},{16,0},... | collective-permute-start | bytes 393224 | tf_op jit(solution)/shard_map/ppermute | solution.py:159
  676.7 10.7 %collective-permute-start.34 = (bf16[64,1024]{1,0:T(8,128)(2,1)S(1)}, bf16[64,1024]{1,0:T(8,128)(2,1)S(1)}, u32[]{:S(2)}, u32[]{:S(2)}) collective-permute-start(bf16[64,1024]{1,0:T(8,128)(2,1)S(1)} %dynamic-slice_bitcast_fusion.29), channel_id=1, source_target_pairs={{0,16},{2,18},{4,20},{6,22},{8,24},{10,26},{12,28},{14,30},{16,0},... | collective-permute-start | bytes 393224 | tf_op jit(solution)/shard_map/ppermute | solution.py:159
  681.9 45.0 %collective-permute-start.46 = (bf16[512,1024]{1,0:T(8,128)(2,1)S(1)}, bf16[512,1024]{1,0:T(8,128)(2,1)}, u32[]{:S(2)}, u32[]{:S(2)}) collective-permute-start(bf16[512,1024]{1,0:T(8,128)(2,1)S(1)} %maximum_select_fusion.11), channel_id=1, source_target_pairs={{0,2},{2,0},{4,6},{6,4},{8,10},{10,8},{12,14},{14,12},{16,18},{18,... | collective-permute-start | bytes 3145736 | tf_op jit(solution)/shard_map/ppermute | solution.py:165
  683.4 48.4 %collective-permute-start.54 = (bf16[512,1024]{1,0:T(8,128)(2,1)}, bf16[512,1024]{1,0:T(8,128)(2,1)}, u32[]{:S(2)}, u32[]{:S(2)}) collective-permute-start(bf16[512,1024]{1,0:T(8,128)(2,1)} %maximum_select_fusion.12), channel_id=1, source_target_pairs={{0,2},{2,0},{4,6},{6,4},{8,10},{10,8},{12,14},{14,12},{16,18},{18,... | collective-permute-start | bytes 3145736 | tf_op jit(solution)/shard_map/ppermute | solution.py:165
  686.5 11.8 %collective-permute-start.19 = (bf16[64,1024]{1,0:T(8,128)(2,1)S(1)}, bf16[64,1024]{1,0:T(8,128)(2,1)S(1)}, u32[]{:S(2)}, u32[]{:S(2)}) collective-permute-start(bf16[64,1024]{1,0:T(8,128)(2,1)S(1)} %fusion.141), channel_id=1, source_target_pairs={{0,16},{2,18},{4,20},{6,22},{8,24},{10,26},{12,28},{14,30},{16,0},... | collective-permute-start | bytes 393224 | tf_op jit(solution)/shard_map/ppermute | solution.py:165
  687.4 13.7 %collective-permute-start.35 = (bf16[64,1024]{1,0:T(8,128)(2,1)S(1)}, bf16[64,1024]{1,0:T(8,128)(2,1)S(1)}, u32[]{:S(2)}, u32[]{:S(2)}) collective-permute-start(bf16[64,1024]{1,0:T(8,128)(2,1)S(1)} %fusion.140), channel_id=1, source_target_pairs={{0,16},{2,18},{4,20},{6,22},{8,24},{10,26},{12,28},{14,30},{16,0},... | collective-permute-start | bytes 393224 | tf_op jit(solution)/shard_map/ppermute | solution.py:165
  698.4 8.3 %collective-permute-start.20 = (bf16[128,1024]{1,0:T(8,128)(2,1)S(1)}, bf16[128,1024]{1,0:T(8,128)(2,1)S(1)}, u32[]{:S(2)}, u32[]{:S(2)}) collective-permute-start(bf16[128,1024]{1,0:T(8,128)(2,1)S(1)} %maximum_select_fusion.23), channel_id=1, source_target_pairs={{0,8},{2,10},{4,12},{6,14},{8,0},{10,2},{12,4},{14,6},{16,24},{18,... | collective-permute-start | bytes 786440 | tf_op jit(solution)/shard_map/ppermute | solution.py:165
  701.1 9.0 %collective-permute-start.36 = (bf16[128,1024]{1,0:T(8,128)(2,1)S(1)}, bf16[128,1024]{1,0:T(8,128)(2,1)S(1)}, u32[]{:S(2)}, u32[]{:S(2)}) collective-permute-start(bf16[128,1024]{1,0:T(8,128)(2,1)S(1)} %maximum_select_fusion.24), channel_id=1, source_target_pairs={{0,4},{2,6},{4,0},{6,2},{8,12},{10,14},{12,8},{14,10},{16,20},{18,... | collective-permute-start | bytes 786440 | tf_op jit(solution)/shard_map/ppermute | solution.py:165
  706.8 13.9 %collective-permute-start.21 = (bf16[256,1024]{1,0:T(8,128)(2,1)S(1)}, bf16[256,1024]{1,0:T(8,128)(2,1)}, u32[]{:S(2)}, u32[]{:S(2)}) collective-permute-start(bf16[256,1024]{1,0:T(8,128)(2,1)S(1)} %maximum_select_fusion.16), channel_id=1, source_target_pairs={{0,4},{2,6},{4,0},{6,2},{8,12},{10,14},{12,8},{14,10},{16,20},{18,... | collective-permute-start | bytes 1572872 | tf_op jit(solution)/shard_map/ppermute | solution.py:165
  711.0 13.8 %collective-permute-start.37 = (bf16[256,1024]{1,0:T(8,128)(2,1)}, bf16[256,1024]{1,0:T(8,128)(2,1)}, u32[]{:S(2)}, u32[]{:S(2)}) collective-permute-start(bf16[256,1024]{1,0:T(8,128)(2,1)} %maximum_select_fusion.17), channel_id=1, source_target_pairs={{0,8},{2,10},{4,12},{6,14},{8,0},{10,2},{12,4},{14,6},{16,24},{18,... | collective-permute-start | bytes 1572872 | tf_op jit(solution)/shard_map/ppermute | solution.py:165
  720.7 16.3 %collective-permute-start.62 = (bf16[512,1024]{1,0:T(8,128)(2,1)S(1)}, bf16[512,1024]{1,0:T(8,128)(2,1)S(1)}, u32[]{:S(2)}, u32[]{:S(2)}) collective-permute-start(bf16[512,1024]{1,0:T(8,128)(2,1)S(1)} %copy-done.25), channel_id=1, source_target_pairs={{0,2},{2,0},{4,6},{6,4},{8,10},{10,8},{12,14},{14,12},{16,18},{18,... | collective-permute-start | bytes 3145736 | tf_op jit(solution)/shard_map/ppermute | solution.py:165
  722.9 19.3 %collective-permute-start.22 = (bf16[512,1024]{1,0:T(8,128)(2,1)S(1)}, bf16[512,1024]{1,0:T(8,128)(2,1)S(1)}, u32[]{:S(2)}, u32[]{:S(2)}) collective-permute-start(bf16[512,1024]{1,0:T(8,128)(2,1)S(1)} %maximum_select_fusion.9), channel_id=1, source_target_pairs={{0,2},{2,0},{4,6},{6,4},{8,10},{10,8},{12,14},{14,12},{16,18},{18,... | collective-permute-start | bytes 3145736 | tf_op jit(solution)/shard_map/ppermute | solution.py:165
  724.9 15.3 %collective-permute-start.30 = (bf16[512,768]{1,0:T(8,128)(2,1)S(1)}, bf16[512,768]{1,0:T(8,128)(2,1)S(1)}, u32[]{:S(2)}, u32[]{:S(2)}) collective-permute-start(bf16[512,768]{1,0:T(8,128)(2,1)S(1)} %maximum_select_fusion.14), channel_id=1, source_target_pairs={{0,2},{2,0},{4,6},{6,4},{8,10},{10,8},{12,14},{14,12},{16,18},{18,... | collective-permute-start | bytes 2359304 | tf_op jit(solution)/shard_map/ppermute | solution.py:165
  726.9 19.3 %collective-permute-start.38 = (bf16[512,1024]{1,0:T(8,128)(2,1)S(1)}, bf16[512,1024]{1,0:T(8,128)(2,1)S(1)}, u32[]{:S(2)}, u32[]{:S(2)}) collective-permute-start(bf16[512,1024]{1,0:T(8,128)(2,1)S(1)} %maximum_select_fusion.10), channel_id=1, source_target_pairs={{0,2},{2,0},{4,6},{6,4},{8,10},{10,8},{12,14},{14,12},{16,18},{18,... | collective-permute-start | bytes 3145736 | tf_op jit(solution)/shard_map/ppermute | solution.py:165
  (152 other events, 803.9 us)

commit v2 on v1

--- a/solution.py
+++ b/solution.py
@@ -2,7 +2,10 @@
 
 import jax
 import jax.numpy as jnp
+import numpy as np
 from jax import lax
+from jax.experimental import pallas as pl
+from jax.experimental.pallas import tpu as pltpu
 from jax.sharding import PartitionSpec as P
 
 HD = 64
@@ -17,115 +20,6 @@
 PRECISE = lax.Precision.HIGHEST
 
 
-def ssd_block(rates, carry, block):
-    inputs, steps, entry, readout = block
-    logdec = steps * rates[None, :]
-    cumul = jnp.cumsum(logdec, axis=0)
-    count = cumul.shape[0]
-    lower = jnp.arange(count)[:, None] >= jnp.arange(count)[None, :]
-    spread = cumul[:, None, :] - cumul[None, :, :]
-    decay = jnp.exp(jnp.where(lower[:, :, None], spread, -jnp.inf))
-    intersection = jnp.dot(readout, entry.T, precision=PRECISE)
-    scaled = inputs * steps[:, :, None]
-    within = jnp.einsum("ijh,jhp->ihp", decay * intersection[:, :, None], scaled, precision=PRECISE)
-    carried = (
-        jnp.einsum("in,hpn->ihp", readout, carry, precision=PRECISE) * jnp.exp(cumul)[:, :, None]
-    )
-    tail = jnp.exp(cumul[-1][None, :] - cumul)
-    update = jnp.einsum("jhp,jn->hpn", scaled * tail[:, :, None], entry, precision=PRECISE)
-    carry = carry * jnp.exp(cumul[-1])[:, None, None] + update
-    return (carry, within + carried)
-
-
-def ssd_sequence(inputs, steps, entry, readout, rates):
-    length = inputs.shape[0]
-    blocks = length // SPAN
-    heads = inputs.shape[1]
-    size = inputs.shape[2]
-    states = entry.shape[1]
-    stacked = (
-        inputs.reshape(blocks, SPAN, heads, size),
-        steps.reshape(blocks, SPAN, heads),
-        entry.reshape(blocks, SPAN, states),
-        readout.reshape(blocks, SPAN, states),
-    )
-    start = jnp.zeros((heads, size, states), jnp.float32)
-    final, outputs = lax.scan(jax.checkpoint(partial(ssd_block, rates)), start, stacked)
-    return outputs.reshape(length, heads, size)
-
-
-def ssm_branch(
-    ssm_gate,
-    ssm_input,
-    step_raw,
-    state_raw,
-    input_kernel,
-    input_shift,
-    state_kernel,
-    state_shift,
-    step_bias,
-    decay_log,
-    skip_gain,
-    length,
-):
-    total_rows = ssm_input.shape[0]
-    seqs = total_rows // length
-    heads = step_raw.shape[1]
-    channels = ssm_input.shape[1]
-    head_size = channels // heads
-    states = state_raw.shape[1] // 2
-    joined = jnp.concatenate([ssm_input, state_raw], axis=1)
-    kernel = jnp.concatenate([input_kernel, state_kernel], axis=1)
-    shifts = jnp.concatenate([input_shift, state_shift], axis=0)
-    taps = kernel.shape[0]
-    seqwise = joined.reshape(seqs, length, joined.shape[1])
-    padded = jnp.pad(seqwise, ((0, 0), (taps - 1, 0), (0, 0)))
-    filtered = jnp.broadcast_to(shifts, seqwise.shape)
-    for index in range(taps):
-        filtered = filtered + kernel[index] * padded[:, index : index + length]
-    active = jax.nn.silu(filtered)
-    inputs = active[:, :, :channels].reshape(seqs, length, heads, head_size)
-    entry = active[:, :, channels : channels + states]
-    readout = active[:, :, channels + states :]
-    steps = jax.nn.softplus(step_raw.reshape(seqs, length, heads) + step_bias)
-    rates = -jnp.exp(decay_log)
-    outputs = lax.map(
-        lambda group: ssd_sequence(group[0], group[1], group[2], group[3], rates),
-        (inputs, steps, entry, readout),
-    )
-    outputs = outputs + skip_gain[:, None] * inputs
-    return outputs.reshape(total_rows, channels) * jax.nn.silu(ssm_gate)
-
-
-def rope_tables(length, head_size):
-    half = head_size // 2
-    freqs = ROPE_BASE ** (-jnp.arange(half, dtype=jnp.float32) * 2.0 / head_size)
-    angles = jnp.arange(length, dtype=jnp.float32)[:, None] * freqs[None, :]
-    return (jnp.cos(angles), jnp.sin(angles))
-
-
-def rotate(vecs, cosine, sine):
-    half = vecs.shape[-1] // 2
-    first = vecs[..., :half]
-    second = vecs[..., half:]
-    cosine = cosine[:, None, :]
-    sine = sine[:, None, :]
-    return jnp.concatenate(
-        [first * cosine - second * sine, second * cosine + first * sine], axis=-1
-    )
-
-
-def unrotate(vecs, cosine, sine):
-    half = vecs.shape[-1] // 2
-    first = vecs[..., :half]
-    second = vecs[..., half:]
-    cosine = cosine[:, None, :]
-    sine = sine[:, None, :]
-    return jnp.concatenate(
-        [first * cosine + second * sine, second * cosine - first * sine], axis=-1
-    )
-
-
 def forward_dot(left, right):
     return jnp.dot(left, right, preferred_element_type=jnp.float32)
 
@@ -145,6 +39,681 @@
 def norm_back(upstream, gain, normal, factor):
     scaled = upstream * gain
     return factor * (scaled - normal * jnp.mean(scaled * normal, axis=-1, keepdims=True))
+
+
+LANES = 128
+VMEM_LIMIT = 44 * 1024 * 1024
+
+
+def exact_dot(left, right):
+    return jnp.dot(left, right, precision=PRECISE, preferred_element_type=jnp.float32)
+
+
+def low_dot(left, right):
+    return jnp.dot(
+        left.astype(jnp.bfloat16), right.astype(jnp.bfloat16), preferred_element_type=jnp.float32
+    )
+
+
+def low_against(left, right):
+    return lax.dot_general(
+        left.astype(jnp.bfloat16),
+        right.astype(jnp.bfloat16),
+        (((1,), (1,)), ((), ())),
+        preferred_element_type=jnp.float32,
+    )
+
+
+def low_inner(left, right):
+    return lax.dot_general(
+        left.astype(jnp.bfloat16),
+        right.astype(jnp.bfloat16),
+        (((0,), (0,)), ((), ())),
+        preferred_element_type=jnp.float32,
+    )
+
+
+def row_index(shape):
+    return lax.broadcasted_iota(jnp.int32, shape, 0)
+
+
+def lane_index(shape):
+    return lax.broadcasted_iota(jnp.int32, shape, 1)
+
+
+def later(part, count):
+    if count == 0:
+        return part
+    return jnp.where(row_index(part.shape) >= count, pltpu.roll(part, count, 0), 0.0)
+
+
+def sooner(part, count):
+    if count == 0:
+        return part
+    rows = part.shape[0]
+    return jnp.where(row_index(part.shape) < rows - count, pltpu.roll(part, rows - count, 0), 0.0)
+
+
+def slabs(width):
+    return [(start, min(LANES, width - start)) for start in range(0, width, LANES)]
+
+
+def soft_plus(value):
+    return jnp.maximum(value, 0.0) + jnp.log1p(jnp.exp(-jnp.abs(value)))
+
+
+def stacked_heads(part, heads):
+    if heads == 1:
+        return part
+    lane = lane_index(part.shape)
+    return jnp.concatenate(
+        [jnp.where((lane >= head * HD) & (lane < head * HD + HD), part, 0.0) for head in range(heads)],
+        axis=0,
+    )
+
+
+def convolve(raw, kernel_ref, shift_ref, cols):
+    taps = kernel_ref.shape[0]
+    out = shift_ref[:, cols] + kernel_ref[taps - 1 : taps, cols] * raw
+    for tap in range(taps - 1):
+        out = out + kernel_ref[tap : tap + 1, cols] * later(raw, taps - 1 - tap)
+    return out
+
+
+def chunk_steps(step_ref, bias_ref, rate_ref, expand_ref, rows):
+    raw = step_ref[rows, :] + bias_ref[...]
+    steps = soft_plus(raw)
+    logdec = steps * rate_ref[...]
+    square = (SPAN, SPAN)
+    lower = (row_index(square) >= lane_index(square)).astype(jnp.float32)
+    cumul = exact_dot(lower, logdec)
+    grown = jnp.exp(cumul)
+    tail = jnp.exp(cumul[SPAN - 1 : SPAN, :] - cumul)
+    wide = exact_dot(jnp.concatenate([steps, grown, tail], axis=0), expand_ref[...])
+    return raw, steps, cumul, wide[:SPAN], wide[SPAN : 2 * SPAN], wide[2 * SPAN :]
+
+
+def ssd_forward_kernel(
+    input_ref,
+    state_ref,
+    gate_ref,
+    step_ref,
+    input_kernel_ref,
+    input_shift_ref,
+    state_kernel_ref,
+    state_shift_ref,
+    bias_ref,
+    rate_ref,
+    skip_ref,
+    expand_ref,
+    gated_ref,
+    out_ref,
+    carry_ref,
+    act_ref,
+    both_ref,
+    held_ref,
+):
+    channels = input_ref.shape[1]
+    states = state_ref.shape[1] // 2
+    for start, width in slabs(channels):
+        cols = pl.ds(start, width)
+        pre = convolve(input_ref[:, cols], input_kernel_ref, input_shift_ref, cols)
+        act_ref[:, cols] = pre * jax.nn.sigmoid(pre)
+    for start, width in slabs(2 * states):
+        cols = pl.ds(start, width)
+        pre = convolve(state_ref[:, cols], state_kernel_ref, state_shift_ref, cols)
+        both_ref[:, cols] = pre * jax.nn.sigmoid(pre)
+    held_ref[...] = jnp.zeros_like(held_ref)
+
+    def chunk(index, unused):
+        rows = pl.ds(pl.multiple_of(index * SPAN, SPAN), SPAN)
+        raw, steps, cumul, step_wide, grown_wide, tail_wide = chunk_steps(
+            step_ref, bias_ref, rate_ref, expand_ref, rows
+        )
+        cumul_turned = cumul.T
+        entry = both_ref[rows, pl.ds(0, states)].astype(jnp.bfloat16)
+        readout = both_ref[rows, pl.ds(states, states)].astype(jnp.bfloat16)
+        cross = low_against(readout, entry)
+        square = (SPAN, SPAN)
+        lower = row_index(square) >= lane_index(square)
+        for start, width in slabs(channels):
+            cols = pl.ds(start, width)
+            span = slice(start, start + width)
+            heads = width // HD
+            values = act_ref[rows, cols]
+            scaled = values * step_wide[:, span]
+            held = held_ref[:, cols]
+            carry_ref[index, :, cols] = held
+            weights = []
+            for head in range(start // HD, start // HD + heads):
+                spread = cumul[:, head : head + 1] - cumul_turned[head : head + 1, :]
+                decay = jnp.exp(jnp.where(lower, spread, -jnp.inf))
+                weights.append((decay * cross).astype(jnp.bfloat16))
+            weights = jnp.concatenate(weights, axis=1) if heads > 1 else weights[0]
+            result = low_dot(weights, stacked_heads(scaled, heads))
+            result = result + low_dot(readout, held) * grown_wide[:, span]
+            held_ref[:, cols] = held * grown_wide[SPAN - 1 : SPAN, span] + low_inner(
+                entry, scaled * tail_wide[:, span]
+            )
+            result = result + skip_ref[:, cols] * values
+            out_ref[rows, cols] = result
+            gate = gate_ref[rows, cols]
+            gated_ref[rows, cols] = (result * (gate * jax.nn.sigmoid(gate))).astype(jnp.bfloat16)
+        return unused
+
+    lax.fori_loop(0, input_ref.shape[0] // SPAN, chunk, 0)
+
+
+def ssd_backward_kernel(
+    input_ref,
+    state_ref,
+    gate_ref,
+    step_ref,
+    grad_ref,
+    carry_ref,
+    input_kernel_ref,
+    input_shift_ref,
+    state_kernel_ref,
+    state_shift_ref,
+    bias_ref,
+    rate_ref,
+    skip_ref,
+    expand_ref,
+    collect_ref,
+    grad_input_ref,
+    grad_state_ref,
+    grad_step_ref,
+    grad_input_conv_ref,
+    grad_state_conv_ref,
+    grad_head_ref,
+    act_ref,
+    slope_ref,
+    both_ref,
+    both_slope_ref,
+    held_ref,
+    wide_ref,
+    turned_ref,
+    column_ref,
+    skip_sum_ref,
+    scale_sum_ref,
+):
+    channels = input_ref.shape[1]
+    states = state_ref.shape[1] // 2
+    taps = input_kernel_ref.shape[0]
+    for start, width in slabs(channels):
+        cols = pl.ds(start, width)
+        pre = convolve(input_ref[:, cols], input_kernel_ref, input_shift_ref, cols)
+        sigma = jax.nn.sigmoid(pre)
+        act_ref[:, cols] = pre * sigma
+        slope_ref[:, cols] = sigma * (1.0 + pre * (1.0 - sigma))
+    for start, width in slabs(2 * states):
+        cols = pl.ds(start, width)
+        pre = convolve(state_ref[:, cols], state_kernel_ref, state_shift_ref, cols)
+        sigma = jax.nn.sigmoid(pre)
+        both_ref[:, cols] = pre * sigma
+        both_slope_ref[:, cols] = sigma * (1.0 + pre * (1.0 - sigma))
+    held_ref[...] = jnp.zeros_like(held_ref)
+    turned_ref[...] = jnp.zeros_like(turned_ref)
+    column_ref[...] = jnp.zeros_like(column_ref)
+    grad_head_ref[...] = jnp.zeros_like(grad_head_ref)
+    skip_sum_ref[...] = jnp.zeros_like(skip_sum_ref)
+    chunks = input_ref.shape[0] // SPAN
+
+    def chunk(count, unused):
+        index = chunks - 1 - count
+        rows = pl.ds(pl.multiple_of(index * SPAN, SPAN), SPAN)
+        raw, steps, cumul, step_wide, grown_wide, tail_wide = chunk_steps(
+            step_ref, bias_ref, rate_ref, expand_ref, rows
+        )
+        cumul_turned = cumul.T
+        entry = both_ref[rows, pl.ds(0, states)].astype(jnp.bfloat16)
+        readout = both_ref[rows, pl.ds(states, states)].astype(jnp.bfloat16)
+        cross = low_against(entry, readout)
+        square = (SPAN, SPAN)
+        upper = row_index(square) <= lane_index(square)
+        grad_cross = jnp.zeros(square, jnp.float32)
+        grad_entry = jnp.zeros((SPAN, states), jnp.float32)
+        grad_readout = jnp.zeros((SPAN, states), jnp.float32)
+        for start, width in slabs(channels):
+            cols = pl.ds(start, width)
+            span = slice(start, start + width)
+            heads = width // HD
+            values = act_ref[rows, cols]
+            scaled = values * step_wide[:, span]
+            gate = gate_ref[rows, cols]
+            upstream = grad_ref[rows, cols] * (gate * jax.nn.sigmoid(gate))
+            held = held_ref[:, cols]
+            before = carry_ref[index, :, cols]
+            stacked_up = stacked_heads(upstream, heads).astype(jnp.bfloat16)
+            products = low_against(scaled, stacked_up)
+            weights = []
+            for place in range(heads):
+                head = start // HD + place
+                spread = cumul_turned[head : head + 1, :] - cumul[:, head : head + 1]
+                decay = jnp.exp(jnp.where(upper, spread, -jnp.inf))
+                product = products[:, place * SPAN : (place + 1) * SPAN] * decay
+                grad_cross = grad_cross + product
+                flow = product * cross
+                turned_ref[head : head + 1, :] = jnp.sum(flow, axis=0, keepdims=True)
+                column_ref[:, head : head + 1] = jnp.sum(flow, axis=1, keepdims=True)
+                weights.append((decay * cross).astype(jnp.bfloat16))
+            weights = jnp.concatenate(weights, axis=1) if heads > 1 else weights[0]
+            grown_up = upstream * grown_wide[:, span]
+            tailed = scaled * tail_wide[:, span]
+            from_held = low_dot(entry, held)
+            grad_scaled = low_dot(weights, stacked_up) + tail_wide[:, span] * from_held
+            wide_ref[0, :, cols] = grown_up * low_dot(readout, before)
+            wide_ref[1, :, cols] = tailed * from_held
+            wide_ref[2, :, cols] = values * grad_scaled
+            grad_readout = grad_readout + low_against(grown_up, before)
+            grad_entry = grad_entry + low_against(tailed, held)
+            last = grown_wide[SPAN - 1 : SPAN, span]
+            scale_sum_ref[:, cols] = jnp.sum(held * before, axis=0, keepdims=True) * last
+            skip_sum_ref[:, cols] += jnp.sum(upstream * values, axis=0, keepdims=True)
+            held_ref[:, cols] = held * last + low_inner(readout, grown_up)
+            act_ref[rows, cols] = step_wide[:, span] * grad_scaled + skip_ref[:, cols] * upstream
+        sums = exact_dot(
+            jnp.concatenate([wide_ref[0], wide_ref[1], wide_ref[2]], axis=0), collect_ref[...]
+        )
+        scale_sum = exact_dot(jnp.broadcast_to(scale_sum_ref[...], (8, channels)), collect_ref[...])
+        flows = turned_ref[...].T - column_ref[...] + sums[:SPAN]
+        onward = (row_index(square) <= lane_index(square)).astype(jnp.float32)
+        strict = (row_index(square) > lane_index(square)).astype(jnp.float32)
+        grad_log = (
+            exact_dot(onward, flows)
+            + exact_dot(strict, sums[SPAN : 2 * SPAN])
+            + scale_sum[:1]
+        )
+        grad_steps = grad_log * rate_ref[...] + sums[2 * SPAN :]
+        grad_raw = grad_steps * jax.nn.sigmoid(raw)
+        grad_step_ref[rows, :] = grad_raw.astype(jnp.bfloat16)
+        grad_head_ref[0, 0:1, :] += jnp.sum(grad_raw, axis=0, keepdims=True)
+        grad_head_ref[0, 1:2, :] += (
+            jnp.sum(grad_log * steps, axis=0, keepdims=True) * rate_ref[...]
+        )
+        both_ref[rows, pl.ds(0, states)] = grad_entry + low_dot(grad_cross, readout)
+        both_ref[rows, pl.ds(states, states)] = grad_readout + low_inner(grad_cross, entry)
+        return unused
+
+    lax.fori_loop(0, chunks, chunk, 0)
+    grad_head_ref[0, 2:3, :] = exact_dot(
+        jnp.broadcast_to(skip_sum_ref[...], (8, channels)), collect_ref[...]
+    )[:1]
+
+    def convolve_back(raw_ref, grads_ref, slopes_ref, kernel_ref, out_ref, sums_ref, width_all):
+        for start, width in slabs(width_all):
+            cols = pl.ds(start, width)
+            grad = grads_ref[:, cols] * slopes_ref[:, cols]
+            raw = raw_ref[:, cols]
+            total = kernel_ref[taps - 1 : taps, cols] * grad
+            sums_ref[0, taps - 1 : taps, cols] = jnp.sum(grad * raw, axis=0, keepdims=True)
+            for tap in range(taps - 1):
+                shifted = sooner(grad, taps - 1 - tap)
+                total = total + kernel_ref[tap : tap + 1, cols] * shifted
+                sums_ref[0, tap : tap + 1, cols] = jnp.sum(shifted * raw, axis=0, keepdims=True)
+            sums_ref[0, taps : taps + 1, cols] = jnp.sum(grad, axis=0, keepdims=True)
+            out_ref[:, cols] = total.astype(jnp.bfloat16)
+
+    convolve_back(
+        input_ref,
+        act_ref,
+        slope_ref,
+        input_kernel_ref,
+        grad_input_ref,
+        grad_input_conv_ref,
+        channels,
+    )
+    convolve_back(
+        state_ref,
+        both_ref,
+        both_slope_ref,
+        state_kernel_ref,
+        grad_state_ref,
+        grad_state_conv_ref,
+        2 * states,
+    )
+
+
+def by_sequence(length, width):
+    return pl.BlockSpec((length, width), lambda seq: (seq, 0))
+
+
+def fixed(*shape):
+    return pl.BlockSpec(shape, lambda seq: (0,) * len(shape))
+
+
+def head_spread(heads):
+    marks = np.zeros((LANES, heads * HD), np.float32)
+    for head in range(heads):
+        marks[head, head * HD : (head + 1) * HD] = 1.0
+    return marks
+
+
+def pad_lanes(part):
+    return jnp.pad(part, ((0, 0), (0, LANES - part.shape[1])))
+
+
+def ssd_small(input_kernel, input_shift, state_kernel, state_shift, step_bias, decay_log, skip_gain):
+    rates = -jnp.exp(decay_log)
+    return (
+        input_kernel,
+        input_shift[None, :],
+        state_kernel,
+        state_shift[None, :],
+        pad_lanes(step_bias[None, :]),
+        pad_lanes(rates[None, :]),
+        jnp.repeat(skip_gain, HD)[None, :],
+    )
+
+
+def ssd_forward(inputs, states_raw, gate, step, small, heads, length):
+    group, channels = inputs.shape
+    seqs = group // length
+    both = states_raw.shape[1]
+    states = both // 2
+    chunks = length // SPAN
+    taps = small[0].shape[0]
+    return pl.pallas_call(
+        ssd_forward_kernel,
+        grid=(seqs,),
+        in_specs=[
+            by_sequence(length, channels),
+            by_sequence(length, both),
+            by_sequence(length, channels),
+            by_sequence(length, LANES),
+            fixed(taps, channels),
+            fixed(1, channels),
+            fixed(taps, both),
+            fixed(1, both),
+            fixed(1, LANES),
+            fixed(1, LANES),
+            fixed(1, channels),
+            fixed(LANES, channels),
+        ],
+        out_specs=[
+            by_sequence(length, channels),
+            by_sequence(length, channels),
+            pl.BlockSpec((chunks, states, channels), lambda seq: (seq, 0, 0)),
+        ],
+        out_shape=[
+            jax.ShapeDtypeStruct((group, channels), jnp.bfloat16),
+            jax.ShapeDtypeStruct((group, channels), jnp.float32),
+            jax.ShapeDtypeStruct((seqs * chunks, states, channels), jnp.float32),
+        ],
+        scratch_shapes=[
+            pltpu.VMEM((length, channels), jnp.float32),
+            pltpu.VMEM((length, both), jnp.float32),
+            pltpu.VMEM((states, channels), jnp.float32),
+        ],
+        compiler_params=pltpu.CompilerParams(vmem_limit_bytes=VMEM_LIMIT),
+        cost_estimate=pl.CostEstimate(
+            flops=8 * group * channels * SPAN,
+            bytes_accessed=20 * group * channels,
+            transcendentals=group * heads * SPAN,
+        ),
+        name="ssd_forward",
+    )(inputs, states_raw, gate, step, *small, jnp.asarray(head_spread(heads)))
+
+
+def ssd_backward(inputs, states_raw, gate, step, grad, carry, small, heads, length):
+    group, channels = inputs.shape
+    seqs = group // length
+    both = states_raw.shape[1]
+    states = both // 2
+    chunks = length // SPAN
+    taps = small[0].shape[0]
+    return pl.pallas_call(
+        ssd_backward_kernel,
+        grid=(seqs,),
+        in_specs=[
+            by_sequence(length, channels),
+            by_sequence(length, both),
+            by_sequence(length, channels),
+            by_sequence(length, LANES),
+            by_sequence(length, channels),
+            pl.BlockSpec((chunks, states, channels), lambda seq: (seq, 0, 0)),
+            fixed(taps, channels),
+            fixed(1, channels),
+            fixed(taps, both),
+            fixed(1, both),
+            fixed(1, LANES),
+            fixed(1, LANES),
+            fixed(1, channels),
+            fixed(LANES, channels),
+            fixed(channels, LANES),
+        ],
+        out_specs=[
+            by_sequence(length, channels),
+            by_sequence(length, both),
+            by_sequence(length, LANES),
+            pl.BlockSpec((1, 8, channels), lambda seq: (seq, 0, 0)),
+            pl.BlockSpec((1, 8, both), lambda seq: (seq, 0, 0)),
+            pl.BlockSpec((1, 8, LANES), lambda seq: (seq, 0, 0)),
+        ],
+        out_shape=[
+            jax.ShapeDtypeStruct((group, channels), jnp.bfloat16),
+            jax.ShapeDtypeStruct((group, both), jnp.bfloat16),
+            jax.ShapeDtypeStruct((group, LANES), jnp.bfloat16),
+            jax.ShapeDtypeStruct((seqs, 8, channels), jnp.float32),
+            jax.ShapeDtypeStruct((seqs, 8, both), jnp.float32),
+            jax.ShapeDtypeStruct((seqs, 8, LANES), jnp.float32),
+        ],
+        scratch_shapes=[
+            pltpu.VMEM((length, channels), jnp.float32),
+            pltpu.VMEM((length, channels), jnp.float32),
+            pltpu.VMEM((length, both), jnp.float32),
+            pltpu.VMEM((length, both), jnp.float32),
+            pltpu.VMEM((states, channels), jnp.float32),
+            pltpu.VMEM((3, SPAN, channels), jnp.float32),
+            pltpu.VMEM((LANES, SPAN), jnp.float32),
+            pltpu.VMEM((SPAN, LANES), jnp.float32),
+            pltpu.VMEM((1, channels), jnp.float32),
+            pltpu.VMEM((1, channels), jnp.float32),
+        ],
+        compiler_params=pltpu.CompilerParams(vmem_limit_bytes=VMEM_LIMIT),
+        cost_estimate=pl.CostEstimate(
+            flops=20 * group * channels * SPAN,
+            bytes_accessed=20 * group * channels,
+            transcendentals=group * heads * SPAN,
+        ),
+        name="ssd_backward",
+    )(
+        inputs,
+        states_raw,
+        gate,
+        step,
+        grad,
+        carry,
+        *small,
+        jnp.asarray(head_spread(heads)),
+        jnp.asarray(head_spread(heads).T.copy()),
+    )
+
+
+def rope_wide(length):
+    half = HD // 2
+    freqs = np.float32(ROPE_BASE) ** (-np.arange(half, dtype=np.float32) * np.float32(2.0 / HD))
+    angles = np.arange(length, dtype=np.float32)[:, None] * freqs[None, :].astype(np.float32)
+    cosine, sine = np.cos(angles), np.sin(angles)
+    count = LANES // HD
+    return (
+        np.concatenate([cosine, cosine] * count, axis=1).astype(np.float32),
+        np.concatenate([-sine, sine] * count, axis=1).astype(np.float32),
+    )
+
+
+def turn(part, cosine, sine):
+    half = HD // 2
+    first = lane_index(part.shape) % HD < half
+    swapped = jnp.where(first, pltpu.roll(part, LANES - half, 1), pltpu.roll(part, half, 1))
+    return part * cosine + swapped * sine
+
+
+def attend_forward_kernel(
+    query_ref, pair_ref, cosine_ref, sine_ref, context_ref, query_out_ref, pair_out_ref, total_ref
+):
+    length = query_ref.shape[0]
+    cosine, sine = cosine_ref[...], sine_ref[...]
+    pair = pair_ref[...]
+    left = lane_index(pair.shape) < HD
+    pair = jnp.where(left, turn(pair, cosine, sine), pair)
+    pair_out_ref[...] = pair.astype(jnp.bfloat16)
+    moved = pltpu.roll(pair, HD, 1)
+    keys = jnp.where(left, pair, moved).astype(jnp.bfloat16)
+    values = jnp.where(left, moved, pair).astype(jnp.bfloat16)
+    scale = HD ** (-0.5)
+    for slab in range(query_ref.shape[1] // LANES):
+        cols = pl.ds(slab * LANES, LANES)
+        query_out_ref[:, cols] = turn(query_ref[:, cols], cosine, sine).astype(jnp.bfloat16)
+        for tile in range(length // SPAN):
+            rows = slice(tile * SPAN, (tile + 1) * SPAN)
+            count = (tile + 1) * SPAN
+            query = query_out_ref[rows, cols]
+            lane = lane_index(query.shape)
+            square = (SPAN, count)
+            causal = row_index(square) + tile * SPAN >= lane_index(square)
+            results = []
+            for place in range(LANES // HD):
+                mine = (lane >= place * HD) & (lane < place * HD + HD)
+                scores = low_against(jnp.where(mine, query, 0), keys[:count]) * scale
+                scores = jnp.where(causal, scores, -jnp.inf)
+                peak = jnp.max(scores, axis=-1, keepdims=True)
+                grown = jnp.exp(scores - peak)
+                total = jnp.sum(grown, axis=-1, keepdims=True)
+                probs = grown * (1.0 / total)
+                results.append(low_dot(probs, values[:count]))
+                head = slab * (LANES // HD) + place
+                total_ref[rows, head : head + 1] = jnp.log(total) + peak
+            context_ref[rows, cols] = jnp.where(lane < HD, results[0], results[1]).astype(
+                jnp.bfloat16
+            )
+
+
+def attend_backward_kernel(
+    query_ref,
+    pair_ref,
+    total_ref,
+    grad_ref,
+    cosine_ref,
+    sine_ref,
+    grad_query_ref,
+    grad_pair_ref,
+    key_sum_ref,
+    value_sum_ref,
+):
+    length = query_ref.shape[0]
+    cosine, sine = cosine_ref[...], -sine_ref[...]
+    pair = pair_ref[...].astype(jnp.float32)
+    left = lane_index(pair.shape) < HD
+    moved = pltpu.roll(pair, HD, 1)
+    keys = jnp.where(left, pair, moved).astype(jnp.bfloat16)
+    values = jnp.where(left, moved, pair).astype(jnp.bfloat16)
+    scale = HD ** (-0.5)
+    key_sum_ref[...] = jnp.zeros_like(key_sum_ref)
+    value_sum_ref[...] = jnp.zeros_like(value_sum_ref)
+    for slab in range(query_ref.shape[1] // LANES):
+        cols = pl.ds(slab * LANES, LANES)
+        for tile in range(length // SPAN):
+            rows = slice(tile * SPAN, (tile + 1) * SPAN)
+            count = (tile + 1) * SPAN
+            query = query_ref[rows, cols]
+            upstream = grad_ref[rows, cols]
+            lane = lane_index(query.shape)
+            square = (SPAN, count)
+            causal = row_index(square) + tile * SPAN >= lane_index(square)
+            results = []
+            for place in range(LANES // HD):
+                mine = (lane >= place * HD) & (lane < place * HD + HD)
+                head = slab * (LANES // HD) + place
+                own_query = jnp.where(mine, query, 0)
+                own_up = jnp.where(mine, upstream, 0)
+                scores = low_against(own_query, keys[:count]) * scale
+                scores = jnp.where(causal, scores, -jnp.inf)
+                probs = jnp.exp(scores - total_ref[rows, head : head + 1])
+                grad_probs = low_against(own_up, values[:count])
+                mean = jnp.sum(probs * grad_probs, axis=-1, keepdims=True)
+                grad_scores = (probs * (grad_probs - mean)).astype(jnp.bfloat16)
+                results.append(low_dot(grad_scores, keys[:count]))
+                key_sum_ref[0:count, :] += low_inner(grad_scores, own_query)
+                value_sum_ref[0:count, :] += low_inner(probs, own_up)
+            grad_query = jnp.where(lane < HD, results[0], results[1]) * scale
+            grad_query_ref[rows, cols] = turn(
+                grad_query, cosine[rows, :], sine[rows, :]
+            ).astype(jnp.bfloat16)
+    grad_key = key_sum_ref[...]
+    grad_key = turn((grad_key + pltpu.roll(grad_key, HD, 1)) * scale, cosine, sine)
+    grad_value = value_sum_ref[...]
+    grad_value = grad_value + pltpu.roll(grad_value, HD, 1)
+    grad_pair_ref[...] = jnp.where(left, grad_key, grad_value).astype(jnp.bfloat16)
+
+
+def attend_forward(query, pair, length):
+    group, width = query.shape
+    heads = width // HD
+    cosine, sine = rope_wide(length)
+    return pl.pallas_call(
+        attend_forward_kernel,
+        grid=(group // length,),
+        in_specs=[
+            by_sequence(length, width),
+            by_sequence(length, LANES),
+            fixed(length, LANES),
+            fixed(length, LANES),
+        ],
+        out_specs=[
+            by_sequence(length, width),
+            by_sequence(length, width),
+            by_sequence(length, LANES),
+            by_sequence(length, LANES),
+        ],
+        out_shape=[
+            jax.ShapeDtypeStruct((group, width), jnp.bfloat16),
+            jax.ShapeDtypeStruct((group, width), jnp.bfloat16),
+            jax.ShapeDtypeStruct((group, LANES), jnp.bfloat16),
+            jax.ShapeDtypeStruct((group, LANES), jnp.float32),
+        ],
+        compiler_params=pltpu.CompilerParams(vmem_limit_bytes=VMEM_LIMIT),
+        cost_estimate=pl.CostEstimate(
+            flops=4 * group * width * length,
+            bytes_accessed=12 * group * width,
+            transcendentals=group * heads * length // 2,
+        ),
+        name="attend_forward",
+    )(query, pair, jnp.asarray(cosine), jnp.asarray(sine))
+
+
+def attend_backward(query, pair, total, grad, length):
+    group, width = query.shape
+    heads = width // HD
+    cosine, sine = rope_wide(length)
+    return pl.pallas_call(
+        attend_backward_kernel,
+        grid=(group // length,),
+        in_specs=[
+            by_sequence(length, width),
+            by_sequence(length, LANES),
+            by_sequence(length, LANES),
+            by_sequence(length, width),
+            fixed(length, LANES),
+            fixed(length, LANES),
+        ],
+        out_specs=[by_sequence(length, width), by_sequence(length, LANES)],
+        out_shape=[
+            jax.ShapeDtypeStruct((group, width), jnp.bfloat16),
+            jax.ShapeDtypeStruct((group, LANES), jnp.bfloat16),
+        ],
+        scratch_shapes=[
+            pltpu.VMEM((length, LANES), jnp.float32),
+            pltpu.VMEM((length, LANES), jnp.float32),
+        ],
+        compiler_params=pltpu.CompilerParams(vmem_limit_bytes=VMEM_LIMIT),
+        cost_estimate=pl.CostEstimate(
+            flops=10 * group * width * length,
+            bytes_accessed=12 * group * width,
+            transcendentals=group * heads * length // 2,
+        ),
+        name="attend_backward",
+    )(query, pair, total, grad, jnp.asarray(cosine), jnp.asarray(sine))
 
 
 def bit_pairs(size, bit):
@@ -285,13 +854,18 @@
     key_cols = lax.dynamic_slice_in_dim(keyvalue_weight, kv_head * HD, HD, 1)
     value_cols = lax.dynamic_slice_in_dim(keyvalue_weight, (KVH + kv_head) * HD, HD, 1)
     pair_weight = jnp.concatenate([key_cols, value_cols], axis=1)
+    query_cols = query_weight.shape[1]
+    query_pad = -query_cols % LANES
+    query_wide = jnp.pad(query_weight, ((0, 0), (0, query_pad)))
+    step_wide = pad_lanes(step_weight)
+    heads = step_weight.shape[1]
+    input_raw = forward_dot(whole, mamba_input)
+    state_raw = forward_dot(whole, state_weight)
+    step_raw = forward_dot(whole, step_wide)
     gate_raw = forward_dot(whole, mamba_gate)
-    input_raw = forward_dot(whole, mamba_input)
-    step_raw = forward_dot(whole, step_weight)
-    state_raw = forward_dot(whole, state_weight)
-    query_raw = forward_dot(whole, query_weight)
+    query_raw = forward_dot(whole, query_wide)
     pair_raw = forward_dot(whole, pair_weight)
-    small = (
+    small = ssd_small(
         input_kernel.astype(jnp.float32),
         input_shift.astype(jnp.float32),
         state_kernel.astype(jnp.float32),
@@ -300,49 +874,11 @@
         decay_log.astype(jnp.float32),
         skip_gain.astype(jnp.float32),
     )
-    gated, mamba_pull = jax.vjp(
-        partial(ssm_branch, length=length),
-        gate_raw,
-        input_raw,
-        step_raw,
-        state_raw,
-        small[0],
-        small[1],
-        small[2],
-        small[3],
-        small[4],
-        small[5],
-        small[6],
-    )
-    gated_low = gated.astype(jnp.bfloat16)
-    cosine, sine = rope_tables(length, HD)
-    scale = HD ** (-0.5)
-    causal = jnp.arange(length)[:, None] >= jnp.arange(length)[None, :]
-
-    def attend_forward(seq):
-        query_seq, pair_seq = seq
-        query = rotate(query_seq.reshape(length, heads_here, HD), cosine, sine).astype(jnp.bfloat16)
-        key = rotate(pair_seq[:, None, :HD], cosine, sine)[:, 0].astype(jnp.bfloat16)
-        value = pair_seq[:, HD:].astype(jnp.bfloat16)
-        scores = jnp.einsum("ihd,jd->hij", query, key, preferred_element_type=jnp.float32) * scale
-        scores = jnp.where(causal[None], scores, -jnp.inf)
-        peak = jnp.max(scores, axis=-1, keepdims=True)
-        total = jnp.log(jnp.sum(jnp.exp(scores - peak), axis=-1, keepdims=True)) + peak
-        probs = jnp.exp(scores - total).astype(jnp.bfloat16)
-        context = jnp.einsum("hij,jd->ihd", probs, value, preferred_element_type=jnp.float32)
-        return (
-            context.reshape(length, heads_here * HD).astype(jnp.bfloat16),
-            total,
-            query,
-            key,
-            value,
-        )
-
-    context_seq, totals, queries, keys, values = lax.map(
-        attend_forward,
-        (query_raw.reshape(seqs, length, heads_here * HD), pair_raw.reshape(seqs, length, 2 * HD)),
-    )
-    context_rows = context_seq.reshape(group, heads_here * HD)
+    gated_low, ssm_out, carries = ssd_forward(
+        input_raw, state_raw, gate_raw, step_raw, small, heads, length
+    )
+    context_wide, queries, pairs, totals = attend_forward(query_raw, pair_raw, length)
+    context_rows = context_wide[:, :query_cols]
     mixed_part = forward_dot(gated_low, mamba_output) + forward_dot(context_rows, context_weight)
     resid = rows + sum_all(mixed_part.astype(jnp.bfloat16), shards)
     factor_second = lax.rsqrt(jnp.mean(resid * resid, axis=-1, keepdims=True) + EPSILON)
@@ -382,76 +918,50 @@
     grad_mamba_out = grad_mixer_out[:ssm_rows]
     grad_context_w = grad_mixer_out[ssm_rows:]
     grad_gated = against(mixer_all, mamba_output)
-    pulled = mamba_pull(grad_gated)
-    grad_gate_raw = pulled[0].astype(jnp.bfloat16)
-    grad_input_raw = pulled[1].astype(jnp.bfloat16)
-    grad_step_raw = pulled[2].astype(jnp.bfloat16)
-    grad_state_raw = pulled[3].astype(jnp.bfloat16)
+    sigmoid_raw = jax.nn.sigmoid(gate_raw)
+    grad_gate_raw = (
+        grad_gated * ssm_out * (sigmoid_raw * (1.0 + gate_raw * (1.0 - sigmoid_raw)))
+    ).astype(jnp.bfloat16)
     grad_context = against(mixer_all, context_weight).astype(jnp.bfloat16)
-
-    def attend_backward(seq):
-        grad_seq, query, key, value, total = seq
-        grad_seq = grad_seq.reshape(length, heads_here, HD)
-        scores = jnp.einsum("ihd,jd->hij", query, key, preferred_element_type=jnp.float32) * scale
-        scores = jnp.where(causal[None], scores, -jnp.inf)
-        probs = jnp.exp(scores - total)
-        grad_value = jnp.einsum(
-            "hij,ihd->jd", probs.astype(jnp.bfloat16), grad_seq, preferred_element_type=jnp.float32
-        )
-        grad_probs = jnp.einsum("ihd,jd->hij", grad_seq, value, preferred_element_type=jnp.float32)
-        grad_scores = (
-            probs * (grad_probs - jnp.sum(probs * grad_probs, axis=-1, keepdims=True))
-        ).astype(jnp.bfloat16)
-        grad_query = (
-            jnp.einsum("hij,jd->ihd", grad_scores, key, preferred_element_type=jnp.float32) * scale
-        )
-        grad_key = (
-            jnp.einsum("hij,ihd->jd", grad_scores, query, preferred_element_type=jnp.float32)
-            * scale
-        )
-        grad_query = (
-            unrotate(grad_query, cosine, sine).reshape(length, heads_here * HD).astype(jnp.bfloat16)
-        )
-        grad_key = unrotate(grad_key[:, None, :], cosine, sine)[:, 0]
-        return (grad_query, jnp.concatenate([grad_key, grad_value], axis=1).astype(jnp.bfloat16))
-
-    grad_query_seq, grad_pair_seq = lax.map(
-        attend_backward,
-        (grad_context.reshape(seqs, length, heads_here * HD), queries, keys, values, totals),
-    )
-    grad_query_raw = grad_query_seq.reshape(group, heads_here * HD)
-    grad_pair_raw = grad_pair_seq.reshape(group, 2 * HD)
-    total = against(grad_gate_raw, mamba_gate)
-    total = total + against(grad_input_raw, mamba_input)
-    total = total + against(grad_step_raw, step_weight)
-    total = total + against(grad_state_raw, state_weight)
-    total = total + against(grad_query_raw, query_weight)
-    total = total + against(grad_pair_raw, pair_weight)
+    grad_query_raw, grad_pair_raw = attend_backward(
+        queries, pairs, totals, jnp.pad(grad_context, ((0, 0), (0, query_pad))), length
+    )
+    grad_query_raw = grad_query_raw[:, :query_cols]
+    early_cols = jnp.concatenate([grad_gate_raw, grad_query_raw], axis=1)
+    early = inner_rows(whole, early_cols)
+    early = sum_dp(early.astype(jnp.bfloat16), dp_size, False)
+    grad_input_raw, grad_state_raw, grad_step_raw, input_sums, state_sums, head_sums = ssd_backward(
+        input_raw, state_raw, gate_raw, step_raw, grad_gated, carries, small, heads, length
+    )
+    input_sums = jnp.sum(input_sums, axis=0)
+    state_sums = jnp.sum(state_sums, axis=0)
+    head_sums = jnp.sum(head_sums, axis=0)[:, :heads]
+    taps = input_kernel.shape[0]
+    late_cols = jnp.concatenate(
+        [grad_input_raw, grad_state_raw, grad_pair_raw, grad_step_raw], axis=1
+    )
+    total = against(early_cols, jnp.concatenate([mamba_gate, query_weight], axis=1))
+    total = total + against(
+        late_cols, jnp.concatenate([mamba_input, state_weight, pair_weight, step_wide], axis=1)
+    )
     total_low = total.astype(jnp.bfloat16)
     grad_first = jnp.sum(total_low.astype(jnp.float32) * normal_first, axis=0)
     width = whole.shape[1]
     gate_cols = grad_gate_raw.shape[1]
-    query_cols = grad_query_raw.shape[1]
     input_cols = grad_input_raw.shape[1]
     state_cols = grad_state_raw.shape[1]
-    step_cols = grad_step_raw.shape[1]
+    step_cols = heads
     pair_cols = grad_pair_raw.shape[1]
 
-    own_vectors = (pulled[4], pulled[5], pulled[8], pulled[9], pulled[10])
-    shared_vectors = (grad_first, grad_middle, pulled[6], pulled[7])
+    own_vectors = (input_sums[:taps], input_sums[taps], head_sums[0], head_sums[1], head_sums[2])
+    shared_vectors = (grad_first, grad_middle, state_sums[:taps], state_sums[taps])
     own_pack = column_pack(own_vectors, width).astype(jnp.bfloat16)
     shared_pack = column_pack(shared_vectors, width).astype(jnp.bfloat16)
     own_width = own_pack.shape[1]
     shared_width = shared_pack.shape[1]
 
-    early = inner_rows(whole, jnp.concatenate([grad_gate_raw, grad_query_raw], axis=1))
-    early = sum_dp(early.astype(jnp.bfloat16), dp_size, False)
-
     split_pairs = shards == KVH
-    late = inner_rows(
-        whole,
-        jnp.concatenate([grad_input_raw, grad_state_raw, grad_pair_raw, grad_step_raw], axis=1),
-    ).astype(jnp.bfloat16)
+    late = inner_rows(whole, late_cols).astype(jnp.bfloat16)
     marks = (input_cols, input_cols + state_cols, input_cols + state_cols + pair_cols)
     late_pair = late[:, marks[1] : marks[2]]
     if not split_pairs:
@@ -461,7 +971,7 @@
             spread, late_pair[:, HD:], (KVH + kv_head) * HD, 1
         )
     tail = jnp.concatenate(
-        [late[:, input_cols : marks[1]], late_pair, shared_pack, late[:, marks[2] :], own_pack],
+        [late[:, input_cols : marks[1]], late_pair, shared_pack, late[:, marks[2] : marks[2] + step_cols], own_pack],
         axis=1,
     )
     sent = state_cols + late_pair.shape[1] + shared_width

time: 765 us -> 438 us (0.57); the launches traced: 751 us -> 432 us
  local copies, waits for them, and re-layouts: 229 us -> 45.7 us
  matrix products: 144 us -> 33.2 us
  other arithmetic: 145 us -> 72 us
  Pallas kernels: 0 us -> 43.3 us
    dot_general x62 -> x0, matrix products: 91 us -> none  [the longest x12 34.5 us: ssd_block(): jnp.einsum('ijh,jhp->ihp', decay * intersection[:, :, None], scaled, prec...]
    dynamic_update_slice x8 -> x0, local copies, waits for them, and re-layouts: 85.4 us -> none  [ssd_sequence(): lax.scan(jax.checkpoint(partial(ssd_block, rates)), start, stacked)]
    pallas_call x0 -> x4, Pallas kernels: none -> 43.3 us  [the longest x1 22.7 us: ssd_backward(): pl.pallas_call(ssd_backward_kernel, grid=(seqs,), in_specs=[by_sequence(l...]
    squeeze x25 -> x1, local copies, waits for them, and re-layouts: 22.3 us -> 0.01 us  [body(): head_sums[2]]
    another operation x24 -> x3, other arithmetic: 17.8 us -> 0.01 us  [the longest x12 15.1 us: ssd_block(): cumul = jnp.cumsum(logdec, axis=0)]
    dot_general x11 -> x7, matrix products: 28 us -> 12.2 us  [against(): lax.dot_general(left, right, (((1,), (1,)), ((), ())), preferred_element_...]
    ppermute x28, waiting for transfers between devices: 48.8 us -> 63.4 us  [split_half(): got = lax.ppermute(give, 'dp', bit_pairs(size, bit))]
    exp x24 -> x0, local copies, waits for them, and re-layouts: 13.9 us -> none  [the longest x8 7.19 us: ssd_block(): jnp.exp(cumul)[:, :, None]]
  transfers between devices with their start and end apart: 63 -> 63, of which waited for: 27 -> 26; matrix products, arithmetic and copies ran while one was open for 44% -> 27% of each run, Pallas kernels for 0% -> 7%
where the time goes in v2:
time: 438 us; the launch traced here: 432 us
  waiting for transfers between devices  168 us (38%)
  other arithmetic  72 us (16%)
  starting transfers between devices  67.4 us (15%)
  local copies, waits for them, and re-layouts  45.7 us (10%)
  Pallas kernels  43.3 us (10%)
  matrix products  33.2 us (8%)
    ppermute x28, waiting for transfers between devices, split_half(): got = lax.ppermute(give, 'dp', bit_pairs(size, bit))  63.4 us
    ppermute x28, waiting for transfers between devices, join_half(): got = lax.ppermute(part, 'dp', bit_pairs(size, bit))  58.5 us
    ppermute x7, waiting for transfers between devices, other(): return lax.ppermute(part, 'tensor', [(0, 1), (1, 0)])  45.8 us
    ppermute x28, starting transfers between devices, split_half(): got = lax.ppermute(give, 'dp', bit_pairs(size, bit))  35.8 us
    convert_element_type x16, other arithmetic, body(): item.astype(jnp.float32)  26.1 us
    pallas_call x1, Pallas kernels, ssd_backward(): pl.pallas_call(ssd_backward_kernel, grid=(seqs,), in_specs=[by_sequence(l...  22.7 us
    ppermute x28, starting transfers between devices, join_half(): got = lax.ppermute(part, 'dp', bit_pairs(size, bit))  22.7 us
    unnamed x182, local copies, waits for them, and re-layouts  17.3 us
  transfers between devices with their start and end apart: 63, of which 26 were waited for; matrix products, arithmetic and copies ran while one was open for 27% of the time, Pallas kernels for 7%

profile of v2, /device:TPU:0, one launch (start us, length us, event | category | flops | bytes accessed | tf_op | source)
XLA Modules:
  0.0 432.4 jit_solution(6283981116346829141)
XLA Ops:
  0.7 3.0 collective-permute-start
  10.7 5.2 %collective-permute-done = bf16[256,1024]{1,0:T(8,128)(2,1)S(1)} collective-permute-done((bf16[256,1024]{1,0:T(8,128)(2,1)}, bf16[256,1024]{1,0:T(8,128)(2,1)S(1)}, u32[]{:S(2)}, u32[]{:S(2)}) %collective-permute-start) | collective-permute-done | bytes 524320 | tf_op jit(solution)/shard_map/ppermute | solution.py:762
  15.9 1.8 fusion.2
  23.0 8.7 %ssd_forward.1 = (bf16[512,768]{1,0:T(8,128)(2,1)S(1)}, f32[512,768]{1,0:T(8,128)S(1)}, f32[4,128,768]{2,1,0:T(8,128)S(1)}) custom-call(f32[512,768]{1,0:T(8,128)S(1)} %fusion.74.input_ref, f32[512,256]{1,0:T(8,128)S(1)} %fusion.75.state_ref, f32[512,768]{1,0:T(8,128)S(1)} %fusion.76.gate_ref, f32[512,128]{1,0:T(8,128)S(1)} %fusion.52.step_ref, ...), custom_call_target="tpu_custom_call" | custom-call | flops 402653184 | bytes 7864320 | tf_op jit(solution)/shard_map/ssd_forward/pallas_call | solution.py:416
  34.1 5.7 %attend_forward.1 = (bf16[512,256]{1,0:T(8,128)(2,1)S(1)}, bf16[512,256]{1,0:T(8,128)(2,1)S(1)}, bf16[512,128]{1,0:T(8,128)(2,1)S(1)}, f32[512,128]{1,0:T(8,128)S(1)}) custom-call(f32[512,256]{1,0:T(8,128)S(1)} %fusion.78.query_ref, f32[512,128]{1,0:T(8,128)S(1)} %fusion.40.pair_ref, f32[512,128]{1,0:T(8,128)S(1)} %copy-done.12, f32[512,128]{1,0:T(8,128)S(1)} %copy-done.13), custom_call_target="tpu_custom_call" | custom-call | flops 268435456 | bytes 1572864 | tf_op jit(solution)/shard_map/attend_forward/pallas_call | solution.py:654
  41.9 1.7 collective-permute-start.1
  46.8 1.7 pad.23.clone
  48.5 5.3 %concatenate.222 = bf16[1024,1280]{1,0:T(8,128)(2,1)} concatenate(bf16[1024,768]{1,0:T(8,128)(2,1)} %param.33, bf16[1024,256]{1,0:T(8,128)(2,1)} %param.35, bf16[1024,64]{1,0:T(8,128)(2,1)} %copy-done.48, bf16[1024,64]{1,0:T(8,128)(2,1)} %copy-done.49, bf16[1024,128]{1,0:T(8,128)(2,1)} %pad.23.clone), dimensions={1} | concatenate | bytes 5242880 | tf_op jit(solution)/shard_map/concatenate | solution.py:945
  55.2 13.1 %collective-permute-done.1 = bf16[512,1024]{1,0:T(8,128)(2,1)} collective-permute-done((bf16[512,1024]{1,0:T(8,128)(2,1)}, bf16[512,1024]{1,0:T(8,128)(2,1)}, u32[]{:S(2)}, u32[]{:S(2)}) %collective-permute-start.1) | collective-permute-done | bytes 1048608 | tf_op jit(solution)/shard_map/ppermute | solution.py:762
  68.3 2.9 multiply_reduce_fusion.2
  75.7 2.1 collective-permute-done.3
  77.8 3.6 multiply_convert_fusion
  92.7 2.9 convolution_convert_fusion.1
  97.3 25.4 %collective-permute-done.2 = bf16[256,1024]{1,0:T(8,128)(2,1)S(1)} collective-permute-done((bf16[256,1024]{1,0:T(8,128)(2,1)S(1)}, bf16[256,1024]{1,0:T(8,128)(2,1)S(1)}, u32[]{:S(2)}, u32[]{:S(2)}) %collective-permute-start.2) | collective-permute-done | bytes 524320 | tf_op jit(solution)/shard_map/ppermute | solution.py:762
  124.6 2.5 multiply_add_fusion
  130.0 22.7 %ssd_backward.1 = (bf16[512,768]{1,0:T(8,128)(2,1)S(1)}, bf16[512,256]{1,0:T(8,128)(2,1)S(1)}, bf16[512,128]{1,0:T(8,128)(2,1)S(1)}, f32[1,8,768]{2,1,0:T(8,128)...) custom-call(f32[512,768]{1,0:T(8,128)S(1)} %copy-done.5, f32[512,256]{1,0:T(8,128)S(1)} %fusion.75.state_ref, ...), custom_call_target="tpu_custom_call" | custom-call | flops 1006632960 | bytes 7864320 | tf_op jit(solution)/shard_map/ssd_backward/pallas_call | solution.py:465
  153.8 6.3 %attend_backward.1 = (bf16[512,256]{1,0:T(8,128)(2,1)S(1)}, bf16[512,128]{1,0:T(8,128)(2,1)S(1)}) custom-call(bf16[512,256]{1,0:T(8,128)(2,1)S(1)} %copy-done.30, bf16[512,128]{1,0:T(8,128)(2,1)S(1)} %copy-done.34, f32[512,128]{1,0:T(8,128)S(1)} %copy-done.32, bf16[512,256]{1,0:T(8,128)(2,1)S(1)} %convolution_convert_fusion.7.grad_ref, ...), custom_call_target="tpu_custom_call" | custom-call | flops 671088640 | bytes 1572864 | tf_op jit(solution)/shard_map/attend_backward/pallas_call | solution.py:689
  167.2 2.6 convolution_convert_fusion.5
  169.8 2.9 multiply_reduce_fusion
  183.3 1.7 copy-done.57
  186.7 1.8 fusion.11
  189.0 1.6 fusion.10
  193.5 12.2 %collective-permute-done.40 = bf16[256,1024]{1,0:T(8,128)(2,1)S(1)} collective-permute-done((bf16[256,1024]{1,0:T(8,128)(2,1)S(1)}, bf16[256,1024]{1,0:T(8,128)(2,1)S(1)}, u32[]{:S(2)}, u32[]{:S(2)}) %collective-permute-start.40) | collective-permute-done | bytes 524320 | tf_op jit(solution)/shard_map/ppermute | solution.py:728
  208.2 7.8 %collective-permute-done.56 = bf16[256,1024]{1,0:T(8,128)(2,1)S(1)} collective-permute-done((bf16[256,1024]{1,0:T(8,128)(2,1)S(1)}, bf16[256,1024]{1,0:T(8,128)(2,1)S(1)}, u32[]{:S(2)}, u32[]{:S(2)}) %collective-permute-start.56) | collective-permute-done | bytes 524320 | tf_op jit(solution)/shard_map/ppermute | solution.py:728
  219.9 5.4 %collective-permute-done.7 = bf16[256,404]{1,0:T(8,128)(2,1)S(1)} collective-permute-done((bf16[256,404]{1,0:T(8,128)(2,1)S(1)}, bf16[256,404]{1,0:T(8,128)(2,1)S(1)}, u32[]{:S(2)}, u32[]{:S(2)}) %collective-permute-start.7) | collective-permute-done | bytes 206880 | tf_op jit(solution)/shard_map/ppermute | solution.py:728
  227.7 2.8 collective-permute-done.8
  230.7 2.6 collective-permute-start.9
  234.1 3.4 collective-permute-done.9
  243.5 3.4 collective-permute-done.49
  248.2 2.8 collective-permute-start.42
  252.0 10.7 %collective-permute-done.11 = bf16[64,532]{0,1:T(8,128)(2,1)S(1)} collective-permute-done((bf16[64,532]{0,1:T(8,128)(2,1)S(1)}, bf16[64,532]{0,1:T(8,128)(2,1)S(1)}, u32[]{:S(2)}, u32[]{:S(2)}) %collective-permute-start.11) | collective-permute-done | bytes 68128 | tf_op jit(solution)/shard_map/ppermute | solution.py:734
  262.9 3.0 collective-permute-start.58
  265.9 10.8 %collective-permute-done.50 = bf16[64,1024]{1,0:T(8,128)(2,1)S(1)} collective-permute-done((bf16[64,1024]{1,0:T(8,128)(2,1)S(1)}, bf16[64,1024]{1,0:T(8,128)(2,1)S(1)}, u32[]{:S(2)}, u32[]{:S(2)}) %collective-permute-start.50) | collective-permute-done | bytes 131104 | tf_op jit(solution)/shard_map/ppermute | solution.py:728
  277.3 2.0 collective-permute-done.58
  279.4 3.9 collective-permute-done.12
  283.4 3.0 collective-permute-start.59
  286.4 1.9 fusion.14
  288.4 1.6 fusion.13
  290.9 2.1 collective-permute-start.32
  294.8 3.1 collective-permute-done.13
  298.8 10.1 %collective-permute-done.44 = bf16[128,1024]{1,0:T(8,128)(2,1)S(1)} collective-permute-done((bf16[128,1024]{1,0:T(8,128)(2,1)S(1)}, bf16[128,1024]{1,0:T(8,128)(2,1)S(1)}, u32[]{:S(2)}, u32[]{:S(2)}) %collective-permute-start.44) | collective-permute-done | bytes 262176 | tf_op jit(solution)/shard_map/ppermute | solution.py:734
  309.3 5.3 %collective-permute-done.25 = bf16[128,768]{1,0:T(8,128)(2,1)S(1)} collective-permute-done((bf16[128,768]{1,0:T(8,128)(2,1)S(1)}, bf16[128,768]{1,0:T(8,128)(2,1)S(1)}, u32[]{:S(2)}, u32[]{:S(2)}) %collective-permute-start.25) | collective-permute-done | bytes 196640 | tf_op jit(solution)/shard_map/ppermute | solution.py:728
  315.6 2.3 collective-permute-start.26
  318.1 3.3 collective-permute-done.26
  321.4 3.0 collective-permute-start.53
  324.4 3.1 collective-permute-start.27
  327.8 7.0 %collective-permute-done.27 = bf16[64,768]{1,0:T(8,128)(2,1)S(1)} collective-permute-done((bf16[64,768]{1,0:T(8,128)(2,1)S(1)}, bf16[64,768]{1,0:T(8,128)(2,1)S(1)}, u32[]{:S(2)}, u32[]{:S(2)}) %collective-permute-start.27) | collective-permute-done | bytes 98336 | tf_op jit(solution)/shard_map/ppermute | solution.py:734
  334.8 5.8 %collective-permute-start.17 = (bf16[128,1024]{1,0:T(8,128)(2,1)S(1)}, bf16[128,1024]{1,0:T(8,128)(2,1)S(1)}, u32[]{:S(2)}, u32[]{:S(2)}) collective-permute-start(bf16[128,1024]{1,0:T(8,128)(2,1)S(1)} %dynamic-slice_bitcast_fusion.19), channel_id=1, source_target_pairs={{0,8},{2,10},{4,12},{6,14},{8,0},{10,2},{12,4},{14,6},{16,24},{18,... | collective-permute-start | bytes 786440 | tf_op jit(solution)/shard_map/ppermute | solution.py:728
  341.0 6.1 %collective-permute-done.28 = bf16[128,768]{1,0:T(8,128)(2,1)S(1)} collective-permute-done((bf16[128,768]{1,0:T(8,128)(2,1)S(1)}, bf16[128,768]{1,0:T(8,128)(2,1)S(1)}, u32[]{:S(2)}, u32[]{:S(2)}) %collective-permute-start.28) | collective-permute-done | bytes 196640 | tf_op jit(solution)/shard_map/ppermute | solution.py:734
  349.3 7.0 %collective-permute-done.33 = bf16[128,1024]{1,0:T(8,128)(2,1)S(1)} collective-permute-done((bf16[128,1024]{1,0:T(8,128)(2,1)S(1)}, bf16[128,1024]{1,0:T(8,128)(2,1)S(1)}, u32[]{:S(2)}, u32[]{:S(2)}) %collective-permute-start.33) | collective-permute-done | bytes 262176 | tf_op jit(solution)/shard_map/ppermute | solution.py:728
  358.3 3.0 collective-permute-start.34
  368.1 1.7 collective-permute-start.19
  371.2 9.8 %collective-permute-done.19 = bf16[64,1024]{1,0:T(8,128)(2,1)S(1)} collective-permute-done((bf16[64,1024]{1,0:T(8,128)(2,1)S(1)}, bf16[64,1024]{1,0:T(8,128)(2,1)S(1)}, u32[]{:S(2)}, u32[]{:S(2)}) %collective-permute-start.19) | collective-permute-done | bytes 131104 | tf_op jit(solution)/shard_map/ppermute | solution.py:734
  384.2 4.3 collective-permute-done.20
  393.3 2.6 copy.80
  399.8 2.0 collective-permute-done.21
  402.4 2.0 maximum_select_fusion.9
  406.4 2.0 maximum_select_fusion.10
  409.0 4.4 %fusion.7 = f32[1024,1024]{1,0:T(8,128)} fusion(bf16[512,1024]{1,0:T(8,128)(2,1)} %collective-permute-done.46, bf16[512,1024]{1,0:T(8,128)(2,1)S(1)} %maximum_select_fusion.11, pred[]{:T(512)S(6)} %eq.11), kind=kLoop, calls=%fused_computation.16 | loop fusion | flops 10485760 | bytes 6291457 | tf_op jit(solution)/shard_map/convert_element_type | solution.py:1038
  413.4 5.2 %fusion.8 = f32[1024,1024]{1,0:T(8,128)} fusion(bf16[512,1024]{1,0:T(8,128)(2,1)} %collective-permute-done.54, bf16[512,1024]{1,0:T(8,128)(2,1)} %maximum_select_fusion.12, pred[]{:T(512)S(6)} %eq.11), kind=kLoop, calls=%fused_computation.18 | loop fusion | flops 10485760 | bytes 6291457 | tf_op jit(solution)/shard_map/convert_element_type | solution.py:1038
  418.5 3.2 fusion.9
  421.7 2.1 fusion.16
  425.9 1.9 slice_convert_fusion.1
  428.8 2.1 slice_convert_fusion
  (430 shorter events, 122.5 us)
Async XLA Ops:
  0.7 77.1 %copy-start = (bf16[1024,1024]{1,0:T(8,128)(2,1)S(1)}, bf16[1024,1024]{1,0:T(8,128)(2,1)}, u32[]{:S(2)}) copy-start(bf16[1024,1024]{1,0:T(8,128)(2,1)} %param.49) | copy-start | bytes 6291460
  0.7 15.2 %collective-permute-start = (bf16[256,1024]{1,0:T(8,128)(2,1)}, bf16[256,1024]{1,0:T(8,128)(2,1)S(1)}, u32[]{:S(2)}, u32[]{:S(2)}) collective-permute-start(bf16[256,1024]{1,0:T(8,128)(2,1)} %param.29), channel_id=1, source_target_pairs={{0,1},{1,0},{2,3},{3,2},{4,5},{5,4},{6,7},{7,6},{8,9},{9,8},{10,11... | collective-permute-start | bytes 1572872 | tf_op jit(solution)/shard_map/ppermute | solution.py:762
  41.9 26.4 %collective-permute-start.1 = (bf16[512,1024]{1,0:T(8,128)(2,1)}, bf16[512,1024]{1,0:T(8,128)(2,1)}, u32[]{:S(2)}, u32[]{:S(2)}) collective-permute-start(bf16[512,1024]{1,0:T(8,128)(2,1)} %add_convert_fusion.2), channel_id=1, source_target_pairs={{0,1},{1,0},{2,3},{3,2},{4,5},{5,4},{6,7},{7,6},{8,9},{9,8},{10,11... | collective-permute-start | bytes 3145736 | tf_op jit(solution)/shard_map/ppermute | solution.py:762
  43.6 34.2 %collective-permute-start.3 = (bf16[256,1024]{1,0:T(8,128)(2,1)}, bf16[256,1024]{1,0:T(8,128)(2,1)}, u32[]{:S(2)}, u32[]{:S(2)}) collective-permute-start(bf16[256,1024]{1,0:T(8,128)(2,1)} %param.50), channel_id=1, source_target_pairs={{0,1},{1,0},{2,3},{3,2},{4,5},{5,4},{6,7},{7,6},{8,9},{9,8},{10,11... | collective-permute-start | bytes 1572872 | tf_op jit(solution)/shard_map/ppermute | solution.py:762
  87.9 35.8 %collective-permute-start.4 = (bf16[512,1024]{1,0:T(8,128)(2,1)S(1)}, bf16[512,1024]{1,0:T(8,128)(2,1)S(1)}, u32[]{:S(2)}, u32[]{:S(2)}) collective-permute-start(bf16[512,1024]{1,0:T(8,128)(2,1)S(1)} %add_convert_fusion.1), channel_id=1, source_target_pairs={{0,1},{1,0},{2,3},{3,2},{4,5},{5,4},{6,7},{7,6},{8,9},{9,8},{10,11... | collective-permute-start | bytes 3145736 | tf_op jit(solution)/shard_map/ppermute | solution.py:762
  89.5 33.2 %collective-permute-start.2 = (bf16[256,1024]{1,0:T(8,128)(2,1)S(1)}, bf16[256,1024]{1,0:T(8,128)(2,1)S(1)}, u32[]{:S(2)}, u32[]{:S(2)}) collective-permute-start(bf16[256,1024]{1,0:T(8,128)(2,1)S(1)} %dynamic-slice_bitcast_fusion.13), channel_id=1, source_target_pairs={{0,1},{1,0},{2,3},{3,2},{4,5},{5,4},{6,7},{7,6},{8,9},{9,8},{10,11... | collective-permute-start | bytes 1572872 | tf_op jit(solution)/shard_map/ppermute | solution.py:762
  91.2 92.1 %collective-permute-start.39 = (bf16[512,1024]{1,0:T(8,128)(2,1)}, bf16[512,1024]{1,0:T(8,128)(2,1)}, u32[]{:S(2)}, u32[]{:S(2)}) collective-permute-start(bf16[512,1024]{1,0:T(8,128)(2,1)} %dynamic-slice_bitcast_fusion.2), channel_id=1, source_target_pairs={{0,2},{2,0},{4,6},{6,4},{8,10},{10,8},{12,14},{14,12},{16,18},{18,... | collective-permute-start | bytes 3145736 | tf_op jit(solution)/shard_map/ppermute | solution.py:728
  92.2 94.4 %collective-permute-start.47 = (bf16[512,1024]{1,0:T(8,128)(2,1)}, bf16[512,1024]{1,0:T(8,128)(2,1)}, u32[]{:S(2)}, u32[]{:S(2)}) collective-permute-start(bf16[512,1024]{1,0:T(8,128)(2,1)} %dynamic-slice_bitcast_fusion.1), channel_id=1, source_target_pairs={{0,2},{2,0},{4,6},{6,4},{8,10},{10,8},{12,14},{14,12},{16,18},{18,... | collective-permute-start | bytes 3145736 | tf_op jit(solution)/shard_map/ppermute | solution.py:728
  96.8 91.7 %collective-permute-start.55 = (bf16[512,1024]{1,0:T(8,128)(2,1)}, bf16[512,1024]{1,0:T(8,128)(2,1)}, u32[]{:S(2)}, u32[]{:S(2)}) collective-permute-start(bf16[512,1024]{1,0:T(8,128)(2,1)} %dynamic-slice_bitcast_fusion), channel_id=1, source_target_pairs={{0,2},{2,0},{4,6},{6,4},{8,10},{10,8},{12,14},{14,12},{16,18},{18,... | collective-permute-start | bytes 3145736 | tf_op jit(solution)/shard_map/ppermute | solution.py:728
  173.6 18.9 %collective-permute-start.5 = (bf16[256,1024]{1,0:T(8,128)(2,1)}, bf16[256,1024]{1,0:T(8,128)(2,1)S(1)}, u32[]{:S(2)}, u32[]{:S(2)}) collective-permute-start(bf16[256,1024]{1,0:T(8,128)(2,1)} %dynamic-slice_bitcast_fusion.12), channel_id=1, source_target_pairs={{0,1},{1,0},{2,3},{3,2},{4,5},{5,4},{6,7},{7,6},{8,9},{9,8},{10,11... | collective-permute-start | bytes 1572872 | tf_op jit(solution)/shard_map/ppermute | solution.py:762
  178.4 12.4 %collective-permute-start.6 = (bf16[512,404]{1,0:T(8,128)(2,1)S(1)}, bf16[512,404]{1,0:T(8,128)(2,1)S(1)}, u32[]{:S(2)}, u32[]{:S(2)}) collective-permute-start(bf16[512,404]{1,0:T(8,128)(2,1)S(1)} %dynamic-slice_bitcast_fusion.11), channel_id=1, source_target_pairs={{0,2},{2,0},{4,6},{6,4},{8,10},{10,8},{12,14},{14,12},{16,18},{18,... | collective-permute-start | bytes 1241096 | tf_op jit(solution)/shard_map/ppermute | solution.py:728
  183.3 100.0 %collective-permute-start.15 = (bf16[512,1024]{1,0:T(8,128)(2,1)}, bf16[512,1024]{1,0:T(8,128)(2,1)}, u32[]{:S(2)}, u32[]{:S(2)}) collective-permute-start(bf16[512,1024]{1,0:T(8,128)(2,1)} %dynamic-slice_bitcast_fusion.4), channel_id=1, source_target_pairs={{0,2},{2,0},{4,6},{6,4},{8,10},{10,8},{12,14},{14,12},{16,18},{18,... | collective-permute-start | bytes 3145736 | tf_op jit(solution)/shard_map/ppermute | solution.py:728
  186.7 52.3 %collective-permute-start.23 = (bf16[512,768]{1,0:T(8,128)(2,1)}, bf16[512,768]{1,0:T(8,128)(2,1)}, u32[]{:S(2)}, u32[]{:S(2)}) collective-permute-start(bf16[512,768]{1,0:T(8,128)(2,1)} %dynamic-slice_bitcast_fusion.5), channel_id=1, source_target_pairs={{0,2},{2,0},{4,6},{6,4},{8,10},{10,8},{12,14},{14,12},{16,18},{18,... | collective-permute-start | bytes 2359304 | tf_op jit(solution)/shard_map/ppermute | solution.py:728
  188.5 99.8 %collective-permute-start.31 = (bf16[512,1024]{1,0:T(8,128)(2,1)}, bf16[512,1024]{1,0:T(8,128)(2,1)}, u32[]{:S(2)}, u32[]{:S(2)}) collective-permute-start(bf16[512,1024]{1,0:T(8,128)(2,1)} %dynamic-slice_bitcast_fusion.3), channel_id=1, source_target_pairs={{0,2},{2,0},{4,6},{6,4},{8,10},{10,8},{12,14},{14,12},{16,18},{18,... | collective-permute-start | bytes 3145736 | tf_op jit(solution)/shard_map/ppermute | solution.py:728
  190.8 14.8 %collective-permute-start.40 = (bf16[256,1024]{1,0:T(8,128)(2,1)S(1)}, bf16[256,1024]{1,0:T(8,128)(2,1)S(1)}, u32[]{:S(2)}, u32[]{:S(2)}) collective-permute-start(bf16[256,1024]{1,0:T(8,128)(2,1)S(1)} %dynamic-slice_bitcast_fusion.8), channel_id=1, source_target_pairs={{0,4},{2,6},{4,0},{6,2},{8,12},{10,14},{12,8},{14,10},{16,20},{18,... | collective-permute-start | bytes 1572872 | tf_op jit(solution)/shard_map/ppermute | solution.py:728
  192.5 23.5 %collective-permute-start.56 = (bf16[256,1024]{1,0:T(8,128)(2,1)S(1)}, bf16[256,1024]{1,0:T(8,128)(2,1)S(1)}, u32[]{:S(2)}, u32[]{:S(2)}) collective-permute-start(bf16[256,1024]{1,0:T(8,128)(2,1)S(1)} %dynamic-slice_bitcast_fusion.6), channel_id=1, source_target_pairs={{0,4},{2,6},{4,0},{6,2},{8,12},{10,14},{12,8},{14,10},{16,20},{18,... | collective-permute-start | bytes 1572872 | tf_op jit(solution)/shard_map/ppermute | solution.py:728
  205.6 13.5 %collective-permute-start.48 = (bf16[256,1024]{1,0:T(8,128)(2,1)S(1)}, bf16[256,1024]{1,0:T(8,128)(2,1)S(1)}, u32[]{:S(2)}, u32[]{:S(2)}) collective-permute-start(bf16[256,1024]{1,0:T(8,128)(2,1)S(1)} %dynamic-slice_bitcast_fusion.7), channel_id=1, source_target_pairs={{0,8},{2,10},{4,12},{6,14},{8,0},{10,2},{12,4},{14,6},{16,24},{18,... | collective-permute-start | bytes 1572872 | tf_op jit(solution)/shard_map/ppermute | solution.py:728
  216.1 9.2 %collective-permute-start.7 = (bf16[256,404]{1,0:T(8,128)(2,1)S(1)}, bf16[256,404]{1,0:T(8,128)(2,1)S(1)}, u32[]{:S(2)}, u32[]{:S(2)}) collective-permute-start(bf16[256,404]{1,0:T(8,128)(2,1)S(1)} %dynamic-slice_bitcast_fusion.20), channel_id=1, source_target_pairs={{0,8},{2,10},{4,12},{6,14},{8,0},{10,2},{12,4},{14,6},{16,24},{18,... | collective-permute-start | bytes 620552 | tf_op jit(solution)/shard_map/ppermute | solution.py:728
  219.2 21.9 %collective-permute-start.41 = (bf16[128,1024]{1,0:T(8,128)(2,1)}, bf16[128,1024]{1,0:T(8,128)(2,1)}, u32[]{:S(2)}, u32[]{:S(2)}) collective-permute-start(bf16[128,1024]{1,0:T(8,128)(2,1)} %dynamic-slice_bitcast_fusion.17), channel_id=1, source_target_pairs={{0,8},{2,10},{4,12},{6,14},{8,0},{10,2},{12,4},{14,6},{16,24},{18,... | collective-permute-start | bytes 786440 | tf_op jit(solution)/shard_map/ppermute | solution.py:728
  225.4 5.0 %collective-permute-start.8 = (bf16[128,404]{1,0:T(8,128)(2,1)S(1)}, bf16[128,404]{1,0:T(8,128)(2,1)S(1)}, u32[]{:S(2)}, u32[]{:S(2)}) collective-permute-start(bf16[128,404]{1,0:T(8,128)(2,1)S(1)} %dynamic-slice_bitcast_fusion.27), channel_id=1, source_target_pairs={{0,4},{2,6},{4,0},{6,2},{8,12},{10,14},{12,8},{14,10},{16,20},{18,... | collective-permute-start | bytes 310280 | tf_op jit(solution)/shard_map/ppermute | solution.py:728
  230.7 6.9 %collective-permute-start.9 = (bf16[64,404]{0,1:T(8,128)(2,1)S(1)}, bf16[64,404]{0,1:T(8,128)(2,1)S(1)}, u32[]{:S(2)}, u32[]{:S(2)}) collective-permute-start(bf16[64,404]{0,1:T(8,128)(2,1)S(1)} %bitcast.314), channel_id=1, source_target_pairs={{0,16},{2,18},{4,20},{6,22},{8,24},{10,26},{12,28},{14,30},{16,0},... | collective-permute-start | bytes 155144 | tf_op jit(solution)/shard_map/ppermute | solution.py:728
  237.5 9.4 %collective-permute-start.49 = (bf16[128,1024]{1,0:T(8,128)(2,1)}, bf16[128,1024]{1,0:T(8,128)(2,1)S(1)}, u32[]{:S(2)}, u32[]{:S(2)}) collective-permute-start(bf16[128,1024]{1,0:T(8,128)(2,1)} %dynamic-slice_bitcast_fusion.16), channel_id=1, source_target_pairs={{0,4},{2,6},{4,0},{6,2},{8,12},{10,14},{12,8},{14,10},{16,20},{18,... | collective-permute-start | bytes 786440 | tf_op jit(solution)/shard_map/ppermute | solution.py:728
  239.0 9.2 %collective-permute-start.57 = (bf16[128,1024]{1,0:T(8,128)(2,1)}, bf16[128,1024]{1,0:T(8,128)(2,1)S(1)}, u32[]{:S(2)}, u32[]{:S(2)}) collective-permute-start(bf16[128,1024]{1,0:T(8,128)(2,1)} %dynamic-slice_bitcast_fusion.15), channel_id=1, source_target_pairs={{0,8},{2,10},{4,12},{6,14},{8,0},{10,2},{12,4},{14,6},{16,24},{18,... | collective-permute-start | bytes 786440 | tf_op jit(solution)/shard_map/ppermute | solution.py:728
  241.1 10.0 %collective-permute-start.10 = (bf16[64,388]{0,1:T(8,128)(2,1)S(1)}, bf16[64,388]{0,1:T(8,128)(2,1)S(1)}, u32[]{:S(2)}, u32[]{:S(2)}) collective-permute-start(bf16[64,388]{0,1:T(8,128)(2,1)S(1)} %slice.177), channel_id=1, source_target_pairs={{0,1},{1,0},{2,3},{3,2},{4,5},{5,4},{6,7},{7,6},{8,9},{9,8},{10,11... | collective-permute-start | bytes 149000 | tf_op jit(solution)/shard_map/ppermute | solution.py:762
  246.9 46.3 %collective-permute-start.24 = (bf16[256,768]{1,0:T(8,128)(2,1)}, bf16[256,768]{1,0:T(8,128)(2,1)S(1)}, u32[]{:S(2)}, u32[]{:S(2)}) collective-permute-start(bf16[256,768]{1,0:T(8,128)(2,1)} %dynamic-slice_bitcast_fusion.14), channel_id=1, source_target_pairs={{0,4},{2,6},{4,0},{6,2},{8,12},{10,14},{12,8},{14,10},{16,20},{18,... | collective-permute-start | bytes 1179656 | tf_op jit(solution)/shard_map/ppermute | solution.py:728
  248.2 14.7 %collective-permute-start.42 = (bf16[64,1024]{1,0:T(8,128)(2,1)S(1)}, bf16[64,1024]{1,0:T(8,128)(2,1)S(1)}, u32[]{:S(2)}, u32[]{:S(2)}) collective-permute-start(bf16[64,1024]{1,0:T(8,128)(2,1)S(1)} %dynamic-slice_bitcast_fusion.24), channel_id=1, source_target_pairs={{0,16},{2,18},{4,20},{6,22},{8,24},{10,26},{12,28},{14,30},{16,0},... | collective-permute-start | bytes 393224 | tf_op jit(solution)/shard_map/ppermute | solution.py:728
  251.7 11.0 %collective-permute-start.11 = (bf16[64,532]{0,1:T(8,128)(2,1)S(1)}, bf16[64,532]{0,1:T(8,128)(2,1)S(1)}, u32[]{:S(2)}, u32[]{:S(2)}) collective-permute-start(bf16[64,532]{0,1:T(8,128)(2,1)S(1)} %concatenate.226), channel_id=1, source_target_pairs={{0,16},{2,18},{4,20},{6,22},{8,24},{10,26},{12,28},{14,30},{16,0},... | collective-permute-start | bytes 204296 | tf_op jit(solution)/shard_map/ppermute | solution.py:734
  262.7 14.0 %collective-permute-start.50 = (bf16[64,1024]{1,0:T(8,128)(2,1)S(1)}, bf16[64,1024]{1,0:T(8,128)(2,1)S(1)}, u32[]{:S(2)}, u32[]{:S(2)}) collective-permute-start(bf16[64,1024]{1,0:T(8,128)(2,1)S(1)} %dynamic-slice_bitcast_fusion.23), channel_id=1, source_target_pairs={{0,16},{2,18},{4,20},{6,22},{8,24},{10,26},{12,28},{14,30},{16,0},... | collective-permute-start | bytes 393224 | tf_op jit(solution)/shard_map/ppermute | solution.py:728
  262.9 16.5 %collective-permute-start.58 = (bf16[64,1024]{1,0:T(8,128)(2,1)S(1)}, bf16[64,1024]{1,0:T(8,128)(2,1)S(1)}, u32[]{:S(2)}, u32[]{:S(2)}) collective-permute-start(bf16[64,1024]{1,0:T(8,128)(2,1)S(1)} %dynamic-slice_bitcast_fusion.22), channel_id=1, source_target_pairs={{0,16},{2,18},{4,20},{6,22},{8,24},{10,26},{12,28},{14,30},{16,0},... | collective-permute-start | bytes 393224 | tf_op jit(solution)/shard_map/ppermute | solution.py:728
  276.7 6.6 %collective-permute-start.12 = (bf16[128,532]{0,1:T(8,128)(2,1)S(1)}, bf16[128,532]{0,1:T(8,128)(2,1)S(1)}, u32[]{:S(2)}, u32[]{:S(2)}) collective-permute-start(bf16[128,532]{0,1:T(8,128)(2,1)S(1)} %maximum_select_fusion.29), channel_id=1, source_target_pairs={{0,4},{2,6},{4,0},{6,2},{8,12},{10,14},{12,8},{14,10},{16,20},{18,... | collective-permute-start | bytes 408584 | tf_op jit(solution)/shard_map/ppermute | solution.py:734
  279.3 10.8 %collective-permute-start.43 = (bf16[64,1024]{1,0:T(8,128)(2,1)S(1)}, bf16[64,1024]{1,0:T(8,128)(2,1)S(1)}, u32[]{:S(2)}, u32[]{:S(2)}) collective-permute-start(bf16[64,1024]{1,0:T(8,128)(2,1)S(1)} %fusion.46), channel_id=1, source_target_pairs={{0,16},{2,18},{4,20},{6,22},{8,24},{10,26},{12,28},{14,30},{16,0},... | collective-permute-start | bytes 393224 | tf_op jit(solution)/shard_map/ppermute | solution.py:734
  283.3 7.6 %collective-permute-start.51 = (bf16[64,1024]{1,0:T(8,128)(2,1)S(1)}, bf16[64,1024]{1,0:T(8,128)(2,1)S(1)}, u32[]{:S(2)}, u32[]{:S(2)}) collective-permute-start(bf16[64,1024]{1,0:T(8,128)(2,1)S(1)} %fusion.45), channel_id=1, source_target_pairs={{0,16},{2,18},{4,20},{6,22},{8,24},{10,26},{12,28},{14,30},{16,0},... | collective-permute-start | bytes 393224 | tf_op jit(solution)/shard_map/ppermute | solution.py:734
  283.4 9.6 %collective-permute-start.59 = (bf16[64,1024]{1,0:T(8,128)(2,1)S(1)}, bf16[64,1024]{1,0:T(8,128)(2,1)S(1)}, u32[]{:S(2)}, u32[]{:S(2)}) collective-permute-start(bf16[64,1024]{1,0:T(8,128)(2,1)S(1)} %fusion.44), channel_id=1, source_target_pairs={{0,16},{2,18},{4,20},{6,22},{8,24},{10,26},{12,28},{14,30},{16,0},... | collective-permute-start | bytes 393224 | tf_op jit(solution)/shard_map/ppermute | solution.py:734
  288.3 9.6 %collective-permute-start.13 = (bf16[256,532]{0,1:T(8,128)(2,1)S(1)}, bf16[256,532]{0,1:T(8,128)(2,1)S(1)}, u32[]{:S(2)}, u32[]{:S(2)}) collective-permute-start(bf16[256,532]{0,1:T(8,128)(2,1)S(1)} %maximum_select_fusion.22), channel_id=1, source_target_pairs={{0,8},{2,10},{4,12},{6,14},{8,0},{10,2},{12,4},{14,6},{16,24},{18,... | collective-permute-start | bytes 817160 | tf_op jit(solution)/shard_map/ppermute | solution.py:734
  290.1 34.3 %collective-permute-start.16 = (bf16[256,1024]{1,0:T(8,128)(2,1)S(1)}, bf16[256,1024]{1,0:T(8,128)(2,1)S(1)}, u32[]{:S(2)}, u32[]{:S(2)}) collective-permute-start(bf16[256,1024]{1,0:T(8,128)(2,1)S(1)} %dynamic-slice_bitcast_fusion.10), channel_id=1, source_target_pairs={{0,4},{2,6},{4,0},{6,2},{8,12},{10,14},{12,8},{14,10},{16,20},{18,... | collective-permute-start | bytes 1572872 | tf_op jit(solution)/shard_map/ppermute | solution.py:728
  290.9 49.8 %collective-permute-start.32 = (bf16[256,1024]{1,0:T(8,128)(2,1)S(1)}, bf16[256,1024]{1,0:T(8,128)(2,1)S(1)}, u32[]{:S(2)}, u32[]{:S(2)}) collective-permute-start(bf16[256,1024]{1,0:T(8,128)(2,1)S(1)} %dynamic-slice_bitcast_fusion.9), channel_id=1, source_target_pairs={{0,8},{2,10},{4,12},{6,14},{8,0},{10,2},{12,4},{14,6},{16,24},{18,... | collective-permute-start | bytes 1572872 | tf_op jit(solution)/shard_map/ppermute | solution.py:728
  293.0 15.9 %collective-permute-start.44 = (bf16[128,1024]{1,0:T(8,128)(2,1)S(1)}, bf16[128,1024]{1,0:T(8,128)(2,1)S(1)}, u32[]{:S(2)}, u32[]{:S(2)}) collective-permute-start(bf16[128,1024]{1,0:T(8,128)(2,1)S(1)} %maximum_select_fusion.25), channel_id=1, source_target_pairs={{0,8},{2,10},{4,12},{6,14},{8,0},{10,2},{12,4},{14,6},{16,24},{18,... | collective-permute-start | bytes 786440 | tf_op jit(solution)/shard_map/ppermute | solution.py:734
  293.2 15.9 %collective-permute-start.52 = (bf16[128,1024]{1,0:T(8,128)(2,1)S(1)}, bf16[128,1024]{1,0:T(8,128)(2,1)S(1)}, u32[]{:S(2)}, u32[]{:S(2)}) collective-permute-start(bf16[128,1024]{1,0:T(8,128)(2,1)S(1)} %maximum_select_fusion.26), channel_id=1, source_target_pairs={{0,4},{2,6},{4,0},{6,2},{8,12},{10,14},{12,8},{14,10},{16,20},{18,... | collective-permute-start | bytes 786440 | tf_op jit(solution)/shard_map/ppermute | solution.py:734
  297.9 17.7 %collective-permute-start.60 = (bf16[128,1024]{1,0:T(8,128)(2,1)S(1)}, bf16[128,1024]{1,0:T(8,128)(2,1)S(1)}, u32[]{:S(2)}, u32[]{:S(2)}) collective-permute-start(bf16[128,1024]{1,0:T(8,128)(2,1)S(1)} %maximum_select_fusion.27), channel_id=1, source_target_pairs={{0,8},{2,10},{4,12},{6,14},{8,0},{10,2},{12,4},{14,6},{16,24},{18,... | collective-permute-start | bytes 786440 | tf_op jit(solution)/shard_map/ppermute | solution.py:734
  308.9 5.7 %collective-permute-start.25 = (bf16[128,768]{1,0:T(8,128)(2,1)S(1)}, bf16[128,768]{1,0:T(8,128)(2,1)S(1)}, u32[]{:S(2)}, u32[]{:S(2)}) collective-permute-start(bf16[128,768]{1,0:T(8,128)(2,1)S(1)} %dynamic-slice_bitcast_fusion.21), channel_id=1, source_target_pairs={{0,8},{2,10},{4,12},{6,14},{8,0},{10,2},{12,4},{14,6},{16,24},{18,... | collective-permute-start | bytes 589832 | tf_op jit(solution)/shard_map/ppermute | solution.py:728
  309.1 55.3 %collective-permute-start.14 = (bf16[512,532]{0,1:T(8,128)(2,1)S(1)}, bf16[512,532]{0,1:T(8,128)(2,1)S(1)}, u32[]{:S(2)}, u32[]{:S(2)}) collective-permute-start(bf16[512,532]{0,1:T(8,128)(2,1)S(1)} %maximum_select_fusion.15), channel_id=1, source_target_pairs={{0,2},{2,0},{4,6},{6,4},{8,10},{10,8},{12,14},{14,12},{16,18},{18,... | collective-permute-start | bytes 1634312 | tf_op jit(solution)/shard_map/ppermute | solution.py:734
  314.6 43.1 %collective-permute-start.45 = (bf16[256,1024]{1,0:T(8,128)(2,1)S(1)}, bf16[256,1024]{1,0:T(8,128)(2,1)S(1)}, u32[]{:S(2)}, u32[]{:S(2)}) collective-permute-start(bf16[256,1024]{1,0:T(8,128)(2,1)S(1)} %maximum_select_fusion.18), channel_id=1, source_target_pairs={{0,4},{2,6},{4,0},{6,2},{8,12},{10,14},{12,8},{14,10},{16,20},{18,... | collective-permute-start | bytes 1572872 | tf_op jit(solution)/shard_map/ppermute | solution.py:734
  315.6 5.8 %collective-permute-start.26 = (bf16[64,768]{1,0:T(8,128)(2,1)S(1)}, bf16[64,768]{1,0:T(8,128)(2,1)S(1)}, u32[]{:S(2)}, u32[]{:S(2)}) collective-permute-start(bf16[64,768]{1,0:T(8,128)(2,1)S(1)} %dynamic-slice_bitcast_fusion.28), channel_id=1, source_target_pairs={{0,16},{2,18},{4,20},{6,22},{8,24},{10,26},{12,28},{14,30},{16,0},... | collective-permute-start | bytes 294920 | tf_op jit(solution)/shard_map/ppermute | solution.py:728
  321.4 36.9 %collective-permute-start.53 = (bf16[256,1024]{1,0:T(8,128)(2,1)S(1)}, bf16[256,1024]{1,0:T(8,128)(2,1)S(1)}, u32[]{:S(2)}, u32[]{:S(2)}) collective-permute-start(bf16[256,1024]{1,0:T(8,128)(2,1)S(1)} %maximum_select_fusion.19), channel_id=1, source_target_pairs={{0,8},{2,10},{4,12},{6,14},{8,0},{10,2},{12,4},{14,6},{16,24},{18,... | collective-permute-start | bytes 1572872 | tf_op jit(solution)/shard_map/ppermute | solution.py:734
  324.4 10.4 %collective-permute-start.27 = (bf16[64,768]{1,0:T(8,128)(2,1)S(1)}, bf16[64,768]{1,0:T(8,128)(2,1)S(1)}, u32[]{:S(2)}, u32[]{:S(2)}) collective-permute-start(bf16[64,768]{1,0:T(8,128)(2,1)S(1)} %fusion.51), channel_id=1, source_target_pairs={{0,16},{2,18},{4,20},{6,22},{8,24},{10,26},{12,28},{14,30},{16,0},... | collective-permute-start | bytes 294920 | tf_op jit(solution)/shard_map/ppermute | solution.py:734
  334.8 13.6 %collective-permute-start.17 = (bf16[128,1024]{1,0:T(8,128)(2,1)S(1)}, bf16[128,1024]{1,0:T(8,128)(2,1)S(1)}, u32[]{:S(2)}, u32[]{:S(2)}) collective-permute-start(bf16[128,1024]{1,0:T(8,128)(2,1)S(1)} %dynamic-slice_bitcast_fusion.19), channel_id=1, source_target_pairs={{0,8},{2,10},{4,12},{6,14},{8,0},{10,2},{12,4},{14,6},{16,24},{18,... | collective-permute-start | bytes 786440 | tf_op jit(solution)/shard_map/ppermute | solution.py:728
  340.6 6.4 %collective-permute-start.28 = (bf16[128,768]{1,0:T(8,128)(2,1)S(1)}, bf16[128,768]{1,0:T(8,128)(2,1)S(1)}, u32[]{:S(2)}, u32[]{:S(2)}) collective-permute-start(bf16[128,768]{1,0:T(8,128)(2,1)S(1)} %maximum_select_fusion.28), channel_id=1, source_target_pairs={{0,8},{2,10},{4,12},{6,14},{8,0},{10,2},{12,4},{14,6},{16,24},{18,... | collective-permute-start | bytes 589832 | tf_op jit(solution)/shard_map/ppermute | solution.py:734
  347.0 9.2 %collective-permute-start.33 = (bf16[128,1024]{1,0:T(8,128)(2,1)S(1)}, bf16[128,1024]{1,0:T(8,128)(2,1)S(1)}, u32[]{:S(2)}, u32[]{:S(2)}) collective-permute-start(bf16[128,1024]{1,0:T(8,128)(2,1)S(1)} %dynamic-slice_bitcast_fusion.18), channel_id=1, source_target_pairs={{0,4},{2,6},{4,0},{6,2},{8,12},{10,14},{12,8},{14,10},{16,20},{18,... | collective-permute-start | bytes 786440 | tf_op jit(solution)/shard_map/ppermute | solution.py:728
  348.4 14.5 %collective-permute-start.61 = (bf16[256,1024]{1,0:T(8,128)(2,1)S(1)}, bf16[256,1024]{1,0:T(8,128)(2,1)S(1)}, u32[]{:S(2)}, u32[]{:S(2)}) collective-permute-start(bf16[256,1024]{1,0:T(8,128)(2,1)S(1)} %maximum_select_fusion.20), channel_id=1, source_target_pairs={{0,4},{2,6},{4,0},{6,2},{8,12},{10,14},{12,8},{14,10},{16,20},{18,... | collective-permute-start | bytes 1572872 | tf_op jit(solution)/shard_map/ppermute | solution.py:734
  356.3 48.2 %collective-permute-start.29 = (bf16[256,768]{1,0:T(8,128)(2,1)S(1)}, bf16[256,768]{1,0:T(8,128)(2,1)}, u32[]{:S(2)}, u32[]{:S(2)}) collective-permute-start(bf16[256,768]{1,0:T(8,128)(2,1)S(1)} %maximum_select_fusion.21), channel_id=1, source_target_pairs={{0,4},{2,6},{4,0},{6,2},{8,12},{10,14},{12,8},{14,10},{16,20},{18,... | collective-permute-start | bytes 1179656 | tf_op jit(solution)/shard_map/ppermute | solution.py:734
  357.7 10.3 %collective-permute-start.18 = (bf16[64,1024]{1,0:T(8,128)(2,1)S(1)}, bf16[64,1024]{1,0:T(8,128)(2,1)S(1)}, u32[]{:S(2)}, u32[]{:S(2)}) collective-permute-start(bf16[64,1024]{1,0:T(8,128)(2,1)S(1)} %dynamic-slice_bitcast_fusion.26), channel_id=1, source_target_pairs={{0,16},{2,18},{4,20},{6,22},{8,24},{10,26},{12,28},{14,30},{16,0},... | collective-permute-start | bytes 393224 | tf_op jit(solution)/shard_map/ppermute | solution.py:728
  358.3 11.5 %collective-permute-start.34 = (bf16[64,1024]{1,0:T(8,128)(2,1)S(1)}, bf16[64,1024]{1,0:T(8,128)(2,1)S(1)}, u32[]{:S(2)}, u32[]{:S(2)}) collective-permute-start(bf16[64,1024]{1,0:T(8,128)(2,1)S(1)} %dynamic-slice_bitcast_fusion.25), channel_id=1, source_target_pairs={{0,16},{2,18},{4,20},{6,22},{8,24},{10,26},{12,28},{14,30},{16,0},... | collective-permute-start | bytes 393224 | tf_op jit(solution)/shard_map/ppermute | solution.py:728
  362.9 45.5 %collective-permute-start.46 = (bf16[512,1024]{1,0:T(8,128)(2,1)S(1)}, bf16[512,1024]{1,0:T(8,128)(2,1)}, u32[]{:S(2)}, u32[]{:S(2)}) collective-permute-start(bf16[512,1024]{1,0:T(8,128)(2,1)S(1)} %maximum_select_fusion.11), channel_id=1, source_target_pairs={{0,2},{2,0},{4,6},{6,4},{8,10},{10,8},{12,14},{14,12},{16,18},{18,... | collective-permute-start | bytes 3145736 | tf_op jit(solution)/shard_map/ppermute | solution.py:734
  364.4 49.0 %collective-permute-start.54 = (bf16[512,1024]{1,0:T(8,128)(2,1)}, bf16[512,1024]{1,0:T(8,128)(2,1)}, u32[]{:S(2)}, u32[]{:S(2)}) collective-permute-start(bf16[512,1024]{1,0:T(8,128)(2,1)} %maximum_select_fusion.12), channel_id=1, source_target_pairs={{0,2},{2,0},{4,6},{6,4},{8,10},{10,8},{12,14},{14,12},{16,18},{18,... | collective-permute-start | bytes 3145736 | tf_op jit(solution)/shard_map/ppermute | solution.py:734
  368.1 12.8 %collective-permute-start.19 = (bf16[64,1024]{1,0:T(8,128)(2,1)S(1)}, bf16[64,1024]{1,0:T(8,128)(2,1)S(1)}, u32[]{:S(2)}, u32[]{:S(2)}) collective-permute-start(bf16[64,1024]{1,0:T(8,128)(2,1)S(1)} %fusion.48), channel_id=1, source_target_pairs={{0,16},{2,18},{4,20},{6,22},{8,24},{10,26},{12,28},{14,30},{16,0},... | collective-permute-start | bytes 393224 | tf_op jit(solution)/shard_map/ppermute | solution.py:734
  369.8 13.2 %collective-permute-start.35 = (bf16[64,1024]{1,0:T(8,128)(2,1)S(1)}, bf16[64,1024]{1,0:T(8,128)(2,1)S(1)}, u32[]{:S(2)}, u32[]{:S(2)}) collective-permute-start(bf16[64,1024]{1,0:T(8,128)(2,1)S(1)} %fusion.47), channel_id=1, source_target_pairs={{0,16},{2,18},{4,20},{6,22},{8,24},{10,26},{12,28},{14,30},{16,0},... | collective-permute-start | bytes 393224 | tf_op jit(solution)/shard_map/ppermute | solution.py:734
  381.0 7.5 %collective-permute-start.20 = (bf16[128,1024]{1,0:T(8,128)(2,1)S(1)}, bf16[128,1024]{1,0:T(8,128)(2,1)S(1)}, u32[]{:S(2)}, u32[]{:S(2)}) collective-permute-start(bf16[128,1024]{1,0:T(8,128)(2,1)S(1)} %maximum_select_fusion.23), channel_id=1, source_target_pairs={{0,8},{2,10},{4,12},{6,14},{8,0},{10,2},{12,4},{14,6},{16,24},{18,... | collective-permute-start | bytes 786440 | tf_op jit(solution)/shard_map/ppermute | solution.py:734
  383.0 8.7 %collective-permute-start.36 = (bf16[128,1024]{1,0:T(8,128)(2,1)S(1)}, bf16[128,1024]{1,0:T(8,128)(2,1)S(1)}, u32[]{:S(2)}, u32[]{:S(2)}) collective-permute-start(bf16[128,1024]{1,0:T(8,128)(2,1)S(1)} %maximum_select_fusion.24), channel_id=1, source_target_pairs={{0,4},{2,6},{4,0},{6,2},{8,12},{10,14},{12,8},{14,10},{16,20},{18,... | collective-permute-start | bytes 786440 | tf_op jit(solution)/shard_map/ppermute | solution.py:734
  389.4 12.5 %collective-permute-start.21 = (bf16[256,1024]{1,0:T(8,128)(2,1)}, bf16[256,1024]{1,0:T(8,128)(2,1)}, u32[]{:S(2)}, u32[]{:S(2)}) collective-permute-start(bf16[256,1024]{1,0:T(8,128)(2,1)} %maximum_select_fusion.16), channel_id=1, source_target_pairs={{0,4},{2,6},{4,0},{6,2},{8,12},{10,14},{12,8},{14,10},{16,20},{18,... | collective-permute-start | bytes 1572872 | tf_op jit(solution)/shard_map/ppermute | solution.py:734
  392.7 13.7 %collective-permute-start.37 = (bf16[256,1024]{1,0:T(8,128)(2,1)}, bf16[256,1024]{1,0:T(8,128)(2,1)}, u32[]{:S(2)}, u32[]{:S(2)}) collective-permute-start(bf16[256,1024]{1,0:T(8,128)(2,1)} %maximum_select_fusion.17), channel_id=1, source_target_pairs={{0,8},{2,10},{4,12},{6,14},{8,0},{10,2},{12,4},{14,6},{16,24},{18,... | collective-permute-start | bytes 1572872 | tf_op jit(solution)/shard_map/ppermute | solution.py:734
  401.9 16.7 %collective-permute-start.62 = (bf16[512,1024]{1,0:T(8,128)(2,1)S(1)}, bf16[512,1024]{1,0:T(8,128)(2,1)S(1)}, u32[]{:S(2)}, u32[]{:S(2)}) collective-permute-start(bf16[512,1024]{1,0:T(8,128)(2,1)S(1)} %copy-done.43), channel_id=1, source_target_pairs={{0,2},{2,0},{4,6},{6,4},{8,10},{10,8},{12,14},{14,12},{16,18},{18,... | collective-permute-start | bytes 3145736 | tf_op jit(solution)/shard_map/ppermute | solution.py:734
  404.5 19.3 %collective-permute-start.22 = (bf16[512,1024]{1,0:T(8,128)(2,1)S(1)}, bf16[512,1024]{1,0:T(8,128)(2,1)S(1)}, u32[]{:S(2)}, u32[]{:S(2)}) collective-permute-start(bf16[512,1024]{1,0:T(8,128)(2,1)S(1)} %maximum_select_fusion.9), channel_id=1, source_target_pairs={{0,2},{2,0},{4,6},{6,4},{8,10},{10,8},{12,14},{14,12},{16,18},{18,... | collective-permute-start | bytes 3145736 | tf_op jit(solution)/shard_map/ppermute | solution.py:734
  406.4 15.3 %collective-permute-start.30 = (bf16[512,768]{1,0:T(8,128)(2,1)S(1)}, bf16[512,768]{1,0:T(8,128)(2,1)S(1)}, u32[]{:S(2)}, u32[]{:S(2)}) collective-permute-start(bf16[512,768]{1,0:T(8,128)(2,1)S(1)} %maximum_select_fusion.14), channel_id=1, source_target_pairs={{0,2},{2,0},{4,6},{6,4},{8,10},{10,8},{12,14},{14,12},{16,18},{18,... | collective-permute-start | bytes 2359304 | tf_op jit(solution)/shard_map/ppermute | solution.py:734
  408.4 19.3 %collective-permute-start.38 = (bf16[512,1024]{1,0:T(8,128)(2,1)S(1)}, bf16[512,1024]{1,0:T(8,128)(2,1)S(1)}, u32[]{:S(2)}, u32[]{:S(2)}) collective-permute-start(bf16[512,1024]{1,0:T(8,128)(2,1)S(1)} %maximum_select_fusion.10), channel_id=1, source_target_pairs={{0,2},{2,0},{4,6},{6,4},{8,10},{10,8},{12,14},{14,12},{16,18},{18,... | collective-permute-start | bytes 3145736 | tf_op jit(solution)/shard_map/ppermute | solution.py:734
  (84 other events, 533.6 us)

commit v3 on v2

--- a/solution.py
+++ b/solution.py
@@ -720,11 +720,15 @@
     return [(index, index ^ (1 << bit)) for index in range(size)]
 
 
-def split_half(part, bit, size):
+def split_sides(part, bit):
     side = (lax.axis_index("dp") >> bit) & 1
     halves = part.reshape(2, part.shape[0] // 2, part.shape[1])
     keep = lax.dynamic_index_in_dim(halves, side, 0, False)
     give = lax.dynamic_index_in_dim(halves, 1 - side, 0, False)
+    return keep, give
+
+
+def add_half(keep, give, bit, size):
     got = lax.ppermute(give, "dp", bit_pairs(size, bit))
     return (keep.astype(jnp.float32) + got.astype(jnp.float32)).astype(jnp.bfloat16)
 
@@ -737,25 +741,55 @@
     )
 
 
+def after(part, *deps):
+    return lax.optimization_barrier((part,) + deps)[0]
+
+
+def behind(part, dep):
+    zero = jnp.minimum(jnp.abs(dep[:1, :1].astype(jnp.float32)), 0.0)
+    return part + zero.astype(part.dtype)
+
+
+class Sum:
+    def __init__(self, part, size, swapped):
+        self.size = size
+        self.direct = bool(size & (size - 1) or part.shape[0] % size)
+        self.order = [] if self.direct else bit_order(size, swapped)
+        self.part = part
+        self.step = 0
+        self.give = part
+        self.prepare()
+
+    def prepare(self):
+        if self.step < len(self.order):
+            self.keep, self.give = split_sides(self.part, self.order[self.step])
+        else:
+            self.give = self.part
+
+    def advance(self):
+        if self.step < len(self.order):
+            self.part = add_half(self.keep, self.give, self.order[self.step], self.size)
+            self.step += 1
+            self.prepare()
+        return self.give
+
+    def finish(self, middle=None):
+        while self.step < len(self.order):
+            self.advance()
+        if self.direct:
+            self.part = lax.psum(self.part, "dp")
+        if middle is not None:
+            self.part = middle(self.part)
+        for bit in reversed(self.order):
+            self.part = join_half(self.part, bit, self.size)
+        return self.part
+
+
 def bit_order(size, swapped):
     order = list(range(size.bit_length() - 1))
     if swapped and len(order) > 2:
         order[1], order[2] = order[2], order[1]
     return order
-
-
-def sum_dp(part, size, swapped, middle=None):
-    if size & (size - 1) or part.shape[0] % size:
-        part = lax.psum(part, "dp")
-        return part if middle is None else middle(part)
-    order = bit_order(size, swapped)
-    for bit in order:
-        part = split_half(part, bit, size)
-    if middle is not None:
-        part = middle(part)
-    for bit in reversed(order):
-        part = join_half(part, bit, size)
-    return part
 
 
 def other(part):
@@ -877,7 +911,9 @@
     gated_low, ssm_out, carries = ssd_forward(
         input_raw, state_raw, gate_raw, step_raw, small, heads, length
     )
-    context_wide, queries, pairs, totals = attend_forward(query_raw, pair_raw, length)
+    context_wide, queries, pairs, totals = attend_forward(
+        after(query_raw, cotan_low), pair_raw, length
+    )
     context_rows = context_wide[:, :query_cols]
     mixed_part = forward_dot(gated_low, mamba_output) + forward_dot(context_rows, context_weight)
     resid = rows + sum_all(mixed_part.astype(jnp.bfloat16), shards)
@@ -897,26 +933,28 @@
         jnp.bfloat16
     )
     back_mid = sum_all(back_part, shards)
-    feed = sum_own(forward_dot(hidden, down_weight).astype(jnp.bfloat16), shards)
+    hidden_late = after(hidden, back_part)
+    mid_late = after(whole_mid, back_part)
+    grad_down = inner_rows(hidden_late, cotan_low).astype(jnp.bfloat16)
+    grad_gate = inner_rows(mid_late, grad_gate_low).astype(jnp.bfloat16)
+    grad_up = inner_rows(mid_late, grad_upper_low).astype(jnp.bfloat16)
+    grad_gate, grad_up, grad_down = lax.psum((grad_gate, grad_up, grad_down), "dp")
+    feed_part = behind(forward_dot(hidden_late, down_weight), back_mid).astype(jnp.bfloat16)
+    feed = sum_own(feed_part, shards)
     layer_output = (own_rows(resid, own) + feed).astype(jnp.bfloat16)
-    grad_down = inner_rows(hidden, cotan_low).astype(jnp.bfloat16)
-    grad_gate = inner_rows(whole_mid, grad_gate_low).astype(jnp.bfloat16)
-    grad_up = inner_rows(whole_mid, grad_upper_low).astype(jnp.bfloat16)
-    grad_gate = sum_dp(grad_gate, dp_size, False)
-    grad_up = sum_dp(grad_up, dp_size, True)
-    grad_down = sum_dp(grad_down, dp_size, False)
     grad_middle = jnp.sum(back_part.astype(jnp.float32) * normal_second, axis=0)
     grad_resid = cotan_low.astype(jnp.float32) + norm_back(
         back_mid, gain_second, normal_second, factor_second
     )
     mixer_all = grad_resid.astype(jnp.bfloat16)
-    grad_mixer_out = inner_rows(
-        jnp.concatenate([gated_low, context_rows], axis=1), mixer_all
-    ).astype(jnp.bfloat16)
-    grad_mixer_out = sum_dp(grad_mixer_out, dp_size, True)
+    mixer_sum = Sum(
+        inner_rows(jnp.concatenate([gated_low, context_rows], axis=1), mixer_all).astype(
+            jnp.bfloat16
+        ),
+        dp_size,
+        False,
+    )
     ssm_rows = gated_low.shape[1]
-    grad_mamba_out = grad_mixer_out[:ssm_rows]
-    grad_context_w = grad_mixer_out[ssm_rows:]
     grad_gated = against(mixer_all, mamba_output)
     sigmoid_raw = jax.nn.sigmoid(gate_raw)
     grad_gate_raw = (
@@ -924,12 +962,16 @@
     ).astype(jnp.bfloat16)
     grad_context = against(mixer_all, context_weight).astype(jnp.bfloat16)
     grad_query_raw, grad_pair_raw = attend_backward(
-        queries, pairs, totals, jnp.pad(grad_context, ((0, 0), (0, query_pad))), length
+        queries,
+        pairs,
+        totals,
+        after(jnp.pad(grad_context, ((0, 0), (0, query_pad))), mixer_sum.give),
+        length,
     )
     grad_query_raw = grad_query_raw[:, :query_cols]
     early_cols = jnp.concatenate([grad_gate_raw, grad_query_raw], axis=1)
-    early = inner_rows(whole, early_cols)
-    early = sum_dp(early.astype(jnp.bfloat16), dp_size, False)
+    early_sum = Sum(inner_rows(whole, early_cols).astype(jnp.bfloat16), dp_size, True)
+    grad_gated = after(grad_gated, early_sum.give, mixer_sum.advance())
     grad_input_raw, grad_state_raw, grad_step_raw, input_sums, state_sums, head_sums = ssd_backward(
         input_raw, state_raw, gate_raw, step_raw, grad_gated, carries, small, heads, length
     )
@@ -937,6 +979,9 @@
     state_sums = jnp.sum(state_sums, axis=0)
     head_sums = jnp.sum(head_sums, axis=0)[:, :heads]
     taps = input_kernel.shape[0]
+    early_sum.advance()
+    mixer_sum.advance()
+    grad_input_raw = after(grad_input_raw, early_sum.give, mixer_sum.give)
     late_cols = jnp.concatenate(
         [grad_input_raw, grad_state_raw, grad_pair_raw, grad_step_raw], axis=1
     )
@@ -998,20 +1043,26 @@
             axis=1,
         )
 
-    tail = sum_dp(tail, dp_size, True, over_tensor)
-    grad_mamba_input = sum_dp(late[:, :input_cols], dp_size, False)
+    tail_sum = Sum(tail, dp_size, True)
+    input_sum = Sum(late[:, :input_cols], dp_size, False)
+    tail = tail_sum.finish(over_tensor)
+    grad_mamba_input = input_sum.finish()
+    grad_mixer_out = mixer_sum.finish()
+    grad_mamba_out = grad_mixer_out[:ssm_rows]
+    grad_context_w = grad_mixer_out[ssm_rows:]
+    early = early_sum.finish()
     back_in = sum_own(total_low, shards)
     normal_own = own_rows(normal_first, own)
     factor_own = own_rows(factor_first, own)
     input_grad = own_rows(grad_resid, own) + norm_back(back_in, gain_first, normal_own, factor_own)
-    after = state_cols + keyvalue_weight.shape[1]
+    start = state_cols + keyvalue_weight.shape[1]
     grad_first, grad_middle, grad_st_kernel, grad_st_shift = column_unpack(
-        tail[:, after : after + shared_width], [item.shape for item in shared_vectors]
-    )
-    after = after + shared_width
-    grad_step = tail[:, after : after + step_cols]
+        tail[:, start : start + shared_width], [item.shape for item in shared_vectors]
+    )
+    start = start + shared_width
+    grad_step = tail[:, start : start + step_cols]
     grad_in_kernel, grad_in_shift, grad_bias, grad_decay, grad_skip = column_unpack(
-        tail[:, after + step_cols :], [item.shape for item in own_vectors]
+        tail[:, start + step_cols :], [item.shape for item in own_vectors]
     )
     results = (
         grad_first,

time: 438 us -> 372 us (0.85)
  starting transfers between devices: 67.4 us -> 27.6 us
  waiting for transfers between devices: 168 us -> 130 us
  between operations: 3.05 us -> 17.3 us
  local copies, waits for them, and re-layouts: 45.7 us -> 37.9 us
    ppermute x28 -> x16, waiting for transfers between devices: 58.5 us -> 17.8 us  [join_half(): got = lax.ppermute(part, 'dp', bit_pairs(size, bit))]
    ppermute x28 -> x16, starting transfers between devices: 35.8 us -> 9.64 us  [add_half(): got = lax.ppermute(give, 'dp', bit_pairs(size, bit))]
    ppermute x28 -> x16, starting transfers between devices: 22.7 us -> 8.97 us  [join_half(): got = lax.ppermute(part, 'dp', bit_pairs(size, bit))]
    ppermute x28 -> x16, waiting for transfers between devices: 63.4 us -> 74.7 us  [add_half(): got = lax.ppermute(give, 'dp', bit_pairs(size, bit))]
    select_n x24 -> x15, other arithmetic: 14 us -> 22.6 us  [join_half(): jnp.where(side == 0, jnp.concatenate([part, got], axis=0), jnp.concatenat...]
    ppermute x7, waiting for transfers between devices: 45.8 us -> 37.3 us  [other(): return lax.ppermute(part, 'tensor', [(0, 1), (1, 0)])]
    squeeze x27 -> x15, local copies, waits for them, and re-layouts: 9.75 us -> 4.07 us  [split_sides(): give = lax.dynamic_index_in_dim(halves, 1 - side, 0, False)]
    convert_element_type x28 -> x16, other arithmetic: 12.8 us -> 8.14 us  [add_half(): (keep.astype(jnp.float32) + got.astype(jnp.float32)).astype(jnp.bfloat16)]
  transfers between devices with their start and end apart: 63 -> 40, of which waited for: 26 -> 17; matrix products, arithmetic and copies ran while one was open for 27% -> 33% of each run, Pallas kernels for 7% -> 8%
where the time goes in v3:
time: 372 us; the launch traced here: 365 us
  waiting for transfers between devices  130 us (35%)
  other arithmetic  74 us (20%)
  Pallas kernels  43.1 us (12%)
  local copies, waits for them, and re-layouts  37.9 us (10%)
  matrix products  35.2 us (9%)
  starting transfers between devices  27.6 us (7%)
  between operations  17.3 us (5%)
    ppermute x16, waiting for transfers between devices, add_half(): got = lax.ppermute(give, 'dp', bit_pairs(size, bit))  74.7 us
    ppermute x7, waiting for transfers between devices, other(): return lax.ppermute(part, 'tensor', [(0, 1), (1, 0)])  37.3 us
    select_n x15, other arithmetic, join_half(): jnp.where(side == 0, jnp.concatenate([part, got], axis=0), jnp.concatenat...  22.6 us
    pallas_call x1, Pallas kernels, ssd_backward(): pl.pallas_call(ssd_backward_kernel, grid=(seqs,), in_specs=[by_sequence(l...  22.3 us
    convert_element_type x16, other arithmetic, body(): item.astype(jnp.float32)  21.6 us
    ppermute x16, waiting for transfers between devices, join_half(): got = lax.ppermute(part, 'dp', bit_pairs(size, bit))  17.8 us
    unnamed x218, local copies, waits for them, and re-layouts  16 us
    dot_general x6, matrix products, inner_rows(): lax.dot_general(left, right, (((0,), (0,)), ((), ())), preferred_element_...  13.7 us
  transfers between devices with their start and end apart: 40, of which 17 were waited for; matrix products, arithmetic and copies ran while one was open for 33% of the time, Pallas kernels for 8%

profile of v3, /device:TPU:0, one launch (start us, length us, event | category | flops | bytes accessed | tf_op | source)
XLA Modules:
  0.0 364.8 jit_solution(14938383817014952384)
XLA Ops:
  7.3 3.0 collective-permute-start
  16.0 1.4 constant_dynamic-slice_fusion.3
  17.3 5.9 %collective-permute-done = bf16[256,1024]{1,0:T(8,128)(2,1)S(1)} collective-permute-done((bf16[256,1024]{1,0:T(8,128)(2,1)}, bf16[256,1024]{1,0:T(8,128)(2,1)S(1)}, u32[]{:S(2)}, u32[]{:S(2)}) %collective-permute-start) | collective-permute-done | bytes 524320 | tf_op jit(solution)/shard_map/ppermute | solution.py:796
  23.3 1.8 fusion.1
  30.8 2.9 collective-permute-done.1
  33.8 1.6 maximum_select_fusion.5
  35.5 8.7 %ssd_forward.1 = (bf16[512,768]{1,0:T(8,128)(2,1)S(1)}, f32[512,768]{1,0:T(8,128)S(1)}, f32[4,128,768]{2,1,0:T(8,128)S(1)}) custom-call(f32[512,768]{1,0:T(8,128)S(1)} %fusion.57.input_ref, f32[512,256]{1,0:T(8,128)S(1)} %fusion.58.state_ref, f32[512,768]{1,0:T(8,128)S(1)} %fusion.59.gate_ref, f32[512,128]{1,0:T(8,128)S(1)} %fusion.36.step_ref, ...), custom_call_target="tpu_custom_call" | custom-call | flops 402653184 | bytes 7864320 | tf_op jit(solution)/shard_map/ssd_forward/pallas_call | solution.py:416
  46.7 5.7 %attend_forward.1 = (bf16[512,256]{1,0:T(8,128)(2,1)S(1)}, bf16[512,256]{1,0:T(8,128)(2,1)S(1)}, bf16[512,128]{1,0:T(8,128)(2,1)S(1)}, f32[512,128]{1,0:T(8,128)S(1)}) custom-call(f32[512,256]{1,0:T(8,128)S(1)} %fusion.61.query_ref, f32[512,128]{1,0:T(8,128)S(1)} %fusion.27.pair_ref, f32[512,128]{1,0:T(8,128)S(1)} %copy-done.12, f32[512,128]{1,0:T(8,128)S(1)} %copy-done.13), custom_call_target="tpu_custom_call" | custom-call | flops 268435456 | bytes 1572864 | tf_op jit(solution)/shard_map/attend_forward/pallas_call | solution.py:654
  52.9 1.8 collective-permute-start.2
  54.7 22.6 %collective-permute-done.2 = bf16[512,1024]{1,0:T(8,128)(2,1)S(1)} collective-permute-done((bf16[512,1024]{1,0:T(8,128)(2,1)S(1)}, bf16[512,1024]{1,0:T(8,128)(2,1)S(1)}, u32[]{:S(2)}, u32[]{:S(2)}) %collective-permute-start.2) | collective-permute-done | bytes 1048608 | tf_op jit(solution)/shard_map/ppermute | solution.py:796
  78.4 2.1 copy-done.94
  83.7 3.1 multiply_convert_fusion
  88.1 2.3 add_convert_fusion.2
  90.3 1.4 collective-permute-start.3
  91.8 1.6 copy.88
  93.8 1.7 pad.23.clone
  95.5 5.1 %concatenate.151 = bf16[1024,1280]{1,0:T(8,128)(2,1)} concatenate(bf16[1024,768]{1,0:T(8,128)(2,1)} %param.33, bf16[1024,256]{1,0:T(8,128)(2,1)} %param.35, bf16[1024,64]{1,0:T(8,128)(2,1)} %copy-done.59, bf16[1024,64]{1,0:T(8,128)(2,1)} %copy-done.60, bf16[1024,128]{1,0:T(8,128)(2,1)} %pad.23.clone), dimensions={1} | concatenate | bytes 5242880 | tf_op jit(solution)/shard_map/concatenate | solution.py:990
  101.8 4.3 %convolution_convert_fusion.3 = bf16[1024,1024]{1,0:T(8,128)(2,1)} fusion(bf16[512,1024]{1,0:T(8,128)(2,1)} %copy-done.75, bf16[512,1024]{1,0:T(8,128)(2,1)} %copy-done.102), kind=kOutput, calls=%fused_computation.35 | convolution fusion | flops 1074790400 | bytes 4194304 | tf_op jit(solution)/shard_map/dot_general | solution.py:28
  106.1 2.6 convolution_convert_fusion.2
  108.7 2.6 convolution_convert_fusion.1
  111.4 2.6 collective-permute-done.3
  114.1 3.6 fusion
  117.8 2.4 multiply_add_fusion
  130.4 6.5 %attend_backward.1 = (bf16[512,256]{1,0:T(8,128)(2,1)S(1)}, bf16[512,128]{1,0:T(8,128)(2,1)S(1)}) custom-call(bf16[512,256]{1,0:T(8,128)(2,1)S(1)} %copy-done.30, bf16[512,128]{1,0:T(8,128)(2,1)S(1)} %copy-done.34, f32[512,128]{1,0:T(8,128)S(1)} %copy-done.32, bf16[512,256]{1,0:T(8,128)(2,1)S(1)} %convolution_convert_fusion.6.grad_ref, ...), custom_call_target="tpu_custom_call" | custom-call | flops 671088640 | bytes 1572864 | tf_op jit(solution)/shard_map/attend_backward/pallas_call | solution.py:689
  141.0 1.6 collective-permute-start.7
  142.8 22.3 %ssd_backward.1 = (bf16[512,768]{1,0:T(8,128)(2,1)S(1)}, bf16[512,256]{1,0:T(8,128)(2,1)S(1)}, bf16[512,128]{1,0:T(8,128)(2,1)S(1)}, f32[1,8,768]{2,1,0:T(8,128)...) custom-call(f32[512,768]{1,0:T(8,128)S(1)} %copy-done.5, f32[512,256]{1,0:T(8,128)S(1)} %fusion.58.state_ref, ...), custom_call_target="tpu_custom_call" | custom-call | flops 1006632960 | bytes 7864320 | tf_op jit(solution)/shard_map/ssd_backward/pallas_call | solution.py:465
  166.2 2.0 fusion.6
  169.2 1.6 collective-permute-start.18
  173.1 1.6 convolution_convert_fusion
  177.4 1.5 fusion.65
  179.0 2.8 multiply_reduce_fusion
  185.7 3.4 collective-permute-done.18
  189.1 1.4 fusion.16
  194.8 8.7 %collective-permute-done.19 = bf16[128,1024]{1,0:T(8,128)(2,1)S(1)} collective-permute-done((bf16[128,1024]{1,0:T(8,128)(2,1)S(1)}, bf16[128,1024]{1,0:T(8,128)(2,1)S(1)}, u32[]{:S(2)}, u32[]{:S(2)}) %collective-permute-start.19) | collective-permute-done | bytes 262176 | tf_op jit(solution)/shard_map/ppermute | solution.py:732
  203.6 2.5 collective-permute-start.20
  208.0 9.6 %collective-permute-done.20 = bf16[64,1024]{1,0:T(8,128)(2,1)S(1)} collective-permute-done((bf16[64,1024]{1,0:T(8,128)(2,1)S(1)}, bf16[64,1024]{1,0:T(8,128)(2,1)S(1)}, u32[]{:S(2)}, u32[]{:S(2)}) %collective-permute-start.20) | collective-permute-done | bytes 131104 | tf_op jit(solution)/shard_map/ppermute | solution.py:732
  217.8 9.1 %collective-permute-done.34 = bf16[64,1024]{1,0:T(8,128)(2,1)S(1)} collective-permute-done((bf16[64,1024]{1,0:T(8,128)(2,1)S(1)}, bf16[64,1024]{1,0:T(8,128)(2,1)S(1)}, u32[]{:S(2)}, u32[]{:S(2)}) %collective-permute-start.34) | collective-permute-done | bytes 131104 | tf_op jit(solution)/shard_map/ppermute | solution.py:732
  228.6 16.7 %collective-permute-done.10 = bf16[256,404]{1,0:T(8,128)(2,1)S(1)} collective-permute-done((bf16[256,404]{1,0:T(8,128)(2,1)S(1)}, bf16[256,404]{1,0:T(8,128)(2,1)S(1)}, u32[]{:S(2)}, u32[]{:S(2)}) %collective-permute-start.10) | collective-permute-done | bytes 206880 | tf_op jit(solution)/shard_map/ppermute | solution.py:732
  245.6 2.1 collective-permute-start.22
  247.7 6.6 %collective-permute-done.11 = bf16[128,404]{1,0:T(8,128)(2,1)S(1)} collective-permute-done((bf16[128,404]{1,0:T(8,128)(2,1)S(1)}, bf16[128,404]{1,0:T(8,128)(2,1)S(1)}, u32[]{:S(2)}, u32[]{:S(2)}) %collective-permute-start.11) | collective-permute-done | bytes 103456 | tf_op jit(solution)/shard_map/ppermute | solution.py:732
  254.5 1.8 maximum_select_fusion.15
  257.7 6.2 %collective-permute-done.12 = bf16[64,404]{0,1:T(8,128)(2,1)S(1)} collective-permute-done((bf16[64,404]{0,1:T(8,128)(2,1)S(1)}, bf16[64,404]{0,1:T(8,128)(2,1)S(1)}, u32[]{:S(2)}, u32[]{:S(2)}) %collective-permute-start.12) | collective-permute-done | bytes 51744 | tf_op jit(solution)/shard_map/ppermute | solution.py:732
  265.5 3.2 collective-permute-done.13
  269.4 2.0 maximum_select_fusion.10
  272.7 8.0 %collective-permute-done.14 = bf16[64,532]{0,1:T(8,128)(2,1)S(1)} collective-permute-done((bf16[64,532]{0,1:T(8,128)(2,1)S(1)}, bf16[64,532]{0,1:T(8,128)(2,1)S(1)}, u32[]{:S(2)}, u32[]{:S(2)}) %collective-permute-start.14) | collective-permute-done | bytes 68128 | tf_op jit(solution)/shard_map/ppermute | solution.py:738
  281.3 2.4 maximum_select_fusion.11
  283.7 1.8 collective-permute-start.37
  285.5 1.8 collective-permute-done.15
  287.5 14.4 %collective-permute-done.27 = bf16[128,768]{1,0:T(8,128)(2,1)S(1)} collective-permute-done((bf16[128,768]{1,0:T(8,128)(2,1)S(1)}, bf16[128,768]{1,0:T(8,128)(2,1)S(1)}, u32[]{:S(2)}, u32[]{:S(2)}) %collective-permute-start.27) | collective-permute-done | bytes 196640 | tf_op jit(solution)/shard_map/ppermute | solution.py:732
  302.1 7.1 %collective-permute-done.16 = bf16[256,532]{0,1:T(8,128)(2,1)S(1)} collective-permute-done((bf16[256,532]{0,1:T(8,128)(2,1)S(1)}, bf16[256,532]{0,1:T(8,128)(2,1)S(1)}, u32[]{:S(2)}, u32[]{:S(2)}) %collective-permute-start.16) | collective-permute-done | bytes 272416 | tf_op jit(solution)/shard_map/ppermute | solution.py:738
  310.3 2.3 multiply_add_fusion.1
  312.6 4.2 %convert_element_type.542 = f32[1024,1024]{1,0:T(8,128)} convert(bf16[1024,1024]{1,0:T(8,128)(2,1)} %get-tuple-element.176) | non-fusion elementwise | flops 1048576 | bytes 6291456 | tf_op jit(solution)/shard_map/convert_element_type | solution.py:1089
  316.9 2.5 convert_element_type.544
  319.3 2.5 convert_element_type.546
  322.9 2.0 maximum_select_fusion.6
  325.0 3.0 maximum_select_fusion.7
  330.5 2.0 maximum_select_fusion.3
  334.4 2.5 copy.80
  341.8 1.7 maximum_select_fusion.8
  343.6 2.5 maximum_select_fusion
  347.2 3.2 maximum_select_fusion.1
  351.5 1.9 slice_convert_fusion.1
  353.4 2.1 slice_convert_fusion
  355.5 2.0 fusion.9
  (390 shorter events, 73.7 us)
Async XLA Ops:
  7.2 76.5 %copy-start = (bf16[1024,1024]{1,0:T(8,128)(2,1)S(1)}, bf16[1024,1024]{1,0:T(8,128)(2,1)}, u32[]{:S(2)}) copy-start(bf16[1024,1024]{1,0:T(8,128)(2,1)} %param.49) | copy-start | bytes 6291460
  7.2 305.4 %all-reduce.8.cloned.1.call-start = ((), (), s32[]{:S(2)}) async-start(), calls=%async_computation | async-start | bytes 12582912 | tf_op jit(solution)/shard_map/psum | solution.py:941
  7.3 16.0 %collective-permute-start = (bf16[256,1024]{1,0:T(8,128)(2,1)}, bf16[256,1024]{1,0:T(8,128)(2,1)S(1)}, u32[]{:S(2)}, u32[]{:S(2)}) collective-permute-start(bf16[256,1024]{1,0:T(8,128)(2,1)} %param.29), channel_id=1, source_target_pairs={{0,1},{1,0},{2,3},{3,2},{4,5},{5,4},{6,7},{7,6},{8,9},{9,8},{10,11... | collective-permute-start | bytes 1572872 | tf_op jit(solution)/shard_map/ppermute | solution.py:796
  10.3 23.5 %collective-permute-start.1 = (bf16[256,1024]{1,0:T(8,128)(2,1)}, bf16[256,1024]{1,0:T(8,128)(2,1)}, u32[]{:S(2)}, u32[]{:S(2)}) collective-permute-start(bf16[256,1024]{1,0:T(8,128)(2,1)} %param.50), channel_id=1, source_target_pairs={{0,1},{1,0},{2,3},{3,2},{4,5},{5,4},{6,7},{7,6},{8,9},{9,8},{10,11... | collective-permute-start | bytes 1572872 | tf_op jit(solution)/shard_map/ppermute | solution.py:796
  12.4 23.0 %copy-start.17 = (f32[1,768]{1,0:T(1,128)}, f32[1,768]{1,0:T(1,128)S(1)}, u32[]{:S(2)}) copy-start(f32[1,768]{1,0:T(1,128)S(1)} %reshape.242.input_shift_ref) | copy-start | bytes 9220
  13.8 21.6 %copy-start.21 = (f32[256]{0:T(256)}, f32[256]{0:T(256)S(1)}, u32[]{:S(2)}) copy-start(f32[256]{0:T(256)S(1)} %broadcast_in_dim.36) | copy-start | bytes 3076
  14.6 20.8 %copy-start.19 = (f32[1,768]{1,0:T(1,128)}, f32[1,768]{1,0:T(1,128)S(1)}, u32[]{:S(2)}) copy-start(f32[1,768]{1,0:T(1,128)S(1)} %broadcast_in_dim_reshape.3.skip_ref) | copy-start | bytes 9220
  15.3 20.2 %copy-start.23 = (f32[1,128]{1,0:T(1,128)}, f32[1,128]{1,0:T(1,128)S(1)}, u32[]{:S(2)}) copy-start(f32[1,128]{1,0:T(1,128)S(1)} %pad.26.rate_ref) | copy-start | bytes 1540
  16.0 19.5 %copy-start.25 = (f32[1,128]{1,0:T(1,128)}, f32[1,128]{1,0:T(1,128)S(1)}, u32[]{:S(2)}) copy-start(f32[1,128]{1,0:T(1,128)S(1)} %pad_convert_fusion.bias_ref) | copy-start | bytes 1540
  17.3 28.8 %copy-start.59 = (bf16[1024,64]{1,0:T(8,128)(2,1)}, bf16[1024,64]{1,0:T(8,128)(2,1)S(1)}, u32[]{:S(2)}) copy-start(bf16[1024,64]{1,0:T(8,128)(2,1)S(1)} %get-tuple-element.194) | copy-start | bytes 393220
  17.3 28.8 %copy-start.60 = (bf16[1024,64]{1,0:T(8,128)(2,1)}, bf16[1024,64]{1,0:T(8,128)(2,1)S(1)}, u32[]{:S(2)}) copy-start(bf16[1024,64]{1,0:T(8,128)(2,1)S(1)} %get-tuple-element.195) | copy-start | bytes 393220
  25.6 20.5 %copy-start.37 = (bf16[512,1024]{1,0:T(8,128)(2,1)}, bf16[512,1024]{1,0:T(8,128)(2,1)S(1)}, u32[]{:S(2)}) copy-start(bf16[512,1024]{1,0:T(8,128)(2,1)S(1)} %multiply_convert_fusion.4) | copy-start | bytes 3145732
  35.4 48.3 %copy-start.51 = (bf16[512,1024]{1,0:T(8,128)(2,1)}, bf16[512,1024]{1,0:T(8,128)(2,1)S(1)}, u32[]{:S(2)}) copy-start(bf16[512,1024]{1,0:T(8,128)(2,1)S(1)} %maximum_select_fusion.5) | copy-start | bytes 3145732
  52.4 25.6 %copy-start.15 = (bf16[512,256]{1,0:T(8,128)(2,1)}, bf16[512,256]{1,0:T(8,128)(2,1)S(1)}, u32[]{:S(2)}) copy-start(bf16[512,256]{1,0:T(8,128)(2,1)S(1)} %get-tuple-element.45) | copy-start | bytes 786436
  52.4 25.6 %copy-start.29 = (bf16[512,256]{1,0:T(8,128)(2,1)}, bf16[512,256]{1,0:T(8,128)(2,1)S(1)}, u32[]{:S(2)}) copy-start(bf16[512,256]{1,0:T(8,128)(2,1)S(1)} %get-tuple-element.48.query_ref) | copy-start | bytes 786436
  52.4 25.6 %copy-start.31 = (f32[512,128]{1,0:T(8,128)}, f32[512,128]{1,0:T(8,128)S(1)}, u32[]{:S(2)}) copy-start(f32[512,128]{1,0:T(8,128)S(1)} %get-tuple-element.50.total_ref) | copy-start | bytes 786436
  52.4 25.6 %copy-start.33 = (bf16[512,128]{1,0:T(8,128)(2,1)}, bf16[512,128]{1,0:T(8,128)(2,1)S(1)}, u32[]{:S(2)}) copy-start(bf16[512,128]{1,0:T(8,128)(2,1)S(1)} %get-tuple-element.49.pair_ref) | copy-start | bytes 393220
  52.4 24.9 %copy-start.43 = (bf16[256,1024]{1,0:T(8,128)(2,1)S(1)}, bf16[256,1024]{1,0:T(8,128)(2,1)}, u32[]{:S(2)}) copy-start(bf16[256,1024]{1,0:T(8,128)(2,1)} %param.29) | copy-start | bytes 1572868
  52.4 24.9 %copy-start.46 = (bf16[256,1024]{1,0:T(8,128)(2,1)S(1)}, bf16[256,1024]{1,0:T(8,128)(2,1)}, u32[]{:S(2)}) copy-start(bf16[256,1024]{1,0:T(8,128)(2,1)} %copy-done.45) | copy-start | bytes 1572868
  52.9 24.4 %collective-permute-start.2 = (bf16[512,1024]{1,0:T(8,128)(2,1)S(1)}, bf16[512,1024]{1,0:T(8,128)(2,1)S(1)}, u32[]{:S(2)}, u32[]{:S(2)}) collective-permute-start(bf16[512,1024]{1,0:T(8,128)(2,1)S(1)} %add_convert_fusion.3), channel_id=1, source_target_pairs={{0,1},{1,0},{2,3},{3,2},{4,5},{5,4},{6,7},{7,6},{8,9},{9,8},{10,11... | collective-permute-start | bytes 3145736 | tf_op jit(solution)/shard_map/ppermute | solution.py:796
  54.7 23.4 %copy-start.85 = (f32[1024]{0:T(1024)}, f32[1024]{0:T(1024)S(1)}, u32[]{:S(2)}) copy-start(f32[1024]{0:T(1024)S(1)} %convert_element_type.424) | copy-start | bytes 12292
  90.3 23.7 %collective-permute-start.3 = (bf16[512,1024]{1,0:T(8,128)(2,1)}, bf16[512,1024]{1,0:T(8,128)(2,1)}, u32[]{:S(2)}, u32[]{:S(2)}) collective-permute-start(bf16[512,1024]{1,0:T(8,128)(2,1)} %add_convert_fusion.2), channel_id=1, source_target_pairs={{0,1},{1,0},{2,3},{3,2},{4,5},{5,4},{6,7},{7,6},{8,9},{9,8},{10,11... | collective-permute-start | bytes 3145736 | tf_op jit(solution)/shard_map/ppermute | solution.py:796
  126.0 13.4 %collective-permute-start.4 = (bf16[256,1024]{1,0:T(8,128)(2,1)S(1)}, bf16[256,1024]{1,0:T(8,128)(2,1)S(1)}, u32[]{:S(2)}, u32[]{:S(2)}) collective-permute-start(bf16[256,1024]{1,0:T(8,128)(2,1)S(1)} %dynamic-slice_bitcast_fusion.7), channel_id=1, source_target_pairs={{0,1},{1,0},{2,3},{3,2},{4,5},{5,4},{6,7},{7,6},{8,9},{9,8},{10,11... | collective-permute-start | bytes 1572872 | tf_op jit(solution)/shard_map/ppermute | solution.py:796
  127.4 13.1 %collective-permute-start.5 = (bf16[512,1024]{1,0:T(8,128)(2,1)S(1)}, bf16[512,1024]{1,0:T(8,128)(2,1)S(1)}, u32[]{:S(2)}, u32[]{:S(2)}) collective-permute-start(bf16[512,1024]{1,0:T(8,128)(2,1)S(1)} %dynamic-slice_bitcast_fusion.1), channel_id=1, source_target_pairs={{0,2},{2,0},{4,6},{6,4},{8,10},{10,8},{12,14},{14,12},{16,18},{18,... | collective-permute-start | bytes 3145736 | tf_op jit(solution)/shard_map/ppermute | solution.py:732
  139.3 26.9 %collective-permute-start.6 = (bf16[512,1024]{1,0:T(8,128)(2,1)}, bf16[512,1024]{1,0:T(8,128)(2,1)}, u32[]{:S(2)}, u32[]{:S(2)}) collective-permute-start(bf16[512,1024]{1,0:T(8,128)(2,1)} %dynamic-slice_bitcast_fusion), channel_id=1, source_target_pairs={{0,2},{2,0},{4,6},{6,4},{8,10},{10,8},{12,14},{14,12},{16,18},{18,... | collective-permute-start | bytes 3145736 | tf_op jit(solution)/shard_map/ppermute | solution.py:732
  141.0 29.8 %collective-permute-start.7 = (bf16[256,1024]{1,0:T(8,128)(2,1)S(1)}, bf16[256,1024]{1,0:T(8,128)(2,1)}, u32[]{:S(2)}, u32[]{:S(2)}) collective-permute-start(bf16[256,1024]{1,0:T(8,128)(2,1)S(1)} %dynamic-slice_bitcast_fusion.6), channel_id=1, source_target_pairs={{0,4},{2,6},{4,0},{6,2},{8,12},{10,14},{12,8},{14,10},{16,20},{18,... | collective-permute-start | bytes 1572872 | tf_op jit(solution)/shard_map/ppermute | solution.py:732
  169.2 19.9 %collective-permute-start.18 = (bf16[256,1024]{1,0:T(8,128)(2,1)}, bf16[256,1024]{1,0:T(8,128)(2,1)}, u32[]{:S(2)}, u32[]{:S(2)}) collective-permute-start(bf16[256,1024]{1,0:T(8,128)(2,1)} %dynamic-slice_bitcast_fusion.5), channel_id=1, source_target_pairs={{0,8},{2,10},{4,12},{6,14},{8,0},{10,2},{12,4},{14,6},{16,24},{18,... | collective-permute-start | bytes 1572872 | tf_op jit(solution)/shard_map/ppermute | solution.py:732
  176.5 29.6 %collective-permute-start.33 = (bf16[128,1024]{1,0:T(8,128)(2,1)}, bf16[128,1024]{1,0:T(8,128)(2,1)}, u32[]{:S(2)}, u32[]{:S(2)}) collective-permute-start(bf16[128,1024]{1,0:T(8,128)(2,1)} %dynamic-slice_bitcast_fusion.11), channel_id=1, source_target_pairs={{0,8},{2,10},{4,12},{6,14},{8,0},{10,2},{12,4},{14,6},{16,24},{18,... | collective-permute-start | bytes 786440 | tf_op jit(solution)/shard_map/ppermute | solution.py:732
  183.6 43.7 %collective-permute-start.8 = (bf16[256,1024]{1,0:T(8,128)(2,1)}, bf16[256,1024]{1,0:T(8,128)(2,1)}, u32[]{:S(2)}, u32[]{:S(2)}) collective-permute-start(bf16[256,1024]{1,0:T(8,128)(2,1)} %dynamic-slice_bitcast_fusion.4), channel_id=1, source_target_pairs={{0,1},{1,0},{2,3},{3,2},{4,5},{5,4},{6,7},{7,6},{8,9},{9,8},{10,11... | collective-permute-start | bytes 1572872 | tf_op jit(solution)/shard_map/ppermute | solution.py:796
  190.6 12.9 %collective-permute-start.19 = (bf16[128,1024]{1,0:T(8,128)(2,1)S(1)}, bf16[128,1024]{1,0:T(8,128)(2,1)S(1)}, u32[]{:S(2)}, u32[]{:S(2)}) collective-permute-start(bf16[128,1024]{1,0:T(8,128)(2,1)S(1)} %dynamic-slice_bitcast_fusion.9), channel_id=1, source_target_pairs={{0,4},{2,6},{4,0},{6,2},{8,12},{10,14},{12,8},{14,10},{16,20},{18,... | collective-permute-start | bytes 786440 | tf_op jit(solution)/shard_map/ppermute | solution.py:732
  193.3 33.7 %collective-permute-start.9 = (bf16[512,404]{1,0:T(8,128)(2,1)S(1)}, bf16[512,404]{1,0:T(8,128)(2,1)S(1)}, u32[]{:S(2)}, u32[]{:S(2)}) collective-permute-start(bf16[512,404]{1,0:T(8,128)(2,1)S(1)} %dynamic-slice_bitcast_fusion.3), channel_id=1, source_target_pairs={{0,2},{2,0},{4,6},{6,4},{8,10},{10,8},{12,14},{14,12},{16,18},{18,... | collective-permute-start | bytes 1241096 | tf_op jit(solution)/shard_map/ppermute | solution.py:732
  194.3 69.8 %collective-permute-start.25 = (bf16[512,768]{1,0:T(8,128)(2,1)}, bf16[512,768]{1,0:T(8,128)(2,1)}, u32[]{:S(2)}, u32[]{:S(2)}) collective-permute-start(bf16[512,768]{1,0:T(8,128)(2,1)} %dynamic-slice_bitcast_fusion.2), channel_id=1, source_target_pairs={{0,2},{2,0},{4,6},{6,4},{8,10},{10,8},{12,14},{14,12},{16,18},{18,... | collective-permute-start | bytes 2359304 | tf_op jit(solution)/shard_map/ppermute | solution.py:732
  203.5 23.7 %copy-start.57 = (bf16[512,1024]{1,0:T(8,128)(2,1)S(1)}, bf16[512,1024]{1,0:T(8,128)(2,1)}, u32[]{:S(2)}) copy-start(bf16[512,1024]{1,0:T(8,128)(2,1)} %copy-done.56) | copy-start | bytes 3145732
  203.5 23.7 %copy-start.63 = (f32[512,1024]{1,0:T(8,128)S(1)}, f32[512,1024]{1,0:T(8,128)}, u32[]{:S(2)}) copy-start(f32[512,1024]{1,0:T(8,128)} %get-tuple-element.193) | copy-start | bytes 6291460
  203.6 23.7 %copy-start.84 = (f32[1024]{0:T(1024)S(1)}, f32[1024]{0:T(1024)}, u32[]{:S(2)}) copy-start(f32[1024]{0:T(1024)} %copy-done.83) | copy-start | bytes 12292
  203.6 14.1 %collective-permute-start.20 = (bf16[64,1024]{1,0:T(8,128)(2,1)S(1)}, bf16[64,1024]{1,0:T(8,128)(2,1)S(1)}, u32[]{:S(2)}, u32[]{:S(2)}) collective-permute-start(bf16[64,1024]{1,0:T(8,128)(2,1)S(1)} %dynamic-slice_bitcast_fusion.14), channel_id=1, source_target_pairs={{0,16},{2,18},{4,20},{6,22},{8,24},{10,26},{12,28},{14,30},{16,0},... | collective-permute-start | bytes 393224 | tf_op jit(solution)/shard_map/ppermute | solution.py:732
  207.1 19.8 %collective-permute-start.34 = (bf16[64,1024]{1,0:T(8,128)(2,1)S(1)}, bf16[64,1024]{1,0:T(8,128)(2,1)S(1)}, u32[]{:S(2)}, u32[]{:S(2)}) collective-permute-start(bf16[64,1024]{1,0:T(8,128)(2,1)S(1)} %dynamic-slice_bitcast_fusion.13), channel_id=1, source_target_pairs={{0,16},{2,18},{4,20},{6,22},{8,24},{10,26},{12,28},{14,30},{16,0},... | collective-permute-start | bytes 393224 | tf_op jit(solution)/shard_map/ppermute | solution.py:732
  217.7 27.8 %collective-permute-start.21 = (bf16[64,1024]{1,0:T(8,128)(2,1)S(1)}, bf16[64,1024]{1,0:T(8,128)(2,1)S(1)}, u32[]{:S(2)}, u32[]{:S(2)}) collective-permute-start(bf16[64,1024]{1,0:T(8,128)(2,1)S(1)} %fusion.32), channel_id=1, source_target_pairs={{0,16},{2,18},{4,20},{6,22},{8,24},{10,26},{12,28},{14,30},{16,0},... | collective-permute-start | bytes 393224 | tf_op jit(solution)/shard_map/ppermute | solution.py:738
  226.9 27.6 %collective-permute-start.35 = (bf16[64,1024]{1,0:T(8,128)(2,1)S(1)}, bf16[64,1024]{1,0:T(8,128)(2,1)}, u32[]{:S(2)}, u32[]{:S(2)}) collective-permute-start(bf16[64,1024]{1,0:T(8,128)(2,1)S(1)} %fusion.31), channel_id=1, source_target_pairs={{0,16},{2,18},{4,20},{6,22},{8,24},{10,26},{12,28},{14,30},{16,0},... | collective-permute-start | bytes 393224 | tf_op jit(solution)/shard_map/ppermute | solution.py:738
  227.2 18.2 %collective-permute-start.10 = (bf16[256,404]{1,0:T(8,128)(2,1)S(1)}, bf16[256,404]{1,0:T(8,128)(2,1)S(1)}, u32[]{:S(2)}, u32[]{:S(2)}) collective-permute-start(bf16[256,404]{1,0:T(8,128)(2,1)S(1)} %dynamic-slice_bitcast_fusion.10), channel_id=1, source_target_pairs={{0,8},{2,10},{4,12},{6,14},{8,0},{10,2},{12,4},{14,6},{16,24},{18,... | collective-permute-start | bytes 620552 | tf_op jit(solution)/shard_map/ppermute | solution.py:732
  245.5 8.8 %collective-permute-start.11 = (bf16[128,404]{1,0:T(8,128)(2,1)S(1)}, bf16[128,404]{1,0:T(8,128)(2,1)S(1)}, u32[]{:S(2)}, u32[]{:S(2)}) collective-permute-start(bf16[128,404]{1,0:T(8,128)(2,1)S(1)} %dynamic-slice_bitcast_fusion.15), channel_id=1, source_target_pairs={{0,4},{2,6},{4,0},{6,2},{8,12},{10,14},{12,8},{14,10},{16,20},{18,... | collective-permute-start | bytes 310280 | tf_op jit(solution)/shard_map/ppermute | solution.py:732
  245.6 23.8 %collective-permute-start.22 = (bf16[128,1024]{1,0:T(8,128)(2,1)S(1)}, bf16[128,1024]{1,0:T(8,128)(2,1)}, u32[]{:S(2)}, u32[]{:S(2)}) collective-permute-start(bf16[128,1024]{1,0:T(8,128)(2,1)S(1)} %maximum_select_fusion.14), channel_id=1, source_target_pairs={{0,4},{2,6},{4,0},{6,2},{8,12},{10,14},{12,8},{14,10},{16,20},{18,... | collective-permute-start | bytes 786440 | tf_op jit(solution)/shard_map/ppermute | solution.py:738
  254.4 9.5 %collective-permute-start.12 = (bf16[64,404]{0,1:T(8,128)(2,1)S(1)}, bf16[64,404]{0,1:T(8,128)(2,1)S(1)}, u32[]{:S(2)}, u32[]{:S(2)}) collective-permute-start(bf16[64,404]{0,1:T(8,128)(2,1)S(1)} %bitcast.221), channel_id=1, source_target_pairs={{0,16},{2,18},{4,20},{6,22},{8,24},{10,26},{12,28},{14,30},{16,0},... | collective-permute-start | bytes 155144 | tf_op jit(solution)/shard_map/ppermute | solution.py:732
  256.3 25.0 %collective-permute-start.36 = (bf16[128,1024]{1,0:T(8,128)(2,1)}, bf16[128,1024]{1,0:T(8,128)(2,1)}, u32[]{:S(2)}, u32[]{:S(2)}) collective-permute-start(bf16[128,1024]{1,0:T(8,128)(2,1)} %maximum_select_fusion.15), channel_id=1, source_target_pairs={{0,8},{2,10},{4,12},{6,14},{8,0},{10,2},{12,4},{14,6},{16,24},{18,... | collective-permute-start | bytes 786440 | tf_op jit(solution)/shard_map/ppermute | solution.py:738
  264.0 4.7 %collective-permute-start.13 = (bf16[64,388]{0,1:T(8,128)(2,1)S(1)}, bf16[64,388]{0,1:T(8,128)(2,1)S(1)}, u32[]{:S(2)}, u32[]{:S(2)}) collective-permute-start(bf16[64,388]{0,1:T(8,128)(2,1)S(1)} %slice.182), channel_id=1, source_target_pairs={{0,1},{1,0},{2,3},{3,2},{4,5},{5,4},{6,7},{7,6},{8,9},{9,8},{10,11... | collective-permute-start | bytes 149000 | tf_op jit(solution)/shard_map/ppermute | solution.py:796
  265.5 15.5 %collective-permute-start.26 = (bf16[256,768]{1,0:T(8,128)(2,1)S(1)}, bf16[256,768]{1,0:T(8,128)(2,1)S(1)}, u32[]{:S(2)}, u32[]{:S(2)}) collective-permute-start(bf16[256,768]{1,0:T(8,128)(2,1)S(1)} %dynamic-slice_bitcast_fusion.8), channel_id=1, source_target_pairs={{0,4},{2,6},{4,0},{6,2},{8,12},{10,14},{12,8},{14,10},{16,20},{18,... | collective-permute-start | bytes 1179656 | tf_op jit(solution)/shard_map/ppermute | solution.py:732
  269.3 11.3 %collective-permute-start.14 = (bf16[64,532]{0,1:T(8,128)(2,1)S(1)}, bf16[64,532]{0,1:T(8,128)(2,1)S(1)}, u32[]{:S(2)}, u32[]{:S(2)}) collective-permute-start(bf16[64,532]{0,1:T(8,128)(2,1)S(1)} %concatenate.155), channel_id=1, source_target_pairs={{0,16},{2,18},{4,20},{6,22},{8,24},{10,26},{12,28},{14,30},{16,0},... | collective-permute-start | bytes 204296 | tf_op jit(solution)/shard_map/ppermute | solution.py:738
  271.4 51.5 %collective-permute-start.23 = (bf16[256,1024]{1,0:T(8,128)(2,1)}, bf16[256,1024]{1,0:T(8,128)(2,1)}, u32[]{:S(2)}, u32[]{:S(2)}) collective-permute-start(bf16[256,1024]{1,0:T(8,128)(2,1)} %maximum_select_fusion.10), channel_id=1, source_target_pairs={{0,8},{2,10},{4,12},{6,14},{8,0},{10,2},{12,4},{14,6},{16,24},{18,... | collective-permute-start | bytes 1572872 | tf_op jit(solution)/shard_map/ppermute | solution.py:738
  280.8 6.6 %collective-permute-start.15 = (bf16[128,532]{0,1:T(8,128)(2,1)S(1)}, bf16[128,532]{0,1:T(8,128)(2,1)S(1)}, u32[]{:S(2)}, u32[]{:S(2)}) collective-permute-start(bf16[128,532]{0,1:T(8,128)(2,1)S(1)} %maximum_select_fusion.17), channel_id=1, source_target_pairs={{0,4},{2,6},{4,0},{6,2},{8,12},{10,14},{12,8},{14,10},{16,20},{18,... | collective-permute-start | bytes 408584 | tf_op jit(solution)/shard_map/ppermute | solution.py:738
  280.9 29.3 %copy-start.64 = (f32[512,1024]{1,0:T(8,128)S(1)}, f32[512,1024]{1,0:T(8,128)}, u32[]{:S(2)}) copy-start(f32[512,1024]{1,0:T(8,128)} %get-tuple-element.193) | copy-start | bytes 6291460
  281.0 29.2 %copy-start.41 = (f32[512,1024]{1,0:T(8,128)S(1)}, f32[512,1024]{1,0:T(8,128)}, u32[]{:S(2)}) copy-start(f32[512,1024]{1,0:T(8,128)} %copy-done.40) | copy-start | bytes 6291460
  281.1 29.2 %copy-start.58 = (bf16[512,1024]{1,0:T(8,128)(2,1)S(1)}, bf16[512,1024]{1,0:T(8,128)(2,1)}, u32[]{:S(2)}) copy-start(bf16[512,1024]{1,0:T(8,128)(2,1)} %copy-done.56) | copy-start | bytes 3145732
  281.1 29.2 %copy-start.92 = (f32[256]{0:T(256)S(1)}, f32[256]{0:T(256)}, u32[]{:S(2)}) copy-start(f32[256]{0:T(256)} %dynamic-slice.3) | copy-start | bytes 3076
  281.1 20.8 %collective-permute-start.27 = (bf16[128,768]{1,0:T(8,128)(2,1)S(1)}, bf16[128,768]{1,0:T(8,128)(2,1)S(1)}, u32[]{:S(2)}, u32[]{:S(2)}) collective-permute-start(bf16[128,768]{1,0:T(8,128)(2,1)S(1)} %dynamic-slice_bitcast_fusion.12), channel_id=1, source_target_pairs={{0,8},{2,10},{4,12},{6,14},{8,0},{10,2},{12,4},{14,6},{16,24},{18,... | collective-permute-start | bytes 589832 | tf_op jit(solution)/shard_map/ppermute | solution.py:732
  283.7 41.3 %collective-permute-start.37 = (bf16[256,1024]{1,0:T(8,128)(2,1)}, bf16[256,1024]{1,0:T(8,128)(2,1)}, u32[]{:S(2)}, u32[]{:S(2)}) collective-permute-start(bf16[256,1024]{1,0:T(8,128)(2,1)} %maximum_select_fusion.11), channel_id=1, source_target_pairs={{0,4},{2,6},{4,0},{6,2},{8,12},{10,14},{12,8},{14,10},{16,20},{18,... | collective-permute-start | bytes 1572872 | tf_op jit(solution)/shard_map/ppermute | solution.py:738
  287.4 21.8 %collective-permute-start.16 = (bf16[256,532]{0,1:T(8,128)(2,1)S(1)}, bf16[256,532]{0,1:T(8,128)(2,1)S(1)}, u32[]{:S(2)}, u32[]{:S(2)}) collective-permute-start(bf16[256,532]{0,1:T(8,128)(2,1)S(1)} %maximum_select_fusion.13), channel_id=1, source_target_pairs={{0,8},{2,10},{4,12},{6,14},{8,0},{10,2},{12,4},{14,6},{16,24},{18,... | collective-permute-start | bytes 817160 | tf_op jit(solution)/shard_map/ppermute | solution.py:738
  302.0 8.2 %collective-permute-start.28 = (bf16[64,768]{1,0:T(8,128)(2,1)S(1)}, bf16[64,768]{1,0:T(8,128)(2,1)S(1)}, u32[]{:S(2)}, u32[]{:S(2)}) collective-permute-start(bf16[64,768]{1,0:T(8,128)(2,1)S(1)} %dynamic-slice_bitcast_fusion.16), channel_id=1, source_target_pairs={{0,16},{2,18},{4,20},{6,22},{8,24},{10,26},{12,28},{14,30},{16,0},... | collective-permute-start | bytes 294920 | tf_op jit(solution)/shard_map/ppermute | solution.py:732
  310.1 20.4 %collective-permute-start.17 = (bf16[512,532]{0,1:T(8,128)(2,1)}, bf16[512,532]{0,1:T(8,128)(2,1)}, u32[]{:S(2)}, u32[]{:S(2)}) collective-permute-start(bf16[512,532]{0,1:T(8,128)(2,1)} %maximum_select_fusion.9), channel_id=1, source_target_pairs={{0,2},{2,0},{4,6},{6,4},{8,10},{10,8},{12,14},{14,12},{16,18},{18,... | collective-permute-start | bytes 1634312 | tf_op jit(solution)/shard_map/ppermute | solution.py:738
  310.2 11.7 %collective-permute-start.29 = (bf16[64,768]{1,0:T(8,128)(2,1)S(1)}, bf16[64,768]{1,0:T(8,128)(2,1)S(1)}, u32[]{:S(2)}, u32[]{:S(2)}) collective-permute-start(bf16[64,768]{1,0:T(8,128)(2,1)S(1)} %fusion.35), channel_id=1, source_target_pairs={{0,16},{2,18},{4,20},{6,22},{8,24},{10,26},{12,28},{14,30},{16,0},... | collective-permute-start | bytes 294920 | tf_op jit(solution)/shard_map/ppermute | solution.py:738
  321.9 7.4 %collective-permute-start.30 = (bf16[128,768]{1,0:T(8,128)(2,1)S(1)}, bf16[128,768]{1,0:T(8,128)(2,1)S(1)}, u32[]{:S(2)}, u32[]{:S(2)}) collective-permute-start(bf16[128,768]{1,0:T(8,128)(2,1)S(1)} %maximum_select_fusion.16), channel_id=1, source_target_pairs={{0,8},{2,10},{4,12},{6,14},{8,0},{10,2},{12,4},{14,6},{16,24},{18,... | collective-permute-start | bytes 589832 | tf_op jit(solution)/shard_map/ppermute | solution.py:738
  324.9 18.7 %collective-permute-start.24 = (bf16[512,1024]{1,0:T(8,128)(2,1)S(1)}, bf16[512,1024]{1,0:T(8,128)(2,1)}, u32[]{:S(2)}, u32[]{:S(2)}) collective-permute-start(bf16[512,1024]{1,0:T(8,128)(2,1)S(1)} %maximum_select_fusion.6), channel_id=1, source_target_pairs={{0,2},{2,0},{4,6},{6,4},{8,10},{10,8},{12,14},{14,12},{16,18},{18,... | collective-permute-start | bytes 3145736 | tf_op jit(solution)/shard_map/ppermute | solution.py:738
  327.9 19.2 %collective-permute-start.38 = (bf16[512,1024]{1,0:T(8,128)(2,1)}, bf16[512,1024]{1,0:T(8,128)(2,1)}, u32[]{:S(2)}, u32[]{:S(2)}) collective-permute-start(bf16[512,1024]{1,0:T(8,128)(2,1)} %maximum_select_fusion.7), channel_id=1, source_target_pairs={{0,2},{2,0},{4,6},{6,4},{8,10},{10,8},{12,14},{14,12},{16,18},{18,... | collective-permute-start | bytes 3145736 | tf_op jit(solution)/shard_map/ppermute | solution.py:738
  330.1 11.7 %collective-permute-start.31 = (bf16[256,768]{1,0:T(8,128)(2,1)}, bf16[256,768]{1,0:T(8,128)(2,1)}, u32[]{:S(2)}, u32[]{:S(2)}) collective-permute-start(bf16[256,768]{1,0:T(8,128)(2,1)} %maximum_select_fusion.12), channel_id=1, source_target_pairs={{0,4},{2,6},{4,0},{6,2},{8,12},{10,14},{12,8},{14,10},{16,20},{18,... | collective-permute-start | bytes 1179656 | tf_op jit(solution)/shard_map/ppermute | solution.py:738
  343.5 12.0 %collective-permute-start.32 = (bf16[512,768]{1,0:T(8,128)(2,1)S(1)}, bf16[512,768]{1,0:T(8,128)(2,1)S(1)}, u32[]{:S(2)}, u32[]{:S(2)}) collective-permute-start(bf16[512,768]{1,0:T(8,128)(2,1)S(1)} %maximum_select_fusion.8), channel_id=1, source_target_pairs={{0,2},{2,0},{4,6},{6,4},{8,10},{10,8},{12,14},{14,12},{16,18},{18,... | collective-permute-start | bytes 2359304 | tf_op jit(solution)/shard_map/ppermute | solution.py:738
  (79 other events, 304.1 us)
Sparse Core Ops, SparseCore 0:
  111.5 185.7 all-reduce.7

commit v4 on v3

--- a/solution.py
+++ b/solution.py
@@ -716,29 +716,9 @@
     )(query, pair, total, grad, jnp.asarray(cosine), jnp.asarray(sine))
 
 
-def bit_pairs(size, bit):
-    return [(index, index ^ (1 << bit)) for index in range(size)]
-
-
-def split_sides(part, bit):
-    side = (lax.axis_index("dp") >> bit) & 1
-    halves = part.reshape(2, part.shape[0] // 2, part.shape[1])
-    keep = lax.dynamic_index_in_dim(halves, side, 0, False)
-    give = lax.dynamic_index_in_dim(halves, 1 - side, 0, False)
-    return keep, give
-
-
-def add_half(keep, give, bit, size):
-    got = lax.ppermute(give, "dp", bit_pairs(size, bit))
-    return (keep.astype(jnp.float32) + got.astype(jnp.float32)).astype(jnp.bfloat16)
-
-
-def join_half(part, bit, size):
-    side = (lax.axis_index("dp") >> bit) & 1
-    got = lax.ppermute(part, "dp", bit_pairs(size, bit))
-    return jnp.where(
-        side == 0, jnp.concatenate([part, got], axis=0), jnp.concatenate([got, part], axis=0)
-    )
+def step_groups(size):
+    bits = size.bit_length() - 1
+    return [1] * min(bits, 2) + [2] * (max(bits - 2, 0) // 2) + [1] * (max(bits - 2, 0) % 2)
 
 
 def after(part, *deps):
@@ -751,45 +731,54 @@
 
 
 class Sum:
-    def __init__(self, part, size, swapped):
+    def __init__(self, part, size, place):
         self.size = size
+        self.place = place
         self.direct = bool(size & (size - 1) or part.shape[0] % size)
-        self.order = [] if self.direct else bit_order(size, swapped)
+        self.steps = [] if self.direct else step_groups(size)
+        self.shift = 0
         self.part = part
-        self.step = 0
-        self.give = part
-        self.prepare()
+        self.gives = [part]
+        if not self.direct:
+            self.part = part.reshape(size, part.shape[0] // size, part.shape[1])
+            self.prepare()
 
     def prepare(self):
-        if self.step < len(self.order):
-            self.keep, self.give = split_sides(self.part, self.order[self.step])
-        else:
-            self.give = self.part
+        if not self.steps:
+            self.gives = [self.part]
+            return
+        ways = 1 << self.steps[0]
+        rest = self.part.shape[0] // ways
+        view = self.part.reshape((rest, ways) + self.part.shape[1:])
+        mine = (lax.axis_index("dp") >> self.shift) & (ways - 1)
+        self.keep = lax.dynamic_index_in_dim(view, mine, 1, False)
+        self.gives = [
+            lax.dynamic_index_in_dim(view, mine ^ way, 1, False) for way in range(1, ways)
+        ]
 
     def advance(self):
-        if self.step < len(self.order):
-            self.part = add_half(self.keep, self.give, self.order[self.step], self.size)
-            self.step += 1
+        if self.steps:
+            total = self.keep.astype(jnp.float32)
+            for way, give in enumerate(self.gives, 1):
+                pairs = [(index, index ^ (way << self.shift)) for index in range(self.size)]
+                total = total + lax.ppermute(give, "dp", pairs).astype(jnp.float32)
+            self.part = total.astype(jnp.bfloat16)
+            self.shift += self.steps.pop(0)
             self.prepare()
-        return self.give
+        return self.gives
 
     def finish(self, middle=None):
-        while self.step < len(self.order):
+        while self.steps:
             self.advance()
         if self.direct:
-            self.part = lax.psum(self.part, "dp")
+            part = lax.psum(self.part, "dp")
+            return part if middle is None else middle(part)
+        part = self.part[0]
         if middle is not None:
-            self.part = middle(self.part)
-        for bit in reversed(self.order):
-            self.part = join_half(self.part, bit, self.size)
-        return self.part
-
-
-def bit_order(size, swapped):
-    order = list(range(size.bit_length() - 1))
-    if swapped and len(order) > 2:
-        order[1], order[2] = order[2], order[1]
-    return order
+            part = middle(part)
+        lead = (1,) * (self.place + 1)
+        whole = lax.all_gather(part.reshape(lead + part.shape), "dp", axis=self.place, tiled=True)
+        return whole.reshape(self.size * part.shape[0], part.shape[1])
 
 
 def other(part):
@@ -935,10 +924,18 @@
     back_mid = sum_all(back_part, shards)
     hidden_late = after(hidden, back_part)
     mid_late = after(whole_mid, back_part)
-    grad_down = inner_rows(hidden_late, cotan_low).astype(jnp.bfloat16)
-    grad_gate = inner_rows(mid_late, grad_gate_low).astype(jnp.bfloat16)
-    grad_up = inner_rows(mid_late, grad_upper_low).astype(jnp.bfloat16)
-    grad_gate, grad_up, grad_down = lax.psum((grad_gate, grad_up, grad_down), "dp")
+    down_sum = Sum(inner_rows(hidden_late, cotan_low).astype(jnp.bfloat16), dp_size, 0)
+    hidden_cols = gate_weight.shape[1]
+    wide_sum = Sum(
+        inner_rows(mid_late, jnp.concatenate([grad_gate_low, grad_upper_low], axis=1)).astype(
+            jnp.bfloat16
+        ),
+        dp_size,
+        0,
+    )
+    down_sum.advance()
+    wide_sum.advance()
+    back_mid = after(back_mid, *down_sum.gives, *wide_sum.gives)
     feed_part = behind(forward_dot(hidden_late, down_weight), back_mid).astype(jnp.bfloat16)
     feed = sum_own(feed_part, shards)
     layer_output = (own_rows(resid, own) + feed).astype(jnp.bfloat16)
@@ -952,7 +949,7 @@
             jnp.bfloat16
         ),
         dp_size,
-        False,
+        1,
     )
     ssm_rows = gated_low.shape[1]
     grad_gated = against(mixer_all, mamba_output)
@@ -965,13 +962,15 @@
         queries,
         pairs,
         totals,
-        after(jnp.pad(grad_context, ((0, 0), (0, query_pad))), mixer_sum.give),
+        after(jnp.pad(grad_context, ((0, 0), (0, query_pad))), *mixer_sum.gives, *down_sum.advance()),
         length,
     )
     grad_query_raw = grad_query_raw[:, :query_cols]
     early_cols = jnp.concatenate([grad_gate_raw, grad_query_raw], axis=1)
-    early_sum = Sum(inner_rows(whole, early_cols).astype(jnp.bfloat16), dp_size, True)
-    grad_gated = after(grad_gated, early_sum.give, mixer_sum.advance())
+    early_sum = Sum(inner_rows(whole, early_cols).astype(jnp.bfloat16), dp_size, 2)
+    grad_gated = after(
+        grad_gated, *early_sum.gives, *mixer_sum.advance(), *wide_sum.advance()
+    )
     grad_input_raw, grad_state_raw, grad_step_raw, input_sums, state_sums, head_sums = ssd_backward(
         input_raw, state_raw, gate_raw, step_raw, grad_gated, carries, small, heads, length
     )
@@ -981,7 +980,14 @@
     taps = input_kernel.shape[0]
     early_sum.advance()
     mixer_sum.advance()
-    grad_input_raw = after(grad_input_raw, early_sum.give, mixer_sum.give)
+    down_sum.advance()
+    wide_sum.advance()
+    grad_input_raw = after(
+        grad_input_raw, *early_sum.gives, *mixer_sum.gives, *down_sum.gives, *wide_sum.gives
+    )
+    grad_down = down_sum.finish()
+    grad_wide = wide_sum.finish()
+    grad_gate, grad_up = grad_wide[:, :hidden_cols], grad_wide[:, hidden_cols:]
     late_cols = jnp.concatenate(
         [grad_input_raw, grad_state_raw, grad_pair_raw, grad_step_raw], axis=1
     )
@@ -1000,69 +1006,68 @@
 
     own_vectors = (input_sums[:taps], input_sums[taps], head_sums[0], head_sums[1], head_sums[2])
     shared_vectors = (grad_first, grad_middle, state_sums[:taps], state_sums[taps])
-    own_pack = column_pack(own_vectors, width).astype(jnp.bfloat16)
-    shared_pack = column_pack(shared_vectors, width).astype(jnp.bfloat16)
-    own_width = own_pack.shape[1]
-    shared_width = shared_pack.shape[1]
-
+    own_pack = column_pack(own_vectors, width)
+    shared_pack = column_pack(shared_vectors, width)
+    shared_lane = step_cols + own_pack.shape[1]
+    last_lane = shared_lane + shared_pack.shape[1]
+    packs = jnp.pad(
+        jnp.concatenate([own_pack, shared_pack], axis=1),
+        ((0, 0), (step_cols, LANES - last_lane)),
+    )
     split_pairs = shards == KVH
-    late = inner_rows(whole, late_cols).astype(jnp.bfloat16)
+    late = inner_rows(whole, late_cols)
     marks = (input_cols, input_cols + state_cols, input_cols + state_cols + pair_cols)
     late_pair = late[:, marks[1] : marks[2]]
     if not split_pairs:
-        spread = jnp.zeros((width, 2 * KVH * HD), jnp.bfloat16)
+        spread = jnp.zeros((width, 2 * KVH * HD), jnp.float32)
         spread = lax.dynamic_update_slice_in_dim(spread, late_pair[:, :HD], kv_head * HD, 1)
         late_pair = lax.dynamic_update_slice_in_dim(
             spread, late_pair[:, HD:], (KVH + kv_head) * HD, 1
         )
-    tail = jnp.concatenate(
-        [late[:, input_cols : marks[1]], late_pair, shared_pack, late[:, marks[2] : marks[2] + step_cols], own_pack],
-        axis=1,
-    )
-    sent = state_cols + late_pair.shape[1] + shared_width
+        late = jnp.concatenate([late[:, : marks[1]], late_pair, late[:, marks[2] :]], axis=1)
+    misc = late.shape[1] - LANES
+    late = (late + jnp.pad(packs, ((0, 0), (misc, 0)))).astype(jnp.bfloat16)
+    late_sum = Sum(late, dp_size, 3)
 
     def over_tensor(part):
-        shared, rest = part[:, :sent], part[:, sent:]
-        if not split_pairs:
-            return jnp.concatenate([lax.psum(shared, "tensor"), rest], axis=1)
-        got = other(shared)
-        first = lax.axis_index("tensor") == 0
-        low = jnp.where(first, shared, got)[:, state_cols : state_cols + pair_cols]
-        high = jnp.where(first, got, shared)[:, state_cols : state_cols + pair_cols]
-        both = (shared.astype(jnp.float32) + got.astype(jnp.float32)).astype(jnp.bfloat16)
+        own_part = part[:, input_cols:]
+        if split_pairs:
+            got = other(own_part)
+            both = (own_part.astype(jnp.float32) + got.astype(jnp.float32)).astype(jnp.bfloat16)
+            first = lax.axis_index("tensor") == 0
+            pair_span = slice(state_cols, state_cols + pair_cols)
+            low = jnp.where(first, own_part[:, pair_span], got[:, pair_span])
+            high = jnp.where(first, got[:, pair_span], own_part[:, pair_span])
+            pair = [low[:, :HD], high[:, :HD], low[:, HD:], high[:, HD:]]
+        else:
+            both = lax.psum(own_part, "tensor")
+            pair = [both[:, state_cols:-LANES]]
+        lane = lane_index((part.shape[0], LANES))
+        extra = jnp.where(
+            (lane >= shared_lane) & (lane < last_lane), both[:, -LANES:], own_part[:, -LANES:]
+        )
         return jnp.concatenate(
-            [
-                both[:, :state_cols],
-                low[:, :HD],
-                high[:, :HD],
-                low[:, HD:],
-                high[:, HD:],
-                both[:, state_cols + pair_cols :],
-                rest,
-            ],
-            axis=1,
+            [part[:, :input_cols], both[:, :state_cols]] + pair + [extra], axis=1
         )
 
-    tail_sum = Sum(tail, dp_size, True)
-    input_sum = Sum(late[:, :input_cols], dp_size, False)
-    tail = tail_sum.finish(over_tensor)
-    grad_mamba_input = input_sum.finish()
     grad_mixer_out = mixer_sum.finish()
     grad_mamba_out = grad_mixer_out[:ssm_rows]
     grad_context_w = grad_mixer_out[ssm_rows:]
     early = early_sum.finish()
+    tail = late_sum.finish(over_tensor)
+    grad_mamba_input = tail[:, :input_cols]
+    tail = tail[:, input_cols:]
     back_in = sum_own(total_low, shards)
     normal_own = own_rows(normal_first, own)
     factor_own = own_rows(factor_first, own)
     input_grad = own_rows(grad_resid, own) + norm_back(back_in, gain_first, normal_own, factor_own)
-    start = state_cols + keyvalue_weight.shape[1]
+    extra = tail[:, state_cols + keyvalue_weight.shape[1] :]
+    grad_step = extra[:, :step_cols]
+    grad_in_kernel, grad_in_shift, grad_bias, grad_decay, grad_skip = column_unpack(
+        extra[:, step_cols:shared_lane], [item.shape for item in own_vectors]
+    )
     grad_first, grad_middle, grad_st_kernel, grad_st_shift = column_unpack(
-        tail[:, start : start + shared_width], [item.shape for item in shared_vectors]
-    )
-    start = start + shared_width
-    grad_step = tail[:, start : start + step_cols]
-    grad_in_kernel, grad_in_shift, grad_bias, grad_decay, grad_skip = column_unpack(
-        tail[:, start + step_cols :], [item.shape for item in own_vectors]
+        extra[:, shared_lane:last_lane], [item.shape for item in shared_vectors]
     )
     results = (
         grad_first,

time: 372 us -> 448 us (1.20)
  waiting for transfers between devices: 130 us -> 167 us
  local copies, waits for them, and re-layouts: 37.9 us -> 57.4 us
  starting transfers between devices: 27.6 us -> 41 us
  matrix products: 35.2 us -> 44.6 us
    all_gather x0 -> x5, waiting for transfers between devices: none -> 43.6 us  [finish(): lax.all_gather(part.reshape(lead + part.shape), 'dp', axis=self.place, ti...]
    select_n x16 -> x1, other arithmetic: 22.7 us -> 0.01 us  [over_tensor(): high = jnp.where(first, got[:, pair_span], own_part[:, pair_span])]
    ppermute x32 -> x25, waiting for transfers between devices: 92.5 us -> 70.2 us  [advance(): total = total + lax.ppermute(give, 'dp', pairs).astype(jnp.float32)]
    ppermute x7, waiting for transfers between devices: 37.3 us -> 52.5 us  [other(): return lax.ppermute(part, 'tensor', [(0, 1), (1, 0)])]
    ppermute x32 -> x25, starting transfers between devices: 18.6 us -> 30.9 us  [advance(): total = total + lax.ppermute(give, 'dp', pairs).astype(jnp.float32)]
    convert_element_type x17 -> x15, other arithmetic: 8.17 us -> 20.1 us  [the longest x14 20 us: advance(): self.part = total.astype(jnp.bfloat16)]
    dot_general x6 -> x5, matrix products: 13.7 us -> 21.5 us  [inner_rows(): lax.dot_general(left, right, (((0,), (0,)), ((), ())), preferred_element_...]
    unnamed x218 -> x220, local copies, waits for them, and re-layouts: 16 us -> 21.8 us
  transfers between devices with their start and end apart: 40 -> 37, of which waited for: 17 -> 19; matrix products, arithmetic and copies ran while one was open for 33% -> 27% of each run, Pallas kernels for 8% -> 6%
where the time goes in v4:
time: 448 us; the launch traced here: 441 us
  waiting for transfers between devices  167 us (37%)
  other arithmetic  71.8 us (16%)
  local copies, waits for them, and re-layouts  57.4 us (13%)
  matrix products  44.6 us (10%)
  Pallas kernels  43.1 us (10%)
  starting transfers between devices  41 us (9%)
  between operations  16 us (4%)
    ppermute x25, waiting for transfers between devices, advance(): total = total + lax.ppermute(give, 'dp', pairs).astype(jnp.float32)  70.2 us
    ppermute x7, waiting for transfers between devices, other(): return lax.ppermute(part, 'tensor', [(0, 1), (1, 0)])  52.5 us
    all_gather x5, waiting for transfers between devices, finish(): lax.all_gather(part.reshape(lead + part.shape), 'dp', axis=self.place, ti...  43.6 us
    ppermute x25, starting transfers between devices, advance(): total = total + lax.ppermute(give, 'dp', pairs).astype(jnp.float32)  30.9 us
    convert_element_type x14, other arithmetic, body(): item.astype(jnp.float32)  26.7 us
    pallas_call x1, Pallas kernels, ssd_backward(): pl.pallas_call(ssd_backward_kernel, grid=(seqs,), in_specs=[by_sequence(l...  22.3 us
    unnamed x220, local copies, waits for them, and re-layouts  21.8 us
    dot_general x5, matrix products, inner_rows(): lax.dot_general(left, right, (((0,), (0,)), ((), ())), preferred_element_...  21.5 us
  transfers between devices with their start and end apart: 37, of which 19 were waited for; matrix products, arithmetic and copies ran while one was open for 27% of the time, Pallas kernels for 6%

profile of v4, /device:TPU:0, one launch (start us, length us, event | category | flops | bytes accessed | tf_op | source)
XLA Modules:
  0.0 440.7 jit_solution(1709417528187515603)
XLA Ops:
  7.3 3.0 collective-permute-start
  17.3 5.9 %collective-permute-done = bf16[256,1024]{1,0:T(8,128)(2,1)S(1)} collective-permute-done((bf16[256,1024]{1,0:T(8,128)(2,1)}, bf16[256,1024]{1,0:T(8,128)(2,1)S(1)}, u32[]{:S(2)}, u32[]{:S(2)}) %collective-permute-start) | collective-permute-done | bytes 524320 | tf_op jit(solution)/shard_map/ppermute | solution.py:785
  23.3 1.8 fusion.4
  30.9 2.9 collective-permute-done.1
  33.8 2.6 maximum_select_fusion.1
  36.4 8.8 %ssd_forward.1 = (bf16[512,768]{1,0:T(8,128)(2,1)S(1)}, f32[512,768]{1,0:T(8,128)S(1)}, f32[4,128,768]{2,1,0:T(8,128)S(1)}) custom-call(f32[512,768]{1,0:T(8,128)S(1)} %fusion.49.input_ref, f32[512,256]{1,0:T(8,128)S(1)} %fusion.50.state_ref, f32[512,768]{1,0:T(8,128)S(1)} %fusion.51.gate_ref, f32[512,128]{1,0:T(8,128)S(1)} %fusion.34.step_ref, ...), custom_call_target="tpu_custom_call" | custom-call | flops 402653184 | bytes 7864320 | tf_op jit(solution)/shard_map/ssd_forward/pallas_call | solution.py:416
  47.8 5.7 %attend_forward.1 = (bf16[512,256]{1,0:T(8,128)(2,1)S(1)}, bf16[512,256]{1,0:T(8,128)(2,1)S(1)}, bf16[512,128]{1,0:T(8,128)(2,1)S(1)}, f32[512,128]{1,0:T(8,128)S(1)}) custom-call(f32[512,256]{1,0:T(8,128)S(1)} %fusion.53.query_ref, f32[512,128]{1,0:T(8,128)S(1)} %fusion.29.pair_ref, f32[512,128]{1,0:T(8,128)S(1)} %copy-done.13, f32[512,128]{1,0:T(8,128)S(1)} %copy-done.14), custom_call_target="tpu_custom_call" | custom-call | flops 268435456 | bytes 1572864 | tf_op jit(solution)/shard_map/attend_forward/pallas_call | solution.py:654
  55.6 1.8 collective-permute-start.2
  58.7 21.6 %collective-permute-done.2 = bf16[512,1024]{1,0:T(8,128)(2,1)} collective-permute-done((bf16[512,1024]{1,0:T(8,128)(2,1)}, bf16[512,1024]{1,0:T(8,128)(2,1)}, u32[]{:S(2)}, u32[]{:S(2)}) %collective-permute-start.2) | collective-permute-done | bytes 1048608 | tf_op jit(solution)/shard_map/ppermute | solution.py:785
  80.3 2.9 multiply_reduce_fusion.2
  83.6 2.1 copy-done.100
  88.5 2.1 multiply_convert_fusion
  91.9 2.3 add_convert_fusion.2
  94.2 13.5 %convolution_convert_fusion.3 = bf16[1024,1024]{1,0:T(8,128)(2,1)S(1)} fusion(bf16[512,1024]{1,0:T(8,128)(2,1)S(1)} %get-tuple-element.47, bf16[512,1024]{1,0:T(8,128)(2,1)S(1)} %copy-done.58), kind=kOutput, calls=%fused_computation.50 | convolution fusion | flops 1074790400 | bytes 4194304 | tf_op jit(solution)/shard_map/dot_general | solution.py:28
  109.4 2.4 convolution_convert_fusion
  111.8 1.6 dynamic-slice_bitcast_fusion
  116.4 1.9 fusion.15
  121.6 1.6 copy.120
  123.2 1.7 pad.29.clone
  125.0 5.1 %concatenate.56 = bf16[1024,1280]{1,0:T(8,128)(2,1)} concatenate(bf16[1024,768]{1,0:T(8,128)(2,1)} %param.33, bf16[1024,256]{1,0:T(8,128)(2,1)} %param.35, bf16[1024,64]{1,0:T(8,128)(2,1)} %copy-done.68, bf16[1024,64]{1,0:T(8,128)(2,1)} %copy-done.69, bf16[1024,128]{1,0:T(8,128)(2,1)} %pad.29.clone), dimensions={1} | concatenate | bytes 5242880 | tf_op jit(solution)/shard_map/concatenate | solution.py:996
  130.1 3.9 collective-permute-done.7
  135.4 3.7 collective-permute-start.14
  140.4 2.9 convert_add_fusion.2
  143.8 5.4 %collective-permute-done.13 = bf16[1,64,1024]{2,1,0:T(8,128)(2,1)S(1)} collective-permute-done((bf16[1,64,1024]{2,1,0:T(8,128)(2,1)S(1)}, bf16[1,64,1024]{2,1,0:T(8,128)(2,1)S(1)}, u32[]{:S(2)}, u32[]{:S(2)}) %collective-permute-start.13) | collective-permute-done | bytes 131104 | tf_op jit(solution)/shard_map/ppermute | solution.py:764
  150.0 3.3 fusion.1
  160.9 1.5 collective-permute-start.9
  165.1 6.3 %attend_backward.1 = (bf16[512,256]{1,0:T(8,128)(2,1)S(1)}, bf16[512,128]{1,0:T(8,128)(2,1)S(1)}) custom-call(bf16[512,256]{1,0:T(8,128)(2,1)S(1)} %copy-done.36, bf16[512,128]{1,0:T(8,128)(2,1)S(1)} %copy-done.40, f32[512,128]{1,0:T(8,128)S(1)} %copy-done.38, bf16[512,256]{1,0:T(8,128)(2,1)S(1)} %convolution_convert_fusion.4.grad_ref, ...), custom_call_target="tpu_custom_call" | custom-call | flops 671088640 | bytes 1572864 | tf_op jit(solution)/shard_map/attend_backward/pallas_call | solution.py:689
  173.4 1.6 fusion.14
  176.0 16.8 %collective-permute-done.9 = bf16[4,64,2048]{2,1,0:T(8,128)(2,1)} collective-permute-done((bf16[4,64,2048]{2,1,0:T(8,128)(2,1)S(1)}, bf16[4,64,2048]{2,1,0:T(8,128)(2,1)}, u32[]{:S(2)}, u32[]{:S(2)}) %collective-permute-start.9) | collective-permute-done | bytes 1048608 | tf_op jit(solution)/shard_map/ppermute | solution.py:764
  192.8 1.6 fusion.13
  195.4 2.5 collective-permute-start.17
  197.9 22.3 %ssd_backward.1 = (bf16[512,768]{1,0:T(8,128)(2,1)S(1)}, bf16[512,256]{1,0:T(8,128)(2,1)S(1)}, bf16[512,128]{1,0:T(8,128)(2,1)S(1)}, f32[1,8,768]{2,1,0:T(8,128)...) custom-call(f32[512,768]{1,0:T(8,128)S(1)} %copy-done.4, f32[512,256]{1,0:T(8,128)S(1)} %fusion.50.state_ref, ...), custom_call_target="tpu_custom_call" | custom-call | flops 1006632960 | bytes 7864320 | tf_op jit(solution)/shard_map/ssd_backward/pallas_call | solution.py:465
  224.8 2.0 collective-permute-start.30
  235.2 1.7 add_convert_fusion.6
  237.4 1.9 dynamic-slice_bitcast_fusion.8
  240.9 2.0 add_convert_fusion.4
  245.3 1.5 fusion.57
  247.5 3.1 multiply_reduce_fusion
  251.6 3.0 fusion
  257.9 2.5 collective-permute-start.28
  260.4 2.0 collective-permute-start.26
  262.4 4.7 %collective-permute-done.28 = bf16[1,64,1024]{2,1,0:T(8,128)(2,1)S(1)} collective-permute-done((bf16[1,64,1024]{2,1,0:T(8,128)(2,1)S(1)}, bf16[1,64,1024]{2,1,0:T(8,128)(2,1)S(1)}, u32[]{:S(2)}, u32[]{:S(2)}) %collective-permute-start.28) | collective-permute-done | bytes 131104 | tf_op jit(solution)/shard_map/ppermute | solution.py:764
  267.1 13.3 %collective-permute-done.27 = bf16[1,64,1024]{2,1,0:T(8,128)(2,1)S(1)} collective-permute-done((bf16[1,64,1024]{2,1,0:T(8,128)(2,1)S(1)}, bf16[1,64,1024]{2,1,0:T(8,128)(2,1)S(1)}, u32[]{:S(2)}, u32[]{:S(2)}) %collective-permute-start.27) | collective-permute-done | bytes 131104 | tf_op jit(solution)/shard_map/ppermute | solution.py:764
  281.1 2.0 fusion.2
  284.8 12.8 %collective-permute-done.20 = bf16[4,64,1280]{2,1,0:T(8,128)(2,1)S(1)} collective-permute-done((bf16[4,64,1280]{2,1,0:T(8,128)(2,1)S(1)}, bf16[4,64,1280]{2,1,0:T(8,128)(2,1)S(1)}, u32[]{:S(2)}, u32[]{:S(2)}) %collective-permute-start.20) | collective-permute-done | bytes 655392 | tf_op jit(solution)/shard_map/ppermute | solution.py:764
  297.8 5.6 %collective-permute-start.23 = (bf16[1,64,1280]{2,1,0:T(8,128)(2,1)S(1)}, bf16[1,64,1280]{2,1,0:T(8,128)(2,1)S(1)}, u32[]{:S(2)}, u32[]{:S(2)}) collective-permute-start(bf16[1,64,1280]{2,1,0:T(8,128)(2,1)S(1)} %get-tuple-element.220), channel_id=1, source_target_pairs={{0,24},{2,26},{4,28},{6,30},{8,16},{10,18},{12,20},{14,22},{16,8},... | collective-permute-start | bytes 491528 | tf_op jit(solution)/shard_map/ppermute | solution.py:764
  304.1 4.5 %collective-permute-done.23 = bf16[1,64,1280]{2,1,0:T(8,128)(2,1)S(1)} collective-permute-done((bf16[1,64,1280]{2,1,0:T(8,128)(2,1)S(1)}, bf16[1,64,1280]{2,1,0:T(8,128)(2,1)S(1)}, u32[]{:S(2)}, u32[]{:S(2)}) %collective-permute-start.23) | collective-permute-done | bytes 163872 | tf_op jit(solution)/shard_map/ppermute | solution.py:764
  308.6 8.1 %collective-permute-done.22 = bf16[1,64,1280]{2,1,0:T(8,128)(2,1)S(1)} collective-permute-done((bf16[1,64,1280]{2,1,0:T(8,128)(2,1)S(1)}, bf16[1,64,1280]{2,1,0:T(8,128)(2,1)S(1)}, u32[]{:S(2)}, u32[]{:S(2)}) %collective-permute-start.22) | collective-permute-done | bytes 163872 | tf_op jit(solution)/shard_map/ppermute | solution.py:764
  317.7 3.4 collective-permute-done.24
  324.5 2.6 add_convert_fusion.1
  331.8 12.2 %collective-permute-done.6 = bf16[256,1024]{1,0:T(8,128)(2,1)} collective-permute-done((bf16[256,1024]{1,0:T(8,128)(2,1)}, bf16[256,1024]{1,0:T(8,128)(2,1)}, u32[]{:S(2)}, u32[]{:S(2)}) %collective-permute-start.6) | collective-permute-done | bytes 524320 | tf_op jit(solution)/shard_map/ppermute | solution.py:785
  344.1 2.5 fusion.28
  346.6 5.9 %collective-permute-done.18 = bf16[256,1024]{1,0:T(8,128)(2,1)} collective-permute-done((bf16[256,1024]{1,0:T(8,128)(2,1)}, bf16[256,1024]{1,0:T(8,128)(2,1)}, u32[]{:S(2)}, u32[]{:S(2)}) %collective-permute-start.18) | collective-permute-done | bytes 524320 | tf_op jit(solution)/shard_map/ppermute | solution.py:785
  353.9 2.4 multiply_add_fusion.1
  356.3 4.2 bitcast_convert_fusion
  360.5 2.7 slice.212
  364.3 2.2 slice_convert_fusion.5
  367.6 1.9 slice_convert_fusion.3
  369.5 2.2 bitcast_convert_fusion.1
  371.7 4.7 %all-gather.13.cloned.1.call-done = bf16[1024,1408]{1,0:T(8,128)(2,1)} async-done(((bf16[64,1408]{1,0:T(8,128)(2,1)}), bf16[1024,1408]{1,0:T(8,128)(2,1)}) %all-gather.13.cloned.1.call-update) | async-done | bytes 2883600 | tf_op jit(solution)/shard_map/all_gather | solution.py:780
  383.8 2.7 slice_convert_fusion.4
  386.5 1.9 slice_convert_fusion.2
  388.4 38.9 %all-gather.9.cloned.1.call-done = bf16[16,64,2048]{2,1,0:T(8,128)(2,1)} async-done(((bf16[1,64,2048]{2,1,0:T(8,128)(2,1)}), bf16[16,64,2048]{2,1,0:T(8,128)(2,1)}) %all-gather.9.cloned.1.call-update) | async-done | bytes 4194320 | tf_op jit(solution)/shard_map/all_gather | solution.py:780
  427.3 6.7 %slice_convert_fusion = (f32[1024,1024]{1,0:T(8,128)}, f32[1024,1024]{1,0:T(8,128)}) fusion(bf16[1024,2048]{1,0:T(8,128)(2,1)} %bitcast.169), kind=kLoop, calls=%fused_computation.14 | loop fusion | flops 2097152 | bytes 12582912 | tf_op jit(solution)/shard_map/convert_element_type | solution.py:1094
  (367 shorter events, 93.5 us)
Async XLA Ops:
  7.2 81.3 %copy-start = (bf16[1024,1024]{1,0:T(8,128)(2,1)S(1)}, bf16[1024,1024]{1,0:T(8,128)(2,1)}, u32[]{:S(2)}) copy-start(bf16[1024,1024]{1,0:T(8,128)(2,1)} %param.49) | copy-start | bytes 6291460
  7.2 17.9 %copy-start.52 = (bf16[256,1024]{1,0:T(8,128)(2,1)S(1)}, bf16[256,1024]{1,0:T(8,128)(2,1)}, u32[]{:S(2)}) copy-start(bf16[256,1024]{1,0:T(8,128)(2,1)} %param.29) | copy-start | bytes 1572868
  7.2 349.1 %all-gather.11.cloned.1.call-start = ((), (), s32[]{:S(2)}) async-start(), calls=%async_computation.1 | async-start | bytes 2228224 | tf_op jit(solution)/shard_map/all_gather | solution.py:780
  7.3 16.0 %collective-permute-start = (bf16[256,1024]{1,0:T(8,128)(2,1)}, bf16[256,1024]{1,0:T(8,128)(2,1)S(1)}, u32[]{:S(2)}, u32[]{:S(2)}) collective-permute-start(bf16[256,1024]{1,0:T(8,128)(2,1)} %param.29), channel_id=1, source_target_pairs={{0,1},{1,0},{2,3},{3,2},{4,5},{5,4},{6,7},{7,6},{8,9},{9,8},{10,11... | collective-permute-start | bytes 1572872 | tf_op jit(solution)/shard_map/ppermute | solution.py:785
  10.3 23.5 %collective-permute-start.1 = (bf16[256,1024]{1,0:T(8,128)(2,1)}, bf16[256,1024]{1,0:T(8,128)(2,1)}, u32[]{:S(2)}, u32[]{:S(2)}) collective-permute-start(bf16[256,1024]{1,0:T(8,128)(2,1)} %param.50), channel_id=1, source_target_pairs={{0,1},{1,0},{2,3},{3,2},{4,5},{5,4},{6,7},{7,6},{8,9},{9,8},{10,11... | collective-permute-start | bytes 1572872 | tf_op jit(solution)/shard_map/ppermute | solution.py:785
  11.1 14.4 %copy-start.88 = (f32[1024]{0:T(1024)}, f32[1024]{0:T(1024)S(1)}, u32[]{:S(2)}) copy-start(f32[1024]{0:T(1024)S(1)} %convert_element_type.424) | copy-start | bytes 12292
  12.4 23.9 %copy-start.22 = (f32[1,768]{1,0:T(1,128)}, f32[1,768]{1,0:T(1,128)S(1)}, u32[]{:S(2)}) copy-start(f32[1,768]{1,0:T(1,128)S(1)} %reshape.269.input_shift_ref) | copy-start | bytes 9220
  13.8 22.6 %copy-start.27 = (f32[256]{0:T(256)}, f32[256]{0:T(256)S(1)}, u32[]{:S(2)}) copy-start(f32[256]{0:T(256)S(1)} %broadcast_in_dim.36) | copy-start | bytes 3076
  14.6 21.8 %copy-start.24 = (f32[1,768]{1,0:T(1,128)}, f32[1,768]{1,0:T(1,128)S(1)}, u32[]{:S(2)}) copy-start(f32[1,768]{1,0:T(1,128)S(1)} %broadcast_in_dim_reshape.3.skip_ref) | copy-start | bytes 9220
  15.3 21.1 %copy-start.29 = (f32[1,128]{1,0:T(1,128)}, f32[1,128]{1,0:T(1,128)S(1)}, u32[]{:S(2)}) copy-start(f32[1,128]{1,0:T(1,128)S(1)} %pad.32.rate_ref) | copy-start | bytes 1540
  15.9 20.5 %copy-start.31 = (f32[1,128]{1,0:T(1,128)}, f32[1,128]{1,0:T(1,128)S(1)}, u32[]{:S(2)}) copy-start(f32[1,128]{1,0:T(1,128)S(1)} %pad_convert_fusion.bias_ref) | copy-start | bytes 1540
  16.0 9.7 %copy-start.77 = (bf16[1024,768]{1,0:T(8,128)(2,1)S(1)}, bf16[1024,768]{1,0:T(8,128)(2,1)}, u32[]{:S(2)}) copy-start(bf16[1024,768]{1,0:T(8,128)(2,1)} %param.33) | copy-start | bytes 4718596
  17.3 29.9 %copy-start.68 = (bf16[1024,64]{1,0:T(8,128)(2,1)}, bf16[1024,64]{1,0:T(8,128)(2,1)S(1)}, u32[]{:S(2)}) copy-start(bf16[1024,64]{1,0:T(8,128)(2,1)S(1)} %get-tuple-element.231) | copy-start | bytes 393220
  17.3 29.9 %copy-start.69 = (bf16[1024,64]{1,0:T(8,128)(2,1)}, bf16[1024,64]{1,0:T(8,128)(2,1)S(1)}, u32[]{:S(2)}) copy-start(bf16[1024,64]{1,0:T(8,128)(2,1)S(1)} %get-tuple-element.232) | copy-start | bytes 393220
  25.7 21.6 %copy-start.45 = (bf16[512,1024]{1,0:T(8,128)(2,1)}, bf16[512,1024]{1,0:T(8,128)(2,1)S(1)}, u32[]{:S(2)}) copy-start(bf16[512,1024]{1,0:T(8,128)(2,1)S(1)} %multiply_convert_fusion.4) | copy-start | bytes 3145732
  30.9 14.4 %copy-start.1 = (f32[512,768]{1,0:T(8,128)}, f32[512,768]{1,0:T(8,128)S(1)}, u32[]{:S(2)}) copy-start(f32[512,768]{1,0:T(8,128)S(1)} %fusion.51.gate_ref) | copy-start | bytes 4718596
  55.6 24.7 %collective-permute-start.2 = (bf16[512,1024]{1,0:T(8,128)(2,1)}, bf16[512,1024]{1,0:T(8,128)(2,1)}, u32[]{:S(2)}, u32[]{:S(2)}) collective-permute-start(bf16[512,1024]{1,0:T(8,128)(2,1)} %add_convert_fusion.3), channel_id=1, source_target_pairs={{0,1},{1,0},{2,3},{3,2},{4,5},{5,4},{6,7},{7,6},{8,9},{9,8},{10,11... | collective-permute-start | bytes 3145736 | tf_op jit(solution)/shard_map/ppermute | solution.py:785
  58.7 24.6 %copy-start.91 = (f32[1024]{0:T(1024)S(1)}, f32[1024]{0:T(1024)}, u32[]{:S(2)}) copy-start(f32[1024]{0:T(1024)} %convert_element_type.433) | copy-start | bytes 12292
  109.4 7.0 %collective-permute-start.4 = (bf16[8,64,1024]{2,1,0:T(8,128)(2,1)}, bf16[8,64,1024]{2,1,0:T(8,128)(2,1)}, u32[]{:S(2)}, u32[]{:S(2)}) collective-permute-start(bf16[8,64,1024]{2,1,0:T(8,128)(2,1)} %dynamic-slice_bitcast_fusion.5), channel_id=1, source_target_pairs={{0,2},{2,0},{4,6},{6,4},{8,10},{10,8},{12,14},{14,12},{16,18},{18,... | collective-permute-start | bytes 3145736 | tf_op jit(solution)/shard_map/ppermute | solution.py:764
  114.5 35.5 %collective-permute-start.5 = (bf16[8,64,2048]{2,1,0:T(8,128)(2,1)}, bf16[8,64,2048]{2,1,0:T(8,128)(2,1)}, u32[]{:S(2)}, u32[]{:S(2)}) collective-permute-start(bf16[8,64,2048]{2,1,0:T(8,128)(2,1)} %dynamic-slice_bitcast_fusion), channel_id=1, source_target_pairs={{0,2},{2,0},{4,6},{6,4},{8,10},{10,8},{12,14},{14,12},{16,18},{18,... | collective-permute-start | bytes 6291464 | tf_op jit(solution)/shard_map/ppermute | solution.py:764
  115.0 25.4 %collective-permute-start.3 = (bf16[512,1024]{1,0:T(8,128)(2,1)}, bf16[512,1024]{1,0:T(8,128)(2,1)}, u32[]{:S(2)}, u32[]{:S(2)}) collective-permute-start(bf16[512,1024]{1,0:T(8,128)(2,1)} %add_convert_fusion.2), channel_id=1, source_target_pairs={{0,1},{1,0},{2,3},{3,2},{4,5},{5,4},{6,7},{7,6},{8,9},{9,8},{10,11... | collective-permute-start | bytes 3145736 | tf_op jit(solution)/shard_map/ppermute | solution.py:785
  120.1 13.9 %collective-permute-start.7 = (bf16[4,64,1024]{2,1,0:T(8,128)(2,1)}, bf16[4,64,1024]{2,1,0:T(8,128)(2,1)}, u32[]{:S(2)}, u32[]{:S(2)}) collective-permute-start(bf16[4,64,1024]{2,1,0:T(8,128)(2,1)} %dynamic-slice_bitcast_fusion.11), channel_id=1, source_target_pairs={{0,4},{2,6},{4,0},{6,2},{8,12},{10,14},{12,8},{14,10},{16,20},{18,... | collective-permute-start | bytes 1572872 | tf_op jit(solution)/shard_map/ppermute | solution.py:764
  130.1 10.3 %copy-start.62 = (bf16[512,1024]{1,0:T(8,128)(2,1)S(1)}, bf16[512,1024]{1,0:T(8,128)(2,1)}, u32[]{:S(2)}) copy-start(bf16[512,1024]{1,0:T(8,128)(2,1)} %add_convert_fusion.2) | copy-start | bytes 3145732
  135.4 8.3 %collective-permute-start.14 = (bf16[1,64,1024]{2,1,0:T(8,128)(2,1)S(1)}, bf16[1,64,1024]{2,1,0:T(8,128)(2,1)S(1)}, u32[]{:S(2)}, u32[]{:S(2)}) collective-permute-start(bf16[1,64,1024]{2,1,0:T(8,128)(2,1)S(1)} %get-tuple-element.228), channel_id=1, source_target_pairs={{0,24},{2,26},{4,28},{6,30},{8,16},{10,18},{12,20},{14,22},{16,8},... | collective-permute-start | bytes 393224 | tf_op jit(solution)/shard_map/ppermute | solution.py:764
  139.1 10.1 %collective-permute-start.13 = (bf16[1,64,1024]{2,1,0:T(8,128)(2,1)S(1)}, bf16[1,64,1024]{2,1,0:T(8,128)(2,1)S(1)}, u32[]{:S(2)}, u32[]{:S(2)}) collective-permute-start(bf16[1,64,1024]{2,1,0:T(8,128)(2,1)S(1)} %get-tuple-element.229), channel_id=1, source_target_pairs={{0,16},{2,18},{4,20},{6,22},{8,24},{10,26},{12,28},{14,30},{16,0},... | collective-permute-start | bytes 393224 | tf_op jit(solution)/shard_map/ppermute | solution.py:764
  139.1 10.1 %collective-permute-start.12 = (bf16[1,64,1024]{2,1,0:T(8,128)(2,1)S(1)}, bf16[1,64,1024]{2,1,0:T(8,128)(2,1)S(1)}, u32[]{:S(2)}, u32[]{:S(2)}) collective-permute-start(bf16[1,64,1024]{2,1,0:T(8,128)(2,1)S(1)} %get-tuple-element.230), channel_id=1, source_target_pairs={{0,8},{2,10},{4,12},{6,14},{8,0},{10,2},{12,4},{14,6},{16,24},{18,... | collective-permute-start | bytes 393224 | tf_op jit(solution)/shard_map/ppermute | solution.py:764
  149.9 210.5 %all-gather.17.cloned.1.call-start = ((), (), s32[]{:S(2)}) async-start(), calls=%async_computation.4 | async-start | bytes 2228224 | tf_op jit(solution)/shard_map/all_gather | solution.py:780
  160.9 31.9 %collective-permute-start.9 = (bf16[4,64,2048]{2,1,0:T(8,128)(2,1)S(1)}, bf16[4,64,2048]{2,1,0:T(8,128)(2,1)}, u32[]{:S(2)}, u32[]{:S(2)}) collective-permute-start(bf16[4,64,2048]{2,1,0:T(8,128)(2,1)S(1)} %dynamic-slice_bitcast_fusion.4), channel_id=1, source_target_pairs={{0,4},{2,6},{4,0},{6,2},{8,12},{10,14},{12,8},{14,10},{16,20},{18,... | collective-permute-start | bytes 3145736 | tf_op jit(solution)/shard_map/ppermute | solution.py:764
  162.6 10.9 %collective-permute-start.8 = (bf16[8,64,1024]{2,1,0:T(8,128)(2,1)S(1)}, bf16[8,64,1024]{2,1,0:T(8,128)(2,1)}, u32[]{:S(2)}, u32[]{:S(2)}) collective-permute-start(bf16[8,64,1024]{2,1,0:T(8,128)(2,1)S(1)} %dynamic-slice_bitcast_fusion.3), channel_id=1, source_target_pairs={{0,2},{2,0},{4,6},{6,4},{8,10},{10,8},{12,14},{14,12},{16,18},{18,... | collective-permute-start | bytes 3145736 | tf_op jit(solution)/shard_map/ppermute | solution.py:764
  172.9 47.4 %collective-permute-start.10 = (bf16[8,64,1024]{2,1,0:T(8,128)(2,1)S(1)}, bf16[8,64,1024]{2,1,0:T(8,128)(2,1)S(1)}, u32[]{:S(2)}, u32[]{:S(2)}) collective-permute-start(bf16[8,64,1024]{2,1,0:T(8,128)(2,1)S(1)} %dynamic-slice_bitcast_fusion.2), channel_id=1, source_target_pairs={{0,2},{2,0},{4,6},{6,4},{8,10},{10,8},{12,14},{14,12},{16,18},{18,... | collective-permute-start | bytes 3145736 | tf_op jit(solution)/shard_map/ppermute | solution.py:764
  175.1 22.8 %copy-start.4 = (f32[512,768]{1,0:T(8,128)S(1)}, f32[512,768]{1,0:T(8,128)}, u32[]{:S(2)}) copy-start(f32[512,768]{1,0:T(8,128)} %copy-done.3) | copy-start | bytes 4718596
  175.1 22.8 %copy-start.7 = (f32[4,128,768]{2,1,0:T(8,128)S(1)}, f32[4,128,768]{2,1,0:T(8,128)}, u32[]{:S(2)}) copy-start(f32[4,128,768]{2,1,0:T(8,128)} %copy-done.6) | copy-start | bytes 4718596
  175.1 22.8 %copy-start.12 = (f32[768,128]{1,0:T(8,128)S(1)}, f32[768,128]{1,0:T(8,128)}, u32[]{:S(2)}) copy-start(f32[768,128]{1,0:T(8,128)} %constant.179.clone.collect_ref) | copy-start | bytes 1179652
  175.1 22.8 %copy-start.23 = (f32[1,768]{1,0:T(1,128)S(1)}, f32[1,768]{1,0:T(1,128)}, u32[]{:S(2)}) copy-start(f32[1,768]{1,0:T(1,128)} %copy-done.22) | copy-start | bytes 9220
  175.1 22.8 %copy-start.25 = (f32[1,768]{1,0:T(1,128)S(1)}, f32[1,768]{1,0:T(1,128)}, u32[]{:S(2)}) copy-start(f32[1,768]{1,0:T(1,128)} %copy-done.24) | copy-start | bytes 9220
  175.2 22.8 %copy-start.28 = (f32[256]{0:T(256)S(1)}, f32[256]{0:T(256)}, u32[]{:S(2)}) copy-start(f32[256]{0:T(256)} %copy-done.27) | copy-start | bytes 3076
  175.2 22.8 %copy-start.30 = (f32[1,128]{1,0:T(1,128)S(1)}, f32[1,128]{1,0:T(1,128)}, u32[]{:S(2)}) copy-start(f32[1,128]{1,0:T(1,128)} %copy-done.29) | copy-start | bytes 1540
  175.2 22.8 %copy-start.32 = (f32[1,128]{1,0:T(1,128)S(1)}, f32[1,128]{1,0:T(1,128)}, u32[]{:S(2)}) copy-start(f32[1,128]{1,0:T(1,128)} %copy-done.31) | copy-start | bytes 1540
  175.2 46.5 %collective-permute-start.11 = (bf16[4,64,1024]{2,1,0:T(8,128)(2,1)S(1)}, bf16[4,64,1024]{2,1,0:T(8,128)(2,1)S(1)}, u32[]{:S(2)}, u32[]{:S(2)}) collective-permute-start(bf16[4,64,1024]{2,1,0:T(8,128)(2,1)S(1)} %dynamic-slice_bitcast_fusion.9), channel_id=1, source_target_pairs={{0,4},{2,6},{4,0},{6,2},{8,12},{10,14},{12,8},{14,10},{16,20},{18,... | collective-permute-start | bytes 1572872 | tf_op jit(solution)/shard_map/ppermute | solution.py:764
  195.4 45.4 %collective-permute-start.17 = (bf16[1,64,2048]{2,1,0:T(8,128)(2,1)}, bf16[1,64,2048]{2,1,0:T(8,128)(2,1)}, u32[]{:S(2)}, u32[]{:S(2)}) collective-permute-start(bf16[1,64,2048]{2,1,0:T(8,128)(2,1)} %get-tuple-element.216), channel_id=1, source_target_pairs={{0,24},{2,26},{4,28},{6,30},{8,16},{10,18},{12,20},{14,22},{16,8},... | collective-permute-start | bytes 786440 | tf_op jit(solution)/shard_map/ppermute | solution.py:764
  197.9 42.9 %collective-permute-start.16 = (bf16[1,64,2048]{2,1,0:T(8,128)(2,1)}, bf16[1,64,2048]{2,1,0:T(8,128)(2,1)}, u32[]{:S(2)}, u32[]{:S(2)}) collective-permute-start(bf16[1,64,2048]{2,1,0:T(8,128)(2,1)} %get-tuple-element.217), channel_id=1, source_target_pairs={{0,16},{2,18},{4,20},{6,22},{8,24},{10,26},{12,28},{14,30},{16,0},... | collective-permute-start | bytes 786440 | tf_op jit(solution)/shard_map/ppermute | solution.py:764
  223.5 19.5 %copy-start.11 = (bf16[512,768]{1,0:T(8,128)(2,1)S(1)}, bf16[512,768]{1,0:T(8,128)(2,1)}, u32[]{:S(2)}) copy-start(bf16[512,768]{1,0:T(8,128)(2,1)} %copy-done.10) | copy-start | bytes 2359300
  223.5 10.8 %collective-permute-start.31 = (bf16[1,64,1024]{2,1,0:T(8,128)(2,1)}, bf16[1,64,1024]{2,1,0:T(8,128)(2,1)S(1)}, u32[]{:S(2)}, u32[]{:S(2)}) collective-permute-start(bf16[1,64,1024]{2,1,0:T(8,128)(2,1)} %get-tuple-element.225), channel_id=1, source_target_pairs={{0,24},{2,26},{4,28},{6,30},{8,16},{10,18},{12,20},{14,22},{16,8},... | collective-permute-start | bytes 393224 | tf_op jit(solution)/shard_map/ppermute | solution.py:764
  224.8 10.4 %collective-permute-start.30 = (bf16[1,64,1024]{2,1,0:T(8,128)(2,1)}, bf16[1,64,1024]{2,1,0:T(8,128)(2,1)S(1)}, u32[]{:S(2)}, u32[]{:S(2)}) collective-permute-start(bf16[1,64,1024]{2,1,0:T(8,128)(2,1)} %get-tuple-element.226), channel_id=1, source_target_pairs={{0,16},{2,18},{4,20},{6,22},{8,24},{10,26},{12,28},{14,30},{16,0},... | collective-permute-start | bytes 393224 | tf_op jit(solution)/shard_map/ppermute | solution.py:764
  226.8 8.4 %collective-permute-start.29 = (bf16[1,64,1024]{2,1,0:T(8,128)(2,1)S(1)}, bf16[1,64,1024]{2,1,0:T(8,128)(2,1)}, u32[]{:S(2)}, u32[]{:S(2)}) collective-permute-start(bf16[1,64,1024]{2,1,0:T(8,128)(2,1)S(1)} %get-tuple-element.227), channel_id=1, source_target_pairs={{0,8},{2,10},{4,12},{6,14},{8,0},{10,2},{12,4},{14,6},{16,24},{18,... | collective-permute-start | bytes 393224 | tf_op jit(solution)/shard_map/ppermute | solution.py:764
  234.2 6.7 %collective-permute-start.15 = (bf16[1,64,2048]{2,1,0:T(8,128)(2,1)}, bf16[1,64,2048]{2,1,0:T(8,128)(2,1)}, u32[]{:S(2)}, u32[]{:S(2)}) collective-permute-start(bf16[1,64,2048]{2,1,0:T(8,128)(2,1)} %get-tuple-element.218), channel_id=1, source_target_pairs={{0,8},{2,10},{4,12},{6,14},{8,0},{10,2},{12,4},{14,6},{16,24},{18,... | collective-permute-start | bytes 786440 | tf_op jit(solution)/shard_map/ppermute | solution.py:764
  236.9 127.3 %all-gather.15.cloned.1.call-start = ((), (), s32[]{:S(2)}) async-start(), calls=%async_computation.3 | async-start | bytes 2228224 | tf_op jit(solution)/shard_map/all_gather | solution.py:780
  239.3 16.5 %collective-permute-start.25 = (bf16[4,64,1024]{2,1,0:T(8,128)(2,1)}, bf16[4,64,1024]{2,1,0:T(8,128)(2,1)}, u32[]{:S(2)}, u32[]{:S(2)}) collective-permute-start(bf16[4,64,1024]{2,1,0:T(8,128)(2,1)} %dynamic-slice_bitcast_fusion.8), channel_id=1, source_target_pairs={{0,4},{2,6},{4,0},{6,2},{8,12},{10,14},{12,8},{14,10},{16,20},{18,... | collective-permute-start | bytes 1572872 | tf_op jit(solution)/shard_map/ppermute | solution.py:764
  255.8 25.3 %collective-permute-start.19 = (bf16[8,64,1280]{2,1,0:T(8,128)(2,1)}, bf16[8,64,1280]{2,1,0:T(8,128)(2,1)}, u32[]{:S(2)}, u32[]{:S(2)}) collective-permute-start(bf16[8,64,1280]{2,1,0:T(8,128)(2,1)} %dynamic-slice_bitcast_fusion.1), channel_id=1, source_target_pairs={{0,2},{2,0},{4,6},{6,4},{8,10},{10,8},{12,14},{14,12},{16,18},{18,... | collective-permute-start | bytes 3932168 | tf_op jit(solution)/shard_map/ppermute | solution.py:764
  257.9 9.1 %collective-permute-start.28 = (bf16[1,64,1024]{2,1,0:T(8,128)(2,1)S(1)}, bf16[1,64,1024]{2,1,0:T(8,128)(2,1)S(1)}, u32[]{:S(2)}, u32[]{:S(2)}) collective-permute-start(bf16[1,64,1024]{2,1,0:T(8,128)(2,1)S(1)} %get-tuple-element.223), channel_id=1, source_target_pairs={{0,24},{2,26},{4,28},{6,30},{8,16},{10,18},{12,20},{14,22},{16,8},... | collective-permute-start | bytes 393224 | tf_op jit(solution)/shard_map/ppermute | solution.py:764
  260.4 19.9 %collective-permute-start.27 = (bf16[1,64,1024]{2,1,0:T(8,128)(2,1)S(1)}, bf16[1,64,1024]{2,1,0:T(8,128)(2,1)S(1)}, u32[]{:S(2)}, u32[]{:S(2)}) collective-permute-start(bf16[1,64,1024]{2,1,0:T(8,128)(2,1)S(1)} %get-tuple-element.224), channel_id=1, source_target_pairs={{0,16},{2,18},{4,20},{6,22},{8,24},{10,26},{12,28},{14,30},{16,0},... | collective-permute-start | bytes 393224 | tf_op jit(solution)/shard_map/ppermute | solution.py:764
  260.4 19.9 %collective-permute-start.26 = (bf16[1,64,1024]{2,1,0:T(8,128)(2,1)S(1)}, bf16[1,64,1024]{2,1,0:T(8,128)(2,1)S(1)}, u32[]{:S(2)}, u32[]{:S(2)}) collective-permute-start(bf16[1,64,1024]{2,1,0:T(8,128)(2,1)S(1)} %get-tuple-element.222), channel_id=1, source_target_pairs={{0,8},{2,10},{4,12},{6,14},{8,0},{10,2},{12,4},{14,6},{16,24},{18,... | collective-permute-start | bytes 393224 | tf_op jit(solution)/shard_map/ppermute | solution.py:764
  281.1 95.3 %all-gather.13.cloned.1.call-start = ((), (), s32[]{:S(2)}) async-start(), calls=%async_computation.2 | async-start | bytes 3063808 | tf_op jit(solution)/shard_map/all_gather | solution.py:780
  283.2 14.4 %collective-permute-start.20 = (bf16[4,64,1280]{2,1,0:T(8,128)(2,1)S(1)}, bf16[4,64,1280]{2,1,0:T(8,128)(2,1)S(1)}, u32[]{:S(2)}, u32[]{:S(2)}) collective-permute-start(bf16[4,64,1280]{2,1,0:T(8,128)(2,1)S(1)} %dynamic-slice_bitcast_fusion.6), channel_id=1, source_target_pairs={{0,4},{2,6},{4,0},{6,2},{8,12},{10,14},{12,8},{14,10},{16,20},{18,... | collective-permute-start | bytes 1966088 | tf_op jit(solution)/shard_map/ppermute | solution.py:764
  297.8 10.7 %collective-permute-start.23 = (bf16[1,64,1280]{2,1,0:T(8,128)(2,1)S(1)}, bf16[1,64,1280]{2,1,0:T(8,128)(2,1)S(1)}, u32[]{:S(2)}, u32[]{:S(2)}) collective-permute-start(bf16[1,64,1280]{2,1,0:T(8,128)(2,1)S(1)} %get-tuple-element.220), channel_id=1, source_target_pairs={{0,24},{2,26},{4,28},{6,30},{8,16},{10,18},{12,20},{14,22},{16,8},... | collective-permute-start | bytes 491528 | tf_op jit(solution)/shard_map/ppermute | solution.py:764
  303.4 13.3 %collective-permute-start.22 = (bf16[1,64,1280]{2,1,0:T(8,128)(2,1)S(1)}, bf16[1,64,1280]{2,1,0:T(8,128)(2,1)S(1)}, u32[]{:S(2)}, u32[]{:S(2)}) collective-permute-start(bf16[1,64,1280]{2,1,0:T(8,128)(2,1)S(1)} %get-tuple-element.221), channel_id=1, source_target_pairs={{0,16},{2,18},{4,20},{6,22},{8,24},{10,26},{12,28},{14,30},{16,0},... | collective-permute-start | bytes 491528 | tf_op jit(solution)/shard_map/ppermute | solution.py:764
  303.4 13.3 %collective-permute-start.21 = (bf16[1,64,1280]{2,1,0:T(8,128)(2,1)S(1)}, bf16[1,64,1280]{2,1,0:T(8,128)(2,1)S(1)}, u32[]{:S(2)}, u32[]{:S(2)}) collective-permute-start(bf16[1,64,1280]{2,1,0:T(8,128)(2,1)S(1)} %get-tuple-element.219), channel_id=1, source_target_pairs={{0,8},{2,10},{4,12},{6,14},{8,0},{10,2},{12,4},{14,6},{16,24},{18,... | collective-permute-start | bytes 491528 | tf_op jit(solution)/shard_map/ppermute | solution.py:764
  316.8 4.3 collective-permute-start.24
  322.0 105.3 %all-gather.9.cloned.1.call-start = ((), (), s32[]{:S(2)}) async-start(), calls=%async_computation | async-start | bytes 4456448 | tf_op jit(solution)/shard_map/all_gather | solution.py:780
  328.9 23.7 %copy-start.89 = (f32[1024]{0:T(1024)S(1)}, f32[1024]{0:T(1024)}, u32[]{:S(2)}) copy-start(f32[1024]{0:T(1024)} %copy-done.88) | copy-start | bytes 12292
  328.9 15.2 %collective-permute-start.6 = (bf16[256,1024]{1,0:T(8,128)(2,1)}, bf16[256,1024]{1,0:T(8,128)(2,1)}, u32[]{:S(2)}, u32[]{:S(2)}) collective-permute-start(bf16[256,1024]{1,0:T(8,128)(2,1)} %dynamic-slice_bitcast_fusion.10), channel_id=1, source_target_pairs={{0,1},{1,0},{2,3},{3,2},{4,5},{5,4},{6,7},{7,6},{8,9},{9,8},{10,11... | collective-permute-start | bytes 1572872 | tf_op jit(solution)/shard_map/ppermute | solution.py:785
  330.6 22.0 %collective-permute-start.18 = (bf16[256,1024]{1,0:T(8,128)(2,1)}, bf16[256,1024]{1,0:T(8,128)(2,1)}, u32[]{:S(2)}, u32[]{:S(2)}) collective-permute-start(bf16[256,1024]{1,0:T(8,128)(2,1)} %dynamic-slice_bitcast_fusion.7), channel_id=1, source_target_pairs={{0,1},{1,0},{2,3},{3,2},{4,5},{5,4},{6,7},{7,6},{8,9},{9,8},{10,11... | collective-permute-start | bytes 1572872 | tf_op jit(solution)/shard_map/ppermute | solution.py:785
  331.7 20.8 %copy-start.70 = (f32[512,1024]{1,0:T(8,128)S(1)}, f32[512,1024]{1,0:T(8,128)}, u32[]{:S(2)}) copy-start(f32[512,1024]{1,0:T(8,128)} %get-tuple-element.215) | copy-start | bytes 6291460
  331.8 22.1 %copy-start.49 = (f32[512,1024]{1,0:T(8,128)S(1)}, f32[512,1024]{1,0:T(8,128)}, u32[]{:S(2)}) copy-start(f32[512,1024]{1,0:T(8,128)} %copy-done.48) | copy-start | bytes 6291460
  (78 other events, 216.5 us)
Sparse Core Ops, SparseCore 0:
  150.1 45.3 all-gather.10
  237.1 44.4 all-gather.16
  284.3 46.1 all-gather.14
  333.2 43.1 all-gather.12
  378.4 48.8 all-gather.8

commit v5 on v4

--- a/solution.py
+++ b/solution.py
@@ -43,6 +43,7 @@
 
 LANES = 128
 VMEM_LIMIT = 44 * 1024 * 1024
+LIGHT = pl.CostEstimate(flops=1024, bytes_accessed=1024, transcendentals=0)
 
 
 def exact_dot(left, right):
@@ -205,6 +206,9 @@
 
 
 def ssd_backward_kernel(
+    head_from,
+    begun,
+    ended,
     input_ref,
     state_ref,
     gate_ref,
@@ -220,23 +224,26 @@
     skip_ref,
     expand_ref,
     collect_ref,
-    grad_input_ref,
-    grad_state_ref,
-    grad_step_ref,
-    grad_input_conv_ref,
-    grad_state_conv_ref,
-    grad_head_ref,
-    act_ref,
-    slope_ref,
-    both_ref,
-    both_slope_ref,
-    held_ref,
-    wide_ref,
-    turned_ref,
-    column_ref,
-    skip_sum_ref,
-    scale_sum_ref,
+    *rest,
 ):
+    begun_ref, rest = (rest[0], rest[1:]) if begun else (None, rest)
+    grad_input_ref, grad_step_ref, grad_input_conv_ref, grad_head_ref = rest[:4]
+    if ended:
+        grad_state_ref, grad_state_conv_ref = rest[4:6]
+    else:
+        partial_ref = rest[4]
+    (
+        act_ref,
+        slope_ref,
+        both_ref,
+        both_slope_ref,
+        held_ref,
+        wide_ref,
+        turned_ref,
+        column_ref,
+        skip_sum_ref,
+        scale_sum_ref,
+    ) = rest[-10:]
     channels = input_ref.shape[1]
     states = state_ref.shape[1] // 2
     taps = input_kernel_ref.shape[0]
@@ -288,7 +295,7 @@
             products = low_against(scaled, stacked_up)
             weights = []
             for place in range(heads):
-                head = start // HD + place
+                head = head_from + start // HD + place
                 spread = cumul_turned[head : head + 1, :] - cumul[:, head : head + 1]
                 decay = jnp.exp(jnp.where(upper, spread, -jnp.inf))
                 product = products[:, place * SPAN : (place + 1) * SPAN] * decay
@@ -331,8 +338,14 @@
         grad_head_ref[0, 1:2, :] += (
             jnp.sum(grad_log * steps, axis=0, keepdims=True) * rate_ref[...]
         )
-        both_ref[rows, pl.ds(0, states)] = grad_entry + low_dot(grad_cross, readout)
-        both_ref[rows, pl.ds(states, states)] = grad_readout + low_inner(grad_cross, entry)
+        grad_entry = grad_entry + low_dot(grad_cross, readout)
+        grad_readout = grad_readout + low_inner(grad_cross, entry)
+        if begun:
+            grad_entry = grad_entry + begun_ref[rows, pl.ds(0, states)]
+            grad_readout = grad_readout + begun_ref[rows, pl.ds(states, states)]
+        target_ref = both_ref if ended else partial_ref
+        target_ref[rows, pl.ds(0, states)] = grad_entry
+        target_ref[rows, pl.ds(states, states)] = grad_readout
         return unused
 
     lax.fori_loop(0, chunks, chunk, 0)
@@ -363,15 +376,16 @@
         grad_input_conv_ref,
         channels,
     )
-    convolve_back(
-        state_ref,
-        both_ref,
-        both_slope_ref,
-        state_kernel_ref,
-        grad_state_ref,
-        grad_state_conv_ref,
-        2 * states,
-    )
+    if ended:
+        convolve_back(
+            state_ref,
+            both_ref,
+            both_slope_ref,
+            state_kernel_ref,
+            grad_state_ref,
+            grad_state_conv_ref,
+            2 * states,
+        )
 
 
 def by_sequence(length, width):
@@ -446,76 +460,87 @@
             pltpu.VMEM((states, channels), jnp.float32),
         ],
         compiler_params=pltpu.CompilerParams(vmem_limit_bytes=VMEM_LIMIT),
-        cost_estimate=pl.CostEstimate(
-            flops=8 * group * channels * SPAN,
-            bytes_accessed=20 * group * channels,
-            transcendentals=group * heads * SPAN,
-        ),
+        cost_estimate=LIGHT,
         name="ssd_forward",
     )(inputs, states_raw, gate, step, *small, jnp.asarray(head_spread(heads)))
 
 
-def ssd_backward(inputs, states_raw, gate, step, grad, carry, small, heads, length):
+def ssd_backward(
+    inputs, states_raw, gate, step, grad, carry, small, heads, length, index, count, begun
+):
     group, channels = inputs.shape
+    here = channels // count
     seqs = group // length
     both = states_raw.shape[1]
     states = both // 2
     chunks = length // SPAN
     taps = small[0].shape[0]
+    ended = index == count - 1
+    columns = pl.BlockSpec((length, here), lambda seq: (seq, index))
+
+    def part(rows):
+        return pl.BlockSpec((rows, here), lambda seq: (0, index))
+
+    in_specs = [
+        columns,
+        by_sequence(length, both),
+        columns,
+        by_sequence(length, LANES),
+        columns,
+        pl.BlockSpec((chunks, states, here), lambda seq: (seq, 0, index)),
+        part(taps),
+        part(1),
+        fixed(taps, both),
+        fixed(1, both),
+        fixed(1, LANES),
+        fixed(1, LANES),
+        part(1),
+        part(LANES),
+        pl.BlockSpec((here, LANES), lambda seq: (index, 0)),
+    ]
+    out_specs = [
+        by_sequence(length, here),
+        by_sequence(length, LANES),
+        pl.BlockSpec((1, 8, here), lambda seq: (seq, 0, 0)),
+        pl.BlockSpec((1, 8, LANES), lambda seq: (seq, 0, 0)),
+    ]
+    out_shape = [
+        jax.ShapeDtypeStruct((group, here), jnp.bfloat16),
+        jax.ShapeDtypeStruct((group, LANES), jnp.bfloat16),
+        jax.ShapeDtypeStruct((seqs, 8, here), jnp.float32),
+        jax.ShapeDtypeStruct((seqs, 8, LANES), jnp.float32),
+    ]
+    out_specs.append(by_sequence(length, both))
+    if ended:
+        out_shape.append(jax.ShapeDtypeStruct((group, both), jnp.bfloat16))
+        out_specs.append(pl.BlockSpec((1, 8, both), lambda seq: (seq, 0, 0)))
+        out_shape.append(jax.ShapeDtypeStruct((seqs, 8, both), jnp.float32))
+    else:
+        out_shape.append(jax.ShapeDtypeStruct((group, both), jnp.float32))
+    extra = ()
+    if begun is not None:
+        in_specs.append(by_sequence(length, both))
+        extra = (begun,)
     return pl.pallas_call(
-        ssd_backward_kernel,
+        partial(ssd_backward_kernel, index * (heads // count), begun is not None, ended),
         grid=(seqs,),
-        in_specs=[
-            by_sequence(length, channels),
-            by_sequence(length, both),
-            by_sequence(length, channels),
-            by_sequence(length, LANES),
-            by_sequence(length, channels),
-            pl.BlockSpec((chunks, states, channels), lambda seq: (seq, 0, 0)),
-            fixed(taps, channels),
-            fixed(1, channels),
-            fixed(taps, both),
-            fixed(1, both),
-            fixed(1, LANES),
-            fixed(1, LANES),
-            fixed(1, channels),
-            fixed(LANES, channels),
-            fixed(channels, LANES),
-        ],
-        out_specs=[
-            by_sequence(length, channels),
-            by_sequence(length, both),
-            by_sequence(length, LANES),
-            pl.BlockSpec((1, 8, channels), lambda seq: (seq, 0, 0)),
-            pl.BlockSpec((1, 8, both), lambda seq: (seq, 0, 0)),
-            pl.BlockSpec((1, 8, LANES), lambda seq: (seq, 0, 0)),
-        ],
-        out_shape=[
-            jax.ShapeDtypeStruct((group, channels), jnp.bfloat16),
-            jax.ShapeDtypeStruct((group, both), jnp.bfloat16),
-            jax.ShapeDtypeStruct((group, LANES), jnp.bfloat16),
-            jax.ShapeDtypeStruct((seqs, 8, channels), jnp.float32),
-            jax.ShapeDtypeStruct((seqs, 8, both), jnp.float32),
-            jax.ShapeDtypeStruct((seqs, 8, LANES), jnp.float32),
-        ],
+        in_specs=in_specs,
+        out_specs=out_specs,
+        out_shape=out_shape,
         scratch_shapes=[
-            pltpu.VMEM((length, channels), jnp.float32),
-            pltpu.VMEM((length, channels), jnp.float32),
+            pltpu.VMEM((length, here), jnp.float32),
+            pltpu.VMEM((length, here), jnp.float32),
             pltpu.VMEM((length, both), jnp.float32),
             pltpu.VMEM((length, both), jnp.float32),
-            pltpu.VMEM((states, channels), jnp.float32),
-            pltpu.VMEM((3, SPAN, channels), jnp.float32),
+            pltpu.VMEM((states, here), jnp.float32),
+            pltpu.VMEM((3, SPAN, here), jnp.float32),
             pltpu.VMEM((LANES, SPAN), jnp.float32),
             pltpu.VMEM((SPAN, LANES), jnp.float32),
-            pltpu.VMEM((1, channels), jnp.float32),
-            pltpu.VMEM((1, channels), jnp.float32),
+            pltpu.VMEM((1, here), jnp.float32),
+            pltpu.VMEM((1, here), jnp.float32),
         ],
         compiler_params=pltpu.CompilerParams(vmem_limit_bytes=VMEM_LIMIT),
-        cost_estimate=pl.CostEstimate(
-            flops=20 * group * channels * SPAN,
-            bytes_accessed=20 * group * channels,
-            transcendentals=group * heads * SPAN,
-        ),
+        cost_estimate=LIGHT,
         name="ssd_backward",
     )(
         inputs,
@@ -527,6 +552,7 @@
         *small,
         jnp.asarray(head_spread(heads)),
         jnp.asarray(head_spread(heads).T.copy()),
+        *extra,
     )
 
 
@@ -673,11 +699,7 @@
             jax.ShapeDtypeStruct((group, LANES), jnp.float32),
         ],
         compiler_params=pltpu.CompilerParams(vmem_limit_bytes=VMEM_LIMIT),
-        cost_estimate=pl.CostEstimate(
-            flops=4 * group * width * length,
-            bytes_accessed=12 * group * width,
-            transcendentals=group * heads * length // 2,
-        ),
+        cost_estimate=LIGHT,
         name="attend_forward",
     )(query, pair, jnp.asarray(cosine), jnp.asarray(sine))
 
@@ -707,11 +729,7 @@
             pltpu.VMEM((length, LANES), jnp.float32),
         ],
         compiler_params=pltpu.CompilerParams(vmem_limit_bytes=VMEM_LIMIT),
-        cost_estimate=pl.CostEstimate(
-            flops=10 * group * width * length,
-            bytes_accessed=12 * group * width,
-            transcendentals=group * heads * length // 2,
-        ),
+        cost_estimate=LIGHT,
         name="attend_backward",
     )(query, pair, total, grad, jnp.asarray(cosine), jnp.asarray(sine))
 
@@ -731,9 +749,8 @@
 
 
 class Sum:
-    def __init__(self, part, size, place):
+    def __init__(self, part, size):
         self.size = size
-        self.place = place
         self.direct = bool(size & (size - 1) or part.shape[0] % size)
         self.steps = [] if self.direct else step_groups(size)
         self.shift = 0
@@ -756,9 +773,9 @@
             lax.dynamic_index_in_dim(view, mine ^ way, 1, False) for way in range(1, ways)
         ]
 
-    def advance(self):
+    def advance(self, *deps):
         if self.steps:
-            total = self.keep.astype(jnp.float32)
+            total = after(self.keep, *deps).astype(jnp.float32)
             for way, give in enumerate(self.gives, 1):
                 pairs = [(index, index ^ (way << self.shift)) for index in range(self.size)]
                 total = total + lax.ppermute(give, "dp", pairs).astype(jnp.float32)
@@ -767,18 +784,49 @@
             self.prepare()
         return self.gives
 
-    def finish(self, middle=None):
+    def joined(self, middle=None):
+        groups, shift = step_groups(self.size), self.size.bit_length() - 1
+        part = self.reduced()
+        if middle is not None:
+            part = middle(part)
+        if self.direct:
+            return part
+        rows, width = part.shape
+        for group in reversed(groups):
+            ways = 1 << group
+            shift -= group
+            mine = (lax.axis_index("dp") >> shift) & (ways - 1)
+            part = part.reshape(-1, 1, rows, width)
+            got = [part]
+            for way in range(1, ways):
+                pairs = [(index, index ^ (way << shift)) for index in range(self.size)]
+                got.append(lax.ppermute(part, "dp", pairs))
+            for bit in range(group):
+                flip = ((mine >> bit) & 1) == 1
+                got = [
+                    jnp.where(flip, got[way ^ (1 << bit)], got[way]) for way in range(ways)
+                ]
+            part = jnp.concatenate(got, axis=1)
+        return part.reshape(-1, width)
+
+    def reduced(self):
         while self.steps:
             self.advance()
-        if self.direct:
-            part = lax.psum(self.part, "dp")
-            return part if middle is None else middle(part)
-        part = self.part[0]
-        if middle is not None:
-            part = middle(part)
-        lead = (1,) * (self.place + 1)
-        whole = lax.all_gather(part.reshape(lead + part.shape), "dp", axis=self.place, tiled=True)
-        return whole.reshape(self.size * part.shape[0], part.shape[1])
+        return lax.psum(self.part, "dp") if self.direct else self.part[0]
+
+
+def gather_dp(parts, direct, size, place):
+    widths = [part.shape[1] for part in parts]
+    part = jnp.concatenate(parts, axis=1) if len(parts) > 1 else parts[0]
+    if not direct:
+        lead = (1,) * (place + 1)
+        part = lax.all_gather(part.reshape(lead + part.shape), "dp", axis=place, tiled=True)
+        part = part.reshape(size * part.shape[-2], part.shape[-1])
+    out, start = [], 0
+    for width in widths:
+        out.append(part[:, start : start + width])
+        start += width
+    return out
 
 
 def other(part):
@@ -922,21 +970,23 @@
         jnp.bfloat16
     )
     back_mid = sum_all(back_part, shards)
-    hidden_late = after(hidden, back_part)
-    mid_late = after(whole_mid, back_part)
-    down_sum = Sum(inner_rows(hidden_late, cotan_low).astype(jnp.bfloat16), dp_size, 0)
+    hidden, grad_gate_low, grad_upper_low = (
+        after(hidden, back_part),
+        after(grad_gate_low, back_part),
+        after(grad_upper_low, back_part),
+    )
+    down_sum = Sum(inner_rows(hidden, cotan_low).astype(jnp.bfloat16), dp_size)
     hidden_cols = gate_weight.shape[1]
     wide_sum = Sum(
-        inner_rows(mid_late, jnp.concatenate([grad_gate_low, grad_upper_low], axis=1)).astype(
+        inner_rows(whole_mid, jnp.concatenate([grad_gate_low, grad_upper_low], axis=1)).astype(
             jnp.bfloat16
         ),
         dp_size,
-        0,
     )
     down_sum.advance()
     wide_sum.advance()
     back_mid = after(back_mid, *down_sum.gives, *wide_sum.gives)
-    feed_part = behind(forward_dot(hidden_late, down_weight), back_mid).astype(jnp.bfloat16)
+    feed_part = behind(forward_dot(hidden, down_weight), back_mid).astype(jnp.bfloat16)
     feed = sum_own(feed_part, shards)
     layer_output = (own_rows(resid, own) + feed).astype(jnp.bfloat16)
     grad_middle = jnp.sum(back_part.astype(jnp.float32) * normal_second, axis=0)
@@ -949,7 +999,6 @@
             jnp.bfloat16
         ),
         dp_size,
-        1,
     )
     ssm_rows = gated_low.shape[1]
     grad_gated = against(mixer_all, mamba_output)
@@ -962,32 +1011,55 @@
         queries,
         pairs,
         totals,
-        after(jnp.pad(grad_context, ((0, 0), (0, query_pad))), *mixer_sum.gives, *down_sum.advance()),
+        after(jnp.pad(grad_context, ((0, 0), (0, query_pad))), *mixer_sum.gives),
         length,
     )
     grad_query_raw = grad_query_raw[:, :query_cols]
     early_cols = jnp.concatenate([grad_gate_raw, grad_query_raw], axis=1)
-    early_sum = Sum(inner_rows(whole, early_cols).astype(jnp.bfloat16), dp_size, 2)
+    early_sum = Sum(inner_rows(whole, early_cols).astype(jnp.bfloat16), dp_size)
     grad_gated = after(
-        grad_gated, *early_sum.gives, *mixer_sum.advance(), *wide_sum.advance()
-    )
-    grad_input_raw, grad_state_raw, grad_step_raw, input_sums, state_sums, head_sums = ssd_backward(
-        input_raw, state_raw, gate_raw, step_raw, grad_gated, carries, small, heads, length
-    )
-    input_sums = jnp.sum(input_sums, axis=0)
+        grad_gated,
+        *early_sum.gives,
+        *mixer_sum.advance(early_sum.gives[0]),
+        *down_sum.advance(early_sum.gives[0]),
+    )
+    parts = 2 if heads % 4 == 0 else 1
+    begun = None
+    input_pieces, step_pieces, conv_pieces, head_pieces = [], [], [], []
+    for index in range(parts):
+        piece = ssd_backward(
+            input_raw,
+            state_raw,
+            gate_raw,
+            step_raw,
+            grad_gated,
+            carries,
+            small,
+            heads,
+            length,
+            index,
+            parts,
+            begun,
+        )
+        begun = piece[4]
+        input_pieces.append(piece[0])
+        step_pieces.append(piece[1])
+        conv_pieces.append(jnp.sum(piece[2], axis=0))
+        head_pieces.append(jnp.sum(piece[3], axis=0))
+        if index == 0:
+            begun = after(
+                begun,
+                *wide_sum.advance(piece[1]),
+                *early_sum.advance(piece[1]),
+                *down_sum.advance(piece[1]),
+            )
+    grad_state_raw, state_sums = piece[4:]
+    grad_input_raw = jnp.concatenate(input_pieces, axis=1)
+    grad_step_raw = sum(step_pieces[1:], step_pieces[0])
+    input_sums = jnp.concatenate(conv_pieces, axis=1)
     state_sums = jnp.sum(state_sums, axis=0)
-    head_sums = jnp.sum(head_sums, axis=0)[:, :heads]
+    head_sums = sum(head_pieces[1:], head_pieces[0])[:, :heads]
     taps = input_kernel.shape[0]
-    early_sum.advance()
-    mixer_sum.advance()
-    down_sum.advance()
-    wide_sum.advance()
-    grad_input_raw = after(
-        grad_input_raw, *early_sum.gives, *mixer_sum.gives, *down_sum.gives, *wide_sum.gives
-    )
-    grad_down = down_sum.finish()
-    grad_wide = wide_sum.finish()
-    grad_gate, grad_up = grad_wide[:, :hidden_cols], grad_wide[:, hidden_cols:]
     late_cols = jnp.concatenate(
         [grad_input_raw, grad_state_raw, grad_pair_raw, grad_step_raw], axis=1
     )
@@ -1027,7 +1099,7 @@
         late = jnp.concatenate([late[:, : marks[1]], late_pair, late[:, marks[2] :]], axis=1)
     misc = late.shape[1] - LANES
     late = (late + jnp.pad(packs, ((0, 0), (misc, 0)))).astype(jnp.bfloat16)
-    late_sum = Sum(late, dp_size, 3)
+    late_sum = Sum(late, dp_size)
 
     def over_tensor(part):
         own_part = part[:, input_cols:]
@@ -1050,11 +1122,23 @@
             [part[:, :input_cols], both[:, :state_cols]] + pair + [extra], axis=1
         )
 
-    grad_mixer_out = mixer_sum.finish()
+    queue = late_sum.gives[0]
+    mixer_sum.advance(queue)
+    wide_sum.advance(queue)
+    early_sum.advance(queue)
+    sums = [wide_sum, down_sum, mixer_sum, early_sum]
+    blocks = [item.reduced() for item in sums]
+    if len({block.shape[0] for block in blocks}) == 1:
+        wholes = gather_dp(blocks, wide_sum.direct, dp_size, 0)
+    else:
+        wholes = [
+            gather_dp([block], item.direct, dp_size, 0)[0] for item, block in zip(sums, blocks)
+        ]
+    grad_wide, grad_down, grad_mixer_out, early = wholes
+    grad_gate, grad_up = grad_wide[:, :hidden_cols], grad_wide[:, hidden_cols:]
+    tail = late_sum.joined(over_tensor)
     grad_mamba_out = grad_mixer_out[:ssm_rows]
     grad_context_w = grad_mixer_out[ssm_rows:]
-    early = early_sum.finish()
-    tail = late_sum.finish(over_tensor)
     grad_mamba_input = tail[:, :input_cols]
     tail = tail[:, input_cols:]
     back_in = sum_own(total_low, shards)

time: 448 us -> 439 us (0.980)
  the two profiles are of different devices: /device:TPU:0 before, /device:TPU:20 now
where the time goes in v5:
time: 439 us; the launch traced here: 432 us
  waiting for transfers between devices  176 us (40%)
  other arithmetic  69.2 us (16%)
  local copies, waits for them, and re-layouts  48.1 us (11%)
  Pallas kernels  45.6 us (10%)
  starting transfers between devices  41.8 us (10%)
  matrix products  34.5 us (8%)
  between operations  16.5 us (4%)
    ppermute x7, waiting for transfers between devices, other(): return lax.ppermute(part, 'tensor', [(0, 1), (1, 0)])  70.9 us
    ppermute x25, waiting for transfers between devices, advance(): total = total + lax.ppermute(give, 'dp', pairs).astype(jnp.float32)  58 us
    ppermute x5, waiting for transfers between devices, joined(): got.append(lax.ppermute(part, 'dp', pairs))  47.3 us
    ppermute x25, starting transfers between devices, advance(): total = total + lax.ppermute(give, 'dp', pairs).astype(jnp.float32)  30.6 us
    pallas_call x2, Pallas kernels, ssd_backward(): pl.pallas_call(partial(ssd_backward_kernel, index * (heads // count), beg...  24.9 us
    convert_element_type x13, other arithmetic, body(): item.astype(jnp.float32)  24.4 us
    unnamed x207, local copies, waits for them, and re-layouts  19.9 us
    dot_general x7, matrix products, against(): lax.dot_general(left, right, (((1,), (1,)), ((), ())), preferred_element_...  13.6 us
  transfers between devices with their start and end apart: 38, of which 20 were waited for; matrix products, arithmetic and copies ran while one was open for 22% of the time, Pallas kernels for 7%

profile of v5, /device:TPU:20, one launch (start us, length us, event | category | flops | bytes accessed | tf_op | source)
XLA Modules:
  0.0 431.8 jit_solution(2214227166856411353)
XLA Ops:
  16.2 6.1 %collective-permute-done = bf16[256,1024]{1,0:T(8,128)(2,1)S(1)} collective-permute-done((bf16[256,1024]{1,0:T(8,128)(2,1)}, bf16[256,1024]{1,0:T(8,128)(2,1)S(1)}, u32[]{:S(2)}, u32[]{:S(2)}) %collective-permute-start) | collective-permute-done | bytes 524320 | tf_op jit(solution)/shard_map/ppermute | solution.py:833
  22.4 1.8 fusion.2
  26.5 6.0 %collective-permute-done.1 = bf16[256,1024]{1,0:T(8,128)(2,1)} collective-permute-done((bf16[256,1024]{1,0:T(8,128)(2,1)}, bf16[256,1024]{1,0:T(8,128)(2,1)}, u32[]{:S(2)}, u32[]{:S(2)}) %collective-permute-start.1) | collective-permute-done | bytes 524320 | tf_op jit(solution)/shard_map/ppermute | solution.py:833
  32.5 2.6 maximum_select_fusion.1
  38.9 8.7 %ssd_forward.1 = (bf16[512,768]{1,0:T(8,128)(2,1)S(1)}, f32[512,768]{1,0:T(8,128)S(1)}, f32[4,128,768]{2,1,0:T(8,128)S(1)}) custom-call(f32[512,768]{1,0:T(8,128)S(1)} %fusion.44.input_ref, f32[512,256]{1,0:T(8,128)S(1)} %fusion.45.state_ref, f32[512,768]{1,0:T(8,128)S(1)} %fusion.46.gate_ref, f32[512,128]{1,0:T(8,128)S(1)} %fusion.27.step_ref, ...), custom_call_target="tpu_custom_call" | custom-call | flops 1024 | bytes 1024 | tf_op jit(solution)/shard_map/ssd_forward/pallas_call | solution.py:430
  49.5 5.7 %attend_forward.1 = (bf16[512,256]{1,0:T(8,128)(2,1)S(1)}, bf16[512,256]{1,0:T(8,128)(2,1)S(1)}, bf16[512,128]{1,0:T(8,128)(2,1)S(1)}, f32[512,128]{1,0:T(8,128)S(1)}) custom-call(f32[512,256]{1,0:T(8,128)S(1)} %fusion.48.query_ref, f32[512,128]{1,0:T(8,128)S(1)} %fusion.20.pair_ref, f32[512,128]{1,0:T(8,128)S(1)} %copy-done.12, f32[512,128]{1,0:T(8,128)S(1)} %copy-done.11), custom_call_target="tpu_custom_call" | custom-call | flops 1024 | bytes 1024 | tf_op jit(solution)/shard_map/attend_forward/pallas_call | solution.py:680
  60.5 22.6 %collective-permute-done.2 = bf16[512,1024]{1,0:T(8,128)(2,1)} collective-permute-done((bf16[512,1024]{1,0:T(8,128)(2,1)}, bf16[512,1024]{1,0:T(8,128)(2,1)}, u32[]{:S(2)}, u32[]{:S(2)}) %collective-permute-start.2) | collective-permute-done | bytes 1048608 | tf_op jit(solution)/shard_map/ppermute | solution.py:833
  83.1 2.9 multiply_reduce_fusion.2
  86.3 2.1 copy-done.94
  91.2 2.1 multiply_convert_fusion
  94.6 2.3 add_convert_fusion.8
  96.9 2.8 convolution_convert_fusion
  99.7 2.5 dynamic-slice_bitcast_fusion.1
  106.1 1.6 copy.86
  107.7 1.7 pad.29.clone
  109.4 5.1 %concatenate.71 = bf16[1024,1280]{1,0:T(8,128)(2,1)} concatenate(bf16[1024,768]{1,0:T(8,128)(2,1)} %param.35, bf16[1024,256]{1,0:T(8,128)(2,1)} %param.37, bf16[1024,64]{1,0:T(8,128)(2,1)} %copy-done.64, bf16[1024,64]{1,0:T(8,128)(2,1)} %copy-done.65, bf16[1024,128]{1,0:T(8,128)(2,1)} %pad.29.clone), dimensions={1} | concatenate | bytes 5242880 | tf_op jit(solution)/shard_map/concatenate | solution.py:1068
  114.5 1.9 add_convert_fusion.7
  118.9 12.1 %collective-permute-done.3 = bf16[512,1024]{1,0:T(8,128)(2,1)} collective-permute-done((bf16[512,1024]{1,0:T(8,128)(2,1)}, bf16[512,1024]{1,0:T(8,128)(2,1)}, u32[]{:S(2)}, u32[]{:S(2)}) %collective-permute-start.3) | collective-permute-done | bytes 1048608 | tf_op jit(solution)/shard_map/ppermute | solution.py:833
  131.0 1.9 convert_add_fusion.1
  132.9 3.1 add_convert_fusion
  137.9 2.5 fusion.1
  149.5 6.3 %attend_backward.1 = (bf16[512,256]{1,0:T(8,128)(2,1)S(1)}, bf16[512,128]{1,0:T(8,128)(2,1)S(1)}) custom-call(bf16[512,256]{1,0:T(8,128)(2,1)S(1)} %copy-done.17, bf16[512,128]{1,0:T(8,128)(2,1)S(1)} %copy-done.29, f32[512,128]{1,0:T(8,128)S(1)} %copy-done.19, bf16[512,256]{1,0:T(8,128)(2,1)S(1)} %convolution_convert_fusion.4.grad_ref, ...), custom_call_target="tpu_custom_call" | custom-call | flops 1024 | bytes 1024 | tf_op jit(solution)/shard_map/attend_backward/pallas_call | solution.py:711
  159.5 3.5 collective-permute-start.12
  163.1 1.8 add_convert_fusion.5
  166.0 11.9 %ssd_backward.2 = (bf16[512,384]{1,0:T(8,128)(2,1)S(1)}, bf16[512,128]{1,0:T(8,128)(2,1)S(1)}, f32[1,8,384]{2,1,0:T(8,128)S(1)}, f32[1,8,128]{2,1,0:T(8,128)S(1)}, f32[512,256]{1,0:T(8,128)S(1)}) custom-call(f32[512,768]{1,0:T(8,128)S(1)} %copy-done.4, f32[512,256]{1,0:T(8,128)S(1)} %fusion.45.state_ref, f32[512,768]{1,0:T(8,128)S(1)} %copy-done.2, ...), custom_call_target="tpu_custom_call" | custom-call | flops 1024 | bytes 1024 | tf_op jit(solution)/shard_map/ssd_backward/pallas_call | solution.py:524
  182.9 13.0 %ssd_backward.3 = (bf16[512,384]{1,0:T(8,128)(2,1)S(1)}, bf16[512,128]{1,0:T(8,128)(2,1)S(1)}, f32[1,8,384]{2,1,0:T(8,128)S(1)}, f32[1,8,128]{2,1,0:T(8,128)S(1)...) custom-call(f32[512,768]{1,0:T(8,128)S(1)} %copy-done.4, f32[512,256]{1,0:T(8,128)S(1)} %fusion.45.state_ref, ...), custom_call_target="tpu_custom_call" | custom-call | flops 1024 | bytes 1024 | tf_op jit(solution)/shard_map/ssd_backward/pallas_call | solution.py:524
  197.8 3.8 collective-permute-start.27
  206.0 3.4 fusion.52
  209.5 3.1 multiply_reduce_fusion
  213.6 3.0 fusion
  218.2 2.2 collective-permute-done.27
  223.0 1.7 collective-permute-start.32
  224.7 4.3 collective-permute-start.31
  230.9 3.8 collective-permute-start.35
  234.9 6.0 %collective-permute-done.31 = bf16[1,64,1024]{2,1,0:T(8,128)(2,1)S(1)} collective-permute-done((bf16[1,64,1024]{2,1,0:T(8,128)(2,1)S(1)}, bf16[1,64,1024]{2,1,0:T(8,128)(2,1)S(1)}, u32[]{:S(2)}, u32[]{:S(2)}) %collective-permute-start.31) | collective-permute-done | bytes 131104 | tf_op jit(solution)/shard_map/ppermute | solution.py:781
  241.0 4.3 collective-permute-done.36
  245.2 1.6 collective-permute-done.35
  247.9 3.2 collective-permute-done.15
  252.4 23.0 %collective-permute-done.16 = bf16[4,64,1280]{2,1,0:T(8,128)(2,1)S(1)} collective-permute-done((bf16[4,64,1280]{2,1,0:T(8,128)(2,1)S(1)}, bf16[4,64,1280]{2,1,0:T(8,128)(2,1)S(1)}, u32[]{:S(2)}, u32[]{:S(2)}) %collective-permute-start.16) | collective-permute-done | bytes 655392 | tf_op jit(solution)/shard_map/ppermute | solution.py:781
  276.4 4.3 collective-permute-start.18
  280.7 15.1 %collective-permute-done.19 = bf16[1,64,1280]{2,1,0:T(8,128)(2,1)S(1)} collective-permute-done((bf16[1,64,1280]{2,1,0:T(8,128)(2,1)S(1)}, bf16[1,64,1280]{2,1,0:T(8,128)(2,1)S(1)}, u32[]{:S(2)}, u32[]{:S(2)}) %collective-permute-start.19) | collective-permute-done | bytes 163872 | tf_op jit(solution)/shard_map/ppermute | solution.py:781
  295.8 2.2 collective-permute-done.18
  298.8 3.7 collective-permute-done.20
  302.7 2.5 collective-permute-start.23
  306.8 13.7 %collective-permute-done.23 = bf16[1,1,64,1408]{3,2,1,0:T(8,128)(2,1)S(1)} collective-permute-done((bf16[1,1,64,1408]{3,2,1,0:T(8,128)(2,1)S(1)}, bf16[1,1,64,1408]{3,2,1,0:T(8,128)(2,1)S(1)}, u32[]{:S(2)}, u32[]{:S(2)}) %collective-permute-start.23) | collective-permute-done | bytes 180256 | tf_op jit(solution)/shard_map/ppermute | solution.py:803
  320.5 6.8 %collective-permute-done.22 = bf16[1,1,64,1408]{3,2,1,0:T(8,128)(2,1)S(1)} collective-permute-done((bf16[1,1,64,1408]{3,2,1,0:T(8,128)(2,1)S(1)}, bf16[1,1,64,1408]{3,2,1,0:T(8,128)(2,1)S(1)}, u32[]{:S(2)}, u32[]{:S(2)}) %collective-permute-start.22) | collective-permute-done | bytes 180256 | tf_op jit(solution)/shard_map/ppermute | solution.py:803
  327.2 14.9 %collective-permute-done.21 = bf16[1,1,64,1408]{3,2,1,0:T(8,128)(2,1)S(1)} collective-permute-done((bf16[1,1,64,1408]{3,2,1,0:T(8,128)(2,1)S(1)}, bf16[1,1,64,1408]{3,2,1,0:T(8,128)(2,1)S(1)}, u32[]{:S(2)}, u32[]{:S(2)}) %collective-permute-start.21) | collective-permute-done | bytes 180256 | tf_op jit(solution)/shard_map/ppermute | solution.py:803
  345.5 2.5 add_convert_fusion.6
  348.0 11.9 %collective-permute-done.24 = bf16[4,1,64,1408]{3,2,0,1:T(8,128)(2,1)} collective-permute-done((bf16[4,1,64,1408]{3,2,0,1:T(8,128)(2,1)S(1)}, bf16[4,1,64,1408]{3,2,0,1:T(8,128)(2,1)}, u32[]{:S(2)}, u32[]{:S(2)}) %collective-permute-start.24) | collective-permute-done | bytes 720928 | tf_op jit(solution)/shard_map/ppermute | solution.py:803
  363.6 1.7 collective-permute-start.14
  365.4 12.1 %collective-permute-done.6 = bf16[256,1024]{1,0:T(8,128)(2,1)} collective-permute-done((bf16[256,1024]{1,0:T(8,128)(2,1)}, bf16[256,1024]{1,0:T(8,128)(2,1)}, u32[]{:S(2)}, u32[]{:S(2)}) %collective-permute-start.6) | collective-permute-done | bytes 524320 | tf_op jit(solution)/shard_map/ppermute | solution.py:833
  377.5 2.5 fusion.18
  380.0 8.3 %collective-permute-done.14 = bf16[256,1024]{1,0:T(8,128)(2,1)} collective-permute-done((bf16[256,1024]{1,0:T(8,128)(2,1)}, bf16[256,1024]{1,0:T(8,128)(2,1)}, u32[]{:S(2)}, u32[]{:S(2)}) %collective-permute-start.14) | collective-permute-done | bytes 524320 | tf_op jit(solution)/shard_map/ppermute | solution.py:833
  388.3 1.9 multiply_reduce_fusion.3
  390.2 2.7 multiply_add_fusion.1
  392.9 1.6 broadcast_select_fusion.1
  395.1 1.6 copy-done.52
  403.1 2.7 slice_convert_fusion.7
  405.8 1.9 slice_convert_fusion.4
  407.7 2.1 slice_convert_fusion.6
  409.8 2.2 slice_convert_fusion.8
  412.1 4.2 slice_convert_fusion.3
  416.3 3.3 slice_convert_fusion.5
  419.6 5.1 %slice_convert_fusion = (f32[1024,1024]{1,0:T(8,128)}, f32[1024,1024]{1,0:T(8,128)}, f32[1024,1024]{1,0:T(8,128)}) fusion(bf16[1024,5120]{1,0:T(8,128)(2,1)S(1)} %copy-done.54), kind=kLoop, calls=%fused_computation.13 | loop fusion | flops 3145728 | bytes 18874368 | tf_op jit(solution)/shard_map/convert_element_type | solution.py:1178
  (360 shorter events, 85.8 us)
Async XLA Ops:
  7.2 84.0 %copy-start = (bf16[1024,1024]{1,0:T(8,128)(2,1)S(1)}, bf16[1024,1024]{1,0:T(8,128)(2,1)}, u32[]{:S(2)}) copy-start(bf16[1024,1024]{1,0:T(8,128)(2,1)} %param.51) | copy-start | bytes 6291460
  7.2 17.0 %copy-start.56 = (bf16[256,1024]{1,0:T(8,128)(2,1)S(1)}, bf16[256,1024]{1,0:T(8,128)(2,1)}, u32[]{:S(2)}) copy-start(bf16[256,1024]{1,0:T(8,128)(2,1)} %param.31) | copy-start | bytes 1572868
  7.2 400.5 %all-gather.3.cloned.1.call-start = ((), (), s32[]{:S(2)}) async-start(), calls=%async_computation | async-start | bytes 11141120 | tf_op jit(solution)/shard_map/all_gather | solution.py:823
  7.3 15.1 %collective-permute-start = (bf16[256,1024]{1,0:T(8,128)(2,1)}, bf16[256,1024]{1,0:T(8,128)(2,1)S(1)}, u32[]{:S(2)}, u32[]{:S(2)}) collective-permute-start(bf16[256,1024]{1,0:T(8,128)(2,1)} %param.31), channel_id=1, source_target_pairs={{0,1},{1,0},{2,3},{3,2},{4,5},{5,4},{6,7},{7,6},{8,9},{9,8},{10,11... | collective-permute-start | bytes 1572872 | tf_op jit(solution)/shard_map/ppermute | solution.py:833
  7.8 24.7 %collective-permute-start.1 = (bf16[256,1024]{1,0:T(8,128)(2,1)}, bf16[256,1024]{1,0:T(8,128)(2,1)}, u32[]{:S(2)}, u32[]{:S(2)}) collective-permute-start(bf16[256,1024]{1,0:T(8,128)(2,1)} %param.52), channel_id=1, source_target_pairs={{0,1},{1,0},{2,3},{3,2},{4,5},{5,4},{6,7},{7,6},{8,9},{9,8},{10,11... | collective-permute-start | bytes 1572872 | tf_op jit(solution)/shard_map/ppermute | solution.py:833
  10.0 28.1 %copy-start.34 = (f32[256]{0:T(256)}, f32[256]{0:T(256)S(1)}, u32[]{:S(2)}) copy-start(f32[256]{0:T(256)S(1)} %broadcast_in_dim.36) | copy-start | bytes 3076
  10.7 27.4 %copy-start.30 = (f32[1,768]{1,0:T(1,128)}, f32[1,768]{1,0:T(1,128)S(1)}, u32[]{:S(2)}) copy-start(f32[1,768]{1,0:T(1,128)S(1)} %reshape.236.input_shift_ref) | copy-start | bytes 9220
  11.4 13.2 %copy-start.84 = (f32[1024]{0:T(1024)}, f32[1024]{0:T(1024)S(1)}, u32[]{:S(2)}) copy-start(f32[1024]{0:T(1024)S(1)} %convert_element_type.375) | copy-start | bytes 12292
  12.9 25.3 %copy-start.32 = (f32[1,768]{1,0:T(1,128)}, f32[1,768]{1,0:T(1,128)S(1)}, u32[]{:S(2)}) copy-start(f32[1,768]{1,0:T(1,128)S(1)} %broadcast_in_dim_reshape.3.skip_ref) | copy-start | bytes 9220
  14.3 23.9 %copy-start.36 = (f32[1,128]{1,0:T(1,128)}, f32[1,128]{1,0:T(1,128)S(1)}, u32[]{:S(2)}) copy-start(f32[1,128]{1,0:T(1,128)S(1)} %pad.32.rate_ref) | copy-start | bytes 1540
  14.9 23.2 %copy-start.38 = (f32[1,128]{1,0:T(1,128)}, f32[1,128]{1,0:T(1,128)S(1)}, u32[]{:S(2)}) copy-start(f32[1,128]{1,0:T(1,128)S(1)} %pad_convert_fusion.bias_ref) | copy-start | bytes 1540
  14.9 9.7 %copy-start.70 = (bf16[1024,256]{1,0:T(8,128)(2,1)S(1)}, bf16[1024,256]{1,0:T(8,128)(2,1)}, u32[]{:S(2)}) copy-start(bf16[1024,256]{1,0:T(8,128)(2,1)} %param.37) | copy-start | bytes 1572868
  16.2 21.4 %copy-start.64 = (bf16[1024,64]{1,0:T(8,128)(2,1)}, bf16[1024,64]{1,0:T(8,128)(2,1)S(1)}, u32[]{:S(2)}) copy-start(bf16[1024,64]{1,0:T(8,128)(2,1)S(1)} %get-tuple-element.271) | copy-start | bytes 393220
  16.2 21.4 %copy-start.65 = (bf16[1024,64]{1,0:T(8,128)(2,1)}, bf16[1024,64]{1,0:T(8,128)(2,1)S(1)}, u32[]{:S(2)}) copy-start(bf16[1024,64]{1,0:T(8,128)(2,1)S(1)} %get-tuple-element.272) | copy-start | bytes 393220
  24.6 13.0 %copy-start.46 = (bf16[512,1024]{1,0:T(8,128)(2,1)}, bf16[512,1024]{1,0:T(8,128)(2,1)S(1)}, u32[]{:S(2)}) copy-start(bf16[512,1024]{1,0:T(8,128)(2,1)S(1)} %multiply_convert_fusion.4) | copy-start | bytes 3145732
  26.1 9.1 %copy-start.95 = (bf16[1024,768]{1,0:T(8,128)(2,1)S(1)}, bf16[1024,768]{1,0:T(8,128)(2,1)}, u32[]{:S(2)}) copy-start(bf16[1024,768]{1,0:T(8,128)(2,1)} %param.34) | copy-start | bytes 4718596
  37.6 10.0 %copy-start.3 = (f32[512,768]{1,0:T(8,128)}, f32[512,768]{1,0:T(8,128)S(1)}, u32[]{:S(2)}) copy-start(f32[512,768]{1,0:T(8,128)S(1)} %fusion.44.input_ref) | copy-start | bytes 4718596
  38.8 8.8 %copy-start.72 = (bf16[768,1024]{1,0:T(8,128)(2,1)S(1)}, bf16[768,1024]{1,0:T(8,128)(2,1)}, u32[]{:S(2)}) copy-start(bf16[768,1024]{1,0:T(8,128)(2,1)} %param.45) | copy-start | bytes 4718596
  47.7 9.7 %copy-start.66 = (bf16[256,1024]{1,0:T(8,128)(2,1)S(1)}, bf16[256,1024]{1,0:T(8,128)(2,1)}, u32[]{:S(2)}) copy-start(bf16[256,1024]{1,0:T(8,128)(2,1)} %param.48) | copy-start | bytes 1572868
  58.7 24.3 %collective-permute-start.2 = (bf16[512,1024]{1,0:T(8,128)(2,1)}, bf16[512,1024]{1,0:T(8,128)(2,1)}, u32[]{:S(2)}, u32[]{:S(2)}) collective-permute-start(bf16[512,1024]{1,0:T(8,128)(2,1)} %add_convert_fusion.9), channel_id=1, source_target_pairs={{0,1},{1,0},{2,3},{3,2},{4,5},{5,4},{6,7},{7,6},{8,9},{9,8},{10,11... | collective-permute-start | bytes 3145736 | tf_op jit(solution)/shard_map/ppermute | solution.py:833
  60.5 25.5 %copy-start.86 = (f32[1024]{0:T(1024)S(1)}, f32[1024]{0:T(1024)}, u32[]{:S(2)}) copy-start(f32[1024]{0:T(1024)} %convert_element_type.384) | copy-start | bytes 12292
  93.3 9.0 %copy-start.97 = (bf16[512,1024]{1,0:T(8,128)(2,1)}, bf16[512,1024]{1,0:T(8,128)(2,1)S(1)}, u32[]{:S(2)}) copy-start(bf16[512,1024]{1,0:T(8,128)(2,1)S(1)} %get-tuple-element.61) | copy-start | bytes 3145732
  102.3 30.6 %collective-permute-start.5 = (bf16[8,64,2048]{2,1,0:T(8,128)(2,1)}, bf16[8,64,2048]{2,1,0:T(8,128)(2,1)}, u32[]{:S(2)}, u32[]{:S(2)}) collective-permute-start(bf16[8,64,2048]{2,1,0:T(8,128)(2,1)} %get-tuple-element.215), channel_id=1, source_target_pairs={{0,2},{2,0},{4,6},{6,4},{8,10},{10,8},{12,14},{14,12},{16,18},{18,... | collective-permute-start | bytes 6291464 | tf_op jit(solution)/shard_map/ppermute | solution.py:781
  105.1 9.4 %collective-permute-start.4 = (bf16[8,64,1024]{2,1,0:T(8,128)(2,1)}, bf16[8,64,1024]{2,1,0:T(8,128)(2,1)}, u32[]{:S(2)}, u32[]{:S(2)}) collective-permute-start(bf16[8,64,1024]{2,1,0:T(8,128)(2,1)} %get-tuple-element.234), channel_id=1, source_target_pairs={{0,2},{2,0},{4,6},{6,4},{8,10},{10,8},{12,14},{14,12},{16,18},{18,... | collective-permute-start | bytes 3145736 | tf_op jit(solution)/shard_map/ppermute | solution.py:781
  105.6 25.4 %collective-permute-start.3 = (bf16[512,1024]{1,0:T(8,128)(2,1)}, bf16[512,1024]{1,0:T(8,128)(2,1)}, u32[]{:S(2)}, u32[]{:S(2)}) collective-permute-start(bf16[512,1024]{1,0:T(8,128)(2,1)} %add_convert_fusion.8), channel_id=1, source_target_pairs={{0,1},{1,0},{2,3},{3,2},{4,5},{5,4},{6,7},{7,6},{8,9},{9,8},{10,11... | collective-permute-start | bytes 3145736 | tf_op jit(solution)/shard_map/ppermute | solution.py:833
  117.4 15.5 %copy-start.55 = (bf16[8,64,2048]{2,1,0:T(8,128)(2,1)S(1)}, bf16[8,64,2048]{2,1,0:T(8,128)(2,1)}, u32[]{:S(2)}) copy-start(bf16[8,64,2048]{2,1,0:T(8,128)(2,1)} %get-tuple-element.214) | copy-start | bytes 6291460
  117.4 40.1 %collective-permute-start.8 = (bf16[4,64,1024]{2,1,0:T(8,128)(2,1)}, bf16[4,64,1024]{2,1,0:T(8,128)(2,1)}, u32[]{:S(2)}, u32[]{:S(2)}) collective-permute-start(bf16[4,64,1024]{2,1,0:T(8,128)(2,1)} %get-tuple-element.250), channel_id=1, source_target_pairs={{0,4},{2,6},{4,0},{6,2},{8,12},{10,14},{12,8},{14,10},{16,20},{18,... | collective-permute-start | bytes 1572872 | tf_op jit(solution)/shard_map/ppermute | solution.py:781
  136.3 41.6 %collective-permute-start.9 = (bf16[4,64,2048]{2,1,0:T(8,128)(2,1)S(1)}, bf16[4,64,2048]{2,1,0:T(8,128)(2,1)S(1)}, u32[]{:S(2)}, u32[]{:S(2)}) collective-permute-start(bf16[4,64,2048]{2,1,0:T(8,128)(2,1)S(1)} %get-tuple-element.230), channel_id=1, source_target_pairs={{0,4},{2,6},{4,0},{6,2},{8,12},{10,14},{12,8},{14,10},{16,20},{18,... | collective-permute-start | bytes 3145736 | tf_op jit(solution)/shard_map/ppermute | solution.py:781
  146.0 16.9 %collective-permute-start.7 = (bf16[8,64,1024]{2,1,0:T(8,128)(2,1)}, bf16[8,64,1024]{2,1,0:T(8,128)(2,1)}, u32[]{:S(2)}, u32[]{:S(2)}) collective-permute-start(bf16[8,64,1024]{2,1,0:T(8,128)(2,1)} %get-tuple-element.232), channel_id=1, source_target_pairs={{0,2},{2,0},{4,6},{6,4},{8,10},{10,8},{12,14},{14,12},{16,18},{18,... | collective-permute-start | bytes 3145736 | tf_op jit(solution)/shard_map/ppermute | solution.py:781
  157.4 23.3 %collective-permute-start.10 = (bf16[8,64,1024]{2,1,0:T(8,128)(2,1)S(1)}, bf16[8,64,1024]{2,1,0:T(8,128)(2,1)S(1)}, u32[]{:S(2)}, u32[]{:S(2)}) collective-permute-start(bf16[8,64,1024]{2,1,0:T(8,128)(2,1)S(1)} %get-tuple-element.228), channel_id=1, source_target_pairs={{0,2},{2,0},{4,6},{6,4},{8,10},{10,8},{12,14},{14,12},{16,18},{18,... | collective-permute-start | bytes 3145736 | tf_op jit(solution)/shard_map/ppermute | solution.py:781
  159.0 23.2 %collective-permute-start.13 = (bf16[1,64,1024]{2,1,0:T(8,128)(2,1)S(1)}, bf16[1,64,1024]{2,1,0:T(8,128)(2,1)S(1)}, u32[]{:S(2)}, u32[]{:S(2)}) collective-permute-start(bf16[1,64,1024]{2,1,0:T(8,128)(2,1)S(1)} %get-tuple-element.268), channel_id=1, source_target_pairs={{0,24},{2,26},{4,28},{6,30},{8,16},{10,18},{12,20},{14,22},{16,8},... | collective-permute-start | bytes 393224 | tf_op jit(solution)/shard_map/ppermute | solution.py:781
  159.5 22.7 %collective-permute-start.12 = (bf16[1,64,1024]{2,1,0:T(8,128)(2,1)S(1)}, bf16[1,64,1024]{2,1,0:T(8,128)(2,1)S(1)}, u32[]{:S(2)}, u32[]{:S(2)}) collective-permute-start(bf16[1,64,1024]{2,1,0:T(8,128)(2,1)S(1)} %get-tuple-element.269), channel_id=1, source_target_pairs={{0,16},{2,18},{4,20},{6,22},{8,24},{10,26},{12,28},{14,30},{16,0},... | collective-permute-start | bytes 393224 | tf_op jit(solution)/shard_map/ppermute | solution.py:781
  163.0 19.1 %collective-permute-start.11 = (bf16[1,64,1024]{2,1,0:T(8,128)(2,1)S(1)}, bf16[1,64,1024]{2,1,0:T(8,128)(2,1)S(1)}, u32[]{:S(2)}, u32[]{:S(2)}) collective-permute-start(bf16[1,64,1024]{2,1,0:T(8,128)(2,1)S(1)} %get-tuple-element.270), channel_id=1, source_target_pairs={{0,8},{2,10},{4,12},{6,14},{8,0},{10,2},{12,4},{14,6},{16,24},{18,... | collective-permute-start | bytes 393224 | tf_op jit(solution)/shard_map/ppermute | solution.py:781
  178.0 43.7 %collective-permute-start.29 = (bf16[4,64,1024]{2,1,0:T(8,128)(2,1)}, bf16[4,64,1024]{2,1,0:T(8,128)(2,1)}, u32[]{:S(2)}, u32[]{:S(2)}) collective-permute-start(bf16[4,64,1024]{2,1,0:T(8,128)(2,1)} %get-tuple-element.246), channel_id=1, source_target_pairs={{0,4},{2,6},{4,0},{6,2},{8,12},{10,14},{12,8},{14,10},{16,20},{18,... | collective-permute-start | bytes 1572872 | tf_op jit(solution)/shard_map/ppermute | solution.py:781
  197.4 20.8 %collective-permute-start.28 = (bf16[1,64,2048]{2,1,0:T(8,128)(2,1)}, bf16[1,64,2048]{2,1,0:T(8,128)(2,1)}, u32[]{:S(2)}, u32[]{:S(2)}) collective-permute-start(bf16[1,64,2048]{2,1,0:T(8,128)(2,1)} %get-tuple-element.242), channel_id=1, source_target_pairs={{0,24},{2,26},{4,28},{6,30},{8,16},{10,18},{12,20},{14,22},{16,8},... | collective-permute-start | bytes 786440 | tf_op jit(solution)/shard_map/ppermute | solution.py:781
  197.8 22.5 %collective-permute-start.27 = (bf16[1,64,2048]{2,1,0:T(8,128)(2,1)}, bf16[1,64,2048]{2,1,0:T(8,128)(2,1)}, u32[]{:S(2)}, u32[]{:S(2)}) collective-permute-start(bf16[1,64,2048]{2,1,0:T(8,128)(2,1)} %get-tuple-element.243), channel_id=1, source_target_pairs={{0,16},{2,18},{4,20},{6,22},{8,24},{10,26},{12,28},{14,30},{16,0},... | collective-permute-start | bytes 786440 | tf_op jit(solution)/shard_map/ppermute | solution.py:781
  201.7 18.7 %collective-permute-start.26 = (bf16[1,64,2048]{2,1,0:T(8,128)(2,1)}, bf16[1,64,2048]{2,1,0:T(8,128)(2,1)}, u32[]{:S(2)}, u32[]{:S(2)}) collective-permute-start(bf16[1,64,2048]{2,1,0:T(8,128)(2,1)} %get-tuple-element.244), channel_id=1, source_target_pairs={{0,8},{2,10},{4,12},{6,14},{8,0},{10,2},{12,4},{14,6},{16,24},{18,... | collective-permute-start | bytes 786440 | tf_op jit(solution)/shard_map/ppermute | solution.py:781
  201.7 27.3 %collective-permute-start.33 = (bf16[4,64,1024]{2,1,0:T(8,128)(2,1)}, bf16[4,64,1024]{2,1,0:T(8,128)(2,1)}, u32[]{:S(2)}, u32[]{:S(2)}) collective-permute-start(bf16[4,64,1024]{2,1,0:T(8,128)(2,1)} %get-tuple-element.248), channel_id=1, source_target_pairs={{0,4},{2,6},{4,0},{6,2},{8,12},{10,14},{12,8},{14,10},{16,20},{18,... | collective-permute-start | bytes 1572872 | tf_op jit(solution)/shard_map/ppermute | solution.py:781
  217.9 11.0 %copy-start.69 = (bf16[4,64,1024]{2,1,0:T(8,128)(2,1)S(1)}, bf16[4,64,1024]{2,1,0:T(8,128)(2,1)}, u32[]{:S(2)}) copy-start(bf16[4,64,1024]{2,1,0:T(8,128)(2,1)} %get-tuple-element.93) | copy-start | bytes 1572868
  223.0 23.9 %copy-start.79 = (bf16[1,64,1024]{2,1,0:T(8,128)(2,1)S(1)}, bf16[1,64,1024]{2,1,0:T(8,128)(2,1)}, u32[]{:S(2)}) copy-start(bf16[1,64,1024]{2,1,0:T(8,128)(2,1)} %add_convert_fusion.18) | copy-start | bytes 393220
  223.0 11.7 %collective-permute-start.32 = (bf16[1,64,1024]{2,1,0:T(8,128)(2,1)S(1)}, bf16[1,64,1024]{2,1,0:T(8,128)(2,1)S(1)}, u32[]{:S(2)}, u32[]{:S(2)}) collective-permute-start(bf16[1,64,1024]{2,1,0:T(8,128)(2,1)S(1)} %get-tuple-element.260), channel_id=1, source_target_pairs={{0,24},{2,26},{4,28},{6,30},{8,16},{10,18},{12,20},{14,22},{16,8},... | collective-permute-start | bytes 393224 | tf_op jit(solution)/shard_map/ppermute | solution.py:781
  224.7 16.3 %collective-permute-start.31 = (bf16[1,64,1024]{2,1,0:T(8,128)(2,1)S(1)}, bf16[1,64,1024]{2,1,0:T(8,128)(2,1)S(1)}, u32[]{:S(2)}, u32[]{:S(2)}) collective-permute-start(bf16[1,64,1024]{2,1,0:T(8,128)(2,1)S(1)} %get-tuple-element.261), channel_id=1, source_target_pairs={{0,16},{2,18},{4,20},{6,22},{8,24},{10,26},{12,28},{14,30},{16,0},... | collective-permute-start | bytes 393224 | tf_op jit(solution)/shard_map/ppermute | solution.py:781
  228.9 12.0 %collective-permute-start.30 = (bf16[1,64,1024]{2,1,0:T(8,128)(2,1)S(1)}, bf16[1,64,1024]{2,1,0:T(8,128)(2,1)S(1)}, u32[]{:S(2)}, u32[]{:S(2)}) collective-permute-start(bf16[1,64,1024]{2,1,0:T(8,128)(2,1)S(1)} %get-tuple-element.262), channel_id=1, source_target_pairs={{0,8},{2,10},{4,12},{6,14},{8,0},{10,2},{12,4},{14,6},{16,24},{18,... | collective-permute-start | bytes 393224 | tf_op jit(solution)/shard_map/ppermute | solution.py:781
  230.2 15.0 %collective-permute-start.36 = (bf16[1,64,1024]{2,1,0:T(8,128)(2,1)S(1)}, bf16[1,64,1024]{2,1,0:T(8,128)(2,1)S(1)}, u32[]{:S(2)}, u32[]{:S(2)}) collective-permute-start(bf16[1,64,1024]{2,1,0:T(8,128)(2,1)S(1)} %get-tuple-element.264), channel_id=1, source_target_pairs={{0,24},{2,26},{4,28},{6,30},{8,16},{10,18},{12,20},{14,22},{16,8},... | collective-permute-start | bytes 393224 | tf_op jit(solution)/shard_map/ppermute | solution.py:781
  230.9 15.9 %collective-permute-start.35 = (bf16[1,64,1024]{2,1,0:T(8,128)(2,1)S(1)}, bf16[1,64,1024]{2,1,0:T(8,128)(2,1)S(1)}, u32[]{:S(2)}, u32[]{:S(2)}) collective-permute-start(bf16[1,64,1024]{2,1,0:T(8,128)(2,1)S(1)} %get-tuple-element.265), channel_id=1, source_target_pairs={{0,16},{2,18},{4,20},{6,22},{8,24},{10,26},{12,28},{14,30},{16,0},... | collective-permute-start | bytes 393224 | tf_op jit(solution)/shard_map/ppermute | solution.py:781
  234.7 12.1 %collective-permute-start.34 = (bf16[1,64,1024]{2,1,0:T(8,128)(2,1)S(1)}, bf16[1,64,1024]{2,1,0:T(8,128)(2,1)S(1)}, u32[]{:S(2)}, u32[]{:S(2)}) collective-permute-start(bf16[1,64,1024]{2,1,0:T(8,128)(2,1)S(1)} %get-tuple-element.266), channel_id=1, source_target_pairs={{0,8},{2,10},{4,12},{6,14},{8,0},{10,2},{12,4},{14,6},{16,24},{18,... | collective-permute-start | bytes 393224 | tf_op jit(solution)/shard_map/ppermute | solution.py:781
  247.8 3.3 collective-permute-start.15
  251.5 23.9 %collective-permute-start.16 = (bf16[4,64,1280]{2,1,0:T(8,128)(2,1)S(1)}, bf16[4,64,1280]{2,1,0:T(8,128)(2,1)S(1)}, u32[]{:S(2)}, u32[]{:S(2)}) collective-permute-start(bf16[4,64,1280]{2,1,0:T(8,128)(2,1)S(1)} %get-tuple-element.238), channel_id=1, source_target_pairs={{0,4},{2,6},{4,0},{6,2},{8,12},{10,14},{12,8},{14,10},{16,20},{18,... | collective-permute-start | bytes 1966088 | tf_op jit(solution)/shard_map/ppermute | solution.py:781
  275.7 20.2 %collective-permute-start.19 = (bf16[1,64,1280]{2,1,0:T(8,128)(2,1)S(1)}, bf16[1,64,1280]{2,1,0:T(8,128)(2,1)S(1)}, u32[]{:S(2)}, u32[]{:S(2)}) collective-permute-start(bf16[1,64,1280]{2,1,0:T(8,128)(2,1)S(1)} %get-tuple-element.256), channel_id=1, source_target_pairs={{0,24},{2,26},{4,28},{6,30},{8,16},{10,18},{12,20},{14,22},{16,8},... | collective-permute-start | bytes 491528 | tf_op jit(solution)/shard_map/ppermute | solution.py:781
  276.4 21.7 %collective-permute-start.18 = (bf16[1,64,1280]{2,1,0:T(8,128)(2,1)S(1)}, bf16[1,64,1280]{2,1,0:T(8,128)(2,1)S(1)}, u32[]{:S(2)}, u32[]{:S(2)}) collective-permute-start(bf16[1,64,1280]{2,1,0:T(8,128)(2,1)S(1)} %get-tuple-element.257), channel_id=1, source_target_pairs={{0,16},{2,18},{4,20},{6,22},{8,24},{10,26},{12,28},{14,30},{16,0},... | collective-permute-start | bytes 491528 | tf_op jit(solution)/shard_map/ppermute | solution.py:781
  280.7 17.4 %collective-permute-start.17 = (bf16[1,64,1280]{2,1,0:T(8,128)(2,1)S(1)}, bf16[1,64,1280]{2,1,0:T(8,128)(2,1)S(1)}, u32[]{:S(2)}, u32[]{:S(2)}) collective-permute-start(bf16[1,64,1280]{2,1,0:T(8,128)(2,1)S(1)} %get-tuple-element.258), channel_id=1, source_target_pairs={{0,8},{2,10},{4,12},{6,14},{8,0},{10,2},{12,4},{14,6},{16,24},{18,... | collective-permute-start | bytes 491528 | tf_op jit(solution)/shard_map/ppermute | solution.py:781
  298.2 4.3 %collective-permute-start.20 = (bf16[64,512]{1,0:T(8,128)(2,1)S(1)}, bf16[64,512]{1,0:T(8,128)(2,1)S(1)}, u32[]{:S(2)}, u32[]{:S(2)}) collective-permute-start(bf16[64,512]{1,0:T(8,128)(2,1)S(1)} %slice.198), channel_id=1, source_target_pairs={{0,1},{1,0},{2,3},{3,2},{4,5},{5,4},{6,7},{7,6},{8,9},{9,8},{10,11... | collective-permute-start | bytes 196616 | tf_op jit(solution)/shard_map/ppermute | solution.py:833
  302.7 17.7 %collective-permute-start.23 = (bf16[1,1,64,1408]{3,2,1,0:T(8,128)(2,1)S(1)}, bf16[1,1,64,1408]{3,2,1,0:T(8,128)(2,1)S(1)}, u32[]{:S(2)}, u32[]{:S(2)}) collective-permute-start(bf16[1,1,64,1408]{3,2,1,0:T(8,128)(2,1)S(1)} %bitcast.182), channel_id=1, source_target_pairs={{0,8},{2,10},{4,12},{6,14},{8,0},{10,2},{12,4},{14,6},{16,24},{18,... | collective-permute-start | bytes 540680 | tf_op jit(solution)/shard_map/ppermute | solution.py:803
  305.2 22.0 %collective-permute-start.22 = (bf16[1,1,64,1408]{3,2,1,0:T(8,128)(2,1)S(1)}, bf16[1,1,64,1408]{3,2,1,0:T(8,128)(2,1)S(1)}, u32[]{:S(2)}, u32[]{:S(2)}) collective-permute-start(bf16[1,1,64,1408]{3,2,1,0:T(8,128)(2,1)S(1)} %bitcast.183), channel_id=1, source_target_pairs={{0,16},{2,18},{4,20},{6,22},{8,24},{10,26},{12,28},{14,30},{16,0},... | collective-permute-start | bytes 540680 | tf_op jit(solution)/shard_map/ppermute | solution.py:803
  306.3 35.9 %collective-permute-start.21 = (bf16[1,1,64,1408]{3,2,1,0:T(8,128)(2,1)S(1)}, bf16[1,1,64,1408]{3,2,1,0:T(8,128)(2,1)S(1)}, u32[]{:S(2)}, u32[]{:S(2)}) collective-permute-start(bf16[1,1,64,1408]{3,2,1,0:T(8,128)(2,1)S(1)} %bitcast.184), channel_id=1, source_target_pairs={{0,24},{2,26},{4,28},{6,30},{8,16},{10,18},{12,20},{14,22},{16,8},... | collective-permute-start | bytes 540680 | tf_op jit(solution)/shard_map/ppermute | solution.py:803
  342.4 17.5 %collective-permute-start.24 = (bf16[4,1,64,1408]{3,2,0,1:T(8,128)(2,1)S(1)}, bf16[4,1,64,1408]{3,2,0,1:T(8,128)(2,1)}, u32[]{:S(2)}, u32[]{:S(2)}) collective-permute-start(bf16[4,1,64,1408]{3,2,0,1:T(8,128)(2,1)S(1)} %maximum_bitcast_fusion), channel_id=1, source_target_pairs={{0,4},{2,6},{4,0},{6,2},{8,12},{10,14},{12,8},{14,10},{16,20},{18,... | collective-permute-start | bytes 2162696 | tf_op jit(solution)/shard_map/ppermute | solution.py:803
  348.0 13.6 %copy-start.75 = (bf16[512,1024]{1,0:T(8,128)(2,1)}, bf16[512,1024]{1,0:T(8,128)(2,1)S(1)}, u32[]{:S(2)}) copy-start(bf16[512,1024]{1,0:T(8,128)(2,1)S(1)} %add_convert_fusion.6) | copy-start | bytes 3145732
  361.5 31.4 %collective-permute-start.25 = (bf16[8,1,64,1408]{3,2,0,1:T(8,128)(2,1)S(1)}, bf16[8,1,64,1408]{3,2,0,1:T(8,128)(2,1)}, u32[]{:S(2)}, u32[]{:S(2)}) collective-permute-start(bf16[8,1,64,1408]{3,2,0,1:T(8,128)(2,1)S(1)} %bitcast.167), channel_id=1, source_target_pairs={{0,2},{2,0},{4,6},{6,4},{8,10},{10,8},{12,14},{14,12},{16,18},{18,... | collective-permute-start | bytes 4325384 | tf_op jit(solution)/shard_map/ppermute | solution.py:803
  362.4 25.9 %copy-start.85 = (f32[1024]{0:T(1024)S(1)}, f32[1024]{0:T(1024)}, u32[]{:S(2)}) copy-start(f32[1024]{0:T(1024)} %copy-done.84) | copy-start | bytes 12292
  362.4 15.0 %collective-permute-start.6 = (bf16[256,1024]{1,0:T(8,128)(2,1)}, bf16[256,1024]{1,0:T(8,128)(2,1)}, u32[]{:S(2)}, u32[]{:S(2)}) collective-permute-start(bf16[256,1024]{1,0:T(8,128)(2,1)} %dynamic-slice_bitcast_fusion.20), channel_id=1, source_target_pairs={{0,1},{1,0},{2,3},{3,2},{4,5},{5,4},{6,7},{7,6},{8,9},{9,8},{10,11... | collective-permute-start | bytes 1572872 | tf_op jit(solution)/shard_map/ppermute | solution.py:833
  363.6 24.7 %collective-permute-start.14 = (bf16[256,1024]{1,0:T(8,128)(2,1)}, bf16[256,1024]{1,0:T(8,128)(2,1)}, u32[]{:S(2)}, u32[]{:S(2)}) collective-permute-start(bf16[256,1024]{1,0:T(8,128)(2,1)} %dynamic-slice_bitcast_fusion.16), channel_id=1, source_target_pairs={{0,1},{1,0},{2,3},{3,2},{4,5},{5,4},{6,7},{7,6},{8,9},{9,8},{10,11... | collective-permute-start | bytes 1572872 | tf_op jit(solution)/shard_map/ppermute | solution.py:833
  365.3 23.0 %copy-start.63 = (bf16[512,1024]{1,0:T(8,128)(2,1)S(1)}, bf16[512,1024]{1,0:T(8,128)(2,1)}, u32[]{:S(2)}) copy-start(bf16[512,1024]{1,0:T(8,128)(2,1)} %get-tuple-element.286) | copy-start | bytes 3145732
  365.4 24.8 %copy-start.50 = (f32[512,1024]{1,0:T(8,128)S(1)}, f32[512,1024]{1,0:T(8,128)}, u32[]{:S(2)}) copy-start(f32[512,1024]{1,0:T(8,128)} %copy-done.49) | copy-start | bytes 6291460
  409.8 9.8 %copy-start.54 = (bf16[1024,5120]{1,0:T(8,128)(2,1)S(1)}, bf16[1024,5120]{1,0:T(8,128)(2,1)}, u32[]{:S(2)}) copy-start(bf16[1024,5120]{1,0:T(8,128)(2,1)} %all-gather.3.cloned.1.call-done) | copy-start | bytes 31457284
  (72 other events, 200.8 us)
Sparse Core Ops, SparseCore 0:
  247.9 111.7 all-gather.2

commit v6 on v5

--- a/solution.py
+++ b/solution.py
@@ -784,9 +784,9 @@
             self.prepare()
         return self.gives
 
-    def joined(self, middle=None):
+    def joined(self, middle=None, *deps):
         groups, shift = step_groups(self.size), self.size.bit_length() - 1
-        part = self.reduced()
+        part = after(self.reduced(), *deps)
         if middle is not None:
             part = middle(part)
         if self.direct:
@@ -815,18 +815,55 @@
         return lax.psum(self.part, "dp") if self.direct else self.part[0]
 
 
-def gather_dp(parts, direct, size, place):
-    widths = [part.shape[1] for part in parts]
-    part = jnp.concatenate(parts, axis=1) if len(parts) > 1 else parts[0]
-    if not direct:
-        lead = (1,) * (place + 1)
-        part = lax.all_gather(part.reshape(lead + part.shape), "dp", axis=place, tiled=True)
-        part = part.reshape(size * part.shape[-2], part.shape[-1])
-    out, start = [], 0
-    for width in widths:
-        out.append(part[:, start : start + width])
-        start += width
-    return out
+class Halves:
+    def __init__(self, part, size):
+        self.size = size
+        self.direct = bool(size % 2 or part.shape[0] % 2)
+        self.part = part
+        if not self.direct:
+            self.pairs = [(index, index ^ 1) for index in range(size)]
+            self.side = lax.axis_index("dp") & 1
+            view = part.reshape(2, part.shape[0] // 2, part.shape[1])
+            self.keep = lax.dynamic_index_in_dim(view, self.side, 0, False)
+            self.give = lax.dynamic_index_in_dim(view, 1 - self.side, 0, False)
+
+    def halved(self):
+        if self.direct:
+            return self.part
+        got = lax.ppermute(self.give, "dp", self.pairs)
+        return (self.keep.astype(jnp.float32) + got.astype(jnp.float32)).astype(jnp.bfloat16)
+
+    def summed(self, part):
+        if self.direct:
+            return lax.psum(part, "dp")
+        groups = [list(range(side, self.size, 2)) for side in range(2)]
+        return lax.psum(part, "dp", axis_index_groups=groups)
+
+    def scattered(self, part):
+        if self.direct:
+            return lax.psum(part, "dp")
+        groups = [list(range(side, self.size, 2)) for side in range(2)]
+        if part.shape[0] % len(groups[0]):
+            return lax.psum(part, "dp", axis_index_groups=groups)
+        return lax.psum_scatter(
+            part, "dp", axis_index_groups=groups, scatter_dimension=0, tiled=True
+        )
+
+    def gathered(self, part, rows):
+        if part.shape[0] == rows:
+            return part
+        groups = [list(range(side, self.size, 2)) for side in range(2)]
+        return lax.all_gather(part, "dp", axis_index_groups=groups, axis=0, tiled=True)
+
+    def whole(self, part):
+        if self.direct:
+            return part
+        got = lax.ppermute(part, "dp", self.pairs)
+        return jnp.where(
+            self.side == 0,
+            jnp.concatenate([part, got], axis=0),
+            jnp.concatenate([got, part], axis=0),
+        )
 
 
 def other(part):
@@ -975,17 +1012,21 @@
         after(grad_gate_low, back_part),
         after(grad_upper_low, back_part),
     )
-    down_sum = Sum(inner_rows(hidden, cotan_low).astype(jnp.bfloat16), dp_size)
     hidden_cols = gate_weight.shape[1]
-    wide_sum = Sum(
-        inner_rows(whole_mid, jnp.concatenate([grad_gate_low, grad_upper_low], axis=1)).astype(
-            jnp.bfloat16
-        ),
+    wide_sum = Halves(
+        inner_rows(
+            whole_mid, jnp.concatenate([grad_gate_low, grad_upper_low], axis=1)
+        ).astype(jnp.bfloat16),
         dp_size,
     )
-    down_sum.advance()
-    wide_sum.advance()
-    back_mid = after(back_mid, *down_sum.gives, *wide_sum.gives)
+    down_sum = Halves(inner_rows(hidden, cotan_low).astype(jnp.bfloat16), dp_size)
+    wide_half, down_half = wide_sum.halved(), down_sum.halved()
+    back_mid = after(back_mid, wide_half, down_half)
+    half_rows = wide_half.shape[0]
+    if down_half.shape[0] == half_rows:
+        blocks = [wide_sum.scattered(jnp.concatenate([wide_half, down_half], axis=1))]
+    else:
+        blocks = [wide_sum.scattered(wide_half), down_sum.scattered(down_half)]
     feed_part = behind(forward_dot(hidden, down_weight), back_mid).astype(jnp.bfloat16)
     feed = sum_own(feed_part, shards)
     layer_output = (own_rows(resid, own) + feed).astype(jnp.bfloat16)
@@ -994,40 +1035,28 @@
         back_mid, gain_second, normal_second, factor_second
     )
     mixer_all = grad_resid.astype(jnp.bfloat16)
-    mixer_sum = Sum(
-        inner_rows(jnp.concatenate([gated_low, context_rows], axis=1), mixer_all).astype(
-            jnp.bfloat16
-        ),
-        dp_size,
-    )
     ssm_rows = gated_low.shape[1]
+    width = whole.shape[1]
+    split_pairs = shards == KVH
     grad_gated = against(mixer_all, mamba_output)
+    grad_mixer_out = inner_rows(
+        jnp.concatenate([gated_low, context_rows], axis=1), mixer_all
+    ).astype(jnp.bfloat16)
     sigmoid_raw = jax.nn.sigmoid(gate_raw)
     grad_gate_raw = (
         grad_gated * ssm_out * (sigmoid_raw * (1.0 + gate_raw * (1.0 - sigmoid_raw)))
     ).astype(jnp.bfloat16)
-    grad_context = against(mixer_all, context_weight).astype(jnp.bfloat16)
-    grad_query_raw, grad_pair_raw = attend_backward(
-        queries,
-        pairs,
-        totals,
-        after(jnp.pad(grad_context, ((0, 0), (0, query_pad))), *mixer_sum.gives),
-        length,
-    )
-    grad_query_raw = grad_query_raw[:, :query_cols]
-    early_cols = jnp.concatenate([grad_gate_raw, grad_query_raw], axis=1)
-    early_sum = Sum(inner_rows(whole, early_cols).astype(jnp.bfloat16), dp_size)
-    grad_gated = after(
-        grad_gated,
-        *early_sum.gives,
-        *mixer_sum.advance(early_sum.gives[0]),
-        *down_sum.advance(early_sum.gives[0]),
-    )
+    grad_mamba_gate = inner_rows(whole, grad_gate_raw).astype(jnp.bfloat16)
+    if grad_mixer_out.shape[0] == width:
+        first_sums = [Sum(jnp.concatenate([grad_mixer_out, grad_mamba_gate], axis=1), dp_size)]
+    else:
+        first_sums = [Sum(grad_mixer_out, dp_size), Sum(grad_mamba_gate, dp_size)]
+    grad_gated = after(grad_gated, *[give for item in first_sums for give in item.gives])
+
     parts = 2 if heads % 4 == 0 else 1
-    begun = None
-    input_pieces, step_pieces, conv_pieces, head_pieces = [], [], [], []
-    for index in range(parts):
-        piece = ssd_backward(
+
+    def ssd_part(index, begun):
+        return ssd_backward(
             input_raw,
             state_raw,
             gate_raw,
@@ -1041,125 +1070,137 @@
             parts,
             begun,
         )
-        begun = piece[4]
-        input_pieces.append(piece[0])
-        step_pieces.append(piece[1])
-        conv_pieces.append(jnp.sum(piece[2], axis=0))
-        head_pieces.append(jnp.sum(piece[3], axis=0))
-        if index == 0:
-            begun = after(
-                begun,
-                *wide_sum.advance(piece[1]),
-                *early_sum.advance(piece[1]),
-                *down_sum.advance(piece[1]),
-            )
-    grad_state_raw, state_sums = piece[4:]
-    grad_input_raw = jnp.concatenate(input_pieces, axis=1)
-    grad_step_raw = sum(step_pieces[1:], step_pieces[0])
-    input_sums = jnp.concatenate(conv_pieces, axis=1)
-    state_sums = jnp.sum(state_sums, axis=0)
-    head_sums = sum(head_pieces[1:], head_pieces[0])[:, :heads]
+
+    pieces = [ssd_part(0, None)]
+    if parts == 2:
+        begun = after(
+            pieces[0][4], feed, *[give for item in first_sums for give in item.advance(pieces[0][1])]
+        )
+        pieces.append(ssd_part(1, begun))
+    last = pieces[-1]
+    step_pieces = sum([piece[1] for piece in pieces[1:]], pieces[0][1])
+    input_sums = jnp.concatenate([jnp.sum(piece[2], axis=0) for piece in pieces], axis=1)
+    head_sums = sum([jnp.sum(piece[3], axis=0) for piece in pieces])[:, :heads]
+    state_sums = jnp.sum(last[5], axis=0)
     taps = input_kernel.shape[0]
+    state_cols = state_weight.shape[1]
+    step_cols = heads
     late_cols = jnp.concatenate(
-        [grad_input_raw, grad_state_raw, grad_pair_raw, grad_step_raw], axis=1
-    )
-    total = against(early_cols, jnp.concatenate([mamba_gate, query_weight], axis=1))
-    total = total + against(
-        late_cols, jnp.concatenate([mamba_input, state_weight, pair_weight, step_wide], axis=1)
-    )
-    total_low = total.astype(jnp.bfloat16)
-    grad_first = jnp.sum(total_low.astype(jnp.float32) * normal_first, axis=0)
-    width = whole.shape[1]
-    gate_cols = grad_gate_raw.shape[1]
-    input_cols = grad_input_raw.shape[1]
-    state_cols = grad_state_raw.shape[1]
-    step_cols = heads
-    pair_cols = grad_pair_raw.shape[1]
-
+        [piece[0] for piece in pieces] + [last[4], step_pieces], axis=1
+    )
     own_vectors = (input_sums[:taps], input_sums[taps], head_sums[0], head_sums[1], head_sums[2])
-    shared_vectors = (grad_first, grad_middle, state_sums[:taps], state_sums[taps])
+    shared_vectors = (grad_middle, state_sums[:taps], state_sums[taps])
     own_pack = column_pack(own_vectors, width)
     shared_pack = column_pack(shared_vectors, width)
     shared_lane = step_cols + own_pack.shape[1]
     last_lane = shared_lane + shared_pack.shape[1]
+    late = inner_rows(whole, late_cols)
+    misc = late.shape[1] - LANES
     packs = jnp.pad(
         jnp.concatenate([own_pack, shared_pack], axis=1),
-        ((0, 0), (step_cols, LANES - last_lane)),
-    )
-    split_pairs = shards == KVH
-    late = inner_rows(whole, late_cols)
-    marks = (input_cols, input_cols + state_cols, input_cols + state_cols + pair_cols)
-    late_pair = late[:, marks[1] : marks[2]]
+        ((0, 0), (misc + step_cols, LANES - last_lane)),
+    )
+    late_sum = Sum((late + packs).astype(jnp.bfloat16), dp_size)
+
+    grad_context = against(mixer_all, context_weight).astype(jnp.bfloat16)
+    grad_context = jnp.pad(grad_context, ((0, 0), (0, query_pad)))
+    grad_context = after(grad_context, *late_sum.gives, *blocks)
+    grad_query_raw, grad_pair_raw = attend_backward(queries, pairs, totals, grad_context, length)
+    middle_cols = jnp.concatenate([grad_query_raw[:, :query_cols], grad_pair_raw], axis=1)
+    total = against(
+        jnp.concatenate([grad_gate_raw, middle_cols, late_cols], axis=1),
+        jnp.concatenate(
+            [mamba_gate, query_weight, pair_weight, mamba_input, state_weight, step_wide], axis=1
+        ),
+    )
+    total_low = total.astype(jnp.bfloat16)
+    grad_first = jnp.sum(total_low.astype(jnp.float32) * normal_first, axis=0)
+    middle = inner_rows(whole, middle_cols)
     if not split_pairs:
         spread = jnp.zeros((width, 2 * KVH * HD), jnp.float32)
-        spread = lax.dynamic_update_slice_in_dim(spread, late_pair[:, :HD], kv_head * HD, 1)
-        late_pair = lax.dynamic_update_slice_in_dim(
-            spread, late_pair[:, HD:], (KVH + kv_head) * HD, 1
-        )
-        late = jnp.concatenate([late[:, : marks[1]], late_pair, late[:, marks[2] :]], axis=1)
-    misc = late.shape[1] - LANES
-    late = (late + jnp.pad(packs, ((0, 0), (misc, 0)))).astype(jnp.bfloat16)
-    late_sum = Sum(late, dp_size)
-
-    def over_tensor(part):
-        own_part = part[:, input_cols:]
+        spread = lax.dynamic_update_slice_in_dim(
+            spread, middle[:, -2 * HD : -HD], kv_head * HD, 1
+        )
+        spread = lax.dynamic_update_slice_in_dim(
+            spread, middle[:, -HD:], (KVH + kv_head) * HD, 1
+        )
+        middle = jnp.concatenate([middle[:, : -2 * HD], spread], axis=1)
+    middle = jnp.concatenate([middle, pad_lanes(grad_first[:, None])], axis=1)
+    middle_sum = Halves(middle.astype(jnp.bfloat16), dp_size)
+
+    def pairs_over_tensor(part):
+        count = 2 * HD if split_pairs else 2 * KVH * HD
+        mine = part[:, -count - LANES : -LANES]
         if split_pairs:
-            got = other(own_part)
-            both = (own_part.astype(jnp.float32) + got.astype(jnp.float32)).astype(jnp.bfloat16)
+            got = other(mine)
             first = lax.axis_index("tensor") == 0
-            pair_span = slice(state_cols, state_cols + pair_cols)
-            low = jnp.where(first, own_part[:, pair_span], got[:, pair_span])
-            high = jnp.where(first, got[:, pair_span], own_part[:, pair_span])
-            pair = [low[:, :HD], high[:, :HD], low[:, HD:], high[:, HD:]]
+            low, high = jnp.where(first, mine, got), jnp.where(first, got, mine)
+            both = [low[:, :HD], high[:, :HD], low[:, HD:], high[:, HD:]]
         else:
-            both = lax.psum(own_part, "tensor")
-            pair = [both[:, state_cols:-LANES]]
+            both = [lax.psum(mine, "tensor")]
+        first = part[:, -LANES:]
+        if shards == 2:
+            first = (first.astype(jnp.float32) + other(first).astype(jnp.float32)).astype(
+                jnp.bfloat16
+            )
+        else:
+            first = lax.psum(first, "tensor")
+        return jnp.concatenate([part[:, : -count - LANES]] + both + [first], axis=1)
+
+    def states_over_tensor(part):
+        mine = part[:, -state_cols - LANES :]
+        if shards == 2:
+            got = other(mine)
+            both = (mine.astype(jnp.float32) + got.astype(jnp.float32)).astype(jnp.bfloat16)
+        else:
+            both = lax.psum(mine, "tensor")
         lane = lane_index((part.shape[0], LANES))
         extra = jnp.where(
-            (lane >= shared_lane) & (lane < last_lane), both[:, -LANES:], own_part[:, -LANES:]
+            (lane >= shared_lane) & (lane < last_lane), both[:, state_cols:], mine[:, state_cols:]
         )
         return jnp.concatenate(
-            [part[:, :input_cols], both[:, :state_cols]] + pair + [extra], axis=1
-        )
-
-    queue = late_sum.gives[0]
-    mixer_sum.advance(queue)
-    wide_sum.advance(queue)
-    early_sum.advance(queue)
-    sums = [wide_sum, down_sum, mixer_sum, early_sum]
-    blocks = [item.reduced() for item in sums]
-    if len({block.shape[0] for block in blocks}) == 1:
-        wholes = gather_dp(blocks, wide_sum.direct, dp_size, 0)
-    else:
-        wholes = [
-            gather_dp([block], item.direct, dp_size, 0)[0] for item, block in zip(sums, blocks)
-        ]
-    grad_wide, grad_down, grad_mixer_out, early = wholes
-    grad_gate, grad_up = grad_wide[:, :hidden_cols], grad_wide[:, hidden_cols:]
-    tail = late_sum.joined(over_tensor)
+            [part[:, : -state_cols - LANES], both[:, :state_cols], extra], axis=1
+        )
+
+    firsts = [item.joined(None) for item in first_sums]
+    if len(firsts) == 1:
+        firsts = [firsts[0][:, :width], firsts[0][:, width:]]
+    grad_mixer_out, grad_mamba_gate = firsts
     grad_mamba_out = grad_mixer_out[:ssm_rows]
     grad_context_w = grad_mixer_out[ssm_rows:]
-    grad_mamba_input = tail[:, :input_cols]
-    tail = tail[:, input_cols:]
+    middle_half = pairs_over_tensor(middle_sum.halved())
+    if len(blocks) == 1:
+        both_half = wide_sum.gathered(blocks[0], half_rows)
+        wide_half, down_half = both_half[:, : 2 * hidden_cols], both_half[:, 2 * hidden_cols :]
+    else:
+        wide_half = wide_sum.gathered(blocks[0], half_rows)
+        down_half = down_sum.gathered(blocks[1], down_half.shape[0])
+    middle_half = middle_sum.summed(after(middle_half, wide_half, down_half))
+    middle = middle_sum.whole(middle_half)
+    tail = late_sum.joined(states_over_tensor)
+    grad_mamba_input = tail[:, : -state_cols - LANES]
+    extra = tail[:, -LANES:]
+    grad_state = tail[:, -state_cols - LANES : -LANES]
+    grad_wide, grad_down = wide_sum.whole(wide_half), down_sum.whole(down_half)
+    grad_gate, grad_up = grad_wide[:, :hidden_cols], grad_wide[:, hidden_cols:]
     back_in = sum_own(total_low, shards)
     normal_own = own_rows(normal_first, own)
     factor_own = own_rows(factor_first, own)
     input_grad = own_rows(grad_resid, own) + norm_back(back_in, gain_first, normal_own, factor_own)
-    extra = tail[:, state_cols + keyvalue_weight.shape[1] :]
     grad_step = extra[:, :step_cols]
     grad_in_kernel, grad_in_shift, grad_bias, grad_decay, grad_skip = column_unpack(
         extra[:, step_cols:shared_lane], [item.shape for item in own_vectors]
     )
-    grad_first, grad_middle, grad_st_kernel, grad_st_shift = column_unpack(
+    grad_middle, grad_st_kernel, grad_st_shift = column_unpack(
         extra[:, shared_lane:last_lane], [item.shape for item in shared_vectors]
     )
     results = (
-        grad_first,
+        middle[:, -LANES],
         grad_middle,
-        early[:, :gate_cols],
+        grad_mamba_gate,
         grad_mamba_input,
         grad_step,
-        tail[:, :state_cols],
+        grad_state,
         grad_in_kernel,
         grad_in_shift,
         grad_st_kernel,
@@ -1168,8 +1209,8 @@
         grad_decay,
         grad_skip,
         grad_mamba_out,
-        early[:, gate_cols:],
-        tail[:, state_cols : state_cols + keyvalue_weight.shape[1]],
+        middle[:, :query_cols],
+        middle[:, query_cols:-LANES],
         grad_context_w,
         grad_gate,
         grad_up,

time: 439 us -> 537 us (1.22)
  the two profiles are of different devices: /device:TPU:20 before, /device:TPU:0 now
where the time goes in v6:
time: 537 us; the launch traced here: 530 us
  waiting for transfers between devices  230 us (43%)
  other arithmetic  83.4 us (16%)
  local copies, waits for them, and re-layouts  67.5 us (13%)
  starting transfers between devices  54.9 us (10%)
  Pallas kernels  45.6 us (8%)
  matrix products  32.4 us (6%)
  between operations  16.1 us (3%)
    psum x1, waiting for transfers between devices, summed(): return lax.psum(part, 'dp', axis_index_groups=groups)  64.8 us
    ppermute x9, waiting for transfers between devices, other(): return lax.ppermute(part, 'tensor', [(0, 1), (1, 0)])  51 us
    ppermute x10, waiting for transfers between devices, joined(): got.append(lax.ppermute(part, 'dp', pairs))  44.7 us
    ppermute x10, waiting for transfers between devices, advance(): total = total + lax.ppermute(give, 'dp', pairs).astype(jnp.float32)  37.8 us
    ppermute x10, starting transfers between devices, joined(): got.append(lax.ppermute(part, 'dp', pairs))  30.7 us
    all_gather x1, waiting for transfers between devices, gathered(): lax.all_gather(part, 'dp', axis_index_groups=groups, axis=0, tiled=True)  30.5 us
    convert_element_type x15, other arithmetic, body(): item.astype(jnp.float32)  28.3 us
    unnamed x215, local copies, waits for them, and re-layouts  27.7 us
  transfers between devices with their start and end apart: 38, of which 17 were waited for; matrix products, arithmetic and copies ran while one was open for 18% of the time, Pallas kernels for 3%

profile of v6, /device:TPU:0, one launch (start us, length us, event | category | flops | bytes accessed | tf_op | source)
XLA Modules:
  0.0 529.8 jit_solution(6714372953232924263)
XLA Ops:
  7.3 3.0 collective-permute-start
  17.3 5.9 %collective-permute-done = bf16[256,1024]{1,0:T(8,128)(2,1)S(1)} collective-permute-done((bf16[256,1024]{1,0:T(8,128)(2,1)}, bf16[256,1024]{1,0:T(8,128)(2,1)S(1)}, u32[]{:S(2)}, u32[]{:S(2)}) %collective-permute-start) | collective-permute-done | bytes 524320 | tf_op jit(solution)/shard_map/ppermute | solution.py:870
  23.3 1.8 fusion.3
  30.9 2.9 collective-permute-done.1
  33.8 2.6 maximum_select_fusion.4
  36.4 8.7 %ssd_forward.1 = (bf16[512,768]{1,0:T(8,128)(2,1)S(1)}, f32[512,768]{1,0:T(8,128)S(1)}, f32[4,128,768]{2,1,0:T(8,128)S(1)}) custom-call(f32[512,768]{1,0:T(8,128)S(1)} %fusion.52.input_ref, f32[512,256]{1,0:T(8,128)S(1)} %fusion.53.state_ref, f32[512,768]{1,0:T(8,128)S(1)} %fusion.54.gate_ref, f32[512,128]{1,0:T(8,128)S(1)} %fusion.36.step_ref, ...), custom_call_target="tpu_custom_call" | custom-call | flops 1024 | bytes 1024 | tf_op jit(solution)/shard_map/ssd_forward/pallas_call | solution.py:430
  47.7 5.7 %attend_forward.1 = (bf16[512,256]{1,0:T(8,128)(2,1)S(1)}, bf16[512,256]{1,0:T(8,128)(2,1)S(1)}, bf16[512,128]{1,0:T(8,128)(2,1)S(1)}, f32[512,128]{1,0:T(8,128)S(1)}) custom-call(f32[512,256]{1,0:T(8,128)S(1)} %fusion.56.query_ref, f32[512,128]{1,0:T(8,128)S(1)} %fusion.29.pair_ref, f32[512,128]{1,0:T(8,128)S(1)} %copy-done.15, f32[512,128]{1,0:T(8,128)S(1)} %copy-done.16), custom_call_target="tpu_custom_call" | custom-call | flops 1024 | bytes 1024 | tf_op jit(solution)/shard_map/attend_forward/pallas_call | solution.py:680
  56.9 1.7 collective-permute-start.2
  59.9 21.6 %collective-permute-done.2 = bf16[512,1024]{1,0:T(8,128)(2,1)} collective-permute-done((bf16[512,1024]{1,0:T(8,128)(2,1)}, bf16[512,1024]{1,0:T(8,128)(2,1)}, u32[]{:S(2)}, u32[]{:S(2)}) %collective-permute-start.2) | collective-permute-done | bytes 1048608 | tf_op jit(solution)/shard_map/ppermute | solution.py:870
  81.6 2.8 multiply_reduce_fusion.2
  84.7 2.1 copy-done.97
  89.6 2.1 multiply_convert_fusion
  93.0 2.3 add_convert_fusion.3
  95.3 2.9 convolution_convert_fusion
  98.3 1.6 dynamic-slice_bitcast_fusion
  107.7 2.9 fusion.8
  110.6 19.8 %collective-permute-done.3 = bf16[512,1024]{1,0:T(8,128)(2,1)} collective-permute-done((bf16[512,1024]{1,0:T(8,128)(2,1)}, bf16[512,1024]{1,0:T(8,128)(2,1)}, u32[]{:S(2)}, u32[]{:S(2)}) %collective-permute-start.3) | collective-permute-done | bytes 1048608 | tf_op jit(solution)/shard_map/ppermute | solution.py:870
  130.4 1.9 convert_add_fusion.2
  132.4 4.6 fusion
  137.0 2.5 fusion.2
  145.4 1.6 constant_dynamic-update-slice_fusion.6
  148.0 2.2 pad_maximum_fusion
  150.2 6.1 %copy.96 = bf16[1024,1792]{1,0:T(8,128)(2,1)} copy(bf16[1024,1792]{0,1:T(8,128)(2,1)} %pad_maximum_fusion) | data formatting | bytes 7340032 | tf_op jit(solution)/shard_map/concatenate | solution.py:1051
  156.3 4.3 dynamic-slice_bitcast_fusion.1
  162.4 2.5 add_convert_fusion.2
  178.1 11.9 %ssd_backward.2 = (bf16[512,384]{1,0:T(8,128)(2,1)S(1)}, bf16[512,128]{1,0:T(8,128)(2,1)S(1)}, f32[1,8,384]{2,1,0:T(8,128)S(1)}, f32[1,8,128]{2,1,0:T(8,128)S(1)}, f32[512,256]{1,0:T(8,128)S(1)}) custom-call(f32[512,768]{1,0:T(8,128)S(1)} %copy-done.8, f32[512,256]{1,0:T(8,128)S(1)} %fusion.53.state_ref, f32[512,768]{1,0:T(8,128)S(1)} %copy-done.4, ...), custom_call_target="tpu_custom_call" | custom-call | flops 1024 | bytes 1024 | tf_op jit(solution)/shard_map/ssd_backward/pallas_call | solution.py:524
  191.7 1.9 add_convert_fusion
  195.1 13.0 %ssd_backward.3 = (bf16[512,384]{1,0:T(8,128)(2,1)S(1)}, bf16[512,128]{1,0:T(8,128)(2,1)S(1)}, f32[1,8,384]{2,1,0:T(8,128)S(1)}, f32[1,8,128]{2,1,0:T(8,128)S(1)...) custom-call(f32[512,768]{1,0:T(8,128)S(1)} %copy-done.8, f32[512,256]{1,0:T(8,128)S(1)} %fusion.53.state_ref, ...), custom_call_target="tpu_custom_call" | custom-call | flops 1024 | bytes 1024 | tf_op jit(solution)/shard_map/ssd_backward/pallas_call | solution.py:524
  208.6 2.8 fusion.1
  211.9 2.6 collective-permute-done.13
  218.5 8.0 %concatenate.119 = bf16[1024,2304]{1,0:T(8,128)(2,1)} concatenate(bf16[1024,768]{1,0:T(8,128)(2,1)} %param.34, bf16[1024,256]{1,0:T(8,128)(2,1)} %param.46, bf16[1024,64]{1,0:T(8,128)(2,1)S(1)} %copy-done.65, bf16[1024,64]{1,0:T(8,128)(2,1)S(1)} %copy-done.67, bf16[1024,768]{1,0:T(8,128)(2,1)} %param.35, bf16[1024,256]{1,0:T(8,128)(2,1)S(1)} %copy-done.73, ...), dimensions={1} | concatenate | bytes 9437184 | tf_op jit(solution)/shard_map/concatenate | solution.py:1112
  227.2 3.5 pad_maximum_fusion.2
  230.8 1.7 collective-permute-done.14
  234.0 3.7 collective-permute-start.17
  238.4 17.3 %collective-permute-done.24 = bf16[4,64,1792]{2,1,0:T(8,128)(2,1)} collective-permute-done((bf16[4,64,1792]{2,1,0:T(8,128)(2,1)}, bf16[4,64,1792]{2,1,0:T(8,128)(2,1)}, u32[]{:S(2)}, u32[]{:S(2)}) %collective-permute-start.24) | collective-permute-done | bytes 917536 | tf_op jit(solution)/shard_map/ppermute | solution.py:781
  257.1 4.9 collective-permute-done.16
  262.2 5.0 collective-permute-start.27
  268.0 3.8 collective-permute-start.19
  271.8 3.7 collective-permute-done.27
  275.5 17.5 %collective-permute-start.21 = (bf16[1,1,64,1152]{3,2,1,0:T(8,128)(2,1)S(1)}, bf16[1,1,64,1152]{3,2,1,0:T(8,128)(2,1)S(1)}, u32[]{:S(2)}, u32[]{:S(2)}) collective-permute-start(bf16[1,1,64,1152]{3,2,1,0:T(8,128)(2,1)S(1)} %maximum_bitcast_fusion.1), channel_id=1, source_target_pairs={{0,8},{2,10},{4,12},{6,14},{8,0},{10,2},{12,4},{14,6},{16,24},{18,... | collective-permute-start | bytes 442376 | tf_op jit(solution)/shard_map/ppermute | solution.py:803
  293.0 7.6 %collective-permute-done.26 = bf16[1,64,1792]{2,1,0:T(8,128)(2,1)S(1)} collective-permute-done((bf16[1,64,1792]{2,1,0:T(8,128)(2,1)S(1)}, bf16[1,64,1792]{2,1,0:T(8,128)(2,1)S(1)}, u32[]{:S(2)}, u32[]{:S(2)}) %collective-permute-start.26) | collective-permute-done | bytes 229408 | tf_op jit(solution)/shard_map/ppermute | solution.py:781
  300.7 2.6 collective-permute-start.28
  303.3 1.9 collective-permute-start.30
  305.2 11.6 %collective-permute-done.20 = bf16[1,1,64,1152]{3,2,1,0:T(8,128)(2,1)S(1)} collective-permute-done((bf16[1,1,64,1152]{3,2,1,0:T(8,128)(2,1)S(1)}, bf16[1,1,64,1152]{3,2,1,0:T(8,128)(2,1)S(1)}, u32[]{:S(2)}, u32[]{:S(2)}) %collective-permute-start.20) | collective-permute-done | bytes 147488 | tf_op jit(solution)/shard_map/ppermute | solution.py:803
  317.1 1.6 collective-permute-start.22
  318.6 15.3 %collective-permute-done.29 = bf16[1,1,64,1792]{3,2,1,0:T(8,128)(2,1)S(1)} collective-permute-done((bf16[1,1,64,1792]{3,2,1,0:T(8,128)(2,1)S(1)}, bf16[1,1,64,1792]{3,2,1,0:T(8,128)(2,1)S(1)}, u32[]{:S(2)}, u32[]{:S(2)}) %collective-permute-start.29) | collective-permute-done | bytes 229408 | tf_op jit(solution)/shard_map/ppermute | solution.py:803
  334.1 3.3 collective-permute-start.31
  338.5 17.7 %collective-permute-done.31 = bf16[4,1,64,1792]{3,2,0,1:T(8,128)(2,1)S(1)} collective-permute-done((bf16[4,1,64,1792]{3,2,0,1:T(8,128)(2,1)S(1)}, bf16[4,1,64,1792]{3,2,0,1:T(8,128)(2,1)S(1)}, u32[]{:S(2)}, u32[]{:S(2)}) %collective-permute-start.31) | collective-permute-done | bytes 917536 | tf_op jit(solution)/shard_map/ppermute | solution.py:803
  356.5 1.5 pad_maximum_fusion.4
  368.0 2.2 slice_convert_fusion.8
  370.3 3.5 slice_convert_fusion.3
  373.8 6.3 %attend_backward.1 = (bf16[512,256]{1,0:T(8,128)(2,1)S(1)}, bf16[512,128]{1,0:T(8,128)(2,1)S(1)}) custom-call(bf16[512,256]{1,0:T(8,128)(2,1)S(1)} %copy-done.19, bf16[512,128]{1,0:T(8,128)(2,1)S(1)} %copy-done.25, f32[512,128]{1,0:T(8,128)S(1)} %copy-done.21, bf16[512,256]{1,0:T(8,128)(2,1)S(1)} %convolution_convert_fusion.6.grad_ref, ...), custom_call_target="tpu_custom_call" | custom-call | flops 1024 | bytes 1024 | tf_op jit(solution)/shard_map/attend_backward/pallas_call | solution.py:711
  380.4 4.0 multiply_reduce_fusion
  386.1 2.3 broadcast_select_fusion.1
  389.0 2.2 slice_convert_fusion.4
  395.0 30.5 %all-gather.2.cloned.1.call-done = bf16[512,3072]{1,0:T(8,128)(2,1)} async-done(((bf16[64,3072]{1,0:T(8,128)(2,1)}), bf16[512,3072]{1,0:T(8,128)(2,1)}) %all-gather.2.cloned.1.call-update) | async-done | bytes 3145744 | tf_op jit(solution)/shard_map/all_gather | solution.py:856
  425.5 3.1 slice.198
  431.8 2.1 slice_convert_fusion.5
  434.0 3.6 slice_convert_fusion.2
  439.1 64.8 %all-reduce.9.cloned.1.call-done = bf16[512,640]{1,0:T(8,128)(2,1)} async-done(((bf16[512,640]{1,0:T(8,128)(2,1)}), bf16[512,640]{1,0:T(8,128)(2,1)}) %all-reduce.9.cloned.1.call-update) | async-done | bytes 655376 | tf_op jit(solution)/shard_map/psum | solution.py:840
  503.9 2.8 multiply_add_fusion.1
  506.7 4.4 fusion.7
  513.9 4.8 maximum_select_fusion
  518.7 4.4 slice_convert_fusion
  (384 shorter events, 92.1 us)
Async XLA Ops:
  7.2 82.4 %copy-start = (bf16[1024,1024]{1,0:T(8,128)(2,1)S(1)}, bf16[1024,1024]{1,0:T(8,128)(2,1)}, u32[]{:S(2)}) copy-start(bf16[1024,1024]{1,0:T(8,128)(2,1)} %param.51) | copy-start | bytes 6291460
  7.2 17.9 %copy-start.54 = (bf16[256,1024]{1,0:T(8,128)(2,1)S(1)}, bf16[256,1024]{1,0:T(8,128)(2,1)}, u32[]{:S(2)}) copy-start(bf16[256,1024]{1,0:T(8,128)(2,1)} %param.31) | copy-start | bytes 1572868
  7.2 355.4 %reduce-scatter.2.cloned.1.call-start = ((), (), s32[]{:S(2)}) async-start(), calls=%async_computation.1 | async-start | bytes 3538944 | tf_op jit(solution)/shard_map/reduce_scatter | solution.py:848
  7.3 16.0 %collective-permute-start = (bf16[256,1024]{1,0:T(8,128)(2,1)}, bf16[256,1024]{1,0:T(8,128)(2,1)S(1)}, u32[]{:S(2)}, u32[]{:S(2)}) collective-permute-start(bf16[256,1024]{1,0:T(8,128)(2,1)} %param.31), channel_id=1, source_target_pairs={{0,1},{1,0},{2,3},{3,2},{4,5},{5,4},{6,7},{7,6},{8,9},{9,8},{10,11... | collective-permute-start | bytes 1572872 | tf_op jit(solution)/shard_map/ppermute | solution.py:870
  10.3 23.5 %collective-permute-start.1 = (bf16[256,1024]{1,0:T(8,128)(2,1)}, bf16[256,1024]{1,0:T(8,128)(2,1)}, u32[]{:S(2)}, u32[]{:S(2)}) collective-permute-start(bf16[256,1024]{1,0:T(8,128)(2,1)} %param.52), channel_id=1, source_target_pairs={{0,1},{1,0},{2,3},{3,2},{4,5},{5,4},{6,7},{7,6},{8,9},{9,8},{10,11... | collective-permute-start | bytes 1572872 | tf_op jit(solution)/shard_map/ppermute | solution.py:870
  11.1 14.4 %copy-start.88 = (f32[1024]{0:T(1024)}, f32[1024]{0:T(1024)S(1)}, u32[]{:S(2)}) copy-start(f32[1024]{0:T(1024)S(1)} %convert_element_type.323) | copy-start | bytes 12292
  12.4 23.9 %copy-start.26 = (f32[1,768]{1,0:T(1,128)}, f32[1,768]{1,0:T(1,128)S(1)}, u32[]{:S(2)}) copy-start(f32[1,768]{1,0:T(1,128)S(1)} %reshape.223.input_shift_ref) | copy-start | bytes 9220
  13.8 22.6 %copy-start.31 = (f32[256]{0:T(256)}, f32[256]{0:T(256)S(1)}, u32[]{:S(2)}) copy-start(f32[256]{0:T(256)S(1)} %broadcast_in_dim.41) | copy-start | bytes 3076
  14.6 21.8 %copy-start.29 = (f32[1,768]{1,0:T(1,128)}, f32[1,768]{1,0:T(1,128)S(1)}, u32[]{:S(2)}) copy-start(f32[1,768]{1,0:T(1,128)S(1)} %broadcast_in_dim_reshape.3.skip_ref) | copy-start | bytes 9220
  15.3 21.1 %copy-start.34 = (f32[1,128]{1,0:T(1,128)}, f32[1,128]{1,0:T(1,128)S(1)}, u32[]{:S(2)}) copy-start(f32[1,128]{1,0:T(1,128)S(1)} %pad.33.rate_ref) | copy-start | bytes 1540
  16.0 20.5 %copy-start.36 = (f32[1,128]{1,0:T(1,128)}, f32[1,128]{1,0:T(1,128)S(1)}, u32[]{:S(2)}) copy-start(f32[1,128]{1,0:T(1,128)S(1)} %pad_convert_fusion.bias_ref) | copy-start | bytes 1540
  16.0 9.7 %copy-start.77 = (bf16[1024,768]{1,0:T(8,128)(2,1)S(1)}, bf16[1024,768]{1,0:T(8,128)(2,1)}, u32[]{:S(2)}) copy-start(bf16[1024,768]{1,0:T(8,128)(2,1)} %param.35) | copy-start | bytes 4718596
  17.3 29.8 %copy-start.64 = (bf16[1024,64]{1,0:T(8,128)(2,1)}, bf16[1024,64]{1,0:T(8,128)(2,1)S(1)}, u32[]{:S(2)}) copy-start(bf16[1024,64]{1,0:T(8,128)(2,1)S(1)} %get-tuple-element.244) | copy-start | bytes 393220
  17.3 29.8 %copy-start.66 = (bf16[1024,64]{1,0:T(8,128)(2,1)}, bf16[1024,64]{1,0:T(8,128)(2,1)S(1)}, u32[]{:S(2)}) copy-start(bf16[1024,64]{1,0:T(8,128)(2,1)S(1)} %get-tuple-element.245) | copy-start | bytes 393220
  25.7 21.5 %copy-start.44 = (bf16[512,1024]{1,0:T(8,128)(2,1)}, bf16[512,1024]{1,0:T(8,128)(2,1)S(1)}, u32[]{:S(2)}) copy-start(bf16[512,1024]{1,0:T(8,128)(2,1)S(1)} %multiply_convert_fusion.4) | copy-start | bytes 3145732
  27.1 9.3 %copy-start.7 = (f32[512,768]{1,0:T(8,128)}, f32[512,768]{1,0:T(8,128)S(1)}, u32[]{:S(2)}) copy-start(f32[512,768]{1,0:T(8,128)S(1)} %fusion.52.input_ref) | copy-start | bytes 4718596
  30.9 14.3 %copy-start.2 = (f32[512,768]{1,0:T(8,128)}, f32[512,768]{1,0:T(8,128)S(1)}, u32[]{:S(2)}) copy-start(f32[512,768]{1,0:T(8,128)S(1)} %fusion.54.gate_ref) | copy-start | bytes 4718596
  56.9 24.7 %collective-permute-start.2 = (bf16[512,1024]{1,0:T(8,128)(2,1)}, bf16[512,1024]{1,0:T(8,128)(2,1)}, u32[]{:S(2)}, u32[]{:S(2)}) collective-permute-start(bf16[512,1024]{1,0:T(8,128)(2,1)} %add_convert_fusion.4), channel_id=1, source_target_pairs={{0,1},{1,0},{2,3},{3,2},{4,5},{5,4},{6,7},{7,6},{8,9},{9,8},{10,11... | collective-permute-start | bytes 3145736 | tf_op jit(solution)/shard_map/ppermute | solution.py:870
  59.9 24.5 %copy-start.90 = (f32[1024]{0:T(1024)S(1)}, f32[1024]{0:T(1024)}, u32[]{:S(2)}) copy-start(f32[1024]{0:T(1024)} %convert_element_type.332) | copy-start | bytes 12292
  100.9 31.5 %collective-permute-start.4 = (bf16[512,2048]{1,0:T(8,128)(2,1)}, bf16[512,2048]{1,0:T(8,128)(2,1)}, u32[]{:S(2)}, u32[]{:S(2)}) collective-permute-start(bf16[512,2048]{1,0:T(8,128)(2,1)} %dynamic-slice_bitcast_fusion), channel_id=1, source_target_pairs={{0,2},{2,0},{4,6},{6,4},{8,10},{10,8},{12,14},{14,12},{16,18},{18,... | collective-permute-start | bytes 6291464 | tf_op jit(solution)/shard_map/ppermute | solution.py:833
  104.6 3.1 collective-permute-start.5
  105.1 25.4 %collective-permute-start.3 = (bf16[512,1024]{1,0:T(8,128)(2,1)}, bf16[512,1024]{1,0:T(8,128)(2,1)}, u32[]{:S(2)}, u32[]{:S(2)}) collective-permute-start(bf16[512,1024]{1,0:T(8,128)(2,1)} %add_convert_fusion.3), channel_id=1, source_target_pairs={{0,1},{1,0},{2,3},{3,2},{4,5},{5,4},{6,7},{7,6},{8,9},{9,8},{10,11... | collective-permute-start | bytes 3145736 | tf_op jit(solution)/shard_map/ppermute | solution.py:870
  110.6 21.8 %copy-start.59 = (bf16[1024,2048]{1,0:T(8,128)(2,1)S(1)}, bf16[1024,2048]{1,0:T(8,128)(2,1)}, u32[]{:S(2)}) copy-start(bf16[1024,2048]{1,0:T(8,128)(2,1)} %copy-done.58) | copy-start | bytes 12582916
  160.5 30.6 %collective-permute-start.7 = (bf16[8,64,1792]{2,1,0:T(8,128)(2,1)}, bf16[8,64,1792]{2,1,0:T(8,128)(2,1)}, u32[]{:S(2)}, u32[]{:S(2)}) collective-permute-start(bf16[8,64,1792]{2,1,0:T(8,128)(2,1)} %get-tuple-element.210), channel_id=1, source_target_pairs={{0,2},{2,0},{4,6},{6,4},{8,10},{10,8},{12,14},{14,12},{16,18},{18,... | collective-permute-start | bytes 5505032 | tf_op jit(solution)/shard_map/ppermute | solution.py:781
  166.7 23.4 %collective-permute-start.6 = (bf16[256,1024]{1,0:T(8,128)(2,1)}, bf16[256,1024]{1,0:T(8,128)(2,1)S(1)}, u32[]{:S(2)}, u32[]{:S(2)}) collective-permute-start(bf16[256,1024]{1,0:T(8,128)(2,1)} %dynamic-slice_bitcast_fusion.11), channel_id=1, source_target_pairs={{0,1},{1,0},{2,3},{3,2},{4,5},{5,4},{6,7},{7,6},{8,9},{9,8},{10,11... | collective-permute-start | bytes 1572872 | tf_op jit(solution)/shard_map/ppermute | solution.py:870
  178.1 12.0 %copy-start.43 = (f32[512,1024]{1,0:T(8,128)S(1)}, f32[512,1024]{1,0:T(8,128)}, u32[]{:S(2)}) copy-start(f32[512,1024]{1,0:T(8,128)} %copy-done.41) | copy-start | bytes 6291460
  178.1 12.0 %copy-start.82 = (bf16[512,1024]{1,0:T(8,128)(2,1)S(1)}, bf16[512,1024]{1,0:T(8,128)(2,1)}, u32[]{:S(2)}) copy-start(bf16[512,1024]{1,0:T(8,128)(2,1)} %copy-done.81) | copy-start | bytes 3145732
  195.1 13.1 %copy-start.94 = (f32[1024]{0:T(1024)S(1)}, f32[1024]{0:T(1024)}, u32[]{:S(2)}) copy-start(f32[1024]{0:T(1024)} %get-tuple-element.192) | copy-start | bytes 12292
  211.7 2.9 collective-permute-start.13
  216.0 16.5 %collective-permute-start.14 = (bf16[4,64,1152]{2,1,0:T(8,128)(2,1)}, bf16[4,64,1152]{2,1,0:T(8,128)(2,1)}, u32[]{:S(2)}, u32[]{:S(2)}) collective-permute-start(bf16[4,64,1152]{2,1,0:T(8,128)(2,1)} %get-tuple-element.222), channel_id=1, source_target_pairs={{0,4},{2,6},{4,0},{6,2},{8,12},{10,14},{12,8},{14,10},{16,20},{18,... | collective-permute-start | bytes 1769480 | tf_op jit(solution)/shard_map/ppermute | solution.py:781
  226.7 29.0 %collective-permute-start.24 = (bf16[4,64,1792]{2,1,0:T(8,128)(2,1)}, bf16[4,64,1792]{2,1,0:T(8,128)(2,1)}, u32[]{:S(2)}, u32[]{:S(2)}) collective-permute-start(bf16[4,64,1792]{2,1,0:T(8,128)(2,1)} %get-tuple-element.216), channel_id=1, source_target_pairs={{0,4},{2,6},{4,0},{6,2},{8,12},{10,14},{12,8},{14,10},{16,20},{18,... | collective-permute-start | bytes 2752520 | tf_op jit(solution)/shard_map/ppermute | solution.py:781
  230.8 24.9 %copy-start.63 = (bf16[4,64,1792]{2,1,0:T(8,128)(2,1)S(1)}, bf16[4,64,1792]{2,1,0:T(8,128)(2,1)}, u32[]{:S(2)}) copy-start(bf16[4,64,1792]{2,1,0:T(8,128)(2,1)} %get-tuple-element.215) | copy-start | bytes 2752516
  230.8 194.7 %all-gather.2.cloned.1.call-start = ((), (), s32[]{:S(2)}) async-start(), calls=%async_computation.2 | async-start | bytes 3538944 | tf_op jit(solution)/shard_map/all_gather | solution.py:856
  234.0 23.1 %collective-permute-start.17 = (bf16[1,64,1152]{2,1,0:T(8,128)(2,1)S(1)}, bf16[1,64,1152]{2,1,0:T(8,128)(2,1)S(1)}, u32[]{:S(2)}, u32[]{:S(2)}) collective-permute-start(bf16[1,64,1152]{2,1,0:T(8,128)(2,1)S(1)} %get-tuple-element.240), channel_id=1, source_target_pairs={{0,24},{2,26},{4,28},{6,30},{8,16},{10,18},{12,20},{14,22},{16,8},... | collective-permute-start | bytes 442376 | tf_op jit(solution)/shard_map/ppermute | solution.py:781
  237.7 24.3 %collective-permute-start.16 = (bf16[1,64,1152]{2,1,0:T(8,128)(2,1)S(1)}, bf16[1,64,1152]{2,1,0:T(8,128)(2,1)S(1)}, u32[]{:S(2)}, u32[]{:S(2)}) collective-permute-start(bf16[1,64,1152]{2,1,0:T(8,128)(2,1)S(1)} %get-tuple-element.241), channel_id=1, source_target_pairs={{0,16},{2,18},{4,20},{6,22},{8,24},{10,26},{12,28},{14,30},{16,0},... | collective-permute-start | bytes 442376 | tf_op jit(solution)/shard_map/ppermute | solution.py:781
  237.7 24.3 %collective-permute-start.15 = (bf16[1,64,1152]{2,1,0:T(8,128)(2,1)S(1)}, bf16[1,64,1152]{2,1,0:T(8,128)(2,1)S(1)}, u32[]{:S(2)}, u32[]{:S(2)}) collective-permute-start(bf16[1,64,1152]{2,1,0:T(8,128)(2,1)S(1)} %get-tuple-element.242), channel_id=1, source_target_pairs={{0,8},{2,10},{4,12},{6,14},{8,0},{10,2},{12,4},{14,6},{16,24},{18,... | collective-permute-start | bytes 442376 | tf_op jit(solution)/shard_map/ppermute | solution.py:781
  262.1 5.8 %collective-permute-start.18 = (bf16[64,384]{1,0:T(8,128)(2,1)S(1)}, bf16[64,384]{1,0:T(8,128)(2,1)S(1)}, u32[]{:S(2)}, u32[]{:S(2)}) collective-permute-start(bf16[64,384]{1,0:T(8,128)(2,1)S(1)} %slice.202), channel_id=1, source_target_pairs={{0,1},{1,0},{2,3},{3,2},{4,5},{5,4},{6,7},{7,6},{8,9},{9,8},{10,11... | collective-permute-start | bytes 147464 | tf_op jit(solution)/shard_map/ppermute | solution.py:870
  262.2 13.3 %collective-permute-start.27 = (bf16[1,64,1792]{2,1,0:T(8,128)(2,1)S(1)}, bf16[1,64,1792]{2,1,0:T(8,128)(2,1)S(1)}, u32[]{:S(2)}, u32[]{:S(2)}) collective-permute-start(bf16[1,64,1792]{2,1,0:T(8,128)(2,1)S(1)} %get-tuple-element.230), channel_id=1, source_target_pairs={{0,24},{2,26},{4,28},{6,30},{8,16},{10,18},{12,20},{14,22},{16,8},... | collective-permute-start | bytes 688136 | tf_op jit(solution)/shard_map/ppermute | solution.py:781
  267.3 33.3 %collective-permute-start.26 = (bf16[1,64,1792]{2,1,0:T(8,128)(2,1)S(1)}, bf16[1,64,1792]{2,1,0:T(8,128)(2,1)S(1)}, u32[]{:S(2)}, u32[]{:S(2)}) collective-permute-start(bf16[1,64,1792]{2,1,0:T(8,128)(2,1)S(1)} %get-tuple-element.231), channel_id=1, source_target_pairs={{0,16},{2,18},{4,20},{6,22},{8,24},{10,26},{12,28},{14,30},{16,0},... | collective-permute-start | bytes 688136 | tf_op jit(solution)/shard_map/ppermute | solution.py:781
  267.3 33.3 %collective-permute-start.25 = (bf16[1,64,1792]{2,1,0:T(8,128)(2,1)S(1)}, bf16[1,64,1792]{2,1,0:T(8,128)(2,1)S(1)}, u32[]{:S(2)}, u32[]{:S(2)}) collective-permute-start(bf16[1,64,1792]{2,1,0:T(8,128)(2,1)S(1)} %get-tuple-element.232), channel_id=1, source_target_pairs={{0,8},{2,10},{4,12},{6,14},{8,0},{10,2},{12,4},{14,6},{16,24},{18,... | collective-permute-start | bytes 688136 | tf_op jit(solution)/shard_map/ppermute | solution.py:781
  268.0 35.3 %collective-permute-start.19 = (bf16[1,1,64,1152]{3,2,1,0:T(8,128)(2,1)S(1)}, bf16[1,1,64,1152]{3,2,1,0:T(8,128)(2,1)S(1)}, u32[]{:S(2)}, u32[]{:S(2)}) collective-permute-start(bf16[1,1,64,1152]{3,2,1,0:T(8,128)(2,1)S(1)} %maximum_bitcast_fusion.1), channel_id=1, source_target_pairs={{0,24},{2,26},{4,28},{6,30},{8,16},{10,18},{12,20},{14,22},{16,8},... | collective-permute-start | bytes 442376 | tf_op jit(solution)/shard_map/ppermute | solution.py:803
  271.8 45.0 %collective-permute-start.20 = (bf16[1,1,64,1152]{3,2,1,0:T(8,128)(2,1)S(1)}, bf16[1,1,64,1152]{3,2,1,0:T(8,128)(2,1)S(1)}, u32[]{:S(2)}, u32[]{:S(2)}) collective-permute-start(bf16[1,1,64,1152]{3,2,1,0:T(8,128)(2,1)S(1)} %maximum_bitcast_fusion.1), channel_id=1, source_target_pairs={{0,16},{2,18},{4,20},{6,22},{8,24},{10,26},{12,28},{14,30},{16,0},... | collective-permute-start | bytes 442376 | tf_op jit(solution)/shard_map/ppermute | solution.py:803
  275.5 41.3 %collective-permute-start.21 = (bf16[1,1,64,1152]{3,2,1,0:T(8,128)(2,1)S(1)}, bf16[1,1,64,1152]{3,2,1,0:T(8,128)(2,1)S(1)}, u32[]{:S(2)}, u32[]{:S(2)}) collective-permute-start(bf16[1,1,64,1152]{3,2,1,0:T(8,128)(2,1)S(1)} %maximum_bitcast_fusion.1), channel_id=1, source_target_pairs={{0,8},{2,10},{4,12},{6,14},{8,0},{10,2},{12,4},{14,6},{16,24},{18,... | collective-permute-start | bytes 442376 | tf_op jit(solution)/shard_map/ppermute | solution.py:803
  300.7 17.9 %collective-permute-start.28 = (bf16[1,1,64,1792]{3,2,1,0:T(8,128)(2,1)S(1)}, bf16[1,1,64,1792]{3,2,1,0:T(8,128)(2,1)S(1)}, u32[]{:S(2)}, u32[]{:S(2)}) collective-permute-start(bf16[1,1,64,1792]{3,2,1,0:T(8,128)(2,1)S(1)} %bitcast.200), channel_id=1, source_target_pairs={{0,24},{2,26},{4,28},{6,30},{8,16},{10,18},{12,20},{14,22},{16,8},... | collective-permute-start | bytes 688136 | tf_op jit(solution)/shard_map/ppermute | solution.py:803
  303.3 30.6 %collective-permute-start.29 = (bf16[1,1,64,1792]{3,2,1,0:T(8,128)(2,1)S(1)}, bf16[1,1,64,1792]{3,2,1,0:T(8,128)(2,1)S(1)}, u32[]{:S(2)}, u32[]{:S(2)}) collective-permute-start(bf16[1,1,64,1792]{3,2,1,0:T(8,128)(2,1)S(1)} %bitcast.201), channel_id=1, source_target_pairs={{0,16},{2,18},{4,20},{6,22},{8,24},{10,26},{12,28},{14,30},{16,0},... | collective-permute-start | bytes 688136 | tf_op jit(solution)/shard_map/ppermute | solution.py:803
  303.3 30.6 %collective-permute-start.30 = (bf16[1,1,64,1792]{3,2,1,0:T(8,128)(2,1)S(1)}, bf16[1,1,64,1792]{3,2,1,0:T(8,128)(2,1)S(1)}, u32[]{:S(2)}, u32[]{:S(2)}) collective-permute-start(bf16[1,1,64,1792]{3,2,1,0:T(8,128)(2,1)S(1)} %bitcast.202), channel_id=1, source_target_pairs={{0,8},{2,10},{4,12},{6,14},{8,0},{10,2},{12,4},{14,6},{16,24},{18,... | collective-permute-start | bytes 688136 | tf_op jit(solution)/shard_map/ppermute | solution.py:803
  317.0 20.4 %copy-start.48 = (f32[512,1024]{1,0:T(8,128)S(1)}, f32[512,1024]{1,0:T(8,128)}, u32[]{:S(2)}) copy-start(f32[512,1024]{1,0:T(8,128)} %copy-done.47) | copy-start | bytes 6291460
  317.1 20.4 %copy-start.76 = (bf16[256,1024]{1,0:T(8,128)(2,1)S(1)}, bf16[256,1024]{1,0:T(8,128)(2,1)}, u32[]{:S(2)}) copy-start(bf16[256,1024]{1,0:T(8,128)(2,1)} %param.48) | copy-start | bytes 1572868
  317.1 20.9 %collective-permute-start.22 = (bf16[4,1,64,1152]{3,2,0,1:T(8,128)(2,1)S(1)}, bf16[4,1,64,1152]{3,2,0,1:T(8,128)(2,1)S(1)}, u32[]{:S(2)}, u32[]{:S(2)}) collective-permute-start(bf16[4,1,64,1152]{3,2,0,1:T(8,128)(2,1)S(1)} %maximum_bitcast_fusion), channel_id=1, source_target_pairs={{0,4},{2,6},{4,0},{6,2},{8,12},{10,14},{12,8},{14,10},{16,20},{18,... | collective-permute-start | bytes 1769480 | tf_op jit(solution)/shard_map/ppermute | solution.py:803
  334.1 22.0 %collective-permute-start.31 = (bf16[4,1,64,1792]{3,2,0,1:T(8,128)(2,1)S(1)}, bf16[4,1,64,1792]{3,2,0,1:T(8,128)(2,1)S(1)}, u32[]{:S(2)}, u32[]{:S(2)}) collective-permute-start(bf16[4,1,64,1792]{3,2,0,1:T(8,128)(2,1)S(1)} %fusion.34), channel_id=1, source_target_pairs={{0,4},{2,6},{4,0},{6,2},{8,12},{10,14},{12,8},{14,10},{16,20},{18,... | collective-permute-start | bytes 2752520 | tf_op jit(solution)/shard_map/ppermute | solution.py:803
  338.4 19.6 %collective-permute-start.23 = (bf16[8,1,64,1152]{3,2,0,1:T(8,128)(2,1)S(1)}, bf16[8,1,64,1152]{3,2,0,1:T(8,128)(2,1)S(1)}, u32[]{:S(2)}, u32[]{:S(2)}) collective-permute-start(bf16[8,1,64,1152]{3,2,0,1:T(8,128)(2,1)S(1)} %bitcast.182), channel_id=1, source_target_pairs={{0,2},{2,0},{4,6},{6,4},{8,10},{10,8},{12,14},{14,12},{16,18},{18,... | collective-permute-start | bytes 3538952 | tf_op jit(solution)/shard_map/ppermute | solution.py:803
  358.0 28.1 %collective-permute-start.32 = (bf16[8,1,64,1792]{3,2,1,0:T(8,128)(2,1)}, bf16[8,1,64,1792]{3,2,1,0:T(8,128)(2,1)}, u32[]{:S(2)}, u32[]{:S(2)}) collective-permute-start(bf16[8,1,64,1792]{3,2,1,0:T(8,128)(2,1)} %bitcast.55), channel_id=1, source_target_pairs={{0,2},{2,0},{4,6},{6,4},{8,10},{10,8},{12,14},{14,12},{16,18},{18,... | collective-permute-start | bytes 5505032 | tf_op jit(solution)/shard_map/ppermute | solution.py:803
  362.7 141.2 %all-reduce.9.cloned.1.call-start = ((), (), s32[]{:S(2)}) async-start(), calls=%async_computation.3 | async-start | bytes 1310720 | tf_op jit(solution)/shard_map/psum | solution.py:840
  364.6 15.8 %slice-start = ((s8[4718592]{0:T(1024)(128)(4,1)}), s8[524288]{0:T(1024)(128)(4,1)S(1)}, s32[]{:S(2)}) async-start(s8[4718592]{0:T(1024)(128)(4,1)} %bitcast.184), calls=%async_computation.4 | async-start | bytes 1048576
  368.0 12.1 %copy-start.85 = (bf16[512,2304]{1,0:T(8,128)(2,1)S(1)}, bf16[512,2304]{1,0:T(8,128)(2,1)}, u32[]{:S(2)}) copy-start(bf16[512,2304]{1,0:T(8,128)(2,1)} %get-tuple-element.196) | copy-start | bytes 7077892
  370.3 10.1 %slice-start.1 = ((s8[4718592]{0:T(1024)(128)(4,1)}), s8[4194304]{0:T(1024)(128)(4,1)S(1)}, s32[]{:S(2)}) async-start(s8[4718592]{0:T(1024)(128)(4,1)} %bitcast.184), calls=%async_computation.5 | async-start | bytes 8388608
  385.5 3.3 collective-permute-start.9
  389.0 5.5 %collective-permute-start.10 = (bf16[512,128]{1,0:T(8,128)(2,1)S(1)}, bf16[512,128]{1,0:T(8,128)(2,1)S(1)}, u32[]{:S(2)}, u32[]{:S(2)}) collective-permute-start(bf16[512,128]{1,0:T(8,128)(2,1)S(1)} %slice.192), channel_id=1, source_target_pairs={{0,1},{1,0},{2,3},{3,2},{4,5},{5,4},{6,7},{7,6},{8,9},{9,8},{10,11... | collective-permute-start | bytes 393224 | tf_op jit(solution)/shard_map/ppermute | solution.py:870
  392.5 45.1 %collective-permute-start.8 = (bf16[256,1024]{1,0:T(8,128)(2,1)}, bf16[256,1024]{1,0:T(8,128)(2,1)}, u32[]{:S(2)}, u32[]{:S(2)}) collective-permute-start(bf16[256,1024]{1,0:T(8,128)(2,1)} %dynamic-slice_bitcast_fusion.10), channel_id=1, source_target_pairs={{0,1},{1,0},{2,3},{3,2},{4,5},{5,4},{6,7},{7,6},{8,9},{9,8},{10,11... | collective-permute-start | bytes 1572872 | tf_op jit(solution)/shard_map/ppermute | solution.py:870
  394.5 34.2 %collective-permute-start.11 = (bf16[512,128]{1,0:T(8,128)(2,1)S(1)}, bf16[512,128]{1,0:T(8,128)(2,1)S(1)}, u32[]{:S(2)}, u32[]{:S(2)}) collective-permute-start(bf16[512,128]{1,0:T(8,128)(2,1)S(1)} %get-tuple-element.243), channel_id=1, source_target_pairs={{0,1},{1,0},{2,3},{3,2},{4,5},{5,4},{6,7},{7,6},{8,9},{9,8},{10,11... | collective-permute-start | bytes 393224 | tf_op jit(solution)/shard_map/ppermute | solution.py:870
  428.7 85.3 %collective-permute-start.33 = (bf16[512,2048]{1,0:T(8,128)(2,1)}, bf16[512,2048]{1,0:T(8,128)(2,1)}, u32[]{:S(2)}, u32[]{:S(2)}) collective-permute-start(bf16[512,2048]{1,0:T(8,128)(2,1)} %slice.198), channel_id=1, source_target_pairs={{0,2},{2,0},{4,6},{6,4},{8,10},{10,8},{12,14},{14,12},{16,18},{18,... | collective-permute-start | bytes 6291464 | tf_op jit(solution)/shard_map/ppermute | solution.py:861
  431.2 75.5 %collective-permute-start.34 = (bf16[512,1024]{1,0:T(8,128)(2,1)S(1)}, bf16[512,1024]{1,0:T(8,128)(2,1)}, u32[]{:S(2)}, u32[]{:S(2)}) collective-permute-start(bf16[512,1024]{1,0:T(8,128)(2,1)S(1)} %slice.199), channel_id=1, source_target_pairs={{0,2},{2,0},{4,6},{6,4},{8,10},{10,8},{12,14},{14,12},{16,18},{18,... | collective-permute-start | bytes 3145736 | tf_op jit(solution)/shard_map/ppermute | solution.py:861
  437.6 66.3 %copy-start.49 = (f32[512,1024]{1,0:T(8,128)S(1)}, f32[512,1024]{1,0:T(8,128)}, u32[]{:S(2)}) copy-start(f32[512,1024]{1,0:T(8,128)} %copy-done.47) | copy-start | bytes 6291460
  503.9 7.2 %collective-permute-start.12 = (bf16[512,640]{1,0:T(8,128)(2,1)}, bf16[512,640]{1,0:T(8,128)(2,1)S(1)}, u32[]{:S(2)}, u32[]{:S(2)}) collective-permute-start(bf16[512,640]{1,0:T(8,128)(2,1)} %all-reduce.9.cloned.1.call-done), channel_id=1, source_target_pairs={{0,2},{2,0},{4,6},{6,4},{8,10},{10,8},{12,14},{14,12},{16,18},{18,... | collective-permute-start | bytes 1966088 | tf_op jit(solution)/shard_map/ppermute | solution.py:861
  (76 other events, 225.8 us)
Sparse Core Ops, SparseCore 0:
  230.9 108.8 reduce-scatter.1
  362.8 62.6 all-gather.1
  432.0 71.9 all-reduce.8

commit v7 on v4

--- a/solution.py
+++ b/solution.py
@@ -731,9 +731,8 @@
 
 
 class Sum:
-    def __init__(self, part, size, place):
+    def __init__(self, part, size):
         self.size = size
-        self.place = place
         self.direct = bool(size & (size - 1) or part.shape[0] % size)
         self.steps = [] if self.direct else step_groups(size)
         self.shift = 0
@@ -756,9 +755,9 @@
             lax.dynamic_index_in_dim(view, mine ^ way, 1, False) for way in range(1, ways)
         ]
 
-    def advance(self):
+    def advance(self, *deps):
         if self.steps:
-            total = self.keep.astype(jnp.float32)
+            total = after(self.keep, *deps).astype(jnp.float32)
             for way, give in enumerate(self.gives, 1):
                 pairs = [(index, index ^ (way << self.shift)) for index in range(self.size)]
                 total = total + lax.ppermute(give, "dp", pairs).astype(jnp.float32)
@@ -767,18 +766,37 @@
             self.prepare()
         return self.gives
 
-    def finish(self, middle=None):
+    def joined(self, middle=None, *deps):
+        groups, shift = step_groups(self.size), self.size.bit_length() - 1
+        part = after(self.reduced(), *deps)
+        if middle is not None:
+            part = middle(part)
+        self.trail = [part]
+        if self.direct:
+            return part
+        rows, width = part.shape
+        for group in reversed(groups):
+            ways = 1 << group
+            shift -= group
+            mine = (lax.axis_index("dp") >> shift) & (ways - 1)
+            part = part.reshape(-1, 1, rows, width)
+            got = [part]
+            for way in range(1, ways):
+                pairs = [(index, index ^ (way << shift)) for index in range(self.size)]
+                got.append(lax.ppermute(part, "dp", pairs))
+            for bit in range(group):
+                flip = ((mine >> bit) & 1) == 1
+                got = [
+                    jnp.where(flip, got[way ^ (1 << bit)], got[way]) for way in range(ways)
+                ]
+            part = jnp.concatenate(got, axis=1)
+            self.trail.append(part)
+        return part.reshape(-1, width)
+
+    def reduced(self):
         while self.steps:
             self.advance()
-        if self.direct:
-            part = lax.psum(self.part, "dp")
-            return part if middle is None else middle(part)
-        part = self.part[0]
-        if middle is not None:
-            part = middle(part)
-        lead = (1,) * (self.place + 1)
-        whole = lax.all_gather(part.reshape(lead + part.shape), "dp", axis=self.place, tiled=True)
-        return whole.reshape(self.size * part.shape[0], part.shape[1])
+        return lax.psum(self.part, "dp") if self.direct else self.part[0]
 
 
 def other(part):
@@ -924,18 +942,10 @@
     back_mid = sum_all(back_part, shards)
     hidden_late = after(hidden, back_part)
     mid_late = after(whole_mid, back_part)
-    down_sum = Sum(inner_rows(hidden_late, cotan_low).astype(jnp.bfloat16), dp_size, 0)
-    hidden_cols = gate_weight.shape[1]
-    wide_sum = Sum(
-        inner_rows(mid_late, jnp.concatenate([grad_gate_low, grad_upper_low], axis=1)).astype(
-            jnp.bfloat16
-        ),
-        dp_size,
-        0,
-    )
-    down_sum.advance()
-    wide_sum.advance()
-    back_mid = after(back_mid, *down_sum.gives, *wide_sum.gives)
+    grad_down = inner_rows(hidden_late, cotan_low).astype(jnp.bfloat16)
+    grad_gate = inner_rows(mid_late, grad_gate_low).astype(jnp.bfloat16)
+    grad_up = inner_rows(mid_late, grad_upper_low).astype(jnp.bfloat16)
+    grad_gate, grad_up, grad_down = lax.psum((grad_gate, grad_up, grad_down), "dp")
     feed_part = behind(forward_dot(hidden_late, down_weight), back_mid).astype(jnp.bfloat16)
     feed = sum_own(feed_part, shards)
     layer_output = (own_rows(resid, own) + feed).astype(jnp.bfloat16)
@@ -944,124 +954,121 @@
         back_mid, gain_second, normal_second, factor_second
     )
     mixer_all = grad_resid.astype(jnp.bfloat16)
+    ssm_rows = gated_low.shape[1]
+    width = whole.shape[1]
+    split_pairs = shards == KVH
+    grad_gated = against(mixer_all, mamba_output)
     mixer_sum = Sum(
         inner_rows(jnp.concatenate([gated_low, context_rows], axis=1), mixer_all).astype(
             jnp.bfloat16
         ),
         dp_size,
-        1,
-    )
-    ssm_rows = gated_low.shape[1]
-    grad_gated = against(mixer_all, mamba_output)
+    )
+    grad_input_raw, grad_state_raw, grad_step_raw, input_sums, state_sums, head_sums = ssd_backward(
+        input_raw,
+        state_raw,
+        gate_raw,
+        step_raw,
+        after(grad_gated, *mixer_sum.gives),
+        carries,
+        small,
+        heads,
+        length,
+    )
+    input_sums = jnp.sum(input_sums, axis=0)
+    state_sums = jnp.sum(state_sums, axis=0)
+    head_sums = jnp.sum(head_sums, axis=0)[:, :heads]
+    taps = input_kernel.shape[0]
+    state_cols = state_weight.shape[1]
+    step_cols = heads
+    late_cols = jnp.concatenate([grad_input_raw, grad_state_raw], axis=1)
+    late_sum = Sum(inner_rows(whole, late_cols).astype(jnp.bfloat16), dp_size)
+
     sigmoid_raw = jax.nn.sigmoid(gate_raw)
     grad_gate_raw = (
         grad_gated * ssm_out * (sigmoid_raw * (1.0 + gate_raw * (1.0 - sigmoid_raw)))
     ).astype(jnp.bfloat16)
     grad_context = against(mixer_all, context_weight).astype(jnp.bfloat16)
+    grad_context = jnp.pad(grad_context, ((0, 0), (0, query_pad)))
     grad_query_raw, grad_pair_raw = attend_backward(
-        queries,
-        pairs,
-        totals,
-        after(jnp.pad(grad_context, ((0, 0), (0, query_pad))), *mixer_sum.gives, *down_sum.advance()),
-        length,
-    )
-    grad_query_raw = grad_query_raw[:, :query_cols]
-    early_cols = jnp.concatenate([grad_gate_raw, grad_query_raw], axis=1)
-    early_sum = Sum(inner_rows(whole, early_cols).astype(jnp.bfloat16), dp_size, 2)
-    grad_gated = after(
-        grad_gated, *early_sum.gives, *mixer_sum.advance(), *wide_sum.advance()
-    )
-    grad_input_raw, grad_state_raw, grad_step_raw, input_sums, state_sums, head_sums = ssd_backward(
-        input_raw, state_raw, gate_raw, step_raw, grad_gated, carries, small, heads, length
-    )
-    input_sums = jnp.sum(input_sums, axis=0)
-    state_sums = jnp.sum(state_sums, axis=0)
-    head_sums = jnp.sum(head_sums, axis=0)[:, :heads]
-    taps = input_kernel.shape[0]
-    early_sum.advance()
-    mixer_sum.advance()
-    down_sum.advance()
-    wide_sum.advance()
-    grad_input_raw = after(
-        grad_input_raw, *early_sum.gives, *mixer_sum.gives, *down_sum.gives, *wide_sum.gives
-    )
-    grad_down = down_sum.finish()
-    grad_wide = wide_sum.finish()
-    grad_gate, grad_up = grad_wide[:, :hidden_cols], grad_wide[:, hidden_cols:]
-    late_cols = jnp.concatenate(
-        [grad_input_raw, grad_state_raw, grad_pair_raw, grad_step_raw], axis=1
-    )
-    total = against(early_cols, jnp.concatenate([mamba_gate, query_weight], axis=1))
+        queries, pairs, totals, after(grad_context, *late_sum.gives, *mixer_sum.advance()), length
+    )
+    early_cols = jnp.concatenate(
+        [grad_gate_raw, grad_query_raw[:, :query_cols], grad_pair_raw, grad_step_raw], axis=1
+    )
+    total = against(late_cols, jnp.concatenate([mamba_input, state_weight], axis=1))
     total = total + against(
-        late_cols, jnp.concatenate([mamba_input, state_weight, pair_weight, step_wide], axis=1)
+        early_cols, jnp.concatenate([mamba_gate, query_weight, pair_weight, step_wide], axis=1)
     )
     total_low = total.astype(jnp.bfloat16)
     grad_first = jnp.sum(total_low.astype(jnp.float32) * normal_first, axis=0)
-    width = whole.shape[1]
-    gate_cols = grad_gate_raw.shape[1]
-    input_cols = grad_input_raw.shape[1]
-    state_cols = grad_state_raw.shape[1]
-    step_cols = heads
-    pair_cols = grad_pair_raw.shape[1]
-
     own_vectors = (input_sums[:taps], input_sums[taps], head_sums[0], head_sums[1], head_sums[2])
     shared_vectors = (grad_first, grad_middle, state_sums[:taps], state_sums[taps])
     own_pack = column_pack(own_vectors, width)
     shared_pack = column_pack(shared_vectors, width)
     shared_lane = step_cols + own_pack.shape[1]
     last_lane = shared_lane + shared_pack.shape[1]
+    early = inner_rows(whole, early_cols)
+    if not split_pairs:
+        spread = jnp.zeros((width, 2 * KVH * HD), jnp.float32)
+        spread = lax.dynamic_update_slice_in_dim(
+            spread, early[:, -2 * HD - LANES : -HD - LANES], kv_head * HD, 1
+        )
+        spread = lax.dynamic_update_slice_in_dim(
+            spread, early[:, -HD - LANES : -LANES], (KVH + kv_head) * HD, 1
+        )
+        early = jnp.concatenate(
+            [early[:, : -2 * HD - LANES], spread, early[:, -LANES:]], axis=1
+        )
     packs = jnp.pad(
         jnp.concatenate([own_pack, shared_pack], axis=1),
-        ((0, 0), (step_cols, LANES - last_lane)),
-    )
-    split_pairs = shards == KVH
-    late = inner_rows(whole, late_cols)
-    marks = (input_cols, input_cols + state_cols, input_cols + state_cols + pair_cols)
-    late_pair = late[:, marks[1] : marks[2]]
-    if not split_pairs:
-        spread = jnp.zeros((width, 2 * KVH * HD), jnp.float32)
-        spread = lax.dynamic_update_slice_in_dim(spread, late_pair[:, :HD], kv_head * HD, 1)
-        late_pair = lax.dynamic_update_slice_in_dim(
-            spread, late_pair[:, HD:], (KVH + kv_head) * HD, 1
-        )
-        late = jnp.concatenate([late[:, : marks[1]], late_pair, late[:, marks[2] :]], axis=1)
-    misc = late.shape[1] - LANES
-    late = (late + jnp.pad(packs, ((0, 0), (misc, 0)))).astype(jnp.bfloat16)
-    late_sum = Sum(late, dp_size, 3)
-
-    def over_tensor(part):
-        own_part = part[:, input_cols:]
+        ((0, 0), (early.shape[1] - LANES + step_cols, LANES - last_lane)),
+    )
+    early_sum = Sum((early + packs).astype(jnp.bfloat16), dp_size)
+
+    def early_over_tensor(part):
+        count = (2 * HD if split_pairs else 2 * KVH * HD) + LANES
+        mine = part[:, -count:]
         if split_pairs:
-            got = other(own_part)
-            both = (own_part.astype(jnp.float32) + got.astype(jnp.float32)).astype(jnp.bfloat16)
+            got = other(mine)
+            both = (mine.astype(jnp.float32) + got.astype(jnp.float32)).astype(jnp.bfloat16)
             first = lax.axis_index("tensor") == 0
-            pair_span = slice(state_cols, state_cols + pair_cols)
-            low = jnp.where(first, own_part[:, pair_span], got[:, pair_span])
-            high = jnp.where(first, got[:, pair_span], own_part[:, pair_span])
-            pair = [low[:, :HD], high[:, :HD], low[:, HD:], high[:, HD:]]
+            low, high = jnp.where(first, mine, got), jnp.where(first, got, mine)
+            pair = [low[:, :HD], high[:, :HD], low[:, HD : 2 * HD], high[:, HD : 2 * HD]]
         else:
-            both = lax.psum(own_part, "tensor")
-            pair = [both[:, state_cols:-LANES]]
+            both = lax.psum(mine, "tensor")
+            pair = [both[:, :-LANES]]
         lane = lane_index((part.shape[0], LANES))
         extra = jnp.where(
-            (lane >= shared_lane) & (lane < last_lane), both[:, -LANES:], own_part[:, -LANES:]
+            (lane >= shared_lane) & (lane < last_lane), both[:, -LANES:], mine[:, -LANES:]
         )
-        return jnp.concatenate(
-            [part[:, :input_cols], both[:, :state_cols]] + pair + [extra], axis=1
-        )
-
-    grad_mixer_out = mixer_sum.finish()
+        return jnp.concatenate([part[:, :-count]] + pair + [extra], axis=1)
+
+    def late_over_tensor(part):
+        mine = part[:, -state_cols:]
+        if shards == 2:
+            both = mine.astype(jnp.float32) + other(mine).astype(jnp.float32)
+        else:
+            both = lax.psum(mine, "tensor")
+        return jnp.concatenate([part[:, :-state_cols], both.astype(jnp.bfloat16)], axis=1)
+
+    early_sum.advance()
+    tail = late_sum.joined(late_over_tensor, *early_sum.gives)
+    grad_mixer_out = mixer_sum.joined(None, *early_sum.gives)
+    early = early_sum.joined(early_over_tensor)
+    grad_gate, grad_up, grad_down = [
+        after(item, early_sum.trail[min(1, len(early_sum.trail) - 1)])
+        for item in (grad_gate, grad_up, grad_down)
+    ]
     grad_mamba_out = grad_mixer_out[:ssm_rows]
     grad_context_w = grad_mixer_out[ssm_rows:]
-    early = early_sum.finish()
-    tail = late_sum.finish(over_tensor)
-    grad_mamba_input = tail[:, :input_cols]
-    tail = tail[:, input_cols:]
+    grad_mamba_input, grad_state = tail[:, :-state_cols], tail[:, -state_cols:]
+    gate_cols = gate_raw.shape[1]
+    extra = early[:, -LANES:]
     back_in = sum_own(total_low, shards)
     normal_own = own_rows(normal_first, own)
     factor_own = own_rows(factor_first, own)
     input_grad = own_rows(grad_resid, own) + norm_back(back_in, gain_first, normal_own, factor_own)
-    extra = tail[:, state_cols + keyvalue_weight.shape[1] :]
     grad_step = extra[:, :step_cols]
     grad_in_kernel, grad_in_shift, grad_bias, grad_decay, grad_skip = column_unpack(
         extra[:, step_cols:shared_lane], [item.shape for item in own_vectors]
@@ -1075,7 +1082,7 @@
         early[:, :gate_cols],
         grad_mamba_input,
         grad_step,
-        tail[:, :state_cols],
+        grad_state,
         grad_in_kernel,
         grad_in_shift,
         grad_st_kernel,
@@ -1084,8 +1091,8 @@
         grad_decay,
         grad_skip,
         grad_mamba_out,
-        early[:, gate_cols:],
-        tail[:, state_cols : state_cols + keyvalue_weight.shape[1]],
+        early[:, gate_cols : gate_cols + query_cols],
+        early[:, gate_cols + query_cols : -LANES],
         grad_context_w,
         grad_gate,
         grad_up,

time: 448 us -> 374 us (0.83)
  waiting for transfers between devices: 167 us -> 129 us
  local copies, waits for them, and re-layouts: 57.4 us -> 36.2 us
  other arithmetic: 71.8 us -> 60.9 us
  matrix products: 44.6 us -> 35.4 us
  starting transfers between devices: 41 us -> 46.4 us
    all_gather x5 -> x0, waiting for transfers between devices: 43.6 us -> none  [finish(): lax.all_gather(part.reshape(lead + part.shape), 'dp', axis=self.place, ti...]
    ppermute x0 -> x15, waiting for transfers between devices: none -> 41.8 us  [joined(): got.append(lax.ppermute(part, 'dp', pairs))]
    ppermute x25 -> x15, waiting for transfers between devices: 70.2 us -> 41.2 us  [advance(): total = total + lax.ppermute(give, 'dp', pairs).astype(jnp.float32)]
    convert_element_type x14 -> x6, other arithmetic: 20 us -> 5.25 us  [advance(): self.part = total.astype(jnp.bfloat16)]
    ppermute x0 -> x15, starting transfers between devices: none -> 14.7 us  [joined(): got.append(lax.ppermute(part, 'dp', pairs))]
    ppermute x25 -> x15, starting transfers between devices: 30.9 us -> 22.1 us  [advance(): total = total + lax.ppermute(give, 'dp', pairs).astype(jnp.float32)]
    dot_general x5 -> x6, matrix products: 21.5 us -> 13.3 us  [inner_rows(): lax.dot_general(left, right, (((0,), (0,)), ((), ())), preferred_element_...]
    unnamed x220 -> x204, local copies, waits for them, and re-layouts: 21.8 us -> 13.8 us
  transfers between devices with their start and end apart: 37 -> 39, of which waited for: 19 -> 20; matrix products, arithmetic and copies ran while one was open for 27% -> 25% of each run, Pallas kernels for 6% -> 8%
where the time goes in v7:
time: 374 us; the launch traced here: 368 us
  waiting for transfers between devices  129 us (34%)
  other arithmetic  60.9 us (16%)
  starting transfers between devices  46.4 us (12%)
  Pallas kernels  43 us (11%)
  local copies, waits for them, and re-layouts  36.2 us (10%)
  matrix products  35.4 us (9%)
  between operations  16.9 us (5%)
    ppermute x8, waiting for transfers between devices, other(): return lax.ppermute(part, 'tensor', [(0, 1), (1, 0)])  46.4 us
    ppermute x15, waiting for transfers between devices, joined(): got.append(lax.ppermute(part, 'dp', pairs))  41.8 us
    ppermute x15, waiting for transfers between devices, advance(): total = total + lax.ppermute(give, 'dp', pairs).astype(jnp.float32)  41.2 us
    convert_element_type x15, other arithmetic, body(): item.astype(jnp.float32)  23.2 us
    pallas_call x1, Pallas kernels, ssd_backward(): pl.pallas_call(ssd_backward_kernel, grid=(seqs,), in_specs=[by_sequence(l...  22.3 us
    ppermute x15, starting transfers between devices, advance(): total = total + lax.ppermute(give, 'dp', pairs).astype(jnp.float32)  22.1 us
    ppermute x15, starting transfers between devices, joined(): got.append(lax.ppermute(part, 'dp', pairs))  14.7 us
    unnamed x204, local copies, waits for them, and re-layouts  13.8 us
  transfers between devices with their start and end apart: 39, of which 20 were waited for; matrix products, arithmetic and copies ran while one was open for 25% of the time, Pallas kernels for 8%

profile of v7, /device:TPU:0, one launch (start us, length us, event | category | flops | bytes accessed | tf_op | source)
XLA Modules:
  0.0 368.1 jit_solution(7515685649086137649)
XLA Ops:
  7.3 3.0 collective-permute-start
  17.3 5.9 %collective-permute-done = bf16[256,1024]{1,0:T(8,128)(2,1)S(1)} collective-permute-done((bf16[256,1024]{1,0:T(8,128)(2,1)}, bf16[256,1024]{1,0:T(8,128)(2,1)S(1)}, u32[]{:S(2)}, u32[]{:S(2)}) %collective-permute-start) | collective-permute-done | bytes 524320 | tf_op jit(solution)/shard_map/ppermute | solution.py:803
  23.3 1.8 fusion.1
  30.9 2.9 collective-permute-done.1
  33.8 2.6 maximum_select_fusion.1
  36.4 8.7 %ssd_forward.1 = (bf16[512,768]{1,0:T(8,128)(2,1)S(1)}, f32[512,768]{1,0:T(8,128)S(1)}, f32[4,128,768]{2,1,0:T(8,128)S(1)}) custom-call(f32[512,768]{1,0:T(8,128)S(1)} %fusion.41.input_ref, f32[512,256]{1,0:T(8,128)S(1)} %fusion.42.state_ref, f32[512,768]{1,0:T(8,128)S(1)} %fusion.43.gate_ref, f32[512,128]{1,0:T(8,128)S(1)} %fusion.24.step_ref, ...), custom_call_target="tpu_custom_call" | custom-call | flops 402653184 | bytes 7864320 | tf_op jit(solution)/shard_map/ssd_forward/pallas_call | solution.py:416
  47.1 5.7 %attend_forward.1 = (bf16[512,256]{1,0:T(8,128)(2,1)S(1)}, bf16[512,256]{1,0:T(8,128)(2,1)S(1)}, bf16[512,128]{1,0:T(8,128)(2,1)S(1)}, f32[512,128]{1,0:T(8,128)S(1)}) custom-call(f32[512,256]{1,0:T(8,128)S(1)} %fusion.45.query_ref, f32[512,128]{1,0:T(8,128)S(1)} %fusion.16.pair_ref, f32[512,128]{1,0:T(8,128)S(1)} %copy-done.13, f32[512,128]{1,0:T(8,128)S(1)} %copy-done.14), custom_call_target="tpu_custom_call" | custom-call | flops 268435456 | bytes 1572864 | tf_op jit(solution)/shard_map/attend_forward/pallas_call | solution.py:654
  54.9 1.8 collective-permute-start.2
  56.7 1.6 copy.99
  59.6 1.7 pad.25.clone
  61.3 5.3 %concatenate.82 = bf16[1024,1280]{1,0:T(8,128)(2,1)} concatenate(bf16[1024,768]{1,0:T(8,128)(2,1)} %param.32, bf16[1024,256]{1,0:T(8,128)(2,1)} %param.44, bf16[1024,64]{1,0:T(8,128)(2,1)} %copy-done.59, bf16[1024,64]{1,0:T(8,128)(2,1)} %copy-done.60, bf16[1024,128]{1,0:T(8,128)(2,1)} %pad.25.clone), dimensions={1} | concatenate | bytes 5242880 | tf_op jit(solution)/shard_map/concatenate | solution.py:1001
  66.7 13.0 %collective-permute-done.2 = bf16[512,1024]{1,0:T(8,128)(2,1)} collective-permute-done((bf16[512,1024]{1,0:T(8,128)(2,1)}, bf16[512,1024]{1,0:T(8,128)(2,1)}, u32[]{:S(2)}, u32[]{:S(2)}) %collective-permute-start.2) | collective-permute-done | bytes 1048608 | tf_op jit(solution)/shard_map/ppermute | solution.py:803
  79.7 2.8 multiply_reduce_fusion.2
  87.7 2.0 multiply_convert_fusion
  91.0 2.3 add_convert_fusion.6
  95.9 2.6 convolution_convert_fusion.2
  98.6 2.6 convolution_convert_fusion.1
  101.2 2.6 convolution_convert_fusion
  103.9 13.2 %collective-permute-done.3 = bf16[512,1024]{1,0:T(8,128)(2,1)} collective-permute-done((bf16[512,1024]{1,0:T(8,128)(2,1)}, bf16[512,1024]{1,0:T(8,128)(2,1)}, u32[]{:S(2)}, u32[]{:S(2)}) %collective-permute-start.3) | collective-permute-done | bytes 1048608 | tf_op jit(solution)/shard_map/ppermute | solution.py:803
  117.1 3.7 %fusion = (f32[1024]{0:T(1024)}, f32[512]{0:T(512)S(1)}) fusion(bf16[512,1024]{1,0:T(8,128)(2,1)} %add_convert_fusion.6, f32[512,1024]{1,0:T(8,128)} %copy-done.41, f32[512]{0:T(512)} %copy-done.84, f32[1024]{0:T(1024)} %convert_element_type.334, bf16[512,1024]{1,0:T(8,128)(2,1)} %collective-permute-done.3), kind=kLoop, calls=%fused_computation.8 | loop fusion | flops 4717056 | bytes 4206592 | tf_op jit(solution)/shard_map/reduce_sum | solution.py:952
  120.9 2.5 multiply_add_fusion
  130.9 1.6 dynamic-slice_bitcast_fusion.3
  134.0 22.3 %ssd_backward.1 = (bf16[512,768]{1,0:T(8,128)(2,1)S(1)}, bf16[512,256]{1,0:T(8,128)(2,1)S(1)}, bf16[512,128]{1,0:T(8,128)(2,1)S(1)}, f32[1,8,768]{2,1,0:T(8,128)...) custom-call(f32[512,768]{1,0:T(8,128)S(1)} %copy-done.7, f32[512,256]{1,0:T(8,128)S(1)} %fusion.42.state_ref, ...), custom_call_target="tpu_custom_call" | custom-call | flops 1006632960 | bytes 7864320 | tf_op jit(solution)/shard_map/ssd_backward/pallas_call | solution.py:465
  159.0 1.6 dynamic-slice_bitcast_fusion.2
  164.3 2.2 multiply_convert_fusion.5
  166.5 8.1 %collective-permute-done.4 = bf16[256,1024]{1,0:T(8,128)(2,1)} collective-permute-done((bf16[256,1024]{1,0:T(8,128)(2,1)}, bf16[256,1024]{1,0:T(8,128)(2,1)}, u32[]{:S(2)}, u32[]{:S(2)}) %collective-permute-start.4) | collective-permute-done | bytes 524320 | tf_op jit(solution)/shard_map/ppermute | solution.py:803
  174.6 2.1 fusion.15
  176.8 1.7 add_convert_fusion.4
  180.7 6.3 %attend_backward.1 = (bf16[512,256]{1,0:T(8,128)(2,1)S(1)}, bf16[512,128]{1,0:T(8,128)(2,1)S(1)}) custom-call(bf16[512,256]{1,0:T(8,128)(2,1)S(1)} %copy-done.34, bf16[512,128]{1,0:T(8,128)(2,1)S(1)} %copy-done.38, f32[512,128]{1,0:T(8,128)S(1)} %copy-done.36, bf16[512,256]{1,0:T(8,128)(2,1)S(1)} %copy-done.16, f32[512,128]{1,0:T(8,128)S(1)} %copy-done.13, ...), custom_call_target="tpu_custom_call" | custom-call | flops 671088640 | bytes 1572864 | tf_op jit(solution)/shard_map/attend_backward/pallas_call | solution.py:689
  189.2 2.8 multiply_reduce_fusion
  195.5 2.9 add_convert_fusion
  198.4 1.6 add_convert_fusion.2
  203.1 3.6 collective-permute-start.32
  206.7 12.3 %collective-permute-done.19 = bf16[4,64,1024]{2,1,0:T(8,128)(2,1)S(1)} collective-permute-done((bf16[4,64,1024]{2,1,0:T(8,128)(2,1)S(1)}, bf16[4,64,1024]{2,1,0:T(8,128)(2,1)S(1)}, u32[]{:S(2)}, u32[]{:S(2)}) %collective-permute-start.19) | collective-permute-done | bytes 524320 | tf_op jit(solution)/shard_map/ppermute | solution.py:763
  219.3 3.7 %collective-permute-start.22 = (bf16[1,64,1024]{2,1,0:T(8,128)(2,1)S(1)}, bf16[1,64,1024]{2,1,0:T(8,128)(2,1)S(1)}, u32[]{:S(2)}, u32[]{:S(2)}) collective-permute-start(bf16[1,64,1024]{2,1,0:T(8,128)(2,1)S(1)} %get-tuple-element.250), channel_id=1, source_target_pairs={{0,24},{2,26},{4,28},{6,30},{8,16},{10,18},{12,20},{14,22},{16,8},... | collective-permute-start | bytes 393224 | tf_op jit(solution)/shard_map/ppermute | solution.py:763
  224.0 6.2 %collective-permute-done.22 = bf16[1,64,1024]{2,1,0:T(8,128)(2,1)S(1)} collective-permute-done((bf16[1,64,1024]{2,1,0:T(8,128)(2,1)S(1)}, bf16[1,64,1024]{2,1,0:T(8,128)(2,1)S(1)}, u32[]{:S(2)}, u32[]{:S(2)}) %collective-permute-start.22) | collective-permute-done | bytes 131104 | tf_op jit(solution)/shard_map/ppermute | solution.py:763
  230.3 3.7 %collective-permute-start.31 = (bf16[1,64,1024]{2,1,0:T(8,128)(2,1)S(1)}, bf16[1,64,1024]{2,1,0:T(8,128)(2,1)S(1)}, u32[]{:S(2)}, u32[]{:S(2)}) collective-permute-start(bf16[1,64,1024]{2,1,0:T(8,128)(2,1)S(1)} %get-tuple-element.243), channel_id=1, source_target_pairs={{0,16},{2,18},{4,20},{6,22},{8,24},{10,26},{12,28},{14,30},{16,0},... | collective-permute-start | bytes 393224 | tf_op jit(solution)/shard_map/ppermute | solution.py:763
  233.9 4.3 %collective-permute-done.21 = bf16[1,64,1024]{2,1,0:T(8,128)(2,1)S(1)} collective-permute-done((bf16[1,64,1024]{2,1,0:T(8,128)(2,1)S(1)}, bf16[1,64,1024]{2,1,0:T(8,128)(2,1)S(1)}, u32[]{:S(2)}, u32[]{:S(2)}) %collective-permute-start.21) | collective-permute-done | bytes 131104 | tf_op jit(solution)/shard_map/ppermute | solution.py:763
  238.2 2.0 collective-permute-done.20
  240.9 5.0 %collective-permute-done.31 = bf16[1,64,1024]{2,1,0:T(8,128)(2,1)S(1)} collective-permute-done((bf16[1,64,1024]{2,1,0:T(8,128)(2,1)S(1)}, bf16[1,64,1024]{2,1,0:T(8,128)(2,1)S(1)}, u32[]{:S(2)}, u32[]{:S(2)}) %collective-permute-start.31) | collective-permute-done | bytes 131104 | tf_op jit(solution)/shard_map/ppermute | solution.py:763
  245.9 5.5 %collective-permute-done.30 = bf16[1,64,1024]{2,1,0:T(8,128)(2,1)S(1)} collective-permute-done((bf16[1,64,1024]{2,1,0:T(8,128)(2,1)S(1)}, bf16[1,64,1024]{2,1,0:T(8,128)(2,1)S(1)}, u32[]{:S(2)}, u32[]{:S(2)}) %collective-permute-start.30) | collective-permute-done | bytes 131104 | tf_op jit(solution)/shard_map/ppermute | solution.py:763
  252.3 3.9 %collective-permute-start.34 = (bf16[1,1,64,1024]{3,2,1,0:T(8,128)(2,1)S(1)}, bf16[1,1,64,1024]{3,2,1,0:T(8,128)(2,1)S(1)}, u32[]{:S(2)}, u32[]{:S(2)}) collective-permute-start(bf16[1,1,64,1024]{3,2,1,0:T(8,128)(2,1)S(1)} %bitcast.199), channel_id=1, source_target_pairs={{0,16},{2,18},{4,20},{6,22},{8,24},{10,26},{12,28},{14,30},{16,0},... | collective-permute-start | bytes 393224 | tf_op jit(solution)/shard_map/ppermute | solution.py:786
  257.8 4.5 %collective-permute-done.33 = bf16[1,1,64,1024]{3,2,1,0:T(8,128)(2,1)S(1)} collective-permute-done((bf16[1,1,64,1024]{3,2,1,0:T(8,128)(2,1)S(1)}, bf16[1,1,64,1024]{3,2,1,0:T(8,128)(2,1)S(1)}, u32[]{:S(2)}, u32[]{:S(2)}) %collective-permute-start.33) | collective-permute-done | bytes 131104 | tf_op jit(solution)/shard_map/ppermute | solution.py:786
  263.1 12.4 %collective-permute-done.34 = bf16[1,1,64,1024]{3,2,1,0:T(8,128)(2,1)S(1)} collective-permute-done((bf16[1,1,64,1024]{3,2,1,0:T(8,128)(2,1)S(1)}, bf16[1,1,64,1024]{3,2,1,0:T(8,128)(2,1)S(1)}, u32[]{:S(2)}, u32[]{:S(2)}) %collective-permute-start.34) | collective-permute-done | bytes 131104 | tf_op jit(solution)/shard_map/ppermute | solution.py:786
  276.9 7.3 %collective-permute-done.25 = bf16[1,1,64,1024]{3,2,1,0:T(8,128)(2,1)S(1)} collective-permute-done((bf16[1,1,64,1024]{3,2,1,0:T(8,128)(2,1)S(1)}, bf16[1,1,64,1024]{3,2,1,0:T(8,128)(2,1)S(1)}, u32[]{:S(2)}, u32[]{:S(2)}) %collective-permute-start.25) | collective-permute-done | bytes 131104 | tf_op jit(solution)/shard_map/ppermute | solution.py:786
  284.6 2.0 collective-permute-start.27
  287.0 2.3 collective-permute-start.11
  289.3 5.4 %collective-permute-start.10 = (bf16[1,64,1280]{2,1,0:T(8,128)(2,1)S(1)}, bf16[1,64,1280]{2,1,0:T(8,128)(2,1)S(1)}, u32[]{:S(2)}, u32[]{:S(2)}) collective-permute-start(bf16[1,64,1280]{2,1,0:T(8,128)(2,1)S(1)} %get-tuple-element.235), channel_id=1, source_target_pairs={{0,16},{2,18},{4,20},{6,22},{8,24},{10,26},{12,28},{14,30},{16,0},... | collective-permute-start | bytes 491528 | tf_op jit(solution)/shard_map/ppermute | solution.py:763
  294.7 4.7 %collective-permute-done.36 = bf16[4,1,64,1024]{3,2,1,0:T(8,128)(2,1)S(1)} collective-permute-done((bf16[4,1,64,1024]{3,2,1,0:T(8,128)(2,1)S(1)}, bf16[4,1,64,1024]{3,2,1,0:T(8,128)(2,1)S(1)}, u32[]{:S(2)}, u32[]{:S(2)}) %collective-permute-start.36) | collective-permute-done | bytes 524320 | tf_op jit(solution)/shard_map/ppermute | solution.py:786
  299.6 5.9 %collective-permute-done.10 = bf16[1,64,1280]{2,1,0:T(8,128)(2,1)S(1)} collective-permute-done((bf16[1,64,1280]{2,1,0:T(8,128)(2,1)S(1)}, bf16[1,64,1280]{2,1,0:T(8,128)(2,1)S(1)}, u32[]{:S(2)}, u32[]{:S(2)}) %collective-permute-start.10) | collective-permute-done | bytes 163872 | tf_op jit(solution)/shard_map/ppermute | solution.py:763
  306.3 3.2 collective-permute-done.12
  309.7 2.6 collective-permute-start.13
  312.3 1.9 collective-permute-start.15
  314.6 4.5 %collective-permute-done.13 = bf16[1,1,64,1408]{3,2,1,0:T(8,128)(2,1)S(1)} collective-permute-done((bf16[1,1,64,1408]{3,2,1,0:T(8,128)(2,1)S(1)}, bf16[1,1,64,1408]{3,2,1,0:T(8,128)(2,1)S(1)}, u32[]{:S(2)}, u32[]{:S(2)}) %collective-permute-start.13) | collective-permute-done | bytes 180256 | tf_op jit(solution)/shard_map/ppermute | solution.py:786
  319.1 5.9 %collective-permute-done.14 = bf16[1,1,64,1408]{3,2,1,0:T(8,128)(2,1)S(1)} collective-permute-done((bf16[1,1,64,1408]{3,2,1,0:T(8,128)(2,1)S(1)}, bf16[1,1,64,1408]{3,2,1,0:T(8,128)(2,1)S(1)}, u32[]{:S(2)}, u32[]{:S(2)}) %collective-permute-start.14) | collective-permute-done | bytes 180256 | tf_op jit(solution)/shard_map/ppermute | solution.py:786
  325.3 1.6 collective-permute-start.16
  326.9 4.2 %convert_element_type.422 = f32[1024,1024]{1,0:T(8,128)} convert(bf16[1024,1024]{1,0:T(8,128)(2,1)} %get-tuple-element.69) | non-fusion elementwise | flops 1048576 | bytes 6291456 | tf_op jit(solution)/shard_map/convert_element_type | solution.py:1101
  331.1 2.5 convert_element_type.424
  333.6 2.5 convert_element_type.426
  339.0 2.4 collective-permute-done.16
  345.4 1.9 slice_convert_fusion
  347.4 2.2 bitcast_convert_fusion
  350.7 2.2 slice_convert_fusion.1
  355.7 2.7 slice_convert_fusion.2
  (362 shorter events, 74.6 us)
Async XLA Ops:
  7.2 80.5 %copy-start = (bf16[1024,1024]{1,0:T(8,128)(2,1)S(1)}, bf16[1024,1024]{1,0:T(8,128)(2,1)}, u32[]{:S(2)}) copy-start(bf16[1024,1024]{1,0:T(8,128)(2,1)} %param.49) | copy-start | bytes 6291460
  7.2 17.9 %copy-start.50 = (bf16[256,1024]{1,0:T(8,128)(2,1)S(1)}, bf16[256,1024]{1,0:T(8,128)(2,1)}, u32[]{:S(2)}) copy-start(bf16[256,1024]{1,0:T(8,128)(2,1)} %param.29) | copy-start | bytes 1572868
  7.2 319.7 %all-reduce.9.cloned.1.call-start = ((), (), s32[]{:S(2)}) async-start(), calls=%async_computation | async-start | bytes 12582912 | tf_op jit(solution)/shard_map/psum | solution.py:948
  7.3 16.0 %collective-permute-start = (bf16[256,1024]{1,0:T(8,128)(2,1)}, bf16[256,1024]{1,0:T(8,128)(2,1)S(1)}, u32[]{:S(2)}, u32[]{:S(2)}) collective-permute-start(bf16[256,1024]{1,0:T(8,128)(2,1)} %param.29), channel_id=1, source_target_pairs={{0,1},{1,0},{2,3},{3,2},{4,5},{5,4},{6,7},{7,6},{8,9},{9,8},{10,11... | collective-permute-start | bytes 1572872 | tf_op jit(solution)/shard_map/ppermute | solution.py:803
  10.3 23.5 %collective-permute-start.1 = (bf16[256,1024]{1,0:T(8,128)(2,1)}, bf16[256,1024]{1,0:T(8,128)(2,1)}, u32[]{:S(2)}, u32[]{:S(2)}) collective-permute-start(bf16[256,1024]{1,0:T(8,128)(2,1)} %param.50), channel_id=1, source_target_pairs={{0,1},{1,0},{2,3},{3,2},{4,5},{5,4},{6,7},{7,6},{8,9},{9,8},{10,11... | collective-permute-start | bytes 1572872 | tf_op jit(solution)/shard_map/ppermute | solution.py:803
  11.1 14.4 %copy-start.80 = (f32[1024]{0:T(1024)}, f32[1024]{0:T(1024)S(1)}, u32[]{:S(2)}) copy-start(f32[1024]{0:T(1024)S(1)} %convert_element_type.325) | copy-start | bytes 12292
  12.4 23.9 %copy-start.19 = (f32[1,768]{1,0:T(1,128)}, f32[1,768]{1,0:T(1,128)S(1)}, u32[]{:S(2)}) copy-start(f32[1,768]{1,0:T(1,128)S(1)} %reshape.238.input_shift_ref) | copy-start | bytes 9220
  13.8 22.6 %copy-start.24 = (f32[256]{0:T(256)}, f32[256]{0:T(256)S(1)}, u32[]{:S(2)}) copy-start(f32[256]{0:T(256)S(1)} %broadcast_in_dim.36) | copy-start | bytes 3076
  14.6 21.8 %copy-start.21 = (f32[1,768]{1,0:T(1,128)}, f32[1,768]{1,0:T(1,128)S(1)}, u32[]{:S(2)}) copy-start(f32[1,768]{1,0:T(1,128)S(1)} %broadcast_in_dim_reshape.3.skip_ref) | copy-start | bytes 9220
  15.3 21.1 %copy-start.26 = (f32[1,128]{1,0:T(1,128)}, f32[1,128]{1,0:T(1,128)S(1)}, u32[]{:S(2)}) copy-start(f32[1,128]{1,0:T(1,128)S(1)} %pad.28.rate_ref) | copy-start | bytes 1540
  16.0 20.5 %copy-start.28 = (f32[1,128]{1,0:T(1,128)}, f32[1,128]{1,0:T(1,128)S(1)}, u32[]{:S(2)}) copy-start(f32[1,128]{1,0:T(1,128)S(1)} %pad_convert_fusion.bias_ref) | copy-start | bytes 1540
  17.3 29.2 %copy-start.59 = (bf16[1024,64]{1,0:T(8,128)(2,1)}, bf16[1024,64]{1,0:T(8,128)(2,1)S(1)}, u32[]{:S(2)}) copy-start(bf16[1024,64]{1,0:T(8,128)(2,1)S(1)} %get-tuple-element.253) | copy-start | bytes 393220
  17.3 29.2 %copy-start.60 = (bf16[1024,64]{1,0:T(8,128)(2,1)}, bf16[1024,64]{1,0:T(8,128)(2,1)S(1)}, u32[]{:S(2)}) copy-start(bf16[1024,64]{1,0:T(8,128)(2,1)S(1)} %get-tuple-element.254) | copy-start | bytes 393220
  25.7 20.9 %copy-start.44 = (bf16[512,1024]{1,0:T(8,128)(2,1)}, bf16[512,1024]{1,0:T(8,128)(2,1)S(1)}, u32[]{:S(2)}) copy-start(bf16[512,1024]{1,0:T(8,128)(2,1)S(1)} %multiply_convert_fusion.4) | copy-start | bytes 3145732
  30.9 14.3 %copy-start.2 = (f32[512,768]{1,0:T(8,128)}, f32[512,768]{1,0:T(8,128)S(1)}, u32[]{:S(2)}) copy-start(f32[512,768]{1,0:T(8,128)S(1)} %fusion.43.gate_ref) | copy-start | bytes 4718596
  54.9 24.7 %collective-permute-start.2 = (bf16[512,1024]{1,0:T(8,128)(2,1)}, bf16[512,1024]{1,0:T(8,128)(2,1)}, u32[]{:S(2)}, u32[]{:S(2)}) collective-permute-start(bf16[512,1024]{1,0:T(8,128)(2,1)} %add_convert_fusion.7), channel_id=1, source_target_pairs={{0,1},{1,0},{2,3},{3,2},{4,5},{5,4},{6,7},{7,6},{8,9},{9,8},{10,11... | collective-permute-start | bytes 3145736 | tf_op jit(solution)/shard_map/ppermute | solution.py:803
  66.7 17.2 %copy-start.82 = (f32[1024]{0:T(1024)S(1)}, f32[1024]{0:T(1024)}, u32[]{:S(2)}) copy-start(f32[1024]{0:T(1024)} %convert_element_type.334) | copy-start | bytes 12292
  89.7 11.4 %copy-start.96 = (bf16[512,1024]{1,0:T(8,128)(2,1)}, bf16[512,1024]{1,0:T(8,128)(2,1)S(1)}, u32[]{:S(2)}) copy-start(bf16[512,1024]{1,0:T(8,128)(2,1)S(1)} %get-tuple-element.50) | copy-start | bytes 3145732
  93.3 23.7 %collective-permute-start.3 = (bf16[512,1024]{1,0:T(8,128)(2,1)}, bf16[512,1024]{1,0:T(8,128)(2,1)}, u32[]{:S(2)}, u32[]{:S(2)}) collective-permute-start(bf16[512,1024]{1,0:T(8,128)(2,1)} %add_convert_fusion.6), channel_id=1, source_target_pairs={{0,1},{1,0},{2,3},{3,2},{4,5},{5,4},{6,7},{7,6},{8,9},{9,8},{10,11... | collective-permute-start | bytes 3145736 | tf_op jit(solution)/shard_map/ppermute | solution.py:803
  103.8 17.0 %copy-start.42 = (f32[512,1024]{1,0:T(8,128)S(1)}, f32[512,1024]{1,0:T(8,128)}, u32[]{:S(2)}) copy-start(f32[512,1024]{1,0:T(8,128)} %copy-done.41) | copy-start | bytes 6291460
  103.8 17.0 %copy-start.57 = (bf16[512,1024]{1,0:T(8,128)(2,1)S(1)}, bf16[512,1024]{1,0:T(8,128)(2,1)}, u32[]{:S(2)}) copy-start(bf16[512,1024]{1,0:T(8,128)(2,1)} %maximum_select_fusion.1) | copy-start | bytes 3145732
  103.8 17.0 %copy-start.83 = (f32[1024]{0:T(1024)S(1)}, f32[1024]{0:T(1024)}, u32[]{:S(2)}) copy-start(f32[1024]{0:T(1024)} %convert_element_type.334) | copy-start | bytes 12292
  103.8 17.0 %copy-start.85 = (f32[512]{0:T(512)S(1)}, f32[512]{0:T(512)}, u32[]{:S(2)}) copy-start(f32[512]{0:T(512)} %copy-done.84) | copy-start | bytes 6148
  130.8 29.8 %copy-start.71 = (bf16[512,1024]{1,0:T(8,128)(2,1)}, bf16[512,1024]{1,0:T(8,128)(2,1)S(1)}, u32[]{:S(2)}) copy-start(bf16[512,1024]{1,0:T(8,128)(2,1)S(1)} %add_convert_fusion.5) | copy-start | bytes 3145732
  132.5 44.3 %collective-permute-start.5 = (bf16[8,64,1024]{2,1,0:T(8,128)(2,1)}, bf16[8,64,1024]{2,1,0:T(8,128)(2,1)}, u32[]{:S(2)}, u32[]{:S(2)}) collective-permute-start(bf16[8,64,1024]{2,1,0:T(8,128)(2,1)} %get-tuple-element.210), channel_id=1, source_target_pairs={{0,2},{2,0},{4,6},{6,4},{8,10},{10,8},{12,14},{14,12},{16,18},{18,... | collective-permute-start | bytes 3145736 | tf_op jit(solution)/shard_map/ppermute | solution.py:763
  161.4 13.2 %collective-permute-start.4 = (bf16[256,1024]{1,0:T(8,128)(2,1)}, bf16[256,1024]{1,0:T(8,128)(2,1)}, u32[]{:S(2)}, u32[]{:S(2)}) collective-permute-start(bf16[256,1024]{1,0:T(8,128)(2,1)} %dynamic-slice_bitcast_fusion.13), channel_id=1, source_target_pairs={{0,1},{1,0},{2,3},{3,2},{4,5},{5,4},{6,7},{7,6},{8,9},{9,8},{10,11... | collective-permute-start | bytes 1572872 | tf_op jit(solution)/shard_map/ppermute | solution.py:803
  164.2 34.2 %collective-permute-start.18 = (bf16[8,64,1024]{2,1,0:T(8,128)(2,1)}, bf16[8,64,1024]{2,1,0:T(8,128)(2,1)}, u32[]{:S(2)}, u32[]{:S(2)}) collective-permute-start(bf16[8,64,1024]{2,1,0:T(8,128)(2,1)} %get-tuple-element.208), channel_id=1, source_target_pairs={{0,2},{2,0},{4,6},{6,4},{8,10},{10,8},{12,14},{14,12},{16,18},{18,... | collective-permute-start | bytes 3145736 | tf_op jit(solution)/shard_map/ppermute | solution.py:763
  164.3 10.4 %copy-start.43 = (f32[512,1024]{1,0:T(8,128)S(1)}, f32[512,1024]{1,0:T(8,128)}, u32[]{:S(2)}) copy-start(f32[512,1024]{1,0:T(8,128)} %copy-done.41) | copy-start | bytes 6291460
  166.5 20.5 %copy-start.73 = (bf16[512,768]{1,0:T(8,128)(2,1)}, bf16[512,768]{1,0:T(8,128)(2,1)S(1)}, u32[]{:S(2)}) copy-start(bf16[512,768]{1,0:T(8,128)(2,1)S(1)} %multiply_convert_fusion.5) | copy-start | bytes 2359300
  179.6 21.5 %collective-permute-start.29 = (bf16[4,64,1024]{2,1,0:T(8,128)(2,1)}, bf16[4,64,1024]{2,1,0:T(8,128)(2,1)}, u32[]{:S(2)}, u32[]{:S(2)}) collective-permute-start(bf16[4,64,1024]{2,1,0:T(8,128)(2,1)} %get-tuple-element.222), channel_id=1, source_target_pairs={{0,4},{2,6},{4,0},{6,2},{8,12},{10,14},{12,8},{14,10},{16,20},{18,... | collective-permute-start | bytes 1572872 | tf_op jit(solution)/shard_map/ppermute | solution.py:763
  192.9 30.1 %collective-permute-start.6 = (bf16[256,1024]{1,0:T(8,128)(2,1)}, bf16[256,1024]{1,0:T(8,128)(2,1)S(1)}, u32[]{:S(2)}, u32[]{:S(2)}) collective-permute-start(bf16[256,1024]{1,0:T(8,128)(2,1)} %dynamic-slice_bitcast_fusion.11), channel_id=1, source_target_pairs={{0,1},{1,0},{2,3},{3,2},{4,5},{5,4},{6,7},{7,6},{8,9},{9,8},{10,11... | collective-permute-start | bytes 1572872 | tf_op jit(solution)/shard_map/ppermute | solution.py:803
  200.1 18.9 %collective-permute-start.19 = (bf16[4,64,1024]{2,1,0:T(8,128)(2,1)S(1)}, bf16[4,64,1024]{2,1,0:T(8,128)(2,1)S(1)}, u32[]{:S(2)}, u32[]{:S(2)}) collective-permute-start(bf16[4,64,1024]{2,1,0:T(8,128)(2,1)S(1)} %get-tuple-element.226), channel_id=1, source_target_pairs={{0,4},{2,6},{4,0},{6,2},{8,12},{10,14},{12,8},{14,10},{16,20},{18,... | collective-permute-start | bytes 1572872 | tf_op jit(solution)/shard_map/ppermute | solution.py:763
  201.0 39.4 %collective-permute-start.7 = (bf16[8,64,1280]{2,1,0:T(8,128)(2,1)S(1)}, bf16[8,64,1280]{2,1,0:T(8,128)(2,1)S(1)}, u32[]{:S(2)}, u32[]{:S(2)}) collective-permute-start(bf16[8,64,1280]{2,1,0:T(8,128)(2,1)S(1)} %get-tuple-element.202), channel_id=1, source_target_pairs={{0,2},{2,0},{4,6},{6,4},{8,10},{10,8},{12,14},{14,12},{16,18},{18,... | collective-permute-start | bytes 3932168 | tf_op jit(solution)/shard_map/ppermute | solution.py:763
  203.0 20.7 %copy-start.63 = (f32[512,1024]{1,0:T(8,128)S(1)}, f32[512,1024]{1,0:T(8,128)}, u32[]{:S(2)}) copy-start(f32[512,1024]{1,0:T(8,128)} %get-tuple-element.218) | copy-start | bytes 6291460
  203.0 20.7 %copy-start.81 = (f32[1024]{0:T(1024)S(1)}, f32[1024]{0:T(1024)}, u32[]{:S(2)}) copy-start(f32[1024]{0:T(1024)} %copy-done.80) | copy-start | bytes 12292
  203.1 37.8 %collective-permute-start.32 = (bf16[1,64,1024]{2,1,0:T(8,128)(2,1)S(1)}, bf16[1,64,1024]{2,1,0:T(8,128)(2,1)S(1)}, u32[]{:S(2)}, u32[]{:S(2)}) collective-permute-start(bf16[1,64,1024]{2,1,0:T(8,128)(2,1)S(1)} %get-tuple-element.242), channel_id=1, source_target_pairs={{0,24},{2,26},{4,28},{6,30},{8,16},{10,18},{12,20},{14,22},{16,8},... | collective-permute-start | bytes 393224 | tf_op jit(solution)/shard_map/ppermute | solution.py:763
  219.3 11.0 %collective-permute-start.22 = (bf16[1,64,1024]{2,1,0:T(8,128)(2,1)S(1)}, bf16[1,64,1024]{2,1,0:T(8,128)(2,1)S(1)}, u32[]{:S(2)}, u32[]{:S(2)}) collective-permute-start(bf16[1,64,1024]{2,1,0:T(8,128)(2,1)S(1)} %get-tuple-element.250), channel_id=1, source_target_pairs={{0,24},{2,26},{4,28},{6,30},{8,16},{10,18},{12,20},{14,22},{16,8},... | collective-permute-start | bytes 393224 | tf_op jit(solution)/shard_map/ppermute | solution.py:763
  223.0 15.3 %collective-permute-start.21 = (bf16[1,64,1024]{2,1,0:T(8,128)(2,1)S(1)}, bf16[1,64,1024]{2,1,0:T(8,128)(2,1)S(1)}, u32[]{:S(2)}, u32[]{:S(2)}) collective-permute-start(bf16[1,64,1024]{2,1,0:T(8,128)(2,1)S(1)} %get-tuple-element.251), channel_id=1, source_target_pairs={{0,16},{2,18},{4,20},{6,22},{8,24},{10,26},{12,28},{14,30},{16,0},... | collective-permute-start | bytes 393224 | tf_op jit(solution)/shard_map/ppermute | solution.py:763
  223.0 17.3 %collective-permute-start.20 = (bf16[1,64,1024]{2,1,0:T(8,128)(2,1)S(1)}, bf16[1,64,1024]{2,1,0:T(8,128)(2,1)S(1)}, u32[]{:S(2)}, u32[]{:S(2)}) collective-permute-start(bf16[1,64,1024]{2,1,0:T(8,128)(2,1)S(1)} %get-tuple-element.252), channel_id=1, source_target_pairs={{0,8},{2,10},{4,12},{6,14},{8,0},{10,2},{12,4},{14,6},{16,24},{18,... | collective-permute-start | bytes 393224 | tf_op jit(solution)/shard_map/ppermute | solution.py:763
  230.3 15.6 %collective-permute-start.31 = (bf16[1,64,1024]{2,1,0:T(8,128)(2,1)S(1)}, bf16[1,64,1024]{2,1,0:T(8,128)(2,1)S(1)}, u32[]{:S(2)}, u32[]{:S(2)}) collective-permute-start(bf16[1,64,1024]{2,1,0:T(8,128)(2,1)S(1)} %get-tuple-element.243), channel_id=1, source_target_pairs={{0,16},{2,18},{4,20},{6,22},{8,24},{10,26},{12,28},{14,30},{16,0},... | collective-permute-start | bytes 393224 | tf_op jit(solution)/shard_map/ppermute | solution.py:763
  238.2 13.2 %collective-permute-start.30 = (bf16[1,64,1024]{2,1,0:T(8,128)(2,1)S(1)}, bf16[1,64,1024]{2,1,0:T(8,128)(2,1)S(1)}, u32[]{:S(2)}, u32[]{:S(2)}) collective-permute-start(bf16[1,64,1024]{2,1,0:T(8,128)(2,1)S(1)} %get-tuple-element.244), channel_id=1, source_target_pairs={{0,8},{2,10},{4,12},{6,14},{8,0},{10,2},{12,4},{14,6},{16,24},{18,... | collective-permute-start | bytes 393224 | tf_op jit(solution)/shard_map/ppermute | solution.py:763
  240.7 34.8 %copy-start.48 = (f32[512,1024]{1,0:T(8,128)S(1)}, f32[512,1024]{1,0:T(8,128)}, u32[]{:S(2)}) copy-start(f32[512,1024]{1,0:T(8,128)} %copy-done.47) | copy-start | bytes 6291460
  240.7 34.8 %copy-start.90 = (f32[256]{0:T(256)S(1)}, f32[256]{0:T(256)}, u32[]{:S(2)}) copy-start(f32[256]{0:T(256)} %dynamic-slice.15) | copy-start | bytes 3076
  240.8 15.9 %collective-permute-start.23 = (bf16[64,256]{1,0:T(8,128)(2,1)S(1)}, bf16[64,256]{1,0:T(8,128)(2,1)S(1)}, u32[]{:S(2)}, u32[]{:S(2)}) collective-permute-start(bf16[64,256]{1,0:T(8,128)(2,1)S(1)} %slice.151), channel_id=1, source_target_pairs={{0,1},{1,0},{2,3},{3,2},{4,5},{5,4},{6,7},{7,6},{8,9},{9,8},{10,11... | collective-permute-start | bytes 98312 | tf_op jit(solution)/shard_map/ppermute | solution.py:803
  251.5 35.3 %collective-permute-start.8 = (bf16[4,64,1280]{2,1,0:T(8,128)(2,1)S(1)}, bf16[4,64,1280]{2,1,0:T(8,128)(2,1)S(1)}, u32[]{:S(2)}, u32[]{:S(2)}) collective-permute-start(bf16[4,64,1280]{2,1,0:T(8,128)(2,1)S(1)} %get-tuple-element.216), channel_id=1, source_target_pairs={{0,4},{2,6},{4,0},{6,2},{8,12},{10,14},{12,8},{14,10},{16,20},{18,... | collective-permute-start | bytes 1966088 | tf_op jit(solution)/shard_map/ppermute | solution.py:763
  252.3 10.0 %collective-permute-start.33 = (bf16[1,1,64,1024]{3,2,1,0:T(8,128)(2,1)S(1)}, bf16[1,1,64,1024]{3,2,1,0:T(8,128)(2,1)S(1)}, u32[]{:S(2)}, u32[]{:S(2)}) collective-permute-start(bf16[1,1,64,1024]{3,2,1,0:T(8,128)(2,1)S(1)} %bitcast.198), channel_id=1, source_target_pairs={{0,24},{2,26},{4,28},{6,30},{8,16},{10,18},{12,20},{14,22},{16,8},... | collective-permute-start | bytes 393224 | tf_op jit(solution)/shard_map/ppermute | solution.py:786
  252.3 23.2 %collective-permute-start.34 = (bf16[1,1,64,1024]{3,2,1,0:T(8,128)(2,1)S(1)}, bf16[1,1,64,1024]{3,2,1,0:T(8,128)(2,1)S(1)}, u32[]{:S(2)}, u32[]{:S(2)}) collective-permute-start(bf16[1,1,64,1024]{3,2,1,0:T(8,128)(2,1)S(1)} %bitcast.199), channel_id=1, source_target_pairs={{0,16},{2,18},{4,20},{6,22},{8,24},{10,26},{12,28},{14,30},{16,0},... | collective-permute-start | bytes 393224 | tf_op jit(solution)/shard_map/ppermute | solution.py:786
  256.2 20.6 %collective-permute-start.35 = (bf16[1,1,64,1024]{3,2,1,0:T(8,128)(2,1)S(1)}, bf16[1,1,64,1024]{3,2,1,0:T(8,128)(2,1)S(1)}, u32[]{:S(2)}, u32[]{:S(2)}) collective-permute-start(bf16[1,1,64,1024]{3,2,1,0:T(8,128)(2,1)S(1)} %bitcast.200), channel_id=1, source_target_pairs={{0,8},{2,10},{4,12},{6,14},{8,0},{10,2},{12,4},{14,6},{16,24},{18,... | collective-permute-start | bytes 393224 | tf_op jit(solution)/shard_map/ppermute | solution.py:786
  256.8 27.4 %collective-permute-start.25 = (bf16[1,1,64,1024]{3,2,1,0:T(8,128)(2,1)S(1)}, bf16[1,1,64,1024]{3,2,1,0:T(8,128)(2,1)S(1)}, u32[]{:S(2)}, u32[]{:S(2)}) collective-permute-start(bf16[1,1,64,1024]{3,2,1,0:T(8,128)(2,1)S(1)} %maximum_bitcast_fusion.2), channel_id=1, source_target_pairs={{0,16},{2,18},{4,20},{6,22},{8,24},{10,26},{12,28},{14,30},{16,0},... | collective-permute-start | bytes 393224 | tf_op jit(solution)/shard_map/ppermute | solution.py:786
  262.3 21.9 %collective-permute-start.24 = (bf16[1,1,64,1024]{3,2,1,0:T(8,128)(2,1)S(1)}, bf16[1,1,64,1024]{3,2,1,0:T(8,128)(2,1)S(1)}, u32[]{:S(2)}, u32[]{:S(2)}) collective-permute-start(bf16[1,1,64,1024]{3,2,1,0:T(8,128)(2,1)S(1)} %maximum_bitcast_fusion.2), channel_id=1, source_target_pairs={{0,24},{2,26},{4,28},{6,30},{8,16},{10,18},{12,20},{14,22},{16,8},... | collective-permute-start | bytes 393224 | tf_op jit(solution)/shard_map/ppermute | solution.py:786
  275.5 8.7 %collective-permute-start.26 = (bf16[1,1,64,1024]{3,2,1,0:T(8,128)(2,1)S(1)}, bf16[1,1,64,1024]{3,2,1,0:T(8,128)(2,1)S(1)}, u32[]{:S(2)}, u32[]{:S(2)}) collective-permute-start(bf16[1,1,64,1024]{3,2,1,0:T(8,128)(2,1)S(1)} %maximum_bitcast_fusion.2), channel_id=1, source_target_pairs={{0,8},{2,10},{4,12},{6,14},{8,0},{10,2},{12,4},{14,6},{16,24},{18,... | collective-permute-start | bytes 393224 | tf_op jit(solution)/shard_map/ppermute | solution.py:786
  284.6 29.6 %collective-permute-start.27 = (bf16[4,1,64,1024]{3,2,0,1:T(8,128)(2,1)S(1)}, bf16[4,1,64,1024]{3,2,0,1:T(8,128)(2,1)S(1)}, u32[]{:S(2)}, u32[]{:S(2)}) collective-permute-start(bf16[4,1,64,1024]{3,2,0,1:T(8,128)(2,1)S(1)} %maximum_bitcast_fusion), channel_id=1, source_target_pairs={{0,4},{2,6},{4,0},{6,2},{8,12},{10,14},{12,8},{14,10},{16,20},{18,... | collective-permute-start | bytes 1572872 | tf_op jit(solution)/shard_map/ppermute | solution.py:786
  286.6 12.8 %collective-permute-start.36 = (bf16[4,1,64,1024]{3,2,1,0:T(8,128)(2,1)S(1)}, bf16[4,1,64,1024]{3,2,1,0:T(8,128)(2,1)S(1)}, u32[]{:S(2)}, u32[]{:S(2)}) collective-permute-start(bf16[4,1,64,1024]{3,2,1,0:T(8,128)(2,1)S(1)} %maximum_bitcast_fusion.1), channel_id=1, source_target_pairs={{0,4},{2,6},{4,0},{6,2},{8,12},{10,14},{12,8},{14,10},{16,20},{18,... | collective-permute-start | bytes 1572872 | tf_op jit(solution)/shard_map/ppermute | solution.py:786
  287.0 12.5 %collective-permute-start.11 = (bf16[1,64,1280]{2,1,0:T(8,128)(2,1)S(1)}, bf16[1,64,1280]{2,1,0:T(8,128)(2,1)S(1)}, u32[]{:S(2)}, u32[]{:S(2)}) collective-permute-start(bf16[1,64,1280]{2,1,0:T(8,128)(2,1)S(1)} %get-tuple-element.234), channel_id=1, source_target_pairs={{0,24},{2,26},{4,28},{6,30},{8,16},{10,18},{12,20},{14,22},{16,8},... | collective-permute-start | bytes 491528 | tf_op jit(solution)/shard_map/ppermute | solution.py:763
  289.3 16.1 %collective-permute-start.10 = (bf16[1,64,1280]{2,1,0:T(8,128)(2,1)S(1)}, bf16[1,64,1280]{2,1,0:T(8,128)(2,1)S(1)}, u32[]{:S(2)}, u32[]{:S(2)}) collective-permute-start(bf16[1,64,1280]{2,1,0:T(8,128)(2,1)S(1)} %get-tuple-element.235), channel_id=1, source_target_pairs={{0,16},{2,18},{4,20},{6,22},{8,24},{10,26},{12,28},{14,30},{16,0},... | collective-permute-start | bytes 491528 | tf_op jit(solution)/shard_map/ppermute | solution.py:763
  294.7 10.7 %collective-permute-start.9 = (bf16[1,64,1280]{2,1,0:T(8,128)(2,1)S(1)}, bf16[1,64,1280]{2,1,0:T(8,128)(2,1)S(1)}, u32[]{:S(2)}, u32[]{:S(2)}) collective-permute-start(bf16[1,64,1280]{2,1,0:T(8,128)(2,1)S(1)} %get-tuple-element.236), channel_id=1, source_target_pairs={{0,8},{2,10},{4,12},{6,14},{8,0},{10,2},{12,4},{14,6},{16,24},{18,... | collective-permute-start | bytes 491528 | tf_op jit(solution)/shard_map/ppermute | solution.py:763
  305.5 4.0 %collective-permute-start.12 = (bf16[64,256]{1,0:T(8,128)(2,1)S(1)}, bf16[64,256]{1,0:T(8,128)(2,1)S(1)}, u32[]{:S(2)}, u32[]{:S(2)}) collective-permute-start(bf16[64,256]{1,0:T(8,128)(2,1)S(1)} %slice.169), channel_id=1, source_target_pairs={{0,1},{1,0},{2,3},{3,2},{4,5},{5,4},{6,7},{7,6},{8,9},{9,8},{10,11... | collective-permute-start | bytes 98312 | tf_op jit(solution)/shard_map/ppermute | solution.py:803
  306.2 29.8 %collective-permute-start.37 = (bf16[8,1,64,1024]{3,2,1,0:T(8,128)(2,1)S(1)}, bf16[8,1,64,1024]{3,2,1,0:T(8,128)(2,1)}, u32[]{:S(2)}, u32[]{:S(2)}) collective-permute-start(bf16[8,1,64,1024]{3,2,1,0:T(8,128)(2,1)S(1)} %bitcast.181), channel_id=1, source_target_pairs={{0,2},{2,0},{4,6},{6,4},{8,10},{10,8},{12,14},{14,12},{16,18},{18,... | collective-permute-start | bytes 3145736 | tf_op jit(solution)/shard_map/ppermute | solution.py:786
  309.7 9.4 %collective-permute-start.13 = (bf16[1,1,64,1408]{3,2,1,0:T(8,128)(2,1)S(1)}, bf16[1,1,64,1408]{3,2,1,0:T(8,128)(2,1)S(1)}, u32[]{:S(2)}, u32[]{:S(2)}) collective-permute-start(bf16[1,1,64,1408]{3,2,1,0:T(8,128)(2,1)S(1)} %bitcast.195), channel_id=1, source_target_pairs={{0,24},{2,26},{4,28},{6,30},{8,16},{10,18},{12,20},{14,22},{16,8},... | collective-permute-start | bytes 540680 | tf_op jit(solution)/shard_map/ppermute | solution.py:786
  312.3 12.7 %collective-permute-start.14 = (bf16[1,1,64,1408]{3,2,1,0:T(8,128)(2,1)S(1)}, bf16[1,1,64,1408]{3,2,1,0:T(8,128)(2,1)S(1)}, u32[]{:S(2)}, u32[]{:S(2)}) collective-permute-start(bf16[1,1,64,1408]{3,2,1,0:T(8,128)(2,1)S(1)} %bitcast.196), channel_id=1, source_target_pairs={{0,16},{2,18},{4,20},{6,22},{8,24},{10,26},{12,28},{14,30},{16,0},... | collective-permute-start | bytes 540680 | tf_op jit(solution)/shard_map/ppermute | solution.py:786
  312.3 12.7 %collective-permute-start.15 = (bf16[1,1,64,1408]{3,2,1,0:T(8,128)(2,1)S(1)}, bf16[1,1,64,1408]{3,2,1,0:T(8,128)(2,1)S(1)}, u32[]{:S(2)}, u32[]{:S(2)}) collective-permute-start(bf16[1,1,64,1408]{3,2,1,0:T(8,128)(2,1)S(1)} %bitcast.197), channel_id=1, source_target_pairs={{0,8},{2,10},{4,12},{6,14},{8,0},{10,2},{12,4},{14,6},{16,24},{18,... | collective-permute-start | bytes 540680 | tf_op jit(solution)/shard_map/ppermute | solution.py:786
  314.5 23.1 %collective-permute-start.28 = (bf16[8,1,64,1024]{3,2,1,0:T(8,128)(2,1)S(1)}, bf16[8,1,64,1024]{3,2,1,0:T(8,128)(2,1)}, u32[]{:S(2)}, u32[]{:S(2)}) collective-permute-start(bf16[8,1,64,1024]{3,2,1,0:T(8,128)(2,1)S(1)} %bitcast.183), channel_id=1, source_target_pairs={{0,2},{2,0},{4,6},{6,4},{8,10},{10,8},{12,14},{14,12},{16,18},{18,... | collective-permute-start | bytes 3145736 | tf_op jit(solution)/shard_map/ppermute | solution.py:786
  325.3 16.1 %collective-permute-start.16 = (bf16[4,1,64,1408]{3,2,0,1:T(8,128)(2,1)S(1)}, bf16[4,1,64,1408]{3,2,0,1:T(8,128)(2,1)}, u32[]{:S(2)}, u32[]{:S(2)}) collective-permute-start(bf16[4,1,64,1408]{3,2,0,1:T(8,128)(2,1)S(1)} %pad_maximum_fusion.6), channel_id=1, source_target_pairs={{0,4},{2,6},{4,0},{6,2},{8,12},{10,14},{12,8},{14,10},{16,20},{18,... | collective-permute-start | bytes 2162696 | tf_op jit(solution)/shard_map/ppermute | solution.py:786
  342.9 6.6 %collective-permute-start.17 = (bf16[8,1,64,1408]{3,2,0,1:T(8,128)(2,1)S(1)}, bf16[8,1,64,1408]{3,2,0,1:T(8,128)(2,1)S(1)}, u32[]{:S(2)}, u32[]{:S(2)}) collective-permute-start(bf16[8,1,64,1408]{3,2,0,1:T(8,128)(2,1)S(1)} %bitcast.179), channel_id=1, source_target_pairs={{0,2},{2,0},{4,6},{6,4},{8,10},{10,8},{12,14},{14,12},{16,18},{18,... | collective-permute-start | bytes 4325384 | tf_op jit(solution)/shard_map/ppermute | solution.py:786
  (73 other events, 265.4 us)
Sparse Core Ops, SparseCore 0:
  103.9 193.9 all-reduce.8
